TPU v7x, 32 devices: a whole 2x2x4 slice. The times are simulated.
32 devices in a mesh: dp: 2 (over core), ctx: 4 (over y, x), exp: 4 (over z).
Axes of the slice: x: 2, y: 2, z: 4, core: 2. Of those that a mesh axis runs over, the one named last changes fastest.
Arguments:
- prompt_x: bfloat16 [8, 512, 2048], P(('dp', 'exp'), 'ctx'), may hold values from -6 to 6
- cont_x: bfloat16 [8, 32, 2048], P(('dp', 'exp'), 'ctx'), may hold values from -6 to 6
- cont_ids: int32 [8, 4, 8], P(('dp', 'exp'), 'ctx'), may hold values from 0 to 2, never falling along the last dimension, each value on 1 to 4 neighbouring positions
- routes: int32 [8, 4, 136, 8], P(('dp', 'exp'), 'ctx'), may hold values from 0 to 15, all different within a row; in each aligned block of 136 rows (0 to 135, 136 to 271, ..., all dimensions but the last counted through in order) at most 72 rows name the same one
- qkv_weight: bfloat16 [2048, 6144], P(('dp', 'ctx', 'exp')), may hold values from -0.125 to 0.125
- out_weight: bfloat16 [2048, 2048], P(('dp', 'ctx', 'exp')), may hold values from -1 to 1
- router_weight: bfloat16 [2048, 16], P(('dp', 'ctx', 'exp')), may hold values from -0.0625 to 0.0625
- norm_gains: bfloat16 [2048, 4], P(('dp', 'ctx', 'exp')), may hold values from 0.25 to 1.75
- gate_up_weight: bfloat16 [16, 2048, 2048], P(('ctx', 'exp')), may hold values from -0.125 to 0.125
- down_weight: bfloat16 [16, 1024, 2048], P(('ctx', 'exp')), may hold values from -1.5 to 1.5
- prompt_cot: bfloat16 [8, 512, 2048], P(('dp', 'exp'), 'ctx'), may hold values from -6 to 6
- cont_cot: bfloat16 [8, 32, 2048], P(('dp', 'exp'), 'ctx'), may hold values from -6 to 6
Outputs:
- out_prompt: bfloat16 [8, 512, 2048], P(('dp', 'exp'), 'ctx')
- out_cont: bfloat16 [8, 32, 2048], P(('dp', 'exp'), 'ctx')
- grad_prompt: float32 [8, 512, 2048], P(('dp', 'exp'), 'ctx')
- grad_cont: float32 [8, 32, 2048], P(('dp', 'exp'), 'ctx')
- grad_qkv: float32 [2048, 6144], P(('dp', 'ctx', 'exp'))
- grad_out: float32 [2048, 2048], P(('dp', 'ctx', 'exp'))
- grad_router: float32 [2048, 16], P(('dp', 'ctx', 'exp'))
- grad_gains: float32 [2048, 4], P(('dp', 'ctx', 'exp'))
- grad_gate_up: float32 [16, 2048, 2048], P(('ctx', 'exp'), 'dp')
- grad_down: float32 [16, 1024, 2048], P(('ctx', 'exp'), 'dp')
Inputs may be any that keep to these rules, and one draw needn't show every extreme that they name: `routes`: each row names 8 different experts; the rows of one device name one expert at most 72 times, a bound that some block reaches. `cont_ids`: along each device's 8 positions the numbers never fall; each of the 3 continuations has 1 to 4 positions and one has exactly 4.
All inputs are finite; a program needn't handle non-finite values.
Results may differ from a plain program's by a relative error of at most 0.018.
Values may be sent and summed in bfloat16 or wider, within the bound.
No kernel may reach another device: no remote copies, remote signals or barrier semaphores. Data moves between devices by JAX's collectives and lax.ppermute only.
A program may use at most 256 MiB of HBM per device.

v0:
```python
import jax
import jax.numpy as jnp
from jax import lax
from jax.sharding import PartitionSpec as P

D = 2048
HEADS = 16
HEAD_DIM = 128
FF = 1024
TOP = 8


NORM_EPS = 1e-05
ROPE_BASE = 10000.0
NEGATIVE = -1e30
HIGHEST_PREC = lax.Precision.HIGHEST


def row_scale(values):
    return lax.rsqrt(jnp.mean(values * values, axis=-1, keepdims=True) + NORM_EPS)


def rope_tables(position, half_dim):
    inverse = ROPE_BASE ** (-jnp.arange(half_dim, dtype=jnp.float32) / half_dim)
    angles = position[:, None] * inverse[None, :]
    return (jnp.cos(angles), jnp.sin(angles))


def rotate(values, cosine, sine_rows):
    row_count = values.shape[0]
    shaped = values.reshape(row_count, HEADS, HEAD_DIM)
    half_dim = HEAD_DIM // 2
    first_half = shaped[..., :half_dim]
    second_half = shaped[..., half_dim:]
    cos_heads = cosine[:, None, :]
    sin_heads = sine_rows[:, None, :]
    turned = jnp.concatenate(
        [
            first_half * cos_heads - second_half * sin_heads,
            second_half * cos_heads + first_half * sin_heads,
        ],
        axis=-1,
    )
    return turned.reshape(row_count, -1)


def norm_back(grad_rows, normed, scale_rows, gain_col):
    grad_normed = grad_rows * gain_col
    grad_input = scale_rows * (
        grad_normed - normed * jnp.mean(grad_normed * normed, axis=-1, keepdims=True)
    )
    return (grad_input, jnp.sum(grad_rows * normed, axis=0))


def body(
    prompt_x,
    cont_x,
    cont_ids,
    routes,
    qkv_weight,
    out_weight,
    router_weight,
    norm_gains,
    gate_up_weight,
    down_weight,
    prompt_cot,
    cont_cot,
):
    gathered = (
        lax.all_gather(qkv_weight, ("dp", "ctx", "exp"), axis=0, tiled=True),
        lax.all_gather(out_weight, ("dp", "ctx", "exp"), axis=0, tiled=True),
        lax.all_gather(router_weight, ("dp", "ctx", "exp"), axis=0, tiled=True),
        lax.all_gather(norm_gains, ("dp", "ctx", "exp"), axis=0, tiled=True),
    )
    w_qkv, w_out, w_router, gain_low = gathered
    gain_cols = gain_low.astype(jnp.float32)
    prompt_rows = prompt_x[0]
    cont_rows = cont_x[0]
    prompt_len = prompt_rows.shape[0]
    cont_len = cont_rows.shape[0]
    row_count = prompt_len + cont_len
    ctx_index = lax.axis_index("ctx")
    prompt_total = prompt_len * lax.axis_size("ctx")
    experts = w_router.shape[1]
    capacity = row_count * TOP * 17 // (16 * experts)
    score_scale = HEAD_DIM ** (-0.5)
    inputs = jnp.concatenate([prompt_rows, cont_rows], axis=0).astype(jnp.float32)
    scale_in = row_scale(inputs)
    normed_in = inputs * scale_in
    hidden_in = (normed_in * gain_cols[:, 0]).astype(jnp.bfloat16)
    projected = jnp.dot(hidden_in, w_qkv, preferred_element_type=jnp.float32)
    scale_query = row_scale(projected[:, :D])
    normed_query = projected[:, :D] * scale_query
    scale_key = row_scale(projected[:, D : 2 * D])
    normed_key = projected[:, D : 2 * D] * scale_key
    seg_ids = cont_ids[0, 0]
    starts = jnp.sum((seg_ids[None, :] < seg_ids[:, None]).astype(jnp.int32), axis=1)
    within = jnp.arange(cont_len, dtype=jnp.int32) - starts
    global_query = ctx_index * prompt_len + jnp.arange(row_count, dtype=jnp.int32)
    position = jnp.concatenate([global_query[:prompt_len], prompt_total + within]).astype(
        jnp.float32
    )
    cosine, sine_rows = rope_tables(position, HEAD_DIM // 2)
    query_b = rotate(normed_query * gain_cols[:, 1], cosine, sine_rows).astype(jnp.bfloat16)
    key_b = rotate(normed_key * gain_cols[:, 2], cosine, sine_rows).astype(jnp.bfloat16)
    value_b = projected[:, 2 * D :].astype(jnp.bfloat16)
    prompt_keys, prompt_values = (
        lax.all_gather(key_b[:prompt_len], "ctx", axis=0, tiled=True),
        lax.all_gather(value_b[:prompt_len], "ctx", axis=0, tiled=True),
    )
    key_all = jnp.concatenate([prompt_keys, key_b[prompt_len:]], axis=0)
    value_all = jnp.concatenate([prompt_values, value_b[prompt_len:]], axis=0)
    key_count = prompt_total + cont_len
    query_idx = jnp.arange(row_count, dtype=jnp.int32)
    key_idx = jnp.arange(key_count, dtype=jnp.int32)
    query_prompt = query_idx < prompt_len
    key_prompt = key_idx < prompt_total
    seg_query = jnp.concatenate([jnp.full((prompt_len,), -1, jnp.int32), seg_ids])
    seg_key = jnp.concatenate([jnp.full((prompt_total,), -2, jnp.int32), seg_ids])
    same_doc = (seg_query[:, None] == seg_key[None, :]) & (
        (key_idx - prompt_total)[None, :] <= (query_idx - prompt_len)[:, None]
    )
    allowed = jnp.where(
        query_prompt[:, None],
        key_prompt[None, :] & (key_idx[None, :] <= global_query[:, None]),
        key_prompt[None, :] | same_doc,
    )
    heads_q = query_b.reshape(row_count, HEADS, HEAD_DIM)
    heads_k = key_all.reshape(key_count, HEADS, HEAD_DIM)
    heads_v = value_all.reshape(key_count, HEADS, HEAD_DIM)

    def score_block():
        raw_scores = (
            jnp.einsum("rhd,khd->hrk", heads_q, heads_k, preferred_element_type=jnp.float32)
            * score_scale
        )
        return jnp.where(allowed[None], raw_scores, NEGATIVE)

    scores = score_block()
    row_max = jnp.max(scores, axis=-1, keepdims=True)
    log_total = row_max + jnp.log(jnp.sum(jnp.exp(scores - row_max), axis=-1, keepdims=True))
    attention_b = jnp.exp(scores - log_total).astype(jnp.bfloat16)
    mixed_b = (
        jnp.einsum("hrk,khd->rhd", attention_b, heads_v, preferred_element_type=jnp.float32)
        .reshape(row_count, D)
        .astype(jnp.bfloat16)
    )
    mid_rows = inputs + jnp.dot(mixed_b, w_out, preferred_element_type=jnp.float32)
    scale_ffn = row_scale(mid_rows)
    normed_ffn = mid_rows * scale_ffn
    hidden_ffn = (normed_ffn * gain_cols[:, 3]).astype(jnp.bfloat16)
    logits = jnp.dot(hidden_ffn, w_router, preferred_element_type=jnp.float32)
    shifted = jnp.exp(logits - jnp.max(logits, axis=-1, keepdims=True))
    router = shifted / jnp.sum(shifted, axis=-1, keepdims=True)
    route_rows = routes[0, 0]
    choose_f = (
        route_rows[:, :, None] == jnp.arange(experts, dtype=jnp.int32)[None, None, :]
    ).astype(jnp.float32)
    gate_probs = jnp.sum(choose_f * router[:, None, :], axis=-1)
    routed = jnp.sum(choose_f, axis=1)
    earlier = (jnp.arange(row_count)[:, None] > jnp.arange(row_count)[None, :]).astype(jnp.float32)
    rank_rows = jnp.dot(earlier, routed, precision=HIGHEST_PREC)
    slot_rows = jnp.sum(choose_f * rank_rows[:, None, :], axis=-1).astype(jnp.int32)
    slot_index = (slot_rows * experts + route_rows).reshape(-1)
    slot_table = (
        jnp.full((capacity * experts,), row_count * TOP, jnp.int32)
        .at[slot_index]
        .set(jnp.arange(row_count * TOP, dtype=jnp.int32))
    )
    padded_rows = jnp.concatenate([hidden_ffn, jnp.zeros((1, D), jnp.bfloat16)], axis=0)
    outgoing = padded_rows[slot_table // TOP].reshape(capacity, experts, D)
    w_gate_up = gate_up_weight[0]
    w_down = down_weight[0]
    arrived = lax.all_to_all(outgoing, ("ctx", "exp"), split_axis=1, concat_axis=1, tiled=True)
    item_count = arrived.shape[0]
    flat_rows = arrived.reshape(-1, D)
    gate_up = jnp.dot(flat_rows, w_gate_up, preferred_element_type=jnp.float32)
    activated = (jax.nn.silu(gate_up[:, :FF]) * gate_up[:, FF:]).astype(jnp.bfloat16)
    produced = jnp.dot(activated, w_down, preferred_element_type=jnp.float32).astype(jnp.bfloat16)
    returned = lax.all_to_all(
        produced.reshape(item_count, experts, D),
        ("ctx", "exp"),
        split_axis=1,
        concat_axis=1,
        tiled=True,
    )
    expert_out = returned.reshape(capacity * experts, D)[slot_index].reshape(row_count, TOP, D)
    mixture = jnp.sum(gate_probs[:, :, None] * expert_out.astype(jnp.float32), axis=1)
    final_rows = (mid_rows + mixture).astype(jnp.bfloat16)
    cotangent = jnp.concatenate([prompt_cot[0], cont_cot[0]], axis=0).astype(jnp.float32)
    route_grad = (gate_probs[:, :, None] * cotangent[:, None, :]).astype(jnp.bfloat16)
    gate_grad = jnp.sum(cotangent[:, None, :] * expert_out.astype(jnp.float32), axis=-1)
    prob_grad = jnp.sum(choose_f * gate_grad[:, :, None], axis=1)
    logit_grad = router * (prob_grad - jnp.sum(router * prob_grad, axis=-1, keepdims=True))
    router_f = w_router.astype(jnp.float32)
    ffn_grad = jnp.dot(logit_grad, router_f.T, precision=HIGHEST_PREC)
    router_grad = jnp.einsum(
        "rd,re->de", hidden_ffn.astype(jnp.float32), logit_grad, precision=HIGHEST_PREC
    )
    grad_pad = jnp.concatenate(
        [route_grad.reshape(row_count * TOP, D), jnp.zeros((1, D), jnp.bfloat16)], axis=0
    )
    grad_outgoing = grad_pad[slot_table].reshape(capacity, experts, D)
    grad_arrived = lax.all_to_all(
        grad_outgoing, ("ctx", "exp"), split_axis=1, concat_axis=1, tiled=True
    )
    grad_flat = grad_arrived.reshape(-1, D)
    arrived_flat = arrived.reshape(-1, D)
    gate_up = gate_up.reshape(item_count, experts, 2 * FF).reshape(-1, 2 * FF)
    gate_part = gate_up[:, :FF]
    up_part = gate_up[:, FF:]
    sigmoid_gate = jax.nn.sigmoid(gate_part)
    swish = jax.nn.silu(gate_part)
    activated = (swish * up_part).astype(jnp.bfloat16)
    act_grad = jnp.dot(grad_flat, w_down.T, preferred_element_type=jnp.float32)
    gate_part_grad = act_grad * up_part * sigmoid_gate * (1.0 + gate_part * (1.0 - sigmoid_gate))
    up_part_grad = act_grad * swish
    gu_grad = jnp.concatenate([gate_part_grad, up_part_grad], axis=1).astype(jnp.bfloat16)
    row_grad = jnp.dot(gu_grad, w_gate_up.T, preferred_element_type=jnp.float32).astype(
        jnp.bfloat16
    )
    gate_up_local = jnp.einsum(
        "nd,nf->df", arrived_flat, gu_grad, preferred_element_type=jnp.float32
    )[None]
    down_local = jnp.einsum("nf,nd->fd", activated, grad_flat, preferred_element_type=jnp.float32)[
        None
    ]
    returned_grad = lax.all_to_all(
        row_grad.reshape(capacity, experts, D),
        ("ctx", "exp"),
        split_axis=1,
        concat_axis=1,
        tiled=True,
    )
    token_grad = returned_grad.reshape(capacity * experts, D)[slot_index].reshape(row_count, TOP, D)
    ffn_grad = ffn_grad + jnp.sum(token_grad.astype(jnp.float32), axis=1)
    mid_norm_grad, ffn_gain_grad = norm_back(ffn_grad, normed_ffn, scale_ffn, gain_cols[:, 3])
    mid_grad = cotangent + mid_norm_grad
    attn_grad = mid_grad.astype(jnp.bfloat16)
    out_w_grad = jnp.einsum("rd,re->de", mixed_b, attn_grad, preferred_element_type=jnp.float32)
    mixed_grad = jnp.dot(attn_grad, w_out.T, preferred_element_type=jnp.float32).astype(
        jnp.bfloat16
    )
    mixed_heads = mixed_grad.reshape(row_count, HEADS, HEAD_DIM)
    scores = score_block()
    attention = jnp.exp(scores - log_total)
    attention_b = attention.astype(jnp.bfloat16)
    prob_att = jnp.einsum("rhd,khd->hrk", mixed_heads, heads_v, preferred_element_type=jnp.float32)
    delta = jnp.sum(attention * prob_att, axis=-1, keepdims=True)
    score_grad = (attention * (prob_att - delta)).astype(jnp.bfloat16)
    query_grad = (
        jnp.einsum("hrk,khd->rhd", score_grad, heads_k, preferred_element_type=jnp.float32).reshape(
            row_count, D
        )
        * score_scale
    )
    key_grad = (
        jnp.einsum("hrk,rhd->khd", score_grad, heads_q, preferred_element_type=jnp.float32).reshape(
            key_count, D
        )
        * score_scale
    )
    value_grad = jnp.einsum(
        "hrk,rhd->khd", attention_b, mixed_heads, preferred_element_type=jnp.float32
    ).reshape(key_count, D)
    prompt_key_grad, prompt_value_grad = (
        lax.psum_scatter(
            key_grad[:prompt_total].astype(jnp.bfloat16), "ctx", scatter_dimension=0, tiled=True
        ).astype(jnp.float32),
        lax.psum_scatter(
            value_grad[:prompt_total].astype(jnp.bfloat16), "ctx", scatter_dimension=0, tiled=True
        ).astype(jnp.float32),
    )
    key_grad_local = jnp.concatenate([prompt_key_grad, key_grad[prompt_total:]], axis=0)
    value_grad_local = jnp.concatenate([prompt_value_grad, value_grad[prompt_total:]], axis=0)
    query_turn_grad = rotate(query_grad, cosine, -sine_rows)
    key_turn_grad = rotate(key_grad_local, cosine, -sine_rows)
    raw_query_grad, query_gain_grad = norm_back(
        query_turn_grad, normed_query, scale_query, gain_cols[:, 1]
    )
    raw_key_grad, key_gain_grad = norm_back(key_turn_grad, normed_key, scale_key, gain_cols[:, 2])
    proj_grad = jnp.concatenate([raw_query_grad, raw_key_grad, value_grad_local], axis=1).astype(
        jnp.bfloat16
    )
    hidden_grad = jnp.dot(proj_grad, w_qkv.T, preferred_element_type=jnp.float32)
    qkv_w_grad = jnp.einsum("rd,re->de", hidden_in, proj_grad, preferred_element_type=jnp.float32)
    in_norm_grad, in_gain_grad = norm_back(hidden_grad, normed_in, scale_in, gain_cols[:, 0])
    input_grad = mid_grad + in_norm_grad
    gains_grad = jnp.stack([in_gain_grad, query_gain_grad, key_gain_grad, ffn_gain_grad], axis=1)
    summed = (
        lax.psum_scatter(qkv_w_grad, ("dp", "ctx", "exp"), scatter_dimension=0, tiled=True),
        lax.psum_scatter(out_w_grad, ("dp", "ctx", "exp"), scatter_dimension=0, tiled=True),
        lax.psum_scatter(router_grad, ("dp", "ctx", "exp"), scatter_dimension=0, tiled=True),
        lax.psum_scatter(gains_grad, ("dp", "ctx", "exp"), scatter_dimension=0, tiled=True),
    )
    expert_sums = (
        lax.psum_scatter(
            gate_up_local.astype(jnp.bfloat16), "dp", scatter_dimension=1, tiled=True
        ).astype(jnp.float32),
        lax.psum_scatter(
            down_local.astype(jnp.bfloat16), "dp", scatter_dimension=1, tiled=True
        ).astype(jnp.float32),
    )
    return (
        final_rows[:prompt_len][None],
        final_rows[prompt_len:][None],
        input_grad[:prompt_len][None],
        input_grad[prompt_len:][None],
        summed[0],
        summed[1],
        summed[2],
        summed[3],
        expert_sums[0],
        expert_sums[1],
    )


def solution(mesh):
    return jax.shard_map(
        body,
        mesh=mesh,
        in_specs=(
            P(("dp", "exp"), "ctx", None),
            P(("dp", "exp"), "ctx", None),
            P(("dp", "exp"), "ctx", None),
            P(("dp", "exp"), "ctx", None, None),
            P(("dp", "ctx", "exp"), None),
            P(("dp", "ctx", "exp"), None),
            P(("dp", "ctx", "exp"), None),
            P(("dp", "ctx", "exp"), None),
            P(("ctx", "exp"), None, None),
            P(("ctx", "exp"), None, None),
            P(("dp", "exp"), "ctx", None),
            P(("dp", "exp"), "ctx", None),
        ),
        out_specs=(
            P(("dp", "exp"), "ctx", None),
            P(("dp", "exp"), "ctx", None),
            P(("dp", "exp"), "ctx", None),
            P(("dp", "exp"), "ctx", None),
            P(("dp", "ctx", "exp"), None),
            P(("dp", "ctx", "exp"), None),
            P(("dp", "ctx", "exp"), None),
            P(("dp", "ctx", "exp"), None),
            P(("ctx", "exp"), "dp", None),
            P(("ctx", "exp"), "dp", None),
        ),
        check_vma=False,
    )
```

profile of v0, /device:TPU:16, one launch (start us, length us, event | category | flops | bytes accessed | tf_op | source)
XLA Modules:
  0.0 2144.1 jit_solution(10908300873772648905)
XLA Ops:
  8.0 66.3 %all-gather = bf16[32,64,4]{1,2,0:T(4,128)(2,1)S(1)} all-gather(bf16[1,64,4]{1,2,0:T(4,128)(2,1)} %bitcast.238), channel_id=1, replica_groups=mesh['dp'=2,'ctx'=4,'exp'=4] {'dp','ctx','exp'}, dimensions={0}, use_global_device_ids=true | all-gather | bytes 16896 | tf_op jit(solution)/shard_map/all_gather | solution.py:73
  77.6 88.5 %all-gather.7.cloned.1.call-done = bf16[2048,6144]{1,0:T(8,128)(2,1)} async-done(((bf16[64,6144]{1,0:T(8,128)(2,1)}), bf16[2048,6144]{1,0:T(8,128)(2,1)}) %all-gather.7.cloned.1.call-update) | async-done | bytes 25165840 | tf_op jit(solution)/shard_map/all_gather | solution.py:70
  166.1 13.1 fusion.90
  185.0 1.9 slice.158
  187.7 64.8 %all-gather.1 = bf16[32,64,16]{1,2,0:T(8,128)(2,1)S(1)} all-gather(bf16[1,64,16]{1,2,0:T(8,128)(2,1)S(1)} %bitcast.234), channel_id=1, replica_groups=mesh['dp'=2,'ctx'=4,'exp'=4] {'dp','ctx','exp'}, dimensions={0}, use_global_device_ids=true | all-gather | bytes 67584 | tf_op jit(solution)/shard_map/all_gather | solution.py:72
  254.5 1.8 pad_maximum_fusion.3
  258.0 1.9 exponential_reduce_fusion
  260.5 4.7 fusion.31
  265.3 72.3 %all-gather.13.cloned.1.call-done = bf16[2048,2048]{1,0:T(8,128)(2,1)} async-done(((bf16[64,2048]{1,0:T(8,128)(2,1)}), bf16[2048,2048]{1,0:T(8,128)(2,1)}) %all-gather.13.cloned.1.call-update) | async-done | bytes 8388624 | tf_op jit(solution)/shard_map/all_gather | solution.py:71
  337.6 4.9 multiply_reduce_fusion.5
  343.3 6.4 scatter_custom_fusion
  349.9 6.1 gather_fusion
  356.0 7.0 copy.262
  363.0 6.0 all-to-all-start
  369.9 2.7 concatenate.74
  372.6 13.5 gather_fusion.2
  386.2 7.0 copy.268
  393.2 82.0 %all-to-all-done = bf16[72,16,2048]{2,0,1:T(8,128)(2,1)} async-done(((bf16[72,16,2048]{2,0,1:T(8,128)(2,1)}), bf16[72,16,2048]{2,0,1:T(8,128)(2,1)}, u32[]{:S(2)}, u32[]{:S(2)}) %all-to-all-start) | async-done | bytes 4718624 | tf_op jit(solution)/shard_map/all_to_all | solution.py:174
  475.1 10.4 all-to-all-start.2
  485.6 4.9 copy.263
  490.5 2.2 copy-done.16
  492.7 14.7 fusion.5
  507.4 84.4 %all-to-all-done.2 = bf16[72,16,2048]{2,0,1:T(8,128)(2,1)} async-done(((bf16[72,16,2048]{2,0,1:T(8,128)(2,1)}), bf16[72,16,2048]{2,0,1:T(8,128)(2,1)}, u32[]{:S(2)}, u32[]{:S(2)}) %all-to-all-start.2) | async-done | bytes 4718624 | tf_op jit(solution)/shard_map/all_to_all | solution.py:204
  591.8 5.1 copy.269
  596.9 13.1 multiply_convert_fusion.2
  610.1 12.2 fusion.7
  622.3 4.8 copy.272
  627.1 10.7 all-to-all-start.3
  637.8 7.6 convolution_convert_fusion
  645.4 4.7 copy.264
  650.1 92.2 %all-to-all-done.3 = bf16[72,16,2048]{2,0,1:T(8,128)(2,1)} async-done(((bf16[72,16,2048]{2,0,1:T(8,128)(2,1)}), bf16[72,16,2048]{2,0,1:T(8,128)(2,1)}, u32[]{:S(2)}, u32[]{:S(2)}) %all-to-all-start.3) | async-done | bytes 4718624 | tf_op jit(solution)/shard_map/all_to_all | solution.py:228
  742.3 15.5 all-to-all-start.1
  757.8 7.0 copy.273
  764.8 13.7 gather_fusion.3
  778.5 6.3 convert_reduce_fusion
  784.9 77.4 %all-to-all-done.1 = bf16[72,16,2048]{2,0,1:T(8,128)(2,1)} async-done(((bf16[72,16,2048]{2,0,1:T(8,128)(2,1)}), bf16[72,16,2048]{2,0,1:T(8,128)(2,1)}, u32[]{:S(2)}, u32[]{:S(2)}) %all-to-all-start.1) | async-done | bytes 4718624 | tf_op jit(solution)/shard_map/all_to_all | solution.py:180
  862.3 7.0 copy.265
  869.3 13.5 gather_fusion.1
  882.8 9.4 fusion.1
  892.3 2.3 multiply_reduce_fusion.1
  896.0 6.9 fusion.30
  903.0 2.7 multiply_reduce_fusion
  907.4 1.7 multiply_bitcast_fusion
  909.1 2.0 copy-done.9
  911.2 1.7 slice.231
  912.9 3.9 copy.278
  916.8 4.3 copy.293
  921.2 5.0 convert_bitcast_fusion.2
  929.3 9.6 convert_bitcast_fusion.1
  941.2 2.2 fusion.72
  943.4 3.8 fusion.26
  948.2 14.8 reduce-scatter.25.cloned.1.call-done
  972.0 29.3 %reduce-scatter.15.cloned.1.call-done = bf16[128,2048]{1,0:T(8,128)(2,1)} async-done(((bf16[512,2048]{1,0:T(8,128)(2,1)}), bf16[128,2048]{1,0:T(8,128)(2,1)}) %reduce-scatter.15.cloned.1.call-update) | async-done | bytes 524304 | tf_op jit(solution)/shard_map/reduce_scatter | solution.py:270
  1001.3 14.5 fusion.39
  1017.3 16.5 convert_bitcast_fusion
  1035.2 8.1 fusion.43
  1044.4 19.8 fusion.55
  1064.3 4.3 convert_element_type.173
  1070.0 90.2 %reduce-scatter.27.cloned.1.call-done = f32[64,16]{1,0:T(8,128)} async-done(((f32[2048,16]{1,0:T(8,128)}), f32[64,16]{1,0:T(8,128)}) %reduce-scatter.27.cloned.1.call-update) | async-done | bytes 4112
  1163.7 144.6 %reduce-scatter.29.cloned.1.call-done = f32[64,4]{1,0:T(8,128)} async-done(((f32[2048,4]{1,0:T(8,128)}), f32[64,4]{1,0:T(8,128)}) %reduce-scatter.29.cloned.1.call-update) | async-done | bytes 1040
  1309.7 23.9 %reduce-scatter.21.cloned.1.call-done = bf16[1,1024,2048]{2,1,0:T(8,128)(2,1)} async-done(((bf16[1,2048,2048]{2,1,0:T(8,128)(2,1)}), bf16[1,1024,2048]{2,1,0:T(8,128)(2,1)}) %reduce-scatter.21.cloned.1.call-update) | async-done | bytes 4194320 | tf_op jit(solution)/shard_map/reduce_scatter | solution.py:297
  1333.6 6.7 convert_element_type.170
  1340.3 359.3 %reduce-scatter.19.cloned.1.call-done = f32[64,2048]{1,0:T(8,128)} async-done(((f32[2048,2048]{1,0:T(8,128)}), f32[64,2048]{1,0:T(8,128)}) %reduce-scatter.19.cloned.1.call-update) | async-done | bytes 524304 | tf_op jit(solution)/shard_map/reduce_scatter | solution.py:292
  1699.6 437.4 %reduce-scatter.17.cloned.1.call-done = f32[64,6144]{1,0:T(8,128)} async-done(((f32[2048,6144]{1,0:T(8,128)}), f32[64,6144]{1,0:T(8,128)}) %reduce-scatter.17.cloned.1.call-update) | async-done | bytes 1572880 | tf_op jit(solution)/shard_map/reduce_scatter | solution.py:291
  (240 shorter events, 45.0 us)
Async XLA Ops:
  7.2 158.9 %copy-start.6 = (bf16[1,128,2048]{2,1,0:T(8,128)(2,1)S(1)}, bf16[1,128,2048]{2,1,0:T(8,128)(2,1)}, u32[]{:S(2)}) copy-start(bf16[1,128,2048]{2,1,0:T(8,128)(2,1)} %param.12) | copy-start | bytes 1572868
  7.2 158.9 %all-gather.7.cloned.1.call-start = ((), (), s32[]{:S(2)}) async-start(), calls=%async_computation.12 | async-start | bytes 25952256 | tf_op jit(solution)/shard_map/all_gather | solution.py:70
  7.9 246.5 %all-gather.11.cloned.1.call-start = ((), (), s32[]{:S(2)}) async-start(), calls=%async_computation.14 | async-start | bytes 2621440 | tf_op jit(solution)/shard_map/all_gather | solution.py:108
  76.6 102.6 %copy-start.44 = (f32[136]{0:T(256)}, f32[136]{0:T(256)S(1)}, u32[]{:S(2)}) copy-start(f32[136]{0:T(256)S(1)} %add_rsqrt_fusion.3) | copy-start | bytes 1636
  77.5 104.5 %copy-start.30 = (f32[136,64]{1,0:T(8,128)}, f32[136,64]{1,0:T(8,128)S(1)}, u32[]{:S(2)}) copy-start(f32[136,64]{1,0:T(8,128)S(1)} %get-tuple-element.61) | copy-start | bytes 104452
  77.6 101.6 %copy-start.33 = (f32[2048,1]{0,1:T(1,128)}, f32[2048,1]{0,1:T(1,128)S(1)}, u32[]{:S(2)}) copy-start(f32[2048,1]{0,1:T(1,128)S(1)} %get-tuple-element.56) | copy-start | bytes 24580
  77.6 101.9 %copy-start.36 = (f32[2048,1]{0,1:T(1,128)}, f32[2048,1]{0,1:T(1,128)S(1)}, u32[]{:S(2)}) copy-start(f32[2048,1]{0,1:T(1,128)S(1)} %get-tuple-element.54) | copy-start | bytes 24580
  77.6 101.9 %copy-start.38 = (f32[2048,1]{0,1:T(1,128)}, f32[2048,1]{0,1:T(1,128)S(1)}, u32[]{:S(2)}) copy-start(f32[2048,1]{0,1:T(1,128)S(1)} %get-tuple-element.55) | copy-start | bytes 24580
  183.5 72.8 %copy-start.12 = (bf16[136,16,64]{2,0,1:T(8,128)(2,1)}, bf16[136,16,64]{2,0,1:T(8,128)(2,1)S(1)}, u32[]{:S(2)}) copy-start(bf16[136,16,64]{2,0,1:T(8,128)(2,1)S(1)} %get-tuple-element.35) | copy-start | bytes 835588
  183.5 72.8 %copy-start.14 = (bf16[136,16,64]{2,0,1:T(8,128)(2,1)}, bf16[136,16,64]{2,0,1:T(8,128)(2,1)S(1)}, u32[]{:S(2)}) copy-start(bf16[136,16,64]{2,0,1:T(8,128)(2,1)S(1)} %get-tuple-element.36) | copy-start | bytes 835588
  183.9 3.6 copy-start.53
  183.9 3.6 copy-start.41
  183.9 3.8 copy-start.52
  184.9 75.6 %all-gather.9.cloned.1.call-start = ((), (), s32[]{:S(2)}) async-start(), calls=%async_computation.13 | async-start | bytes 2621440 | tf_op jit(solution)/shard_map/all_gather | solution.py:109
  186.9 150.7 %all-gather.13.cloned.1.call-start = ((), (), s32[]{:S(2)}) async-start(), calls=%async_computation.15 | async-start | bytes 8650752 | tf_op jit(solution)/shard_map/all_gather | solution.py:71
  253.3 7.2 copy-start.25
  254.1 6.5 copy-start.46
  258.0 2.5 copy-start
  260.5 4.8 copy-start.42
  260.5 77.1 %copy-start.28 = (bf16[1,8,2048]{2,1,0:T(8,128)(2,1)S(1)}, bf16[1,8,2048]{2,1,0:T(8,128)(2,1)}, u32[]{:S(2)}) copy-start(bf16[1,8,2048]{2,1,0:T(8,128)(2,1)} %param.13) | copy-start | bytes 98308
  265.3 77.2 %copy-start.20 = (bf16[16,17,8,128]{3,2,1,0:T(8,128)(2,1)}, bf16[16,17,8,128]{3,2,1,0:T(8,128)(2,1)S(1)}, u32[]{:S(2)}) copy-start(bf16[16,17,8,128]{3,2,1,0:T(8,128)(2,1)S(1)} %fusion.31) | copy-start | bytes 1671172
  342.7 13.3 copy-start.10
  363.0 6.0 copy-start.24
  363.0 6.0 copy-start.40
  363.0 112.1 %all-to-all-start = ((bf16[72,16,2048]{2,0,1:T(8,128)(2,1)}), bf16[72,16,2048]{2,0,1:T(8,128)(2,1)}, u32[]{:S(2)}, u32[]{:S(2)}) async-start(bf16[72,16,2048]{2,0,1:T(8,128)(2,1)} %copy.262), calls=%async_computation | async-start | bytes 9437184 | tf_op jit(solution)/shard_map/all_to_all | solution.py:174
  475.1 116.7 %all-to-all-start.2 = ((bf16[72,16,2048]{2,0,1:T(8,128)(2,1)}), bf16[72,16,2048]{2,0,1:T(8,128)(2,1)}, u32[]{:S(2)}, u32[]{:S(2)}) async-start(bf16[72,16,2048]{2,0,1:T(8,128)(2,1)} %copy.268), calls=%async_computation.2 | async-start | bytes 9437184 | tf_op jit(solution)/shard_map/all_to_all | solution.py:204
  490.5 2.2 copy-start.16
  591.8 5.1 copy-start.54
  591.8 18.3 slice-start.2
  596.9 13.2 copy-start.17
  596.9 13.2 slice-start.3
  610.1 12.2 copy-start.56
  627.1 115.2 %all-to-all-start.3 = ((bf16[72,16,2048]{2,0,1:T(8,128)(2,1)}), bf16[72,16,2048]{2,0,1:T(8,128)(2,1)}, u32[]{:S(2)}, u32[]{:S(2)}) async-start(bf16[72,16,2048]{2,0,1:T(8,128)(2,1)} %copy.272), calls=%async_computation.3 | async-start | bytes 9437184 | tf_op jit(solution)/shard_map/all_to_all | solution.py:228
  742.3 120.0 %all-to-all-start.1 = ((bf16[72,16,2048]{2,0,1:T(8,128)(2,1)}), bf16[72,16,2048]{2,0,1:T(8,128)(2,1)}, u32[]{:S(2)}, u32[]{:S(2)}) async-start(bf16[72,16,2048]{2,0,1:T(8,128)(2,1)} %copy.264), calls=%async_computation.1 | async-start | bytes 9437184 | tf_op jit(solution)/shard_map/all_to_all | solution.py:180
  757.7 205.3 %reduce-scatter.25.cloned.1.call-start = ((), (), s32[]{:S(2)}) async-start(), calls=%async_computation.21 | async-start | bytes 2621440
  892.2 2.5 copy-start.18
  894.7 8.2 slice-start
  895.9 7.0 copy-start.4
  895.9 7.0 slice-start.1
  895.9 7.0 copy-start.26
  895.9 7.0 copy-start.43
  895.9 7.0 copy-start.47
  896.0 7.0 copy-start.55
  909.1 2.0 copy-start.9
  921.2 80.1 %reduce-scatter.15.cloned.1.call-start = ((), (), s32[]{:S(2)}) async-start(), calls=%async_computation.16 | async-start | bytes 2621440 | tf_op jit(solution)/shard_map/reduce_scatter | solution.py:270
  929.3 135.0 %reduce-scatter.23.cloned.1.call-start = ((), (), s32[]{:S(2)}) async-start(), calls=%async_computation.20 | async-start | bytes 6291456 | tf_op jit(solution)/shard_map/reduce_scatter | solution.py:300
  938.9 2.3 copy-start.11
  939.0 221.2 %reduce-scatter.27.cloned.1.call-start = ((), (), s32[]{:S(2)}) async-start(), calls=%async_computation.22 | async-start | bytes 1081344
  947.3 17.1 copy-start.19
  948.1 360.2 %reduce-scatter.29.cloned.1.call-start = ((), (), s32[]{:S(2)}) async-start(), calls=%async_computation.23 | async-start | bytes 1081344
  965.8 2.2 copy-start.8
  965.8 2.2 copy-start.31
  965.8 2.2 copy-start.35
  968.0 1.9 copy-start.2
  968.0 1.9 copy-start.37
  971.0 30.4 %copy-start.7 = (bf16[1,128,2048]{2,1,0:T(8,128)(2,1)S(1)}, bf16[1,128,2048]{2,1,0:T(8,128)(2,1)}, u32[]{:S(2)}) copy-start(bf16[1,128,2048]{2,1,0:T(8,128)(2,1)} %param.12) | copy-start | bytes 1572868
  971.0 30.4 %copy-start.29 = (bf16[1,8,2048]{2,1,0:T(8,128)(2,1)S(1)}, bf16[1,8,2048]{2,1,0:T(8,128)(2,1)}, u32[]{:S(2)}) copy-start(bf16[1,8,2048]{2,1,0:T(8,128)(2,1)} %param.13) | copy-start | bytes 98308
  971.0 30.4 %copy-start.34 = (f32[2048,1]{0,1:T(1,128)S(1)}, f32[2048,1]{0,1:T(1,128)}, u32[]{:S(2)}) copy-start(f32[2048,1]{0,1:T(1,128)} %copy-done.33) | copy-start | bytes 24580
  971.0 30.3 %copy-start.45 = (f32[136]{0:T(256)S(1)}, f32[136]{0:T(256)}, u32[]{:S(2)}) copy-start(f32[136]{0:T(256)} %copy-done.44) | copy-start | bytes 1636
  1017.3 316.4 %reduce-scatter.21.cloned.1.call-start = ((), (), s32[]{:S(2)}) async-start(), calls=%async_computation.19 | async-start | bytes 12582912 | tf_op jit(solution)/shard_map/reduce_scatter | solution.py:297
  1033.8 665.8 %reduce-scatter.19.cloned.1.call-start = ((), (), s32[]{:S(2)}) async-start(), calls=%async_computation.18 | async-start | bytes 17301504 | tf_op jit(solution)/shard_map/reduce_scatter | solution.py:292
  1043.4 1093.7 %reduce-scatter.17.cloned.1.call-start = ((), (), s32[]{:S(2)}) async-start(), calls=%async_computation.17 | async-start | bytes 51904512 | tf_op jit(solution)/shard_map/reduce_scatter | solution.py:291
  1064.3 4.3 copy-start.22
  1064.3 97.3 %copy-start.27 = (f32[136,2048]{1,0:T(8,128)S(1)}, f32[136,2048]{1,0:T(8,128)}, u32[]{:S(2)}) copy-start(f32[136,2048]{1,0:T(8,128)} %get-tuple-element.73) | copy-start | bytes 3342340
  (13 other events, 20.6 us)
Sparse Core Ops, SparseCore 0:
  10.9 155.1 all-gather.6
  185.0 34.3 all-gather.10
  221.9 35.7 all-gather.8
  260.5 77.0 all-gather.12
  921.3 41.6 reduce-scatter.24
  966.1 35.1 reduce-scatter.14
  1004.2 12.3 reduce-scatter.22
  1019.0 141.1 reduce-scatter.26
  1162.4 145.8 reduce-scatter.28
  1311.1 22.4 reduce-scatter.20
  1336.5 363.0 reduce-scatter.18
  1706.5 430.5 reduce-scatter.16
where the time goes:
time: 2150 us; the launch traced here: 2140 us
  waiting for transfers between devices  1600 us (74%)
  matrix products  166 us (8%)
  local copies, waits for them, and re-layouts  147 us (7%)
  blocking collectives  131 us (6%)
  other arithmetic  43.5 us (2%)
  starting transfers between devices  43.1 us (2%)
    reduce_scatter x1, waiting for transfers between devices, body(): lax.psum_scatter(qkv_w_grad, ('dp', 'ctx', 'exp'), scatter_dimension=0, t...  437 us
    reduce_scatter x1, waiting for transfers between devices, body(): lax.psum_scatter(out_w_grad, ('dp', 'ctx', 'exp'), scatter_dimension=0, t...  359 us
    unnamed x15, waiting for transfers between devices  251 us
    all_to_all x1, waiting for transfers between devices, body(): lax.all_to_all(row_grad.reshape(capacity, experts, D), ('ctx', 'exp'), sp...  92.2 us
    all_gather x1, waiting for transfers between devices, body(): lax.all_gather(qkv_weight, ('dp', 'ctx', 'exp'), axis=0, tiled=True)  88.5 us
    all_to_all x1, waiting for transfers between devices, body(): lax.all_to_all(grad_outgoing, ('ctx', 'exp'), split_axis=1, concat_axis=1...  84.4 us
    all_to_all x1, waiting for transfers between devices, body(): lax.all_to_all(outgoing, ('ctx', 'exp'), split_axis=1, concat_axis=1, til...  82 us
    all_to_all x1, waiting for transfers between devices, body(): lax.all_to_all(produced.reshape(item_count, experts, D), ('ctx', 'exp'),...  77.4 us
  transfers between devices with their start and end apart: 16, of which 13 were waited for; matrix products, arithmetic and copies ran while one was open for 10% of the time, Pallas kernels for 0%

commit v1 on v0

v1 whole, which is shorter than its diff:
```python
import jax
import jax.numpy as jnp
from jax import lax
from jax.sharding import PartitionSpec as P

D = 2048
HEADS = 16
HEAD_DIM = 128
FF = 1024
TOP = 8

NORM_EPS = 1e-05
ROPE_BASE = 10000.0
NEGATIVE = -1e30
HIGHEST_PREC = lax.Precision.HIGHEST
F32 = jnp.float32
BF16 = jnp.bfloat16


def row_scale(values):
    return lax.rsqrt(jnp.mean(values * values, axis=-1, keepdims=True) + NORM_EPS)


def rope_tables(position, half_dim):
    inverse = ROPE_BASE ** (-jnp.arange(half_dim, dtype=F32) / half_dim)
    angles = position[:, None] * inverse[None, :]
    cosine, sine_rows = jnp.cos(angles), jnp.sin(angles)
    return (
        jnp.concatenate([cosine, cosine], axis=1),
        jnp.concatenate([-sine_rows, sine_rows], axis=1),
    )


def rotate(values, cosine, sine_rows):
    half_dim = HEAD_DIM // 2
    turned = jnp.concatenate([values[..., half_dim:], values[..., :half_dim]], axis=-1)
    return values * cosine[None] + turned * sine_rows[None]


def norm_back(grad_rows, normed, scale_rows, gain_col):
    grad_normed = grad_rows * gain_col
    grad_input = scale_rows * (
        grad_normed - normed * jnp.mean(grad_normed * normed, axis=-1, keepdims=True)
    )
    return (grad_input, jnp.sum(grad_rows * normed, axis=0))


def dot(a, b):
    return jnp.dot(a, b, preferred_element_type=F32)


def dot_bt(a, b):
    return lax.dot_general(a, b, (((1,), (1,)), ((), ())), preferred_element_type=F32)


def dot_at(a, b):
    return lax.dot_general(a, b, (((0,), (0,)), ((), ())), preferred_element_type=F32)


def body(
    prompt_x,
    cont_x,
    cont_ids,
    routes,
    qkv_weight,
    out_weight,
    router_weight,
    norm_gains,
    gate_up_weight,
    down_weight,
    prompt_cot,
    cont_cot,
):
    n_dp, n_ctx, n_exp = lax.axis_size("dp"), lax.axis_size("ctx"), lax.axis_size("exp")
    d, c, z = lax.axis_index("dp"), lax.axis_index("ctx"), lax.axis_index("exp")
    prompt_len = prompt_x.shape[1]
    cont_len = cont_x.shape[1]
    rows = prompt_len + cont_len
    prompt_total = prompt_len * n_ctx
    experts = router_weight.shape[1]
    capacity = rows * TOP * 17 // (16 * experts)
    score_scale = HEAD_DIM ** (-0.5)
    shard = qkv_weight.shape[0]
    heads_own = HEADS // n_ctx
    width = heads_own * HEAD_DIM
    head_groups = n_dp if (D // (n_dp * n_ctx)) % HEAD_DIM == 0 else 1
    head_run = D // (head_groups * n_ctx)
    own_expert = c * n_exp + z

    def ctx_swap(x, k):
        return lax.ppermute(x, "ctx", [(i, i ^ k) for i in range(n_ctx)])

    def exp_shift(x, s):
        return lax.ppermute(x, "exp", [(i, (i + s) % n_exp) for i in range(n_exp)])

    def dp_shift(x, m):
        return lax.ppermute(x, "dp", [(i, (i + m) % n_dp) for i in range(n_dp)])

    def pick(x, axis, k):
        return lax.dynamic_index_in_dim(x, c ^ k, axis, keepdims=False)

    def place(buffer, x, *index):
        start, shape = [], []
        for at, size in zip(index, buffer.shape):
            start.append(0 if at is None else at)
            shape.append(size if at is None else 1)
        shape += buffer.shape[len(index) :]
        start += [0] * (buffer.ndim - len(index))
        return lax.dynamic_update_slice(buffer, x.reshape(shape), start)

    x_own = jnp.concatenate([prompt_x[0], cont_x[0]], axis=0)
    cot_own = jnp.concatenate([prompt_cot[0], cont_cot[0]], axis=0)

    small = jnp.concatenate([router_weight, norm_gains], axis=1)
    small_width = small.shape[1]
    small_ctx = jnp.zeros((n_ctx,) + small.shape, BF16)
    for k in range(n_ctx):
        small_ctx = place(small_ctx, ctx_swap(small, k) if k else small, c ^ k)
    small_all = jnp.zeros((n_dp, n_ctx, n_exp) + small.shape, BF16)
    small_exp = jnp.zeros((n_ctx, n_exp) + small.shape, BF16)
    for s in range(n_exp):
        small_exp = place(
            small_exp, exp_shift(small_ctx, s) if s else small_ctx, None, (z - s) % n_exp
        )
    for m in range(n_dp):
        small_all = place(small_all, dp_shift(small_exp, m) if m else small_exp, (d - m) % n_dp)
    small_all = small_all.reshape(D, small_width)
    w_router = small_all[:, :experts]
    gains_t = small_all[:, experts:].astype(F32).T
    gain_in, gain_ffn = gains_t[0], gains_t[3]

    def own_features(v):
        shaped = v.reshape(v.shape[:-1] + (head_groups, n_ctx, head_run))
        return pick(shaped, v.ndim, 0).reshape(v.shape[:-1] + (width,))

    gain_query, gain_key = own_features(gains_t[1]), own_features(gains_t[2])

    x_blocks = [x_own] + [ctx_swap(x_own, k) for k in range(1, n_ctx)]
    id_row = cont_ids[0]
    ids = [id_row] + [ctx_swap(id_row, k) for k in range(1, n_ctx)]
    route_rows = routes[0, 0]
    route_blocks = [route_rows] + [exp_shift(route_rows, s) for s in range(1, n_exp)]

    def by_owner(v):
        runs = v.shape[1] // (n_ctx * head_run)
        return jnp.stack(
            [
                jnp.concatenate(
                    [
                        v[:, (i * n_ctx + j) * head_run : (i * n_ctx + j + 1) * head_run]
                        for i in range(runs)
                    ],
                    axis=1,
                )
                for j in range(n_ctx)
            ]
        )

    def all_owners(v):
        runs = v.shape[2] // head_run
        return jnp.concatenate(
            [
                v[j][:, i * head_run : (i + 1) * head_run]
                for i in range(runs)
                for j in range(n_ctx)
            ],
            axis=1,
        )

    parts_w = by_owner(qkv_weight)
    slab = jnp.zeros((n_ctx, shard, 3 * width), BF16)
    for k in range(n_ctx):
        piece = pick(parts_w, 0, k)
        slab = place(slab, ctx_swap(piece, k) if k else piece, c ^ k)
    w_qkv = jnp.zeros((n_dp, n_ctx, n_exp, shard, 3 * width), BF16)
    moving = slab
    for s in range(n_exp):
        if s:
            moving = exp_shift(moving, 1)
        for m in range(n_dp):
            w_qkv = place(
                w_qkv,
                dp_shift(moving, m) if m else moving,
                (d - m) % n_dp,
                None,
                (z - s) % n_exp,
            )
    w_qkv = w_qkv.reshape(D, 3 * width)

    moving = out_weight
    out_exp = jnp.zeros((n_exp, shard, D), BF16)
    for s in range(n_exp):
        if s:
            moving = exp_shift(moving, 1)
        out_exp = place(out_exp, moving, (z - s) % n_exp)
    w_out = jnp.zeros((n_dp, n_ctx, n_exp, shard, D), BF16)
    for k in range(n_ctx):
        from_ctx = ctx_swap(out_exp, k) if k else out_exp
        for m in range(n_dp):
            w_out = place(
                w_out, dp_shift(from_ctx, m) if m else from_ctx, (d - m) % n_dp, c ^ k
            )
    w_out = w_out.reshape(D, D)

    upper = (
        jnp.arange(rows, dtype=jnp.int32)[:, None] < jnp.arange(rows, dtype=jnp.int32)[None, :]
    ).astype(BF16)
    send_experts = jnp.stack([(c ^ k) * n_exp + z for k in range(n_ctx)])
    spread = []
    for s in range(n_exp):
        named = jnp.any(
            route_blocks[s][None, :, :] == send_experts[:, None, None], axis=-1
        )
        rank = dot(named.astype(BF16), upper)
        slots = jnp.where(named, rank, -1.0)
        spread.append(
            (slots[:, None, :] == jnp.arange(capacity, dtype=F32)[None, :, None])
            .astype(BF16)
            .reshape(n_ctx * capacity, rows)
        )

    def dispatch(own_rows):
        arrived = [None] * (n_exp * n_ctx)
        block = own_rows
        for s in range(n_exp):
            if s:
                block = exp_shift(block, 1)
            packed = dot(spread[s], block).astype(BF16)
            for k in range(n_ctx):
                piece = packed[k * capacity : (k + 1) * capacity]
                arrived[s * n_ctx + k] = ctx_swap(piece, k) if k else piece
        return jnp.concatenate(arrived, axis=0)

    def give_back(expert_rows):
        total = None
        for s in range(n_exp):
            pieces = []
            for k in range(n_ctx):
                at = (s * n_ctx + k) * capacity
                piece = expert_rows[at : at + capacity]
                pieces.append(ctx_swap(piece, k) if k else piece)
            summed = dot_at(spread[s], jnp.concatenate(pieces, axis=0))
            if s:
                summed = exp_shift(summed.astype(BF16), n_exp - s).astype(F32)
            total = summed if total is None else total + summed
        return total

    cot_rows = dispatch(cot_own)
    w_gate_up = gate_up_weight[0]
    w_down = down_weight[0]
    act_cot = dot_bt(cot_rows, w_down)

    total_rows = rows * n_ctx
    index = jnp.arange(rows, dtype=jnp.int32)
    in_prompt = index < prompt_len
    position, seg_rows, block_rows, order_rows, prompt_rows = [], [], [], [], []
    for k in range(n_ctx):
        seg = ids[k][0]
        starts = jnp.sum((seg[None, :] < seg[:, None]).astype(jnp.int32), axis=1)
        within = jnp.arange(cont_len, dtype=jnp.int32) - starts
        at = (c ^ k) * prompt_len
        position.append(
            jnp.concatenate([at + index[:prompt_len], prompt_total + within])
        )
        order_rows.append(jnp.where(in_prompt, at + index, index))
        seg_rows.append(
            jnp.concatenate([jnp.full((prompt_len,), -1, jnp.int32), k * 64 + seg])
        )
        prompt_rows.append(in_prompt)
    position = jnp.concatenate(position).astype(F32)
    order = jnp.concatenate(order_rows)
    seg_of = jnp.concatenate(seg_rows)
    is_prompt = jnp.concatenate(prompt_rows)
    before = order[None, :] <= order[:, None]
    allowed = jnp.where(
        is_prompt[:, None],
        is_prompt[None, :] & before,
        is_prompt[None, :] | ((seg_of[None, :] == seg_of[:, None]) & before),
    )
    cosine, sine_rows = rope_tables(position, HEAD_DIM // 2)

    x_all = jnp.concatenate(x_blocks, axis=0).astype(F32)
    scale_in = row_scale(x_all)
    hidden_in = (x_all * scale_in * gain_in).astype(BF16)
    projected = dot(hidden_in, w_qkv)

    def ctx_sum(pair):
        total = pair
        for k in range(1, n_ctx):
            turned = [pair[:, (j ^ k) * rows : ((j ^ k) + 1) * rows] for j in range(n_ctx)]
            total = total + ctx_swap(jnp.concatenate(turned, axis=1), k)
        return total

    raw_query, raw_key = projected[:, :width], projected[:, width : 2 * width]
    squares = jnp.stack([jnp.sum(raw_query * raw_query, axis=-1), jnp.sum(raw_key * raw_key, axis=-1)])
    scales = lax.rsqrt(ctx_sum(squares) / D + NORM_EPS)
    scale_query, scale_key = scales[0][:, None], scales[1][:, None]
    normed_query = raw_query * scale_query
    normed_key = raw_key * scale_key

    def by_head(v):
        return jnp.stack([v[:, i * HEAD_DIM : (i + 1) * HEAD_DIM] for i in range(heads_own)])

    def side_by_side(v):
        return jnp.concatenate([v[i] for i in range(heads_own)], axis=1)

    heads_q = rotate(by_head(normed_query * gain_query), cosine, sine_rows).astype(BF16)
    heads_k = rotate(by_head(normed_key * gain_key), cosine, sine_rows).astype(BF16)
    heads_v = by_head(projected[:, 2 * width :].astype(BF16))

    def score_block():
        raw_scores = (
            jnp.einsum("hrd,hkd->hrk", heads_q, heads_k, preferred_element_type=F32) * score_scale
        )
        return jnp.where(allowed[None], raw_scores, NEGATIVE)

    scores = score_block()
    row_max = jnp.max(scores, axis=-1, keepdims=True)
    log_total = row_max + jnp.log(jnp.sum(jnp.exp(scores - row_max), axis=-1, keepdims=True))
    attention = jnp.exp(scores - log_total)
    attention_b = attention.astype(BF16)
    mixed_heads = side_by_side(
        jnp.einsum("hrk,hkd->hrd", attention_b, heads_v, preferred_element_type=F32).astype(BF16)
    )

    mixed = jnp.zeros((n_ctx, rows, width), BF16)
    for k in range(n_ctx):
        piece = mixed_heads[k * rows : (k + 1) * rows]
        mixed = place(mixed, ctx_swap(piece, k) if k else piece, c ^ k)
    mixed = all_owners(mixed)
    inputs = x_own.astype(F32)
    mid_rows = inputs + dot(mixed, w_out)
    scale_ffn = row_scale(mid_rows)
    normed_ffn = mid_rows * scale_ffn
    hidden_ffn = (normed_ffn * gain_ffn).astype(BF16)

    def softmax(logits):
        shifted = jnp.exp(logits - jnp.max(logits, axis=-1, keepdims=True))
        return shifted / jnp.sum(shifted, axis=-1, keepdims=True)

    expert_in = dispatch(hidden_ffn)
    router_in = softmax(dot(expert_in, w_router))
    gate_in = jnp.sum(
        jnp.where(jnp.arange(experts)[None, :] == own_expert, router_in, 0.0), axis=-1, keepdims=True
    )
    gate_up = dot(expert_in, w_gate_up)
    gate_part, up_part = gate_up[:, :FF], gate_up[:, FF:]
    sigmoid_gate = jax.nn.sigmoid(gate_part)
    swish = gate_part * sigmoid_gate
    activated = (swish * up_part).astype(BF16)
    act_grad = gate_in * act_cot
    gate_part_grad = act_grad * up_part * sigmoid_gate * (1.0 + gate_part * (1.0 - sigmoid_gate))
    gu_grad = jnp.concatenate([gate_part_grad, act_grad * swish], axis=1).astype(BF16)
    gate_grad = jnp.sum(act_cot * activated.astype(F32), axis=-1, keepdims=True)
    row_grad = dot_bt(gu_grad, w_gate_up).astype(BF16)
    grad_high = gate_grad.astype(BF16)
    grad_low = (gate_grad - grad_high.astype(F32)).astype(BF16)
    column = jnp.arange(-(-2 * experts // 128) * 128)[None, :]
    zero = jnp.zeros((), BF16)
    gate_cols = jnp.where(
        column == own_expert, grad_high, jnp.where(column == experts + own_expert, grad_low, zero)
    )
    returned = give_back(jnp.concatenate([row_grad, gate_cols], axis=1))

    expert_out = dot(activated, w_down).astype(BF16)
    mixture = give_back((gate_in * expert_out.astype(F32)).astype(BF16))
    final_rows = (mid_rows + mixture).astype(BF16)

    def dp_halves(grad):
        total = lax.dynamic_index_in_dim(grad, d, 0, keepdims=False)
        for m in range(1, n_dp):
            part = lax.dynamic_index_in_dim(grad, (d + m) % n_dp, 0, keepdims=False)
            total = total + dp_shift(part.astype(BF16), m).astype(F32)
        return total

    route_grad = (gate_in * cot_rows.astype(F32)).astype(BF16)
    grad_gate_up = dp_halves(
        dot_at(expert_in, gu_grad).reshape(n_dp, D // n_dp, 2 * FF)
    )
    grad_down = dp_halves(dot_at(activated, route_grad).reshape(n_dp, FF // n_dp, D))

    router = softmax(dot(hidden_ffn, w_router))
    prob_grad = returned[:, D : D + experts] + returned[:, D + experts : D + 2 * experts]
    logit_grad = router * (prob_grad - jnp.sum(router * prob_grad, axis=-1, keepdims=True))
    ffn_grad = returned[:, :D] + jnp.dot(logit_grad, w_router.astype(F32).T, precision=HIGHEST_PREC)
    router_grad_t = jnp.einsum(
        "re,rd->ed", logit_grad, hidden_ffn.astype(F32), precision=HIGHEST_PREC
    )
    mid_norm_grad, ffn_gain_grad = norm_back(ffn_grad, normed_ffn, scale_ffn, gain_ffn)
    mid_grad = cot_own.astype(F32) + mid_norm_grad

    attn_grad = mid_grad.astype(BF16)
    mixed_grad_own = dot_bt(attn_grad, w_out).astype(BF16)
    shaped_grad = by_owner(mixed_grad_own)
    mixed_grad = []
    for k in range(n_ctx):
        piece = pick(shaped_grad, 0, k)
        mixed_grad.append(ctx_swap(piece, k) if k else piece)
    heads_g = by_head(jnp.concatenate(mixed_grad, axis=0))
    prob_att = jnp.einsum("hrd,hkd->hrk", heads_g, heads_v, preferred_element_type=F32)
    attention = jnp.exp(score_block() - log_total)
    attention_b = attention.astype(BF16)
    delta = jnp.sum(attention * prob_att, axis=-1, keepdims=True)
    score_grad = (attention * (prob_att - delta)).astype(BF16)
    query_grad = (
        jnp.einsum("hrk,hkd->hrd", score_grad, heads_k, preferred_element_type=F32) * score_scale
    )
    key_grad = (
        jnp.einsum("hrk,hrd->hkd", score_grad, heads_q, preferred_element_type=F32) * score_scale
    )
    value_grad = jnp.einsum("hrk,hrd->hkd", attention_b, heads_g, preferred_element_type=F32)
    query_turn = side_by_side(rotate(query_grad, cosine, -sine_rows))
    key_turn = side_by_side(rotate(key_grad, cosine, -sine_rows))
    query_up, key_up = query_turn * gain_query, key_turn * gain_key
    sums = jnp.stack(
        [jnp.sum(query_up * normed_query, axis=-1), jnp.sum(key_up * normed_key, axis=-1)]
    )
    means = ctx_sum(sums) / D
    raw_query_grad = scale_query * (query_up - normed_query * means[0][:, None])
    raw_key_grad = scale_key * (key_up - normed_key * means[1][:, None])
    query_gain_grad = jnp.sum(query_turn * normed_query, axis=0)
    key_gain_grad = jnp.sum(key_turn * normed_key, axis=0)
    proj_grad = jnp.concatenate(
        [raw_query_grad, raw_key_grad, side_by_side(value_grad)], axis=1
    ).astype(BF16)

    def exp_reduce(grad):
        moving = None
        for s in range(1, n_exp + 1):
            part = lax.dynamic_index_in_dim(grad, (z - s) % n_exp, 0, keepdims=False)
            moving = part if moving is None else moving.astype(F32) + part
            if s < n_exp:
                moving = exp_shift(moving.astype(BF16), 1)
        return moving

    qkv_local = dot_at(hidden_in, proj_grad).reshape(n_dp, n_ctx, n_exp, shard, 3 * width)
    qkv_dp = dp_halves(qkv_local)
    qkv_exp = exp_reduce(jnp.moveaxis(qkv_dp, 1, 0))
    grad_qkv = jnp.zeros((n_ctx, shard, 3 * width), F32)
    for k in range(n_ctx):
        piece = pick(qkv_exp, 0, k)
        piece = ctx_swap(piece.astype(BF16), k).astype(F32) if k else piece
        grad_qkv = place(grad_qkv, piece, c ^ k)
    grad_qkv = all_owners(grad_qkv)

    if head_groups == n_dp:
        attn_grad_all = jnp.concatenate(
            [attn_grad] + [ctx_swap(attn_grad, k) for k in range(1, n_ctx)], axis=0
        )
        out_local = dot_at(mixed_heads, attn_grad_all).reshape(n_dp, n_exp, shard, D)
        grad_out = exp_reduce(dp_halves(out_local))
    else:
        grad_out = lax.psum_scatter(
            dot_at(mixed, attn_grad), ("dp", "ctx", "exp"), scatter_dimension=0, tiled=True
        )

    hidden_part = dot_bt(proj_grad, w_qkv)
    hidden_grad = hidden_part[:rows]
    for k in range(1, n_ctx):
        piece = hidden_part[k * rows : (k + 1) * rows].astype(BF16)
        hidden_grad = hidden_grad + ctx_swap(piece, k).astype(F32)
    scale_own = scale_in[:rows]
    in_norm_grad, in_gain_grad = norm_back(hidden_grad, inputs * scale_own, scale_own, gain_in)
    input_grad = mid_grad + in_norm_grad

    def spread_features(v):
        shaped = jnp.zeros((head_groups, n_ctx, head_run), F32)
        return place(shaped, v.reshape(head_groups, 1, head_run), None, c).reshape(1, D)

    small_grad = jnp.concatenate(
        [
            router_grad_t,
            in_gain_grad[None],
            spread_features(query_gain_grad),
            spread_features(key_gain_grad),
            ffn_gain_grad[None],
        ],
        axis=0,
    )
    count = small_grad.shape[0]
    part = small_grad.reshape(count, n_dp, n_ctx, n_exp, shard).transpose(1, 2, 3, 0, 4)
    total = lax.dynamic_index_in_dim(part, d, 0, keepdims=False)
    for m in range(1, n_dp):
        total = total + dp_shift(
            lax.dynamic_index_in_dim(part, (d + m) % n_dp, 0, keepdims=False), m
        )
    part = total
    total = pick(part, 0, 0)
    for k in range(1, n_ctx):
        total = total + ctx_swap(pick(part, 0, k), k)
    part = total
    total = lax.dynamic_index_in_dim(part, z, 0, keepdims=False)
    for s in range(1, n_exp):
        total = total + exp_shift(
            lax.dynamic_index_in_dim(part, (z + s) % n_exp, 0, keepdims=False), s
        )
    small_sum = total.T

    return (
        final_rows[:prompt_len][None],
        final_rows[prompt_len:][None],
        input_grad[:prompt_len][None],
        input_grad[prompt_len:][None],
        grad_qkv,
        grad_out,
        small_sum[:, :experts],
        small_sum[:, experts:],
        grad_gate_up[None],
        grad_down[None],
    )


def solution(mesh):
    return jax.shard_map(
        body,
        mesh=mesh,
        in_specs=(
            P(("dp", "exp"), "ctx", None),
            P(("dp", "exp"), "ctx", None),
            P(("dp", "exp"), "ctx", None),
            P(("dp", "exp"), "ctx", None, None),
            P(("dp", "ctx", "exp"), None),
            P(("dp", "ctx", "exp"), None),
            P(("dp", "ctx", "exp"), None),
            P(("dp", "ctx", "exp"), None),
            P(("ctx", "exp"), None, None),
            P(("ctx", "exp"), None, None),
            P(("dp", "exp"), "ctx", None),
            P(("dp", "exp"), "ctx", None),
        ),
        out_specs=(
            P(("dp", "exp"), "ctx", None),
            P(("dp", "exp"), "ctx", None),
            P(("dp", "exp"), "ctx", None),
            P(("dp", "exp"), "ctx", None),
            P(("dp", "ctx", "exp"), None),
            P(("dp", "ctx", "exp"), None),
            P(("dp", "ctx", "exp"), None),
            P(("dp", "ctx", "exp"), None),
            P(("ctx", "exp"), "dp", None),
            P(("ctx", "exp"), "dp", None),
        ),
        check_vma=False,
    )
```

time: 2150 us -> 827 us (0.38)
  waiting for transfers between devices: 1600 us -> 377 us
  blocking collectives: 131 us -> 0 us
  starting transfers between devices: 43.1 us -> 162 us
  local copies, waits for them, and re-layouts: 147 us -> 88.5 us
  matrix products: 166 us -> 139 us
    reduce_scatter x5 -> x0, waiting for transfers between devices: 850 us -> none  [the longest x1 437 us: body(): lax.psum_scatter(qkv_w_grad, ('dp', 'ctx', 'exp'), scatter_dimension=0, t...]
    ppermute x0 -> x134, waiting for transfers between devices: none -> 377 us  [the longest x87 239 us: ctx_swap(): return lax.ppermute(x, 'ctx', [(i, i ^ k) for i in range(n_ctx)])]
    all_to_all x4 -> x0, waiting for transfers between devices: 336 us -> none  [the longest x1 92.2 us: body(): lax.all_to_all(row_grad.reshape(capacity, experts, D), ('ctx', 'exp'), sp...]
    unnamed x15 -> x0, waiting for transfers between devices: 251 us -> none
    ppermute x0 -> x134, starting transfers between devices: none -> 162 us  [the longest x87 89.4 us: ctx_swap(): return lax.ppermute(x, 'ctx', [(i, i ^ k) for i in range(n_ctx)])]
    all_gather x4 -> x0, waiting for transfers between devices: 161 us -> none  [the longest x1 88.5 us: body(): lax.all_gather(qkv_weight, ('dp', 'ctx', 'exp'), axis=0, tiled=True)]
    all_gather x2 -> x0, blocking collectives: 131 us -> none  [the longest x1 66.3 us: body(): lax.all_gather(norm_gains, ('dp', 'ctx', 'exp'), axis=0, tiled=True)]
    gather x4 -> x0, local copies, waits for them, and re-layouts: 46.8 us -> none  [the longest x1 13.7 us: body(): returned_grad.reshape(capacity * experts, D)[slot_index]]
  transfers between devices with their start and end apart: 16 -> 134, of which waited for: 13 -> 67; matrix products, arithmetic and copies ran while one was open for 10% -> 18% of each run, Pallas kernels for 0% -> 0%
where the time goes in v1:
time: 827 us; the launch traced here: 814 us
  waiting for transfers between devices  377 us (46%)
  starting transfers between devices  162 us (20%)
  matrix products  139 us (17%)
  local copies, waits for them, and re-layouts  88.5 us (11%)
  other arithmetic  43.8 us (5%)
    ppermute x87, waiting for transfers between devices, ctx_swap(): return lax.ppermute(x, 'ctx', [(i, i ^ k) for i in range(n_ctx)])  239 us
    ppermute x33, waiting for transfers between devices, exp_shift(): return lax.ppermute(x, 'exp', [(i, (i + s) % n_exp) for i in range(n_exp)])  132 us
    ppermute x87, starting transfers between devices, ctx_swap(): return lax.ppermute(x, 'ctx', [(i, i ^ k) for i in range(n_ctx)])  89.4 us
    ppermute x33, starting transfers between devices, exp_shift(): return lax.ppermute(x, 'exp', [(i, (i + s) % n_exp) for i in range(n_exp)])  71 us
    dot_general x18, matrix products, dot(): return jnp.dot(a, b, preferred_element_type=F32)  49.6 us
    dot_general x12, matrix products, dot_at(): lax.dot_general(a, b, (((0,), (0,)), ((), ())), preferred_element_type=F32)  41.5 us
    unnamed x275, local copies, waits for them, and re-layouts  36.6 us
    dot_general x4, matrix products, dot_bt(): lax.dot_general(a, b, (((1,), (1,)), ((), ())), preferred_element_type=F32)  34 us
  transfers between devices with their start and end apart: 134, of which 67 were waited for; matrix products, arithmetic and copies ran while one was open for 18% of the time, Pallas kernels for 0%

profile of v1, /device:TPU:16, one launch (start us, length us, event | category | flops | bytes accessed | tf_op | source)
XLA Modules:
  0.0 814.4 jit_solution(6989507724021011252)
XLA Ops:
  24.9 3.8 collective-permute-done.2
  58.7 6.2 collective-permute-done.13
  65.5 5.8 collective-permute-done.14
  71.8 6.3 collective-permute-done.15
  81.2 5.1 collective-permute-done.72
  96.5 3.5 collective-permute-done.30
  102.0 8.3 %collective-permute-done.75 = bf16[136,2048]{1,0:T(8,128)(2,1)S(1)} collective-permute-done((bf16[136,2048]{1,0:T(8,128)(2,1)S(1)}, bf16[136,2048]{1,0:T(8,128)(2,1)S(1)}, u32[]{:S(2)}, u32[]{:S(2)}) %collective-permute-start.75) | collective-permute-done | bytes 557088 | tf_op jit(solution)/shard_map/ppermute | solution.py:94
  116.5 12.9 %collective-permute-done.31 = bf16[64,2048]{1,0:T(8,128)(2,1)S(1)} collective-permute-done((bf16[64,2048]{1,0:T(8,128)(2,1)S(1)}, bf16[64,2048]{1,0:T(8,128)(2,1)S(1)}, u32[]{:S(2)}, u32[]{:S(2)}) %collective-permute-start.31) | collective-permute-done | bytes 262176 | tf_op jit(solution)/shard_map/ppermute | solution.py:94
  138.2 8.8 %collective-permute-done.79 = bf16[136,2048]{1,0:T(8,128)(2,1)S(1)} collective-permute-done((bf16[136,2048]{1,0:T(8,128)(2,1)S(1)}, bf16[136,2048]{1,0:T(8,128)(2,1)S(1)}, u32[]{:S(2)}, u32[]{:S(2)}) %collective-permute-start.79) | collective-permute-done | bytes 557088 | tf_op jit(solution)/shard_map/ppermute | solution.py:94
  161.7 11.3 %collective-permute-done.83 = bf16[136,2048]{1,0:T(8,128)(2,1)S(1)} collective-permute-done((bf16[136,2048]{1,0:T(8,128)(2,1)S(1)}, bf16[136,2048]{1,0:T(8,128)(2,1)S(1)}, u32[]{:S(2)}, u32[]{:S(2)}) %collective-permute-start.83) | collective-permute-done | bytes 557088 | tf_op jit(solution)/shard_map/ppermute | solution.py:94
  178.1 8.5 %collective-permute-done.33 = bf16[4,64,2048]{2,1,0:T(8,128)(2,1)S(1)} collective-permute-done((bf16[4,64,2048]{2,1,0:T(8,128)(2,1)S(1)}, bf16[4,64,2048]{2,1,0:T(8,128)(2,1)S(1)}, u32[]{:S(2)}, u32[]{:S(2)}) %collective-permute-start.33) | collective-permute-done | bytes 1048608 | tf_op jit(solution)/shard_map/ppermute | solution.py:91
  186.8 31.1 %collective-permute-done.35 = bf16[4,64,2048]{2,1,0:T(8,128)(2,1)S(1)} collective-permute-done((bf16[4,64,2048]{2,1,0:T(8,128)(2,1)S(1)}, bf16[4,64,2048]{2,1,0:T(8,128)(2,1)S(1)}, u32[]{:S(2)}, u32[]{:S(2)}) %collective-permute-start.35) | collective-permute-done | bytes 1048608 | tf_op jit(solution)/shard_map/ppermute | solution.py:91
  223.3 3.7 fusion.218
  251.8 14.0 %multiply_reduce_fusion.8 = (f32[136]{0:T(256)S(1)}, f32[136,2048]{1,0:T(8,128)S(1)}) fusion(bf16[136,2048]{1,0:T(8,128)(2,1)S(1)} %constant_dynamic-update-slice_fusion.31, bf16[2048,2048]{1,0:T(8,128)(2,1)S(1)} %bitcast.414, bf16[8,2048]{1,0:T(8,128)(2,1)S(1)} %bitcast.438, bf16[128,2048]{1,0:T(8,128)(2,1)S(1)} %bitcast.421), kind=kOutput, calls=%fused_computation.198 | convolution fusion | flops 1142800256 | bytes 10617376 | tf_op jit(solution)/shard_map/dot_general | solution.py:49
  278.7 7.7 collective-permute-done.41
  301.8 12.5 %collective-permute-done.45 = bf16[72,2048]{1,0:T(8,128)(2,1)S(1)} collective-permute-done((bf16[72,2048]{1,0:T(8,128)(2,1)S(1)}, bf16[72,2048]{1,0:T(8,128)(2,1)S(1)}, u32[]{:S(2)}, u32[]{:S(2)}) %collective-permute-start.45) | collective-permute-done | bytes 294944 | tf_op jit(solution)/shard_map/ppermute | solution.py:91
  326.8 5.7 collective-permute-done.50
  339.7 4.8 collective-permute-done.54
  346.2 3.9 collective-permute-done.55
  351.5 3.8 fusion.219
  355.4 16.0 %fusion.3 = f32[1152,2048]{1,0:T(8,128)} fusion(bf16[1152,2048]{1,0:T(8,128)(2,1)} %constant_dynamic-update-slice_fusion.39, bf16[1,2048,2048]{2,1,0:T(8,128)(2,1)} %param.20), kind=kOutput, calls=%fused_computation.21 | convolution fusion | flops 9663676416 | bytes 22544384 | tf_op jit(solution)/shard_map/dot_general | solution.py:49
  371.6 11.1 %multiply_convert_fusion.5 = (bf16[1152,1024]{1,0:T(8,128)(2,1)S(1)}, bf16[1152,1024]{1,0:T(8,128)(2,1)S(1)}, f32[1152]{0:T(1024)S(1)}, bf16[1152,1024]{1,0:T(8,128)(2,1)}) fusion(f32[1152,2048]{1,0:T(8,128)} %fusion.3, f32[1152]{0:T(1024)S(1)} %select_reduce_fusion, bf16[1152,2048]{1,0:T(8,128)(2,1)S(1)} %bitcast.466, bf16[1,1024,2048]{2,1,0:T(8,128)(2,1)S(1)} %copy-done.91), kind=kOutput, calls=%fused_computation.39 | convolution fusion | flops 4854250496 | bytes 25437184 | tf_op jit(solution)/shard_map/dot_general | solution.py:53
  382.7 12.5 %fusion.5 = bf16[1152,2048]{1,0:T(8,128)(2,1)S(1)} fusion(bf16[1,2048,2048]{2,1,0:T(8,128)(2,1)} %param.20, bf16[1152,1024]{1,0:T(8,128)(2,1)S(1)} %get-tuple-element.40, bf16[1152,1024]{1,0:T(8,128)(2,1)S(1)} %get-tuple-element.39), kind=kOutput, calls=%fused_computation.25 | convolution fusion | flops 9675472896 | bytes 17825792 | tf_op jit(solution)/shard_map/dot_general | solution.py:53
  395.2 17.1 %fusion.23 = f32[2048,2048]{1,0:T(8,128)} fusion(bf16[1152,2048]{1,0:T(8,128)(2,1)} %constant_dynamic-update-slice_fusion.39, bf16[1152,1024]{1,0:T(8,128)(2,1)S(1)} %get-tuple-element.40, bf16[1152,1024]{1,0:T(8,128)(2,1)S(1)} %get-tuple-element.39), kind=kOutput, calls=%fused_computation.62 | convolution fusion | flops 9673113600 | bytes 26214400 | tf_op jit(solution)/shard_map/dot_general | solution.py:57
  412.3 7.5 multiply_convert_fusion.1
  419.8 8.4 %fusion.8 = f32[1024,2048]{1,0:T(8,128)} fusion(bf16[1152,1024]{1,0:T(8,128)(2,1)S(1)} %copy-done.92, bf16[1152,2048]{1,0:T(8,128)(2,1)S(1)} %bitcast.466, f32[1152]{0:T(1024)S(1)} %select_reduce_fusion), kind=kOutput, calls=%fused_computation.35 | convolution fusion | flops 4838916096 | bytes 15471104 | tf_op jit(solution)/shard_map/dot_general | solution.py:57
  436.1 3.7 collective-permute-done.59
  440.3 5.9 collective-permute-done.70
  446.7 5.6 collective-permute-done.69
  454.5 4.3 collective-permute-done.66
  458.8 6.1 collective-permute-done.65
  467.1 4.4 collective-permute-done.62
  471.5 6.3 collective-permute-done.61
  479.6 6.0 fusion.15
  487.3 3.9 collective-permute-done.99
  494.1 3.8 collective-permute-done.96
  498.4 6.3 collective-permute-done.95
  511.7 3.8 fusion.37
  519.5 4.1 collective-permute-done.58
  526.5 15.7 %collective-permute-done.71 = bf16[136,2048]{1,0:T(8,128)(2,1)S(1)} collective-permute-done((bf16[136,2048]{1,0:T(8,128)(2,1)S(1)}, bf16[136,2048]{1,0:T(8,128)(2,1)S(1)}, u32[]{:S(2)}, u32[]{:S(2)}) %collective-permute-start.71) | collective-permute-done | bytes 557088 | tf_op jit(solution)/shard_map/ppermute | solution.py:94
  542.2 4.0 collective-permute-done.67
  546.2 19.6 %collective-permute-start.97 = (bf16[136,2176]{1,0:T(8,128)(2,1)S(1)}, bf16[136,2176]{1,0:T(8,128)(2,1)S(1)}, u32[]{:S(2)}, u32[]{:S(2)}) collective-permute-start(bf16[136,2176]{1,0:T(8,128)(2,1)S(1)} %convolution_convert_fusion.2), channel_id=1, source_target_pairs={{0,2},{1,3},{2,0},{3,1},{4,6},{5,7},{6,4},{7,5},{8,10},{9,11},{10,... | collective-permute-start | bytes 1775624 | tf_op jit(solution)/shard_map/ppermute | solution.py:94
  565.8 8.6 %collective-permute-done.63 = bf16[136,2048]{1,0:T(8,128)(2,1)S(1)} collective-permute-done((bf16[136,2048]{1,0:T(8,128)(2,1)S(1)}, bf16[136,2048]{1,0:T(8,128)(2,1)S(1)}, u32[]{:S(2)}, u32[]{:S(2)}) %collective-permute-start.63) | collective-permute-done | bytes 557088 | tf_op jit(solution)/shard_map/ppermute | solution.py:94
  574.3 3.7 collective-permute-start.93
  580.2 6.3 collective-permute-done.87
  586.5 7.7 collective-permute-done.101
  594.2 10.9 %collective-permute-done.93 = bf16[136,2176]{1,0:T(8,128)(2,1)S(1)} collective-permute-done((bf16[136,2176]{1,0:T(8,128)(2,1)S(1)}, bf16[136,2176]{1,0:T(8,128)(2,1)S(1)}, u32[]{:S(2)}, u32[]{:S(2)}) %collective-permute-start.93) | collective-permute-done | bytes 591904 | tf_op jit(solution)/shard_map/ppermute | solution.py:94
  608.7 4.0 convolution_convert_fusion.12
  619.6 12.4 %collective-permute-done.104 = bf16[136,512]{1,0:T(8,128)(2,1)S(1)} collective-permute-done((bf16[136,512]{1,0:T(8,128)(2,1)S(1)}, bf16[136,512]{1,0:T(8,128)(2,1)S(1)}, u32[]{:S(2)}, u32[]{:S(2)}) %collective-permute-start.104) | collective-permute-done | bytes 139296 | tf_op jit(solution)/shard_map/ppermute | solution.py:91
  632.0 13.3 %collective-permute-done.103 = bf16[136,512]{1,0:T(8,128)(2,1)S(1)} collective-permute-done((bf16[136,512]{1,0:T(8,128)(2,1)S(1)}, bf16[136,512]{1,0:T(8,128)(2,1)S(1)}, u32[]{:S(2)}, u32[]{:S(2)}) %collective-permute-start.103) | collective-permute-done | bytes 139296 | tf_op jit(solution)/shard_map/ppermute | solution.py:91
  645.5 5.3 multiply_reduce_fusion
  669.9 6.4 fusion.221
  676.3 8.3 %fusion.118 = f32[2048,1536]{1,0:T(8,128)} fusion(bf16[544,1536]{1,0:T(8,128)(2,1)S(1)} %constant_dynamic-update-slice_fusion.63, bf16[544,2048]{1,0:T(8,128)(2,1)S(1)} %copy-done.19, f32[2048]{0:T(1024)S(1)} %bitcast.450, f32[544]{0:T(1024)S(1)} %add_rsqrt_fusion.1), kind=kOutput, calls=%fused_computation.229 | convolution fusion | flops 3427008512 | bytes 16492672 | tf_op jit(solution)/shard_map/dot_general | solution.py:57
  688.2 4.9 fusion.22
  693.3 3.2 fusion.29
  701.3 10.0 %collective-permute-done.109 = bf16[136,2048]{1,0:T(8,128)(2,1)S(1)} collective-permute-done((bf16[136,2048]{1,0:T(8,128)(2,1)S(1)}, bf16[136,2048]{1,0:T(8,128)(2,1)S(1)}, u32[]{:S(2)}, u32[]{:S(2)}) %collective-permute-start.109) | collective-permute-done | bytes 557088 | tf_op jit(solution)/shard_map/ppermute | solution.py:91
  727.4 5.2 bitcast_add_fusion.1
  737.2 4.9 collective-permute-done.122
  744.6 14.4 %collective-permute-done.112 = bf16[4,64,1536]{2,1,0:T(8,128)(2,1)S(1)} collective-permute-done((bf16[4,64,1536]{2,1,0:T(8,128)(2,1)S(1)}, bf16[4,64,1536]{2,1,0:T(8,128)(2,1)S(1)}, u32[]{:S(2)}, u32[]{:S(2)}) %collective-permute-start.112) | collective-permute-done | bytes 786464 | tf_op jit(solution)/shard_map/ppermute | solution.py:94
  761.6 4.2 fusion.16
  767.9 13.6 %collective-permute-done.113 = bf16[4,64,1536]{2,1,0:T(8,128)(2,1)S(1)} collective-permute-done((bf16[4,64,1536]{2,1,0:T(8,128)(2,1)S(1)}, bf16[4,64,1536]{2,1,0:T(8,128)(2,1)S(1)}, u32[]{:S(2)}, u32[]{:S(2)}) %collective-permute-start.113) | collective-permute-done | bytes 786464 | tf_op jit(solution)/shard_map/ppermute | solution.py:94
  787.9 8.9 %fusion = f32[1,1024,2048]{2,1,0:T(8,128)} fusion(bf16[1024,2048]{1,0:T(8,128)(2,1)S(1)} %collective-permute-done.132, f32[2,1024,2048]{2,1,0:T(8,128)} %bitcast.425, s32[]{:T(128)S(6)} %select_n.352), kind=kLoop, calls=%fused_computation.18 | loop fusion | flops 4194304 | bytes 20971524 | tf_op jit(solution)/shard_map/broadcast_in_dim | solution.py:508
  796.8 4.7 collective-permute-done.114
  805.5 3.9 collective-permute-done.115
  (755 shorter events, 301.8 us)
Async XLA Ops:
  2.1 32.0 %collective-permute-start.6 = (bf16[64,20]{0,1:T(8,128)(2,1)S(1)}, bf16[64,20]{0,1:T(8,128)(2,1)S(1)}, u32[]{:S(2)}, u32[]{:S(2)}) collective-permute-start(bf16[64,20]{0,1:T(8,128)(2,1)S(1)} %constant_dynamic-update-slice_fusion.5), channel_id=1, source_target_pairs={{0,4},{4,0},{8,12},{12,8},{1,5},{5,1},{9,13},{13,9},{2,6},{6,2},{1... | collective-permute-start | bytes 7688 | tf_op jit(solution)/shard_map/ppermute | solution.py:91
  3.6 33.4 %collective-permute-start.7 = (bf16[64,20]{0,1:T(8,128)(2,1)S(1)}, bf16[64,20]{0,1:T(8,128)(2,1)S(1)}, u32[]{:S(2)}, u32[]{:S(2)}) collective-permute-start(bf16[64,20]{0,1:T(8,128)(2,1)S(1)} %constant_dynamic-update-slice_fusion.5), channel_id=1, source_target_pairs={{0,8},{4,12},{8,0},{12,4},{1,9},{5,13},{9,1},{13,5},{2,10},{6,14},... | collective-permute-start | bytes 7688 | tf_op jit(solution)/shard_map/ppermute | solution.py:91
  5.1 32.5 %collective-permute-start.8 = (bf16[64,20]{0,1:T(8,128)(2,1)S(1)}, bf16[64,20]{0,1:T(8,128)(2,1)S(1)}, u32[]{:S(2)}, u32[]{:S(2)}) collective-permute-start(bf16[64,20]{0,1:T(8,128)(2,1)S(1)} %constant_dynamic-update-slice_fusion.5), channel_id=1, source_target_pairs={{0,12},{4,8},{8,4},{12,0},{1,13},{5,9},{9,5},{13,1},{2,14},{6,10},... | collective-permute-start | bytes 7688 | tf_op jit(solution)/shard_map/ppermute | solution.py:91
  5.6 18.6 %collective-permute-start = (s32[1,8]{1,0:T(1,128)}, s32[1,8]{1,0:T(1,128)S(1)}, u32[]{:S(2)}, u32[]{:S(2)}) collective-permute-start(s32[1,8]{1,0:T(1,128)} %bitcast.480), channel_id=1, source_target_pairs={{0,4},{4,0},{8,12},{12,8},{1,5},{5,1},{9,13},{13,9},{2,6},{6,2},{1... | collective-permute-start | bytes 104 | tf_op jit(solution)/shard_map/ppermute | solution.py:91
  7.1 22.2 %collective-permute-start.1 = (s32[1,8]{1,0:T(1,128)}, s32[1,8]{1,0:T(1,128)S(1)}, u32[]{:S(2)}, u32[]{:S(2)}) collective-permute-start(s32[1,8]{1,0:T(1,128)} %bitcast.481), channel_id=1, source_target_pairs={{0,8},{4,12},{8,0},{12,4},{1,9},{5,13},{9,1},{13,5},{2,10},{6,14},... | collective-permute-start | bytes 104 | tf_op jit(solution)/shard_map/ppermute | solution.py:91
  37.0 63.0 %collective-permute-start.3 = (bf16[136,2048]{1,0:T(8,128)(2,1)}, bf16[136,2048]{1,0:T(8,128)(2,1)}, u32[]{:S(2)}, u32[]{:S(2)}) collective-permute-start(bf16[136,2048]{1,0:T(8,128)(2,1)} %pad_maximum_fusion.8), channel_id=1, source_target_pairs={{0,4},{4,0},{8,12},{12,8},{1,5},{5,1},{9,13},{13,9},{2,6},{6,2},{1... | collective-permute-start | bytes 1671176 | tf_op jit(solution)/shard_map/ppermute | solution.py:91
  37.7 73.6 %collective-permute-start.4 = (bf16[136,2048]{1,0:T(8,128)(2,1)}, bf16[136,2048]{1,0:T(8,128)(2,1)}, u32[]{:S(2)}, u32[]{:S(2)}) collective-permute-start(bf16[136,2048]{1,0:T(8,128)(2,1)} %pad_maximum_fusion.8), channel_id=1, source_target_pairs={{0,8},{4,12},{8,0},{12,4},{1,9},{5,13},{9,1},{13,5},{2,10},{6,14},... | collective-permute-start | bytes 1671176 | tf_op jit(solution)/shard_map/ppermute | solution.py:91
  47.0 66.1 %collective-permute-start.5 = (bf16[136,2048]{1,0:T(8,128)(2,1)}, bf16[136,2048]{1,0:T(8,128)(2,1)}, u32[]{:S(2)}, u32[]{:S(2)}) collective-permute-start(bf16[136,2048]{1,0:T(8,128)(2,1)} %pad_maximum_fusion.8), channel_id=1, source_target_pairs={{0,12},{4,8},{8,4},{12,0},{1,13},{5,9},{9,5},{13,1},{2,14},{6,10},... | collective-permute-start | bytes 1671176 | tf_op jit(solution)/shard_map/ppermute | solution.py:91
  49.5 29.9 %collective-permute-start.29 = (bf16[64,2048]{1,0:T(8,128)(2,1)}, bf16[64,2048]{1,0:T(8,128)(2,1)}, u32[]{:S(2)}, u32[]{:S(2)}) collective-permute-start(bf16[64,2048]{1,0:T(8,128)(2,1)} %param.17), channel_id=1, source_target_pairs={{0,1},{1,2},{2,3},{3,0},{4,5},{5,6},{6,7},{7,4},{8,9},{9,10},{10,1... | collective-permute-start | bytes 786440 | tf_op jit(solution)/shard_map/ppermute | solution.py:94
  100.0 38.1 %collective-permute-start.16 = (bf16[4,64,1536]{2,1,0:T(8,128)(2,1)S(1)}, bf16[4,64,1536]{2,1,0:T(8,128)(2,1)S(1)}, u32[]{:S(2)}, u32[]{:S(2)}) collective-permute-start(bf16[4,64,1536]{2,1,0:T(8,128)(2,1)S(1)} %bitcast_dynamic-update-slice_fusion.20), channel_id=1, source_target_pairs={{0,16},{16,0},{1,17},{17,1},{2,18},{18,2},{3,19},{19,3},{4,20},{20... | collective-permute-start | bytes 2359304 | tf_op jit(solution)/shard_map/ppermute | solution.py:97
  100.1 37.7 %collective-permute-start.17 = (bf16[4,64,1536]{2,1,0:T(8,128)(2,1)S(1)}, bf16[4,64,1536]{2,1,0:T(8,128)(2,1)}, u32[]{:S(2)}, u32[]{:S(2)}) collective-permute-start(bf16[4,64,1536]{2,1,0:T(8,128)(2,1)S(1)} %bitcast_dynamic-update-slice_fusion.20), channel_id=1, source_target_pairs={{0,1},{1,2},{2,3},{3,0},{4,5},{5,6},{6,7},{7,4},{8,9},{9,10},{10,1... | collective-permute-start | bytes 2359304 | tf_op jit(solution)/shard_map/ppermute | solution.py:94
  110.3 19.1 %collective-permute-start.31 = (bf16[64,2048]{1,0:T(8,128)(2,1)S(1)}, bf16[64,2048]{1,0:T(8,128)(2,1)S(1)}, u32[]{:S(2)}, u32[]{:S(2)}) collective-permute-start(bf16[64,2048]{1,0:T(8,128)(2,1)S(1)} %collective-permute-done.30), channel_id=1, source_target_pairs={{0,1},{1,2},{2,3},{3,0},{4,5},{5,6},{6,7},{7,4},{8,9},{9,10},{10,1... | collective-permute-start | bytes 786440 | tf_op jit(solution)/shard_map/ppermute | solution.py:94
  137.8 35.7 %collective-permute-start.18 = (bf16[4,64,1536]{2,1,0:T(8,128)(2,1)}, bf16[4,64,1536]{2,1,0:T(8,128)(2,1)S(1)}, u32[]{:S(2)}, u32[]{:S(2)}) collective-permute-start(bf16[4,64,1536]{2,1,0:T(8,128)(2,1)} %collective-permute-done.17), channel_id=1, source_target_pairs={{0,16},{16,0},{1,17},{17,1},{2,18},{18,2},{3,19},{19,3},{4,20},{20... | collective-permute-start | bytes 2359304 | tf_op jit(solution)/shard_map/ppermute | solution.py:97
  137.8 38.4 %collective-permute-start.19 = (bf16[4,64,1536]{2,1,0:T(8,128)(2,1)}, bf16[4,64,1536]{2,1,0:T(8,128)(2,1)S(1)}, u32[]{:S(2)}, u32[]{:S(2)}) collective-permute-start(bf16[4,64,1536]{2,1,0:T(8,128)(2,1)} %collective-permute-done.17), channel_id=1, source_target_pairs={{0,1},{1,2},{2,3},{3,0},{4,5},{5,6},{6,7},{7,4},{8,9},{9,10},{10,1... | collective-permute-start | bytes 2359304 | tf_op jit(solution)/shard_map/ppermute | solution.py:94
  160.6 26.0 %collective-permute-start.33 = (bf16[4,64,2048]{2,1,0:T(8,128)(2,1)S(1)}, bf16[4,64,2048]{2,1,0:T(8,128)(2,1)S(1)}, u32[]{:S(2)}, u32[]{:S(2)}) collective-permute-start(bf16[4,64,2048]{2,1,0:T(8,128)(2,1)S(1)} %bitcast_dynamic-update-slice_fusion.16), channel_id=1, source_target_pairs={{0,4},{4,0},{8,12},{12,8},{1,5},{5,1},{9,13},{13,9},{2,6},{6,2},{1... | collective-permute-start | bytes 3145736 | tf_op jit(solution)/shard_map/ppermute | solution.py:91
  173.0 44.9 %collective-permute-start.35 = (bf16[4,64,2048]{2,1,0:T(8,128)(2,1)S(1)}, bf16[4,64,2048]{2,1,0:T(8,128)(2,1)S(1)}, u32[]{:S(2)}, u32[]{:S(2)}) collective-permute-start(bf16[4,64,2048]{2,1,0:T(8,128)(2,1)S(1)} %bitcast_dynamic-update-slice_fusion.16), channel_id=1, source_target_pairs={{0,8},{4,12},{8,0},{12,4},{1,9},{5,13},{9,1},{13,5},{2,10},{6,14},... | collective-permute-start | bytes 3145736 | tf_op jit(solution)/shard_map/ppermute | solution.py:91
  173.5 44.4 %collective-permute-start.37 = (bf16[4,64,2048]{2,1,0:T(8,128)(2,1)S(1)}, bf16[4,64,2048]{2,1,0:T(8,128)(2,1)S(1)}, u32[]{:S(2)}, u32[]{:S(2)}) collective-permute-start(bf16[4,64,2048]{2,1,0:T(8,128)(2,1)S(1)} %bitcast_dynamic-update-slice_fusion.16), channel_id=1, source_target_pairs={{0,12},{4,8},{8,4},{12,0},{1,13},{5,9},{9,5},{13,1},{2,14},{6,10},... | collective-permute-start | bytes 3145736 | tf_op jit(solution)/shard_map/ppermute | solution.py:91
  176.2 42.3 %collective-permute-start.20 = (bf16[4,64,1536]{2,1,0:T(8,128)(2,1)S(1)}, bf16[4,64,1536]{2,1,0:T(8,128)(2,1)S(1)}, u32[]{:S(2)}, u32[]{:S(2)}) collective-permute-start(bf16[4,64,1536]{2,1,0:T(8,128)(2,1)S(1)} %collective-permute-done.19), channel_id=1, source_target_pairs={{0,16},{16,0},{1,17},{17,1},{2,18},{18,2},{3,19},{19,3},{4,20},{20... | collective-permute-start | bytes 2359304 | tf_op jit(solution)/shard_map/ppermute | solution.py:97
  176.4 42.0 %collective-permute-start.21 = (bf16[4,64,1536]{2,1,0:T(8,128)(2,1)S(1)}, bf16[4,64,1536]{2,1,0:T(8,128)(2,1)S(1)}, u32[]{:S(2)}, u32[]{:S(2)}) collective-permute-start(bf16[4,64,1536]{2,1,0:T(8,128)(2,1)S(1)} %collective-permute-done.19), channel_id=1, source_target_pairs={{0,1},{1,2},{2,3},{3,0},{4,5},{5,6},{6,7},{7,4},{8,9},{9,10},{10,1... | collective-permute-start | bytes 2359304 | tf_op jit(solution)/shard_map/ppermute | solution.py:94
  186.5 32.1 %collective-permute-start.34 = (bf16[4,64,2048]{2,1,0:T(8,128)(2,1)S(1)}, bf16[4,64,2048]{2,1,0:T(8,128)(2,1)S(1)}, u32[]{:S(2)}, u32[]{:S(2)}) collective-permute-start(bf16[4,64,2048]{2,1,0:T(8,128)(2,1)S(1)} %collective-permute-done.33), channel_id=1, source_target_pairs={{0,16},{16,0},{1,17},{17,1},{2,18},{18,2},{3,19},{19,3},{4,20},{20... | collective-permute-start | bytes 3145736 | tf_op jit(solution)/shard_map/ppermute | solution.py:97
  269.6 24.8 %collective-permute-start.84 = (bf16[72,2048]{1,0:T(8,128)(2,1)S(1)}, bf16[72,2048]{1,0:T(8,128)(2,1)S(1)}, u32[]{:S(2)}, u32[]{:S(2)}) collective-permute-start(bf16[72,2048]{1,0:T(8,128)(2,1)S(1)} %get-tuple-element.111), channel_id=1, source_target_pairs={{0,4},{4,0},{8,12},{12,8},{1,5},{5,1},{9,13},{13,9},{2,6},{6,2},{1... | collective-permute-start | bytes 884744 | tf_op jit(solution)/shard_map/ppermute | solution.py:91
  290.1 28.7 %collective-permute-start.85 = (bf16[72,2048]{1,0:T(8,128)(2,1)S(1)}, bf16[72,2048]{1,0:T(8,128)(2,1)S(1)}, u32[]{:S(2)}, u32[]{:S(2)}) collective-permute-start(bf16[72,2048]{1,0:T(8,128)(2,1)S(1)} %get-tuple-element.110), channel_id=1, source_target_pairs={{0,8},{4,12},{8,0},{12,4},{1,9},{5,13},{9,1},{13,5},{2,10},{6,14},... | collective-permute-start | bytes 884744 | tf_op jit(solution)/shard_map/ppermute | solution.py:91
  291.2 30.0 %collective-permute-start.86 = (bf16[72,2048]{1,0:T(8,128)(2,1)S(1)}, bf16[72,2048]{1,0:T(8,128)(2,1)S(1)}, u32[]{:S(2)}, u32[]{:S(2)}) collective-permute-start(bf16[72,2048]{1,0:T(8,128)(2,1)S(1)} %get-tuple-element.109), channel_id=1, source_target_pairs={{0,12},{4,8},{8,4},{12,0},{1,13},{5,9},{9,5},{13,1},{2,14},{6,10},... | collective-permute-start | bytes 884744 | tf_op jit(solution)/shard_map/ppermute | solution.py:91
  292.5 21.7 %collective-permute-start.45 = (bf16[72,2048]{1,0:T(8,128)(2,1)S(1)}, bf16[72,2048]{1,0:T(8,128)(2,1)S(1)}, u32[]{:S(2)}, u32[]{:S(2)}) collective-permute-start(bf16[72,2048]{1,0:T(8,128)(2,1)S(1)} %get-tuple-element.102), channel_id=1, source_target_pairs={{0,8},{4,12},{8,0},{12,4},{1,9},{5,13},{9,1},{13,5},{2,10},{6,14},... | collective-permute-start | bytes 884744 | tf_op jit(solution)/shard_map/ppermute | solution.py:91
  295.2 19.8 %collective-permute-start.46 = (bf16[72,2048]{1,0:T(8,128)(2,1)S(1)}, bf16[72,2048]{1,0:T(8,128)(2,1)S(1)}, u32[]{:S(2)}, u32[]{:S(2)}) collective-permute-start(bf16[72,2048]{1,0:T(8,128)(2,1)S(1)} %get-tuple-element.101), channel_id=1, source_target_pairs={{0,12},{4,8},{8,4},{12,0},{1,13},{5,9},{9,5},{13,1},{2,14},{6,10},... | collective-permute-start | bytes 884744 | tf_op jit(solution)/shard_map/ppermute | solution.py:91
  431.9 20.4 %collective-permute-start.69 = (bf16[72,2048]{1,0:T(8,128)(2,1)S(1)}, bf16[72,2048]{1,0:T(8,128)(2,1)S(1)}, u32[]{:S(2)}, u32[]{:S(2)}) collective-permute-start(bf16[72,2048]{1,0:T(8,128)(2,1)S(1)} %get-tuple-element.61), channel_id=1, source_target_pairs={{0,8},{4,12},{8,0},{12,4},{1,9},{5,13},{9,1},{13,5},{2,10},{6,14},... | collective-permute-start | bytes 884744 | tf_op jit(solution)/shard_map/ppermute | solution.py:91
  432.6 21.8 %collective-permute-start.68 = (bf16[72,2048]{1,0:T(8,128)(2,1)S(1)}, bf16[72,2048]{1,0:T(8,128)(2,1)S(1)}, u32[]{:S(2)}, u32[]{:S(2)}) collective-permute-start(bf16[72,2048]{1,0:T(8,128)(2,1)S(1)} %get-tuple-element.62), channel_id=1, source_target_pairs={{0,4},{4,0},{8,12},{12,8},{1,5},{5,1},{9,13},{13,9},{2,6},{6,2},{1... | collective-permute-start | bytes 884744 | tf_op jit(solution)/shard_map/ppermute | solution.py:91
  434.3 24.5 %collective-permute-start.66 = (bf16[72,2048]{1,0:T(8,128)(2,1)S(1)}, bf16[72,2048]{1,0:T(8,128)(2,1)S(1)}, u32[]{:S(2)}, u32[]{:S(2)}) collective-permute-start(bf16[72,2048]{1,0:T(8,128)(2,1)S(1)} %get-tuple-element.64), channel_id=1, source_target_pairs={{0,12},{4,8},{8,4},{12,0},{1,13},{5,9},{9,5},{13,1},{2,14},{6,10},... | collective-permute-start | bytes 884744 | tf_op jit(solution)/shard_map/ppermute | solution.py:91
  439.8 25.1 %collective-permute-start.65 = (bf16[72,2048]{1,0:T(8,128)(2,1)S(1)}, bf16[72,2048]{1,0:T(8,128)(2,1)S(1)}, u32[]{:S(2)}, u32[]{:S(2)}) collective-permute-start(bf16[72,2048]{1,0:T(8,128)(2,1)S(1)} %get-tuple-element.65), channel_id=1, source_target_pairs={{0,8},{4,12},{8,0},{12,4},{1,9},{5,13},{9,1},{13,5},{2,10},{6,14},... | collective-permute-start | bytes 884744 | tf_op jit(solution)/shard_map/ppermute | solution.py:91
  446.2 20.9 %collective-permute-start.64 = (bf16[72,2048]{1,0:T(8,128)(2,1)S(1)}, bf16[72,2048]{1,0:T(8,128)(2,1)S(1)}, u32[]{:S(2)}, u32[]{:S(2)}) collective-permute-start(bf16[72,2048]{1,0:T(8,128)(2,1)S(1)} %get-tuple-element.66), channel_id=1, source_target_pairs={{0,4},{4,0},{8,12},{12,8},{1,5},{5,1},{9,13},{13,9},{2,6},{6,2},{1... | collective-permute-start | bytes 884744 | tf_op jit(solution)/shard_map/ppermute | solution.py:91
  452.3 19.2 %collective-permute-start.62 = (bf16[72,2048]{1,0:T(8,128)(2,1)S(1)}, bf16[72,2048]{1,0:T(8,128)(2,1)S(1)}, u32[]{:S(2)}, u32[]{:S(2)}) collective-permute-start(bf16[72,2048]{1,0:T(8,128)(2,1)S(1)} %get-tuple-element.68), channel_id=1, source_target_pairs={{0,12},{4,8},{8,4},{12,0},{1,13},{5,9},{9,5},{13,1},{2,14},{6,10},... | collective-permute-start | bytes 884744 | tf_op jit(solution)/shard_map/ppermute | solution.py:91
  454.4 23.4 %collective-permute-start.61 = (bf16[72,2048]{1,0:T(8,128)(2,1)S(1)}, bf16[72,2048]{1,0:T(8,128)(2,1)S(1)}, u32[]{:S(2)}, u32[]{:S(2)}) collective-permute-start(bf16[72,2048]{1,0:T(8,128)(2,1)S(1)} %get-tuple-element.69), channel_id=1, source_target_pairs={{0,8},{4,12},{8,0},{12,4},{1,9},{5,13},{9,1},{13,5},{2,10},{6,14},... | collective-permute-start | bytes 884744 | tf_op jit(solution)/shard_map/ppermute | solution.py:91
  458.8 26.8 %collective-permute-start.60 = (bf16[72,2048]{1,0:T(8,128)(2,1)S(1)}, bf16[72,2048]{1,0:T(8,128)(2,1)S(1)}, u32[]{:S(2)}, u32[]{:S(2)}) collective-permute-start(bf16[72,2048]{1,0:T(8,128)(2,1)S(1)} %get-tuple-element.70), channel_id=1, source_target_pairs={{0,4},{4,0},{8,12},{12,8},{1,5},{5,1},{9,13},{13,9},{2,6},{6,2},{1... | collective-permute-start | bytes 884744 | tf_op jit(solution)/shard_map/ppermute | solution.py:91
  464.9 20.7 %collective-permute-start.100 = (bf16[72,2176]{1,0:T(8,128)(2,1)S(1)}, bf16[72,2176]{1,0:T(8,128)(2,1)S(1)}, u32[]{:S(2)}, u32[]{:S(2)}) collective-permute-start(bf16[72,2176]{1,0:T(8,128)(2,1)S(1)} %get-tuple-element.57), channel_id=1, source_target_pairs={{0,12},{4,8},{8,4},{12,0},{1,13},{5,9},{9,5},{13,1},{2,14},{6,10},... | collective-permute-start | bytes 940040 | tf_op jit(solution)/shard_map/ppermute | solution.py:91
  467.0 24.2 %collective-permute-start.99 = (bf16[72,2176]{1,0:T(8,128)(2,1)S(1)}, bf16[72,2176]{1,0:T(8,128)(2,1)S(1)}, u32[]{:S(2)}, u32[]{:S(2)}) collective-permute-start(bf16[72,2176]{1,0:T(8,128)(2,1)S(1)} %get-tuple-element.58), channel_id=1, source_target_pairs={{0,8},{4,12},{8,0},{12,4},{1,9},{5,13},{9,1},{13,5},{2,10},{6,14},... | collective-permute-start | bytes 940040 | tf_op jit(solution)/shard_map/ppermute | solution.py:91
  471.5 22.6 %collective-permute-start.98 = (bf16[72,2176]{1,0:T(8,128)(2,1)S(1)}, bf16[72,2176]{1,0:T(8,128)(2,1)S(1)}, u32[]{:S(2)}, u32[]{:S(2)}) collective-permute-start(bf16[72,2176]{1,0:T(8,128)(2,1)S(1)} %get-tuple-element.56), channel_id=1, source_target_pairs={{0,4},{4,0},{8,12},{12,8},{1,5},{5,1},{9,13},{13,9},{2,6},{6,2},{1... | collective-permute-start | bytes 940040 | tf_op jit(solution)/shard_map/ppermute | solution.py:91
  477.8 20.1 %collective-permute-start.96 = (bf16[72,2176]{1,0:T(8,128)(2,1)S(1)}, bf16[72,2176]{1,0:T(8,128)(2,1)S(1)}, u32[]{:S(2)}, u32[]{:S(2)}) collective-permute-start(bf16[72,2176]{1,0:T(8,128)(2,1)S(1)} %get-tuple-element.54), channel_id=1, source_target_pairs={{0,12},{4,8},{8,4},{12,0},{1,13},{5,9},{9,5},{13,1},{2,14},{6,10},... | collective-permute-start | bytes 940040 | tf_op jit(solution)/shard_map/ppermute | solution.py:91
  485.6 19.0 %collective-permute-start.95 = (bf16[72,2176]{1,0:T(8,128)(2,1)S(1)}, bf16[72,2176]{1,0:T(8,128)(2,1)S(1)}, u32[]{:S(2)}, u32[]{:S(2)}) collective-permute-start(bf16[72,2176]{1,0:T(8,128)(2,1)S(1)} %get-tuple-element.53), channel_id=1, source_target_pairs={{0,8},{4,12},{8,0},{12,4},{1,9},{5,13},{9,1},{13,5},{2,10},{6,14},... | collective-permute-start | bytes 940040 | tf_op jit(solution)/shard_map/ppermute | solution.py:91
  485.7 20.1 %collective-permute-start.94 = (bf16[72,2176]{1,0:T(8,128)(2,1)S(1)}, bf16[72,2176]{1,0:T(8,128)(2,1)S(1)}, u32[]{:S(2)}, u32[]{:S(2)}) collective-permute-start(bf16[72,2176]{1,0:T(8,128)(2,1)S(1)} %get-tuple-element.52), channel_id=1, source_target_pairs={{0,4},{4,0},{8,12},{12,8},{1,5},{5,1},{9,13},{13,9},{2,6},{6,2},{1... | collective-permute-start | bytes 940040 | tf_op jit(solution)/shard_map/ppermute | solution.py:91
  491.2 20.1 %collective-permute-start.92 = (bf16[72,2176]{1,0:T(8,128)(2,1)S(1)}, bf16[72,2176]{1,0:T(8,128)(2,1)S(1)}, u32[]{:S(2)}, u32[]{:S(2)}) collective-permute-start(bf16[72,2176]{1,0:T(8,128)(2,1)S(1)} %get-tuple-element.50), channel_id=1, source_target_pairs={{0,12},{4,8},{8,4},{12,0},{1,13},{5,9},{9,5},{13,1},{2,14},{6,10},... | collective-permute-start | bytes 940040 | tf_op jit(solution)/shard_map/ppermute | solution.py:91
  494.0 21.4 %collective-permute-start.91 = (bf16[72,2176]{1,0:T(8,128)(2,1)S(1)}, bf16[72,2176]{1,0:T(8,128)(2,1)S(1)}, u32[]{:S(2)}, u32[]{:S(2)}) collective-permute-start(bf16[72,2176]{1,0:T(8,128)(2,1)S(1)} %get-tuple-element.49), channel_id=1, source_target_pairs={{0,8},{4,12},{8,0},{12,4},{1,9},{5,13},{9,1},{13,5},{2,10},{6,14},... | collective-permute-start | bytes 940040 | tf_op jit(solution)/shard_map/ppermute | solution.py:91
  504.7 37.5 %collective-permute-start.71 = (bf16[136,2048]{1,0:T(8,128)(2,1)S(1)}, bf16[136,2048]{1,0:T(8,128)(2,1)S(1)}, u32[]{:S(2)}, u32[]{:S(2)}) collective-permute-start(bf16[136,2048]{1,0:T(8,128)(2,1)S(1)} %convolution_convert_fusion.13), channel_id=1, source_target_pairs={{0,1},{1,2},{2,3},{3,0},{4,5},{5,6},{6,7},{7,4},{8,9},{9,10},{10,1... | collective-permute-start | bytes 1671176 | tf_op jit(solution)/shard_map/ppermute | solution.py:94
  505.7 40.4 %collective-permute-start.67 = (bf16[136,2048]{1,0:T(8,128)(2,1)S(1)}, bf16[136,2048]{1,0:T(8,128)(2,1)S(1)}, u32[]{:S(2)}, u32[]{:S(2)}) collective-permute-start(bf16[136,2048]{1,0:T(8,128)(2,1)S(1)} %convolution_convert_fusion.14), channel_id=1, source_target_pairs={{0,2},{1,3},{2,0},{3,1},{4,6},{5,7},{6,4},{7,5},{8,10},{9,11},{10,... | collective-permute-start | bytes 1671176 | tf_op jit(solution)/shard_map/ppermute | solution.py:94
  511.3 63.0 %collective-permute-start.63 = (bf16[136,2048]{1,0:T(8,128)(2,1)S(1)}, bf16[136,2048]{1,0:T(8,128)(2,1)S(1)}, u32[]{:S(2)}, u32[]{:S(2)}) collective-permute-start(bf16[136,2048]{1,0:T(8,128)(2,1)S(1)} %convolution_convert_fusion.15), channel_id=1, source_target_pairs={{0,3},{1,0},{2,1},{3,2},{4,7},{5,4},{6,5},{7,6},{8,11},{9,8},{10,9... | collective-permute-start | bytes 1671176 | tf_op jit(solution)/shard_map/ppermute | solution.py:94
  523.5 56.0 %collective-permute-start.89 = (bf16[72,2176]{1,0:T(8,128)(2,1)S(1)}, bf16[72,2176]{1,0:T(8,128)(2,1)S(1)}, u32[]{:S(2)}, u32[]{:S(2)}) collective-permute-start(bf16[72,2176]{1,0:T(8,128)(2,1)S(1)} %get-tuple-element.47), channel_id=1, source_target_pairs={{0,12},{4,8},{8,4},{12,0},{1,13},{5,9},{9,5},{13,1},{2,14},{6,10},... | collective-permute-start | bytes 940040 | tf_op jit(solution)/shard_map/ppermute | solution.py:91
  526.2 54.0 %collective-permute-start.88 = (bf16[72,2176]{1,0:T(8,128)(2,1)S(1)}, bf16[72,2176]{1,0:T(8,128)(2,1)S(1)}, u32[]{:S(2)}, u32[]{:S(2)}) collective-permute-start(bf16[72,2176]{1,0:T(8,128)(2,1)S(1)} %get-tuple-element.46), channel_id=1, source_target_pairs={{0,8},{4,12},{8,0},{12,4},{1,9},{5,13},{9,1},{13,5},{2,10},{6,14},... | collective-permute-start | bytes 940040 | tf_op jit(solution)/shard_map/ppermute | solution.py:91
  542.2 52.0 %collective-permute-start.101 = (bf16[136,2176]{1,0:T(8,128)(2,1)S(1)}, bf16[136,2176]{1,0:T(8,128)(2,1)S(1)}, u32[]{:S(2)}, u32[]{:S(2)}) collective-permute-start(bf16[136,2176]{1,0:T(8,128)(2,1)S(1)} %convolution_convert_fusion.1), channel_id=1, source_target_pairs={{0,1},{1,2},{2,3},{3,0},{4,5},{5,6},{6,7},{7,4},{8,9},{9,10},{10,1... | collective-permute-start | bytes 1775624 | tf_op jit(solution)/shard_map/ppermute | solution.py:94
  546.2 48.0 %collective-permute-start.97 = (bf16[136,2176]{1,0:T(8,128)(2,1)S(1)}, bf16[136,2176]{1,0:T(8,128)(2,1)S(1)}, u32[]{:S(2)}, u32[]{:S(2)}) collective-permute-start(bf16[136,2176]{1,0:T(8,128)(2,1)S(1)} %convolution_convert_fusion.2), channel_id=1, source_target_pairs={{0,2},{1,3},{2,0},{3,1},{4,6},{5,7},{6,4},{7,5},{8,10},{9,11},{10,... | collective-permute-start | bytes 1775624 | tf_op jit(solution)/shard_map/ppermute | solution.py:94
  574.3 30.7 %collective-permute-start.93 = (bf16[136,2176]{1,0:T(8,128)(2,1)S(1)}, bf16[136,2176]{1,0:T(8,128)(2,1)S(1)}, u32[]{:S(2)}, u32[]{:S(2)}) collective-permute-start(bf16[136,2176]{1,0:T(8,128)(2,1)S(1)} %convolution_convert_fusion.3), channel_id=1, source_target_pairs={{0,3},{1,0},{2,1},{3,2},{4,7},{5,4},{6,5},{7,6},{8,11},{9,8},{10,9... | collective-permute-start | bytes 1775624 | tf_op jit(solution)/shard_map/ppermute | solution.py:94
  612.7 80.5 %collective-permute-start.120 = (bf16[136,2048]{1,0:T(8,128)(2,1)}, bf16[136,2048]{1,0:T(8,128)(2,1)}, u32[]{:S(2)}, u32[]{:S(2)}) collective-permute-start(bf16[136,2048]{1,0:T(8,128)(2,1)} %get-tuple-element.33), channel_id=1, source_target_pairs={{0,12},{4,8},{8,4},{12,0},{1,13},{5,9},{9,5},{13,1},{2,14},{6,10},... | collective-permute-start | bytes 1671176 | tf_op jit(solution)/shard_map/ppermute | solution.py:91
  613.8 79.4 %collective-permute-start.119 = (bf16[136,2048]{1,0:T(8,128)(2,1)}, bf16[136,2048]{1,0:T(8,128)(2,1)}, u32[]{:S(2)}, u32[]{:S(2)}) collective-permute-start(bf16[136,2048]{1,0:T(8,128)(2,1)} %get-tuple-element.33), channel_id=1, source_target_pairs={{0,8},{4,12},{8,0},{12,4},{1,9},{5,13},{9,1},{13,5},{2,10},{6,14},... | collective-permute-start | bytes 1671176 | tf_op jit(solution)/shard_map/ppermute | solution.py:91
  616.6 28.7 %collective-permute-start.103 = (bf16[136,512]{1,0:T(8,128)(2,1)S(1)}, bf16[136,512]{1,0:T(8,128)(2,1)S(1)}, u32[]{:S(2)}, u32[]{:S(2)}) collective-permute-start(bf16[136,512]{1,0:T(8,128)(2,1)S(1)} %get-tuple-element.183), channel_id=1, source_target_pairs={{0,8},{4,12},{8,0},{12,4},{1,9},{5,13},{9,1},{13,5},{2,10},{6,14},... | collective-permute-start | bytes 417800 | tf_op jit(solution)/shard_map/ppermute | solution.py:91
  618.6 26.7 %collective-permute-start.102 = (bf16[136,512]{1,0:T(8,128)(2,1)S(1)}, bf16[136,512]{1,0:T(8,128)(2,1)S(1)}, u32[]{:S(2)}, u32[]{:S(2)}) collective-permute-start(bf16[136,512]{1,0:T(8,128)(2,1)S(1)} %get-tuple-element.184), channel_id=1, source_target_pairs={{0,4},{4,0},{8,12},{12,8},{1,5},{5,1},{9,13},{13,9},{2,6},{6,2},{1... | collective-permute-start | bytes 417800 | tf_op jit(solution)/shard_map/ppermute | solution.py:91
  666.9 26.4 %collective-permute-start.118 = (bf16[136,2048]{1,0:T(8,128)(2,1)}, bf16[136,2048]{1,0:T(8,128)(2,1)S(1)}, u32[]{:S(2)}, u32[]{:S(2)}) collective-permute-start(bf16[136,2048]{1,0:T(8,128)(2,1)} %get-tuple-element.33), channel_id=1, source_target_pairs={{0,4},{4,0},{8,12},{12,8},{1,5},{5,1},{9,13},{13,9},{2,6},{6,2},{1... | collective-permute-start | bytes 1671176 | tf_op jit(solution)/shard_map/ppermute | solution.py:91
  686.3 25.0 %collective-permute-start.109 = (bf16[136,2048]{1,0:T(8,128)(2,1)S(1)}, bf16[136,2048]{1,0:T(8,128)(2,1)S(1)}, u32[]{:S(2)}, u32[]{:S(2)}) collective-permute-start(bf16[136,2048]{1,0:T(8,128)(2,1)S(1)} %get-tuple-element.81), channel_id=1, source_target_pairs={{0,8},{4,12},{8,0},{12,4},{1,9},{5,13},{9,1},{13,5},{2,10},{6,14},... | collective-permute-start | bytes 1671176 | tf_op jit(solution)/shard_map/ppermute | solution.py:91
  693.3 34.1 %collective-permute-start.111 = (bf16[4,4,64,1536]{3,2,0,1:T(8,128)(2,1)}, bf16[4,4,64,1536]{3,2,0,1:T(8,128)(2,1)}, u32[]{:S(2)}, u32[]{:S(2)}) collective-permute-start(bf16[4,4,64,1536]{3,2,0,1:T(8,128)(2,1)} %fusion.22), channel_id=1, source_target_pairs={{0,16},{16,0},{1,17},{17,1},{2,18},{18,2},{3,19},{19,3},{4,20},{20... | collective-permute-start | bytes 9437192 | tf_op jit(solution)/shard_map/ppermute | solution.py:97
  697.8 25.9 %collective-permute-start.121 = (bf16[4,64,2048]{2,1,0:T(8,128)(2,1)}, bf16[4,64,2048]{2,1,0:T(8,128)(2,1)}, u32[]{:S(2)}, u32[]{:S(2)}) collective-permute-start(bf16[4,64,2048]{2,1,0:T(8,128)(2,1)} %fusion.114), channel_id=1, source_target_pairs={{0,16},{16,0},{1,17},{17,1},{2,18},{18,2},{3,19},{19,3},{4,20},{20... | collective-permute-start | bytes 3145736 | tf_op jit(solution)/shard_map/ppermute | solution.py:97
  719.0 68.9 %collective-permute-start.132 = (bf16[1024,2048]{1,0:T(8,128)(2,1)}, bf16[1024,2048]{1,0:T(8,128)(2,1)S(1)}, u32[]{:S(2)}, u32[]{:S(2)}) collective-permute-start(bf16[1024,2048]{1,0:T(8,128)(2,1)} %fusion.15), channel_id=1, source_target_pairs={{0,16},{16,0},{1,17},{17,1},{2,18},{18,2},{3,19},{19,3},{4,20},{20... | collective-permute-start | bytes 12582920 | tf_op jit(solution)/shard_map/ppermute | solution.py:97
  719.6 42.0 %collective-permute-start.133 = (bf16[512,2048]{1,0:T(8,128)(2,1)S(1)}, bf16[512,2048]{1,0:T(8,128)(2,1)}, u32[]{:S(2)}, u32[]{:S(2)}) collective-permute-start(bf16[512,2048]{1,0:T(8,128)(2,1)S(1)} %copy-done.36), channel_id=1, source_target_pairs={{0,16},{16,0},{1,17},{17,1},{2,18},{18,2},{3,19},{19,3},{4,20},{20... | collective-permute-start | bytes 6291464 | tf_op jit(solution)/shard_map/ppermute | solution.py:97
  735.3 23.7 %collective-permute-start.112 = (bf16[4,64,1536]{2,1,0:T(8,128)(2,1)S(1)}, bf16[4,64,1536]{2,1,0:T(8,128)(2,1)S(1)}, u32[]{:S(2)}, u32[]{:S(2)}) collective-permute-start(bf16[4,64,1536]{2,1,0:T(8,128)(2,1)S(1)} %fusion.115), channel_id=1, source_target_pairs={{0,1},{1,2},{2,3},{3,0},{4,5},{5,6},{6,7},{7,4},{8,9},{9,10},{10,1... | collective-permute-start | bytes 2359304 | tf_op jit(solution)/shard_map/ppermute | solution.py:94
  742.2 23.6 %collective-permute-start.123 = (bf16[64,2048]{1,0:T(8,128)(2,1)S(1)}, bf16[64,2048]{1,0:T(8,128)(2,1)S(1)}, u32[]{:S(2)}, u32[]{:S(2)}) collective-permute-start(bf16[64,2048]{1,0:T(8,128)(2,1)S(1)} %fusion.125), channel_id=1, source_target_pairs={{0,1},{1,2},{2,3},{3,0},{4,5},{5,6},{6,7},{7,4},{8,9},{9,10},{10,1... | collective-permute-start | bytes 786440 | tf_op jit(solution)/shard_map/ppermute | solution.py:94
  759.2 22.2 %collective-permute-start.113 = (bf16[4,64,1536]{2,1,0:T(8,128)(2,1)S(1)}, bf16[4,64,1536]{2,1,0:T(8,128)(2,1)S(1)}, u32[]{:S(2)}, u32[]{:S(2)}) collective-permute-start(bf16[4,64,1536]{2,1,0:T(8,128)(2,1)S(1)} %fusion.39), channel_id=1, source_target_pairs={{0,1},{1,2},{2,3},{3,0},{4,5},{5,6},{6,7},{7,4},{8,9},{9,10},{10,1... | collective-permute-start | bytes 2359304 | tf_op jit(solution)/shard_map/ppermute | solution.py:94
  765.9 21.2 %collective-permute-start.124 = (bf16[64,2048]{1,0:T(8,128)(2,1)S(1)}, bf16[64,2048]{1,0:T(8,128)(2,1)S(1)}, u32[]{:S(2)}, u32[]{:S(2)}) collective-permute-start(bf16[64,2048]{1,0:T(8,128)(2,1)S(1)} %fusion.124), channel_id=1, source_target_pairs={{0,1},{1,2},{2,3},{3,0},{4,5},{5,6},{6,7},{7,4},{8,9},{9,10},{10,1... | collective-permute-start | bytes 786440 | tf_op jit(solution)/shard_map/ppermute | solution.py:94
  781.7 19.8 %collective-permute-start.114 = (bf16[4,64,1536]{2,1,0:T(8,128)(2,1)S(1)}, bf16[4,64,1536]{2,1,0:T(8,128)(2,1)S(1)}, u32[]{:S(2)}, u32[]{:S(2)}) collective-permute-start(bf16[4,64,1536]{2,1,0:T(8,128)(2,1)S(1)} %fusion.38), channel_id=1, source_target_pairs={{0,1},{1,2},{2,3},{3,0},{4,5},{5,6},{6,7},{7,4},{8,9},{9,10},{10,1... | collective-permute-start | bytes 2359304 | tf_op jit(solution)/shard_map/ppermute | solution.py:94
  (171 other events, 2901.0 us)

commit v2 on v1

v2 whole, which is shorter than its diff:
```python
import jax
import jax.numpy as jnp
from jax import lax
from jax.experimental import pallas as pl
from jax.experimental.pallas import tpu as pltpu
from jax.sharding import PartitionSpec as P

D = 2048
HEADS = 16
HEAD_DIM = 128
FF = 1024
TOP = 8

NORM_EPS = 1e-05
ROPE_BASE = 10000.0
NEGATIVE = -1e30
HIGHEST_PREC = lax.Precision.HIGHEST
F32 = jnp.float32
BF16 = jnp.bfloat16


def row_scale(values):
    return lax.rsqrt(jnp.mean(values * values, axis=-1, keepdims=True) + NORM_EPS)


def rope_tables(position, half_dim):
    inverse = ROPE_BASE ** (-jnp.arange(half_dim, dtype=F32) / half_dim)
    angles = position[:, None] * inverse[None, :]
    cosine, sine_rows = jnp.cos(angles), jnp.sin(angles)
    return (
        jnp.concatenate([cosine, cosine], axis=1),
        jnp.concatenate([-sine_rows, sine_rows], axis=1),
    )


def norm_back(grad_rows, normed, scale_rows, gain_col):
    grad_normed = grad_rows * gain_col
    grad_input = scale_rows * (
        grad_normed - normed * jnp.mean(grad_normed * normed, axis=-1, keepdims=True)
    )
    return (grad_input, jnp.sum(grad_rows * normed, axis=0))


def dot(a, b):
    return jnp.dot(a, b, preferred_element_type=F32)


def dot_bt(a, b):
    return lax.dot_general(a, b, (((1,), (1,)), ((), ())), preferred_element_type=F32)


def dot_at(a, b):
    return lax.dot_general(a, b, (((0,), (0,)), ((), ())), preferred_element_type=F32)


def attend(projected, scales, gains, cosine, sine_rows, hidden_pairs):
    rows = projected.shape[0]
    width = projected.shape[1] // 3
    heads = width // HEAD_DIM

    def kernel(pq, pk, pv, scale_ref, gain_ref, cos_ref, sin_ref, pair_ref, mixed, q, k, v, total):
        def turned(values):
            return values * cos_ref[...] + pltpu.roll(values, HEAD_DIM // 2, 1) * sin_ref[...]

        query = turned(pq[...] * scale_ref[:, :1] * gain_ref[:1, :]).astype(BF16)
        key = turned(pk[...] * scale_ref[:, 1:2] * gain_ref[1:2, :]).astype(BF16)
        value = pv[...].astype(BF16)
        scores = dot_bt(query, key) * HEAD_DIM ** (-0.5)
        scores = jnp.where(pair_ref[...] < 0.0, NEGATIVE, scores)
        row_max = jnp.max(scores, axis=-1, keepdims=True)
        log_total = row_max + jnp.log(
            jnp.sum(jnp.exp(scores - row_max), axis=-1, keepdims=True)
        )
        mixed[...] = dot(jnp.exp(scores - log_total).astype(BF16), value).astype(BF16)
        q[...], k[...], v[...] = query, key, value
        total[...] = jnp.broadcast_to(log_total, total.shape)

    def head(part):
        return pl.BlockSpec((rows, HEAD_DIM), lambda h: (0, part * heads + h))

    def whole(shape):
        return pl.BlockSpec(shape, lambda h: (0, 0))

    return pl.pallas_call(
        kernel,
        grid=(heads,),
        in_specs=[
            head(0),
            head(1),
            head(2),
            whole((rows, 2)),
            pl.BlockSpec((2, HEAD_DIM), lambda h: (0, h)),
            whole((rows, HEAD_DIM)),
            whole((rows, HEAD_DIM)),
            whole((rows, rows)),
        ],
        out_specs=[head(0)] * 5,
        out_shape=[jax.ShapeDtypeStruct((rows, width), BF16)] * 4
        + [jax.ShapeDtypeStruct((rows, width), F32)],
        compiler_params=pltpu.CompilerParams(vmem_limit_bytes=48 << 20),
        cost_estimate=pl.CostEstimate(flops=0, bytes_accessed=0, transcendentals=0),
        name="attend",
    )(projected, projected, projected, scales, gains, cosine, sine_rows, hidden_pairs)


def attend_back(grads, kept, projected, scales, gains, cosine, sine_rows, hidden_pairs):
    query_b, key_b, value_b, log_total = kept
    rows = projected.shape[0]
    width = projected.shape[1] // 3
    heads = width // HEAD_DIM
    scale = HEAD_DIM ** (-0.5)

    def kernel(
        g, q, k, v, total, pq, pk, scale_ref, gain_ref, cos_ref, sin_ref, pair_ref,
        query_out, key_out, value_out, gain_out, sum_out,
    ):
        def turned_back(values):
            return values * cos_ref[...] - pltpu.roll(values, HEAD_DIM // 2, 1) * sin_ref[...]

        scores = dot_bt(q[...], k[...]) * scale
        scores = jnp.where(pair_ref[...] < 0.0, NEGATIVE, scores)
        attention = jnp.exp(scores - total[:, :1])
        prob_att = dot_bt(g[...], v[...])
        delta = jnp.sum(attention * prob_att, axis=-1, keepdims=True)
        score_grad = (attention * (prob_att - delta)).astype(BF16)
        query = turned_back(dot(score_grad, k[...]) * scale)
        key = turned_back(dot_at(score_grad, q[...]) * scale)
        value_out[...] = dot_at(attention.astype(BF16), g[...]).astype(BF16)
        query_out[...], key_out[...] = query, key
        query_n = query * (pq[...] * scale_ref[:, :1])
        key_n = key * (pk[...] * scale_ref[:, 1:2])
        gain_out[:1, :] = jnp.sum(query_n, axis=0, keepdims=True)
        gain_out[1:2, :] = jnp.sum(key_n, axis=0, keepdims=True)
        query_sum = jnp.sum(query_n * gain_ref[:1, :], axis=-1, keepdims=True)
        key_sum = jnp.sum(key_n * gain_ref[1:2, :], axis=-1, keepdims=True)
        sums = jnp.concatenate(
            [
                jnp.broadcast_to(query_sum, (rows, HEAD_DIM)),
                jnp.broadcast_to(key_sum, (rows, HEAD_DIM)),
            ],
            axis=1,
        )

        @pl.when(pl.program_id(0) == 0)
        def _():
            sum_out[...] = sums

        @pl.when(pl.program_id(0) > 0)
        def _():
            sum_out[...] += sums

    def head(part):
        return pl.BlockSpec((rows, HEAD_DIM), lambda h: (0, part * heads + h))

    def whole(shape):
        return pl.BlockSpec(shape, lambda h: (0, 0))

    pair = pl.BlockSpec((2, HEAD_DIM), lambda h: (0, h))
    return pl.pallas_call(
        kernel,
        grid=(heads,),
        in_specs=[head(0)] * 5
        + [
            head(0),
            head(1),
            whole((rows, 2)),
            pair,
            whole((rows, HEAD_DIM)),
            whole((rows, HEAD_DIM)),
            whole((rows, rows)),
        ],
        out_specs=[head(0)] * 3 + [pair, whole((rows, 2 * HEAD_DIM))],
        out_shape=[
            jax.ShapeDtypeStruct((rows, width), F32),
            jax.ShapeDtypeStruct((rows, width), F32),
            jax.ShapeDtypeStruct((rows, width), BF16),
            jax.ShapeDtypeStruct((2, width), F32),
            jax.ShapeDtypeStruct((rows, 2 * HEAD_DIM), F32),
        ],
        compiler_params=pltpu.CompilerParams(vmem_limit_bytes=48 << 20),
        cost_estimate=pl.CostEstimate(flops=0, bytes_accessed=0, transcendentals=0),
        name="attend_back",
    )(
        grads, query_b, key_b, value_b, log_total, projected, projected, scales, gains,
        cosine, sine_rows, hidden_pairs,
    )


def norms_back(query_turn, key_turn, value_grad, projected, scales, means, gains):
    rows, width = query_turn.shape

    def kernel(query, key, value, projected_ref, scale_ref, mean_ref, gain_ref, out):
        for i, turn in enumerate((query, key)):
            at = slice(i * width, (i + 1) * width)
            scale = scale_ref[:, i : i + 1]
            normed = projected_ref[:, at] * scale
            out[:, at] = (
                scale * (turn[...] * gain_ref[i : i + 1, :] - normed * mean_ref[:, i : i + 1])
            ).astype(BF16)
        out[:, 2 * width :] = value[...]

    return pl.pallas_call(
        kernel,
        out_shape=jax.ShapeDtypeStruct((rows, 3 * width), BF16),
        compiler_params=pltpu.CompilerParams(vmem_limit_bytes=48 << 20),
        cost_estimate=pl.CostEstimate(flops=0, bytes_accessed=0, transcendentals=0),
        name="norms_back",
    )(query_turn, key_turn, value_grad, projected, scales, means, gains)


def expert_rows(rows, cot, w_gate_up, w_down, w_router, expert, senders, blocks):
    count, experts = rows.shape[0], w_router.shape[1]
    tile = FF // 2
    steps = FF // tile
    extra = -(-2 * experts // 128) * 128
    piece = count // (senders * blocks)

    def kernel(expert_ref, rows_ref, cot_ref, wg_ref, wu_ref, wd_ref, wr_ref, *refs):
        row_refs = refs[:blocks]
        act_ref, gg_ref, ug_ref, gate_ref, row_sum, gate_grad = refs[blocks:]
        step = pl.program_id(0)
        row_block = rows_ref[...]

        @pl.when(step == 0)
        def _():
            logits = dot(row_block, wr_ref[...])
            shifted = jnp.exp(logits - jnp.max(logits, axis=-1, keepdims=True))
            router = shifted / jnp.sum(shifted, axis=-1, keepdims=True)
            lane = lax.broadcasted_iota(jnp.int32, router.shape, 1)
            own = jnp.sum(jnp.where(lane == expert_ref[0], router, 0.0), axis=-1, keepdims=True)
            gate_ref[...] = jnp.broadcast_to(own, gate_ref.shape)

        gate = gate_ref[:, :1]
        gate_part = dot(row_block, wg_ref[...])
        up_part = dot(row_block, wu_ref[...])
        cot_act = dot_bt(cot_ref[...], wd_ref[...])
        sigmoid_gate = jax.nn.sigmoid(gate_part)
        swish = gate_part * sigmoid_gate
        activated = (swish * up_part).astype(BF16)
        act_grad = gate * cot_act
        gate_part_grad = (
            act_grad * up_part * sigmoid_gate * (1.0 + gate_part * (1.0 - sigmoid_gate))
        ).astype(BF16)
        up_part_grad = (act_grad * swish).astype(BF16)
        act_ref[...] = activated
        gg_ref[...] = gate_part_grad
        ug_ref[...] = up_part_grad
        row_part = dot_bt(gate_part_grad, wg_ref[...]) + dot_bt(up_part_grad, wu_ref[...])
        part = jnp.sum(cot_act * activated.astype(F32), axis=-1, keepdims=True)
        part = jnp.broadcast_to(part, gate_grad.shape)

        @pl.when(step == 0)
        def _():
            row_sum[...] = row_part
            gate_grad[...] = part

        @pl.when(step > 0)
        def _():
            row_sum[...] += row_part
            gate_grad[...] += part

        @pl.when(step == steps - 1)
        def _():
            lane = lax.broadcasted_iota(jnp.int32, (piece, extra), 1)
            for j in range(senders):
                for i in range(blocks):
                    at = pl.ds((j * blocks + i) * piece, piece)
                    row_refs[i][j, :, :D] = row_sum[at, :].astype(BF16)
                    both = jnp.broadcast_to(gate_grad[at, :1], (piece, extra))
                    high = both.astype(BF16).astype(F32)
                    row_refs[i][j, :, D:] = jnp.where(
                        lane == expert_ref[0],
                        high,
                        jnp.where(lane == experts + expert_ref[0], both - high, 0.0),
                    ).astype(BF16)

    def whole(shape):
        return pl.BlockSpec(shape, lambda j, at: (0, 0))

    columns = pl.BlockSpec((count, tile), lambda j, at: (0, j))
    return pl.pallas_call(
        kernel,
        grid_spec=pltpu.PrefetchScalarGridSpec(
            num_scalar_prefetch=1,
            grid=(steps,),
            in_specs=[
                whole((count, D)),
                whole((count, D)),
                pl.BlockSpec((D, tile), lambda j, at: (0, j)),
                pl.BlockSpec((D, tile), lambda j, at: (0, steps + j)),
                pl.BlockSpec((tile, D), lambda j, at: (j, 0)),
                whole((D, experts)),
            ],
            out_specs=[pl.BlockSpec((senders, piece, D + extra), lambda j, at: (0, 0, 0))] * blocks
            + [columns, columns, columns, whole((count, 128))],
            scratch_shapes=[pltpu.VMEM((count, D), F32), pltpu.VMEM((count, 128), F32)],
        ),
        out_shape=[jax.ShapeDtypeStruct((senders, piece, D + extra), BF16)] * blocks
        + [
            jax.ShapeDtypeStruct((count, FF), BF16),
            jax.ShapeDtypeStruct((count, FF), BF16),
            jax.ShapeDtypeStruct((count, FF), BF16),
            jax.ShapeDtypeStruct((count, 128), F32),
        ],
        compiler_params=pltpu.CompilerParams(vmem_limit_bytes=56 << 20),
        cost_estimate=pl.CostEstimate(flops=0, bytes_accessed=0, transcendentals=0),
        name="expert",
    )(expert, rows, cot, w_gate_up, w_gate_up, w_down, w_router)


def expert_outs(acts, gates, cot, w_down):
    count = acts.shape[0]
    tile = count // 2

    def kernel(act_ref, gate_ref, cot_ref, wd_ref, mix_ref, route_ref):
        gate = gate_ref[:, :1]
        out = dot(act_ref[...], wd_ref[...]).astype(BF16)
        mix_ref[...] = (gate * out.astype(F32)).astype(BF16)
        route_ref[...] = (gate * cot_ref[...].astype(F32)).astype(BF16)

    def rows_of(columns):
        return pl.BlockSpec((tile, columns), lambda i: (i, 0))

    return pl.pallas_call(
        kernel,
        grid=(count // tile,),
        in_specs=[rows_of(FF), rows_of(128), rows_of(D), pl.BlockSpec((FF, D), lambda i: (0, 0))],
        out_specs=[rows_of(D), rows_of(D)],
        out_shape=[jax.ShapeDtypeStruct((count, D), BF16)] * 2,
        compiler_params=pltpu.CompilerParams(vmem_limit_bytes=56 << 20),
        cost_estimate=pl.CostEstimate(
            flops=2 * count * FF * D, bytes_accessed=6 * count * D + 2 * FF * D, transcendentals=0
        ),
        name="expert_outs",
    )(acts, gates, cot, w_down)


def weight_grad(lefts, rights, part, rows_out, arrived=()):
    blocks, parts = len(lefts), len(rights[0])
    depth = lefts[0].shape[0]
    tile = min(256, rows_out)
    tiles = rows_out // tile
    widths = [v.shape[1] for v in rights[0]]

    def kernel(part_ref, *refs):
        left, right, out = refs[:blocks], refs[blocks : blocks * (1 + parts)], refs[-1]
        at = 0
        for p in range(parts):
            total = dot_at(left[0][...], right[p][...])
            for b in range(1, blocks):
                total = total + dot_at(left[b][...], right[b * parts + p][...])
            for more in refs[blocks * (1 + parts) : -1]:
                total = total + more[:, at : at + widths[p]].astype(F32)
            out[:, at : at + widths[p]] = total.astype(out.dtype)
            at += widths[p]

    row_block = pl.BlockSpec((tile, sum(widths)), lambda i, at: (i, 0))
    return pl.pallas_call(
        kernel,
        grid_spec=pltpu.PrefetchScalarGridSpec(
            num_scalar_prefetch=1,
            grid=(tiles,),
            in_specs=[pl.BlockSpec((depth, tile), lambda i, at: (0, at[0] * tiles + i))] * blocks
            + [
                pl.BlockSpec((depth, w), lambda i, at: (0, 0))
                for _ in range(blocks)
                for w in widths
            ]
            + [row_block] * len(arrived),
            out_specs=row_block,
        ),
        out_shape=jax.ShapeDtypeStruct((rows_out, sum(widths)), F32 if arrived else BF16),
        compiler_params=pltpu.CompilerParams(vmem_limit_bytes=56 << 20),
        cost_estimate=pl.CostEstimate(
            flops=4 * blocks * depth * rows_out * sum(widths),
            bytes_accessed=2 * blocks * depth * (rows_out + sum(widths)) + 4 * rows_out * sum(widths),
            transcendentals=0,
        ),
        name="weight_grad",
    )(part.reshape(1).astype(jnp.int32), *lefts, *[v for r in rights for v in r], *arrived)


def body(
    prompt_x,
    cont_x,
    cont_ids,
    routes,
    qkv_weight,
    out_weight,
    router_weight,
    norm_gains,
    gate_up_weight,
    down_weight,
    prompt_cot,
    cont_cot,
):
    n_dp, n_ctx, n_exp = lax.axis_size("dp"), lax.axis_size("ctx"), lax.axis_size("exp")
    d, c, z = lax.axis_index("dp"), lax.axis_index("ctx"), lax.axis_index("exp")
    prompt_len = prompt_x.shape[1]
    cont_len = cont_x.shape[1]
    rows = prompt_len + cont_len
    prompt_total = prompt_len * n_ctx
    experts = router_weight.shape[1]
    capacity = rows * TOP * 17 // (16 * experts)
    score_scale = HEAD_DIM ** (-0.5)
    shard = qkv_weight.shape[0]
    heads_own = HEADS // n_ctx
    width = heads_own * HEAD_DIM
    head_groups = n_dp if (D // (n_dp * n_ctx)) % HEAD_DIM == 0 else 1
    head_run = D // (head_groups * n_ctx)
    own_expert = c * n_exp + z

    def ctx_swap(x, k):
        return lax.ppermute(x, "ctx", [(i, i ^ k) for i in range(n_ctx)])

    def ctx_trade(x):
        return lax.all_to_all(x, "ctx", 0, 0, tiled=True)

    def ctx_gather(x):
        return ctx_trade(jnp.broadcast_to(x[None], (n_ctx,) + x.shape))

    def exp_shift(x, s):
        return lax.ppermute(x, "exp", [(i, (i + s) % n_exp) for i in range(n_exp)])

    def dp_shift(x, m):
        return lax.ppermute(x, "dp", [(i, (i + m) % n_dp) for i in range(n_dp)])

    def part_of(x, axis, at):
        return lax.dynamic_index_in_dim(x, at, axis, keepdims=False)

    def place(buffer, x, *index):
        start, shape = [], []
        for at, size in zip(index, buffer.shape):
            start.append(0 if at is None else at)
            shape.append(size if at is None else 1)
        shape += buffer.shape[len(index) :]
        start += [0] * (buffer.ndim - len(index))
        return lax.dynamic_update_slice(buffer, x.reshape(shape), start)

    def gate(x, *others):
        out = lax.optimization_barrier((x,) + others)[0]
        return list(out) if isinstance(out, tuple) else out

    mark = jnp.full((8, 128), d, jnp.int32).astype(F32)

    def hand_on(in_ref, out_ref):
        out_ref[...] = in_ref[...]

    def fence(*values):
        nonlocal mark
        mark = pl.pallas_call(
            hand_on,
            out_shape=jax.ShapeDtypeStruct(mark.shape, mark.dtype),
            cost_estimate=pl.CostEstimate(
                flops=2 * 10**11, bytes_accessed=0, transcendentals=0
            ),
            name="fence",
        )(gate(mark, *values))

    def after(*values):
        out = lax.optimization_barrier(values + (mark,))
        return out[0] if len(values) == 1 else out[:-1]

    def by_owner(v):
        runs = v.shape[1] // (n_ctx * head_run)
        return jnp.stack(
            [
                jnp.concatenate(
                    [
                        v[:, (i * n_ctx + j) * head_run : (i * n_ctx + j + 1) * head_run]
                        for i in range(runs)
                    ],
                    axis=1,
                )
                for j in range(n_ctx)
            ]
        )

    def all_owners(v):
        runs = v.shape[2] // head_run
        return jnp.concatenate(
            [
                v[j][:, i * head_run : (i + 1) * head_run]
                for i in range(runs)
                for j in range(n_ctx)
            ],
            axis=1,
        )

    x_own = jnp.concatenate([prompt_x[0], cont_x[0]], axis=0)
    cot_own = jnp.concatenate([prompt_cot[0], cont_cot[0]], axis=0)

    small_width = experts + norm_gains.shape[1]
    route_width = -(-rows * TOP // shard)
    route_cols = routes[0, 0].T.astype(BF16).reshape(-1)
    route_cols = jnp.pad(route_cols, (0, route_width * shard - rows * TOP)).reshape(shard, -1)
    extra = jnp.concatenate(
        [
            router_weight,
            norm_gains,
            jnp.broadcast_to(cont_ids[0].astype(BF16), (shard, cont_len)),
            route_cols,
        ],
        axis=1,
    )
    extra_width = -(-extra.shape[1] // 128) * 128
    extra = jnp.pad(extra, ((0, 0), (0, extra_width - extra.shape[1])))
    all_width = 3 * width + extra_width
    runs = 3 * width // head_run


    def pack(w_ref, extra_ref, out_ref):
        for j in range(n_ctx):
            for i in range(runs):
                out_ref[j, :, i * head_run : (i + 1) * head_run] = w_ref[
                    :, (i * n_ctx + j) * head_run : (i * n_ctx + j + 1) * head_run
                ]
            out_ref[j, :, 3 * width :] = extra_ref[...]

    packed_w = pl.pallas_call(
        pack, out_shape=jax.ShapeDtypeStruct((n_ctx, shard, all_width), BF16), name="pack"
    )(qkv_weight, extra)
    slab = ctx_trade(packed_w)
    out_blocks = [out_weight] + [exp_shift(out_weight, s) for s in range(1, n_exp)]
    fence(packed_w)

    def by_exp(v):
        shaped = v.reshape(v.shape[:-1] + (n_dp, n_ctx, n_exp, shard))
        return jnp.swapaxes(shaped, -3, -2).reshape(v.shape)

    def from_exp(v):
        shaped = v.reshape(v.shape[:-1] + (n_dp, n_exp, n_ctx, shard))
        return jnp.swapaxes(shaped, -3, -2).reshape(v.shape)

    x_turned = by_exp(x_own)
    out_blocks = after(*out_blocks)
    out_exp = jnp.zeros((n_exp, shard, D), BF16)
    for j in range(n_exp):
        out_exp = place(out_exp, out_blocks[j], (z - j) % n_exp)

    slab = after(slab)
    ids_at = 3 * width + small_width
    ids = slab[:, 0, ids_at : ids_at + cont_len].astype(F32).astype(jnp.int32)
    w_blocks = [slab] + [exp_shift(slab, s) for s in range(1, n_exp)]
    w_sets = [[dp_shift(slab, m)] for m in range(1, n_dp)]
    out_ctx = ctx_gather(gate(out_exp, slab))
    fence(slab, out_exp)
    out_ctx = after(out_ctx)
    x_sent = gate(x_turned, out_ctx)
    x_all = ctx_gather(x_sent)
    fence(x_sent)

    x_all = after(x_all).reshape(n_ctx * rows, D).astype(F32)
    scale_in = row_scale(x_all)
    w_blocks = gate(tuple(w_blocks), scale_in)
    for m in range(1, n_dp):
        w_sets[m - 1] += [dp_shift(v, m) for v in w_blocks[1:]]
    cot_blocks = [cot_own]
    routes_at = ids_at + cont_len
    route_rows = [
        part_of(v[..., routes_at : routes_at + route_width], 0, c)
        .reshape(-1)[: rows * TOP]
        .reshape(TOP, rows)
        for v in w_blocks
    ]
    places = jnp.stack(
        [(d - m) % n_dp for m in range(n_dp)] + [(z - s) % n_exp for s in range(n_exp)]
    ).astype(jnp.int32)

    def assemble(at_ref, *refs):
        blocks, (w_ref, small_ref) = refs[: n_dp * n_exp], refs[n_dp * n_exp :]
        for m in range(n_dp):
            for s in range(n_exp):
                block = blocks[m * n_exp + s]
                w_ref[at_ref[m], at_ref[n_dp + s]] = block[:, :, : 3 * width]
                small_ref[at_ref[m], at_ref[n_dp + s]] = block[:, :, 3 * width :]

    in_vmem = pl.BlockSpec(memory_space=pltpu.VMEM)
    w_qkv, w_small = pl.pallas_call(
        assemble,
        in_specs=[pl.BlockSpec(memory_space=pltpu.SMEM)] + [in_vmem] * (n_dp * n_exp),
        out_specs=[in_vmem] * 2,
        out_shape=[
            jax.ShapeDtypeStruct((n_dp, n_exp, n_ctx, shard, 3 * width), BF16),
            jax.ShapeDtypeStruct((n_dp, n_exp, n_ctx, shard, extra_width), BF16),
        ],
        compiler_params=pltpu.CompilerParams(vmem_limit_bytes=56 << 20),
        cost_estimate=pl.CostEstimate(flops=0, bytes_accessed=0, transcendentals=0),
        name="assemble",
    )(places, *w_blocks, *[v for w_set in w_sets for v in w_set])
    w_qkv = w_qkv.reshape(D, 3 * width)
    w_small = jnp.swapaxes(w_small, 1, 2).reshape(D, extra_width)
    w_router = w_small[:, :experts]
    gains_t = w_small[:, experts:small_width].astype(F32).T
    gain_in, gain_ffn = gains_t[0], gains_t[3]

    def own_features(v):
        shaped = v.reshape(v.shape[:-1] + (head_groups, n_ctx, head_run))
        return part_of(shaped, v.ndim, c).reshape(v.shape[:-1] + (width,))

    gain_query, gain_key = own_features(gains_t[1]), own_features(gains_t[2])

    upper = (
        jnp.arange(rows, dtype=jnp.int32)[:, None] < jnp.arange(rows, dtype=jnp.int32)[None, :]
    ).astype(BF16)
    send_experts = (jnp.arange(n_ctx) * n_exp + z).astype(F32)

    def spread_of(route_cols):
        named = jnp.any(
            route_cols.astype(F32)[None] == send_experts[:, None, None], axis=1
        )
        rank = dot(named.astype(BF16), upper)
        slots = jnp.where(named, rank, -1.0)
        return (
            (slots[:, None, :] == jnp.arange(capacity, dtype=F32)[None, :, None])
            .astype(BF16)
            .reshape(n_ctx * capacity, rows)
        )

    spread = [spread_of(v) for v in route_rows]

    def spread_pair(blocks):
        n = len(blocks)
        parts = []
        for i, s in enumerate(blocks):
            part = spread[s].reshape(n_ctx, 1, capacity, rows)
            parts.append(jnp.pad(part, ((0, 0), (0, 0), (0, 0), (i * rows, (n - 1 - i) * rows))))
        return jnp.concatenate(parts, axis=1).reshape(n_ctx * n * capacity, n * rows)

    def pack_of(spread_rows, blocks):
        n = len(blocks)
        sent = dot(spread_rows, blocks[0] if n == 1 else jnp.concatenate(blocks, axis=0))
        return sent.astype(BF16).reshape(n_ctx, n, capacity, -1)

    def pack_cot(blocks):
        return pack_of(
            spread_pair(blocks) if len(blocks) > 1 else spread[blocks[0]],
            [cot_blocks[s] for s in blocks],
        )

    def trade_pieces(pieces):
        return [ctx_swap(pieces[k], k) if k else pieces[k] for k in range(n_ctx)]

    def in_order(pieces):
        whole = jnp.zeros((n_ctx,) + pieces[0].shape, pieces[0].dtype)
        for k in range(n_ctx):
            whole = place(whole, pieces[k], c ^ k)
        return whole

    w_gate_up = gate_up_weight[0]
    w_down = down_weight[0]
    pairs = [list(range(i, i + 2)) for i in range(0, n_exp, 2)]

    total_rows = rows * n_ctx
    index = jnp.arange(rows, dtype=jnp.int32)
    in_prompt = index < prompt_len
    position, seg_rows, order = [], [], []
    for j in range(n_ctx):
        seg = ids[j]
        starts = jnp.sum((seg[None, :] < seg[:, None]).astype(jnp.int32), axis=1)
        within = jnp.arange(cont_len, dtype=jnp.int32) - starts
        at = j * prompt_len
        position.append(jnp.concatenate([at + index[:prompt_len], prompt_total + within]))
        order.append(jnp.where(in_prompt, at + index, index))
        seg_rows.append(
            jnp.concatenate([jnp.full((prompt_len,), -1, jnp.int32), j * 64 + seg])
        )
    position = jnp.concatenate(position).astype(F32)
    order = jnp.concatenate(order)
    seg_of = jnp.concatenate(seg_rows)
    is_prompt = jnp.concatenate([in_prompt] * n_ctx)
    before = order[None, :] <= order[:, None]
    allowed = jnp.where(
        is_prompt[:, None],
        is_prompt[None, :] & before,
        is_prompt[None, :] | ((seg_of[None, :] == seg_of[:, None]) & before),
    )
    hidden_pairs = jnp.where(allowed, 0.0, -1.0)
    cosine, sine_rows = rope_tables(position, HEAD_DIM // 2)

    cot_sent = gate(pack_cot([0]), scale_in)
    cot_trade = ctx_trade(cot_sent)
    fence(cot_sent, w_qkv)
    hidden_in = (x_all * after(scale_in) * by_exp(gain_in)).astype(BF16)
    projected = dot(hidden_in, w_qkv)

    def ctx_sum(total):
        k = 1
        while k < n_ctx:
            total = total + ctx_swap(total, k)
            k *= 2
        return total

    raw_query, raw_key = projected[:, :width], projected[:, width : 2 * width]
    squares = jnp.stack([jnp.sum(raw_query * raw_query, axis=-1), jnp.sum(raw_key * raw_key, axis=-1)])
    cot_flight = [exp_shift(gate(cot_blocks[0], squares), s) for s in range(1, n_exp)]
    scales = lax.rsqrt(ctx_sum(squares) / D + NORM_EPS)
    out_ctx = gate(out_ctx, scales)
    out_halves = [out_ctx] + [dp_shift(out_ctx, m) for m in range(1, n_dp)]
    fence(scales, out_ctx)
    scales = after(scales)
    scales = scales.T
    head_gains = jnp.stack([gain_query, gain_key])
    mixed_heads, *kept = attend(projected, scales, head_gains, cosine, sine_rows, hidden_pairs)

    mixed_heads = gate(mixed_heads, cot_trade)
    mixed = ctx_trade(mixed_heads.reshape(n_ctx, rows, width))
    cot_own_rows = cot_trade
    spreads = [spread_pair(pair) for pair in pairs]
    fence(mixed_heads, *spreads)
    mixed = after(mixed)
    cot_blocks += gate(tuple(cot_flight), mixed)
    mixed = all_owners(mixed)
    cot_sent = gate(pack_cot(list(range(1, n_exp))), mixed)
    cot_trade = ctx_trade(cot_sent)
    fence(mixed, cot_sent)
    mixed = after(mixed)
    half = D // n_dp
    mixed_halves = jnp.stack([mixed[:, i * half : (i + 1) * half] for i in range(n_dp)])
    inputs = x_own.astype(F32)
    mid_rows = inputs
    for m in range(n_dp):
        mid_rows = mid_rows + dot(
            part_of(mixed_halves, 0, (d - m) % n_dp), out_halves[m].reshape(half, D)
        )
    scale_ffn = row_scale(mid_rows)
    normed_ffn = mid_rows * scale_ffn
    hidden_ffn = (normed_ffn * gain_ffn).astype(BF16)

    def softmax(logits):
        shifted = jnp.exp(logits - jnp.max(logits, axis=-1, keepdims=True))
        return shifted / jnp.sum(shifted, axis=-1, keepdims=True)

    cot_rows, made = [], []

    def towards(blocks, back, spread_rows):
        return dot_at(spread_rows, back.reshape(spread_rows.shape[0], -1))

    def home(s, summed):
        return exp_shift(summed, n_exp - s)

    near = exp_shift(hidden_ffn, 1)
    fence(hidden_ffn)

    near = after(near)
    far = [exp_shift(gate(hidden_ffn, near), s) for s in range(2, n_exp)]
    cot_trade = after(cot_trade)
    sent = gate(pack_of(spreads[0], [hidden_ffn, near]), cot_trade)
    plane = ctx_trade(sent)
    fence(near, sent)

    cot_back = [cot_own_rows[:, 0]] + [after(cot_trade)[:, s] for s in range(n_exp - 1)]
    for pair in pairs:
        cot_rows.append(jnp.stack([cot_back[s] for s in pair], axis=1).reshape(-1, D))
    plane = after(plane)
    far = gate(tuple(after(*far)), plane)
    sent = pack_of(spreads[1], far)
    plane_next = ctx_trade(sent)
    fence(sent, plane)

    expert_at = own_expert.reshape(1).astype(jnp.int32)

    def compute(i, in_rows):
        in_rows = in_rows.reshape(-1, D)
        out = expert_rows(
            in_rows, cot_rows[i], w_gate_up, w_down, w_router, expert_at, n_ctx, 2
        )
        made.append([in_rows] + list(out))

    compute(0, plane)
    sent = gate(made[0][2], plane_next)
    back = ctx_trade(sent)
    fence(sent)

    compute(1, after(plane_next))
    back = gate(after(back), made[1][1])
    leaving = towards([1], back, spread[1]).astype(BF16)
    homes = [home(1, leaving)]
    sent = gate(made[1][1], back)
    back = ctx_trade(sent)
    fence(sent, leaving)

    mix_sent, route_grads = [], []

    def weigh(i):
        acts, gates = after(made[i][3], made[i][6])
        mix, route = expert_outs(acts, gates, cot_rows[i], w_down)
        mix_sent.append(mix.reshape(n_ctx, 2, capacity, D))
        route_grads.append(route)

    def grads_sent(lefts, rights, rows_out):
        sent = [weight_grad(lefts, rights, half_rows[m], rows_out) for m in range(1, n_dp)]
        return sent, [dp_shift(v, m + 1) for m, v in enumerate(sent)]

    half_rows = [(d + m) % n_dp for m in range(n_dp)]
    weigh(0)
    back = gate(after(back), mix_sent[0])
    leaving = towards([2], back, spread[2]).astype(BF16)
    homes.append(home(2, leaving))
    sent = gate(made[1][2], back)
    back = ctx_trade(sent)
    fence(sent, leaving)

    weigh(1)
    back = gate(after(back), mix_sent[1])
    leaving = towards([3], back, spread[3]).astype(BF16)
    homes.append(home(3, leaving))
    sent = gate(made[0][1], back)
    back = ctx_trade(sent)
    fence(sent, leaving)

    back = after(back)
    returned = towards([0], back, spread[0])
    sent = gate(mix_sent[1], back)
    mix_trade = ctx_trade(sent)
    fence(sent)
    homes = after(*homes)
    for v in after(*homes):
        returned = returned + v.astype(F32)

    router = softmax(dot(hidden_ffn, w_router))
    prob_grad = returned[:, D : D + experts] + returned[:, D + experts : D + 2 * experts]
    logit_grad = router * (prob_grad - jnp.sum(router * prob_grad, axis=-1, keepdims=True))
    ffn_grad = returned[:, :D] + jnp.dot(logit_grad, w_router.astype(F32).T, precision=HIGHEST_PREC)
    router_grad_t = jnp.einsum(
        "re,rd->ed", logit_grad, hidden_ffn.astype(F32), precision=HIGHEST_PREC
    )
    mid_norm_grad, ffn_gain_grad = norm_back(ffn_grad, normed_ffn, scale_ffn, gain_ffn)
    mid_grad = cot_own.astype(F32) + mid_norm_grad

    attn_grad = mid_grad.astype(BF16)
    grad_halves = jnp.zeros((n_dp, rows, half), BF16)
    for m in range(n_dp):
        grad_halves = place(
            grad_halves,
            dot_bt(attn_grad, out_halves[m].reshape(half, D)).astype(BF16),
            (d - m) % n_dp,
        )
    pieces = by_owner(jnp.concatenate([grad_halves[i] for i in range(n_dp)], axis=1))
    mixed_grad = in_order(trade_pieces([part_of(pieces, 0, c ^ k) for k in range(n_ctx)]))
    back = gate(mix_trade, mixed_grad)
    leaving = towards(pairs[1], back, spreads[1]).astype(BF16)
    mix_homes = [home(2, leaving[:rows]), home(3, leaving[rows:])]
    fence(mixed_grad, leaving)
    mixed_grad = after(mixed_grad)
    query_turn, key_turn, value_grad, head_gain_grads, sums = attend_back(
        mixed_grad.reshape(total_rows, width),
        kept,
        projected,
        scales,
        head_gains,
        cosine,
        sine_rows,
        hidden_pairs,
    )
    sums = jnp.stack([sums[:, 0], sums[:, HEAD_DIM]])
    means = ctx_sum(sums) / D
    attn_sent = gate(attn_grad, means)
    attn_grad_all = ctx_gather(attn_sent)
    fence(means, attn_sent)
    means = after(means)
    proj_grad = norms_back(
        query_turn, key_turn, value_grad, projected, scales, means.T, head_gains
    )

    sent = [
        weight_grad([hidden_in], [[proj_grad]], half_rows[m], half) for m in range(1, n_dp)
    ]
    arrived = [dp_shift(v, m + 1) for m, v in enumerate(sent)]
    fence(*sent)
    hidden_part = dot_bt(gate(proj_grad, *sent), w_qkv).astype(BF16)
    arrived = gate(tuple([after(v) for v in arrived]), hidden_part)
    qkv_dp = weight_grad([hidden_in], [[proj_grad]], half_rows[0], half, arrived)
    qkv_dp = qkv_dp.reshape(n_exp, n_ctx * shard, 3 * width)
    mix_homes = after(*mix_homes)
    qkv_dp = gate(qkv_dp, *mix_homes)
    sent = [part_of(qkv_dp, 0, (z + s) % n_exp).astype(BF16) for s in range(1, n_exp)]
    qkv_arrived = [exp_shift(v, s + 1) for s, v in enumerate(sent)]
    attn_grad_all = gate(attn_grad_all, *sent)
    hidden_part = gate(hidden_part, attn_grad_all)
    hidden_trade = ctx_trade(hidden_part.reshape(n_ctx, rows, D))
    attn_grad_all = attn_grad_all.reshape(total_rows, D)
    fence(hidden_part, *sent)

    in_rows, acts, gate_grads, up_grads = [after(*[v[i] for v in made]) for i in (0, 3, 4, 5)]
    gate_up_grads = [[gate_grads[i], up_grads[i]] for i in range(len(pairs))]
    out_rows = width // n_dp
    if head_groups == n_dp:
        out_left = [after(mixed_heads)]
        out_sent, out_arrived = grads_sent(out_left, [[attn_grad_all]], out_rows)
        acts = gate(tuple(acts), *out_sent)
    down_sent, down_arrived = grads_sent(acts, [[v] for v in route_grads], FF // n_dp)
    in_rows = gate(tuple(in_rows), *down_sent)
    if head_groups == n_dp:
        out_left = gate(tuple(out_left), *down_sent)
        out_dp = weight_grad(out_left, [[attn_grad_all]], half_rows[0], out_rows, out_arrived)
        out_dp = out_dp.reshape(n_exp, shard, D)
        in_rows = gate(tuple(in_rows), out_dp)
    gate_up_sent, gate_up_arrived = grads_sent(in_rows, gate_up_grads, D // n_dp)
    hidden_trade = gate(hidden_trade, *gate_up_sent)
    mix_back = ctx_trade(gate(mix_sent[0], hidden_trade))
    acts = gate(tuple(acts), *gate_up_sent)
    grad_down = weight_grad(acts, [[v] for v in route_grads], d, FF // n_dp, down_arrived)
    mix_back = gate(mix_back, grad_down)
    leaving = towards(pairs[0], mix_back, spreads[0])
    mix_homes = list(mix_homes) + [leaving[:rows], home(1, leaving[rows:].astype(BF16))]
    in_rows = gate(tuple(in_rows), leaving)
    grad_gate_up = weight_grad(in_rows, gate_up_grads, d, D // n_dp, gate_up_arrived)

    hidden_grad = from_exp(jnp.sum(hidden_trade.astype(F32), axis=0))
    scale_own = lax.dynamic_slice_in_dim(scale_in, c * rows, rows, axis=0)
    in_norm_grad, in_gain_grad = norm_back(hidden_grad, inputs * scale_own, scale_own, gain_in)
    input_grad = mid_grad + in_norm_grad

    def spread_features(v):
        shaped = jnp.zeros((head_groups, n_ctx, head_run), F32)
        return place(shaped, v.reshape(head_groups, 1, head_run), None, c).reshape(1, D)

    small_grad = jnp.concatenate(
        [
            router_grad_t,
            in_gain_grad[None],
            spread_features(head_gain_grads[0]),
            spread_features(head_gain_grads[1]),
            ffn_gain_grad[None],
        ],
        axis=0,
    )
    count = small_grad.shape[0]
    part = small_grad.reshape(count, n_dp, n_ctx, n_exp, shard).transpose(1, 2, 3, 0, 4)
    late_d = mark[0, 0].astype(jnp.int32)
    total = lax.dynamic_index_in_dim(part, late_d, 0, keepdims=False)
    for m in range(1, n_dp):
        total = total + dp_shift(
            lax.dynamic_index_in_dim(part, (late_d + m) % n_dp, 0, keepdims=False), m
        )
    part = total
    part = jnp.sum(ctx_trade(gate(part, mix_back)), axis=0)
    if head_groups == n_dp:
        flat = part.reshape(n_exp, count * shard)
        high = flat.astype(BF16)
        flat = jnp.concatenate([high, (flat - high.astype(F32)).astype(BF16)], axis=1)
        lines = -(-2 * count * shard // (8 * D)) * 8
        flat = jnp.pad(flat, ((0, 0), (0, lines * D - 2 * count * shard)))
        out_sent = jnp.concatenate([out_dp.astype(BF16), flat.reshape(n_exp, lines, D)], axis=1)
        out_trade = lax.all_to_all(out_sent, "exp", 0, 0, tiled=True)
        out_trade = gate(out_trade, grad_gate_up)
        grad_out = jnp.sum(out_trade[:, :shard].astype(F32), axis=0)
        flat = jnp.sum(out_trade[:, shard:].astype(F32), axis=0).reshape(-1)
        total = (flat[: count * shard] + flat[count * shard : 2 * count * shard]).reshape(
            count, shard
        )
    else:
        grad_out = lax.psum_scatter(
            dot_at(mixed, attn_grad), ("dp", "ctx", "exp"), scatter_dimension=0, tiled=True
        )
        total = jnp.sum(lax.all_to_all(part, "exp", 0, 0, tiled=True), axis=0)
    small_sum = total.T
    mix_homes = gate(tuple(mix_homes), grad_out)
    mixture = mix_homes[2] + sum(v.astype(F32) for v in mix_homes[:2] + mix_homes[3:])
    final_rows = (mid_rows + mixture).astype(BF16)

    qkv_arrived = gate(tuple(qkv_arrived), final_rows, small_sum)
    qkv_exp = part_of(qkv_dp, 0, z)
    for v in qkv_arrived:
        qkv_exp = qkv_exp + v.astype(F32)
    qkv_exp = qkv_exp.reshape(n_ctx, shard, 3 * width)
    grad_qkv = all_owners(ctx_trade(qkv_exp.astype(BF16)).astype(F32))

    return (
        final_rows[:prompt_len][None],
        final_rows[prompt_len:][None],
        input_grad[:prompt_len][None],
        input_grad[prompt_len:][None],
        grad_qkv,
        grad_out,
        small_sum[:, :experts],
        small_sum[:, experts:],
        grad_gate_up[None],
        grad_down[None],
    )


def solution(mesh):
    return jax.shard_map(
        body,
        mesh=mesh,
        in_specs=(
            P(("dp", "exp"), "ctx", None),
            P(("dp", "exp"), "ctx", None),
            P(("dp", "exp"), "ctx", None),
            P(("dp", "exp"), "ctx", None, None),
            P(("dp", "ctx", "exp"), None),
            P(("dp", "ctx", "exp"), None),
            P(("dp", "ctx", "exp"), None),
            P(("dp", "ctx", "exp"), None),
            P(("ctx", "exp"), None, None),
            P(("ctx", "exp"), None, None),
            P(("dp", "exp"), "ctx", None),
            P(("dp", "exp"), "ctx", None),
        ),
        out_specs=(
            P(("dp", "exp"), "ctx", None),
            P(("dp", "exp"), "ctx", None),
            P(("dp", "exp"), "ctx", None),
            P(("dp", "exp"), "ctx", None),
            P(("dp", "ctx", "exp"), None),
            P(("dp", "ctx", "exp"), None),
            P(("dp", "ctx", "exp"), None),
            P(("dp", "ctx", "exp"), None),
            P(("ctx", "exp"), "dp", None),
            P(("ctx", "exp"), "dp", None),
        ),
        check_vma=False,
    )
```

time: 827 us -> 733 us (0.89)
  Pallas kernels: 0 us -> 177 us
  waiting for transfers between devices: 377 us -> 228 us
  matrix products: 139 us -> 64.4 us
  starting transfers between devices: 162 us -> 124 us
  local copies, waits for them, and re-layouts: 88.5 us -> 77.5 us
    ppermute x87 -> x7, waiting for transfers between devices: 239 us -> 28.2 us  [ctx_swap(): return lax.ppermute(x, 'ctx', [(i, i ^ k) for i in range(n_ctx)])]
    pallas_call x0 -> x36, Pallas kernels: none -> 177 us  [the longest x8 59.8 us: weight_grad(): pl.pallas_call(kernel, grid_spec=pltpu.PrefetchScalarGridSpec(num_scalar_...]
    all_to_all x0 -> x19, waiting for transfers between devices: none -> 168 us  [the longest x18 153 us: ctx_trade(): return lax.all_to_all(x, 'ctx', 0, 0, tiled=True)]
    ppermute x33 -> x21, waiting for transfers between devices: 132 us -> 32.2 us  [exp_shift(): return lax.ppermute(x, 'exp', [(i, (i + s) % n_exp) for i in range(n_exp)])]
    all_to_all x0 -> x19, starting transfers between devices: none -> 85.2 us  [the longest x18 78.5 us: ctx_trade(): return lax.all_to_all(x, 'ctx', 0, 0, tiled=True)]
    ppermute x87 -> x7, starting transfers between devices: 89.4 us -> 9.52 us  [ctx_swap(): return lax.ppermute(x, 'ctx', [(i, i ^ k) for i in range(n_ctx)])]
    ppermute x33 -> x21, starting transfers between devices: 71 us -> 27.3 us  [exp_shift(): return lax.ppermute(x, 'exp', [(i, (i + s) % n_exp) for i in range(n_exp)])]
    dot_general x12 -> x6, matrix products: 41.5 us -> 17.4 us  [dot_at(): lax.dot_general(a, b, (((0,), (0,)), ((), ())), preferred_element_type=F32)]
  transfers between devices with their start and end apart: 134 -> 57, of which waited for: 67 -> 23; matrix products, arithmetic and copies ran while one was open for 18% -> 21% of each run, Pallas kernels for 0% -> 22%
where the time goes in v2:
time: 733 us; the launch traced here: 720 us
  waiting for transfers between devices  228 us (31%)
  Pallas kernels  177 us (24%)
  starting transfers between devices  124 us (17%)
  local copies, waits for them, and re-layouts  77.5 us (11%)
  matrix products  64.4 us (9%)
  other arithmetic  45.5 us (6%)
    all_to_all x18, waiting for transfers between devices, ctx_trade(): return lax.all_to_all(x, 'ctx', 0, 0, tiled=True)  153 us
    all_to_all x18, starting transfers between devices, ctx_trade(): return lax.all_to_all(x, 'ctx', 0, 0, tiled=True)  78.5 us
    pallas_call x8, Pallas kernels, weight_grad(): pl.pallas_call(kernel, grid_spec=pltpu.PrefetchScalarGridSpec(num_scalar_...  59.8 us
    pallas_call x2, Pallas kernels, expert_rows(): pl.pallas_call(kernel, grid_spec=pltpu.PrefetchScalarGridSpec(num_scalar_...  46.5 us
    ppermute x21, waiting for transfers between devices, exp_shift(): return lax.ppermute(x, 'exp', [(i, (i + s) % n_exp) for i in range(n_exp)])  32.2 us
    dot_general x12, matrix products, dot(): return jnp.dot(a, b, preferred_element_type=F32)  28.6 us
    ppermute x7, waiting for transfers between devices, ctx_swap(): return lax.ppermute(x, 'ctx', [(i, i ^ k) for i in range(n_ctx)])  28.2 us
    ppermute x21, starting transfers between devices, exp_shift(): return lax.ppermute(x, 'exp', [(i, (i + s) % n_exp) for i in range(n_exp)])  27.3 us
  transfers between devices with their start and end apart: 57, of which 23 were waited for; matrix products, arithmetic and copies ran while one was open for 21% of the time, Pallas kernels for 22%

profile of v2, /device:TPU:16, one launch (start us, length us, event | category | flops | bytes accessed | tf_op | source)
XLA Modules:
  0.0 720.4 jit_solution(7182817923321295511)
XLA Ops:
  9.7 4.2 all-to-all-start
  37.8 4.9 all-to-all-start.1
  47.4 43.8 %all-to-all-done.1 = bf16[4,4,64,2048]{3,2,1,0:T(8,128)(2,1)} async-done(((bf16[4,4,64,2048]{3,2,1,0:T(8,128)(2,1)}), bf16[4,4,64,2048]{3,2,1,0:T(8,128)(2,1)}, u32[]{:S(2)}, u32[]{:S(2)}) %all-to-all-start.1) | async-done | bytes 4194336 | tf_op jit(solution)/shard_map/all_to_all | solution.py:417
  92.9 4.5 all-to-all-start.2
  98.7 25.4 %all-to-all-done.2 = bf16[4,136,2048]{2,1,0:T(8,128)(2,1)} async-done(((bf16[4,136,2048]{2,1,0:T(8,128)(2,1)}), bf16[4,136,2048]{2,1,0:T(8,128)(2,1)}, u32[]{:S(2)}, u32[]{:S(2)}) %all-to-all-start.2) | async-done | bytes 2228256 | tf_op jit(solution)/shard_map/all_to_all | solution.py:417
  134.6 4.5 all-to-all-start.3
  143.6 6.3 assemble.1
  158.9 5.7 fusion.95.pq.pk.pv.projected_ref
  172.7 6.2 collective-permute-done.10
  180.7 5.7 collective-permute-done.11
  187.8 8.4 %attend.1 = (bf16[544,512]{1,0:T(8,128)(2,1)}, bf16[544,512]{1,0:T(8,128)(2,1)S(1)}, bf16[544,512]{1,0:T(8,128)(2,1)S(1)}, bf16[544,512]{1,0:T(8,128)(2,1)S(1)}, f32[544,512]{1,0:T(8,128)S(1)}) custom-call(f32[544,1536]{1,0:T(8,128)} %copy-done.16, f32[544,1536]{1,0:T(8,128)} %copy-done.16, f32[544,1536]{1,0:T(8,128)} %copy-done.16, f32[544,2]{1,0:T(8,128)S(1)} %bitcast.263, ...), custom_call_target="tpu_custom_call" | custom-call | tf_op jit(solution)/shard_map/attend/pallas_call | solution.py:84
  199.7 4.2 all-to-all-start.4
  205.2 8.1 %all-to-all-done.4 = bf16[4,136,512]{2,1,0:T(8,128)(2,1)} async-done(((bf16[4,136,512]{2,1,0:T(8,128)(2,1)}), bf16[4,136,512]{2,1,0:T(8,128)(2,1)}, u32[]{:S(2)}, u32[]{:S(2)}) %all-to-all-start.4) | async-done | bytes 557088 | tf_op jit(solution)/shard_map/all_to_all | solution.py:417
  219.6 5.2 convolution_convert_fusion
  224.7 4.7 all-to-all-start.5
  243.5 26.5 %all-to-all-done.5 = bf16[4,3,72,2048]{3,2,1,0:T(8,128)(2,1)} async-done(((bf16[4,3,72,2048]{3,2,1,0:T(8,128)(2,1)}), bf16[4,3,72,2048]{3,2,1,0:T(8,128)(2,1)}, u32[]{:S(2)}, u32[]{:S(2)}) %all-to-all-start.5) | async-done | bytes 3538976 | tf_op jit(solution)/shard_map/all_to_all | solution.py:417
  270.8 4.0 convolution_convert_fusion.2
  274.8 4.5 all-to-all-start.6
  284.1 3.4 stack.81
  290.4 14.0 %collective-permute-done.17 = bf16[136,2048]{1,0:T(8,128)(2,1)} collective-permute-done((bf16[136,2048]{1,0:T(8,128)(2,1)}, bf16[136,2048]{1,0:T(8,128)(2,1)}, u32[]{:S(2)}, u32[]{:S(2)}) %collective-permute-start.17) | collective-permute-done | bytes 557088 | tf_op jit(solution)/shard_map/ppermute | solution.py:423
  304.4 11.8 %collective-permute-done.18 = bf16[136,2048]{1,0:T(8,128)(2,1)} collective-permute-done((bf16[136,2048]{1,0:T(8,128)(2,1)}, bf16[136,2048]{1,0:T(8,128)(2,1)}, u32[]{:S(2)}, u32[]{:S(2)}) %collective-permute-start.18) | collective-permute-done | bytes 557088 | tf_op jit(solution)/shard_map/ppermute | solution.py:423
  316.3 4.0 convolution_convert_fusion.1
  320.3 4.5 all-to-all-start.7
  326.1 23.2 %expert.2 = (bf16[4,72,2176]{2,1,0:T(8,128)(2,1)}, bf16[4,72,2176]{2,1,0:T(8,128)(2,1)}, bf16[576,1024]{1,0:T(8,128)(2,1)}, bf16[576,1024]{1,0:T(8,128)(2,1)}, b...) custom-call(s32[1]{0:T(128)} %bitcast.50.expert_ref, bf16[576,2048]{1,0:T(8,128)(2,1)} %bitcast.53.rows_ref.refs_0_, ...), custom_call_target="tpu_custom_call" | custom-call | tf_op jit(solution)/shard_map/expert/pallas_call | solution.py:281
  349.3 3.7 all-to-all-done.7
  353.0 4.7 all-to-all-start.8
  359.0 23.2 %expert.3 = (bf16[4,72,2176]{2,1,0:T(8,128)(2,1)}, bf16[4,72,2176]{2,1,0:T(8,128)(2,1)}, bf16[576,1024]{1,0:T(8,128)(2,1)}, bf16[576,1024]{1,0:T(8,128)(2,1)}, b...) custom-call(s32[1]{0:T(128)} %bitcast.50.expert_ref, bf16[576,2048]{1,0:T(8,128)(2,1)} %bitcast.57.rows_ref.refs_1_, ...), custom_call_target="tpu_custom_call" | custom-call | tf_op jit(solution)/shard_map/expert/pallas_call | solution.py:281
  385.0 4.3 all-to-all-start.9
  393.2 7.0 expert_outs.2
  400.2 4.7 all-to-all-done.9
  407.6 4.3 all-to-all-start.10
  413.3 7.0 expert_outs.3
  420.3 7.0 all-to-all-done.10
  430.0 4.3 all-to-all-start.11
  436.3 13.3 %all-to-all-done.11 = bf16[4,72,2176]{2,1,0:T(8,128)(2,1)} async-done(((bf16[4,72,2176]{2,1,0:T(8,128)(2,1)}), bf16[4,72,2176]{2,1,0:T(8,128)(2,1)}, u32[]{:S(2)}, u32[]{:S(2)}) %all-to-all-start.11) | async-done | bytes 1253408 | tf_op jit(solution)/shard_map/all_to_all | solution.py:417
  449.6 4.7 all-to-all-start.12
  461.6 3.9 fusion.28
  465.5 3.7 fusion.30
  474.5 11.3 %collective-permute-done.22 = bf16[136,512]{1,0:T(8,128)(2,1)S(1)} collective-permute-done((bf16[136,512]{1,0:T(8,128)(2,1)S(1)}, bf16[136,512]{1,0:T(8,128)(2,1)S(1)}, u32[]{:S(2)}, u32[]{:S(2)}) %collective-permute-start.22) | collective-permute-done | bytes 139296 | tf_op jit(solution)/shard_map/ppermute | solution.py:414
  488.3 3.8 fusion.8
  495.5 12.6 %attend_back.1 = (f32[544,512]{1,0:T(8,128)S(1)}, f32[544,512]{1,0:T(8,128)}, bf16[544,512]{1,0:T(8,128)(2,1)S(1)}, f32[2,512]{1,0:T(2,128)S(1)}, f32[544,256]{1,0:T(8,128)S(1)}) custom-call(bf16[544,512]{1,0:T(8,128)(2,1)S(1)} %bitcast.266, bf16[544,512]{1,0:T(8,128)(2,1)S(1)} %copy-done.6, bf16[544,512]{1,0:T(8,128)(2,1)S(1)} %copy-done.8, ...), custom_call_target="tpu_custom_call" | custom-call | tf_op jit(solution)/shard_map/attend_back/pallas_call | solution.py:159
  509.8 3.6 fusion.1.refs_0_
  518.4 3.9 collective-permute-start.26
  527.7 6.1 weight_grad.8
  535.5 5.1 all-to-all-start.13
  542.1 7.7 %convolution_convert_fusion.3 = bf16[544,2048]{1,0:T(8,128)(2,1)} fusion(bf16[544,1536]{1,0:T(8,128)(2,1)S(1)} %copy-done.2, bf16[2048,1536]{1,0:T(8,128)(2,1)} %bitcast.325), kind=kOutput, calls=%fused_computation.19 | convolution fusion | flops 3423666176 | bytes 10190848 | tf_op jit(solution)/shard_map/dot_general | solution.py:49
  556.0 7.3 %weight_grad.9 = f32[1024,1536]{1,0:T(8,128)} custom-call(s32[1]{0:T(128)} %bitcast.15.part_ref, bf16[544,2048]{1,0:T(8,128)(2,1)} %fusion.1.refs_0_, bf16[544,1536]{1,0:T(8,128)(2,1)} %copy-done.1, bf16[1024,1536]{1,0:T(8,128)(2,1)} %collective-permute-done.29.refs_2_), custom_call_target="tpu_custom_call" | custom-call | flops 3422552064 | bytes 9076736 | tf_op jit(solution)/shard_map/weight_grad/pallas_call | solution.py:358
  563.3 3.8 fusion.50
  569.5 3.7 weight_grad.10
  576.0 3.6 all-to-all-start.14
  579.9 7.2 %weight_grad.11 = bf16[512,2048]{1,0:T(8,128)(2,1)} custom-call(s32[1]{0:T(128)} %bitcast.82.part_ref, bf16[576,1024]{1,0:T(8,128)(2,1)} %get-tuple-element.293.act_ref.refs_0_, bf16[576,1024]{1,0:T(8,128)(2,1)} %get-tuple-element.294.act_ref.refs_1_, bf16[576,2048]{1,0:T(8,128)(2,1)} %get-tuple-element.276.refs_2_, bf16[576,2048]{1,0:T(8,128)(2,1)} %get-tuple-element.277.refs_3_), custom_call_target="tpu_custom_call" | custom-call | flops 4831838208 | bytes 10092544 | tf_op jit(solution)/shard_map/weight_grad/pallas_call | solution.py:358
  594.5 4.3 weight_grad.12
  601.5 10.9 %weight_grad.13 = bf16[1024,2048]{1,0:T(8,128)(2,1)} custom-call(s32[1]{0:T(128)} %bitcast.82.part_ref, bf16[576,2048]{1,0:T(8,128)(2,1)} %bitcast.53.rows_ref.refs_0_, bf16[576,2048]{1,0:T(8,128)(2,1)} %bitcast.57.rows_ref.refs_1_, bf16[576,1024]{1,0:T(8,128)(2,1)} %get-tuple-element.285.refs_2_, bf16[576,1024]{1,0:T(8,128)(2,1)} %get-tuple-element.288.refs_3_, ...), custom_call_target="tpu_custom_call" | custom-call | flops 9663676416 | bytes 15466496 | tf_op jit(solution)/shard_map/weight_grad/pallas_call | solution.py:358
  612.3 4.8 all-to-all-start.15
  620.4 3.3 copy.109
  627.0 8.1 %weight_grad.14 = f32[512,2048]{1,0:T(8,128)} custom-call(s32[1]{0:T(128)} %bitcast.92.part_ref, bf16[576,1024]{1,0:T(8,128)(2,1)} %get-tuple-element.293.act_ref.refs_0_, bf16[576,1024]{1,0:T(8,128)(2,1)} %get-tuple-element.294.act_ref.refs_1_, bf16[576,2048]{1,0:T(8,128)(2,1)} %get-tuple-element.276.refs_2_, bf16[576,2048]{1,0:T(8,128)(2,1)} %get-tuple-element.277.refs_3_, ...), custom_call_target="tpu_custom_call" | custom-call | flops 4831838208 | bytes 10092544 | tf_op jit(solution)/shard_map/weight_grad/pallas_call | solution.py:358
  635.1 9.9 %all-to-all-done.15 = bf16[4,2,72,2048]{3,2,1,0:T(8,128)(2,1)} async-done(((bf16[4,2,72,2048]{3,2,1,0:T(8,128)(2,1)}), bf16[4,2,72,2048]{3,2,1,0:T(8,128)(2,1)}, u32[]{:S(2)}, u32[]{:S(2)}) %all-to-all-start.15) | async-done | bytes 2359328 | tf_op jit(solution)/shard_map/all_to_all | solution.py:417
  645.8 3.3 all-to-all-start.16
  656.8 6.7 all-to-all-start.17
  670.1 12.1 %weight_grad.15 = f32[1024,2048]{1,0:T(8,128)} custom-call(s32[1]{0:T(128)} %bitcast.92.part_ref, bf16[576,2048]{1,0:T(8,128)(2,1)} %bitcast.53.rows_ref.refs_0_, bf16[576,2048]{1,0:T(8,128)(2,1)} %bitcast.57.rows_ref.refs_1_, bf16[576,1024]{1,0:T(8,128)(2,1)} %get-tuple-element.285.refs_2_, bf16[576,1024]{1,0:T(8,128)(2,1)} %get-tuple-element.288.refs_3_, ...), custom_call_target="tpu_custom_call" | custom-call | flops 9663676416 | bytes 15466496 | tf_op jit(solution)/shard_map/weight_grad/pallas_call | solution.py:358
  682.2 14.7 %all-to-all-done.17 = bf16[4,72,2048]{2,1,0:T(8,128)(2,1)} async-done(((bf16[4,72,2048]{2,1,0:T(8,128)(2,1)}), bf16[4,72,2048]{2,1,0:T(8,128)(2,1)}, u32[]{:S(2)}, u32[]{:S(2)}) %all-to-all-start.17) | async-done | bytes 1179680 | tf_op jit(solution)/shard_map/all_to_all | solution.py:946
  701.9 3.4 fusion.23
  705.3 3.5 all-to-all-start.18
  711.5 6.7 all-to-all-done.18
  (549 shorter events, 211.5 us)
Async XLA Ops:
  0.6 25.8 %collective-permute-start = (bf16[64,2048]{1,0:T(8,128)(2,1)}, bf16[64,2048]{1,0:T(8,128)(2,1)}, u32[]{:S(2)}, u32[]{:S(2)}) collective-permute-start(bf16[64,2048]{1,0:T(8,128)(2,1)} %param.17), channel_id=1, source_target_pairs={{0,1},{1,2},{2,3},{3,0},{4,5},{5,6},{6,7},{7,4},{8,9},{9,10},{10,1... | collective-permute-start | bytes 786440 | tf_op jit(solution)/shard_map/ppermute | solution.py:423
  2.3 24.2 %collective-permute-start.1 = (bf16[64,2048]{1,0:T(8,128)(2,1)}, bf16[64,2048]{1,0:T(8,128)(2,1)}, u32[]{:S(2)}, u32[]{:S(2)}) collective-permute-start(bf16[64,2048]{1,0:T(8,128)(2,1)} %param.17), channel_id=1, source_target_pairs={{0,2},{1,3},{2,0},{3,1},{4,6},{5,7},{6,4},{7,5},{8,10},{9,11},{10,... | collective-permute-start | bytes 786440 | tf_op jit(solution)/shard_map/ppermute | solution.py:423
  2.6 23.8 %collective-permute-start.2 = (bf16[64,2048]{1,0:T(8,128)(2,1)}, bf16[64,2048]{1,0:T(8,128)(2,1)}, u32[]{:S(2)}, u32[]{:S(2)}) collective-permute-start(bf16[64,2048]{1,0:T(8,128)(2,1)} %param.17), channel_id=1, source_target_pairs={{0,3},{1,0},{2,1},{3,2},{4,7},{5,4},{6,5},{7,6},{8,11},{9,8},{10,9... | collective-permute-start | bytes 786440 | tf_op jit(solution)/shard_map/ppermute | solution.py:423
  9.7 19.8 %all-to-all-start = ((bf16[4,64,1664]{2,1,0:T(8,128)(2,1)}), bf16[4,64,1664]{2,1,0:T(8,128)(2,1)}, u32[]{:S(2)}, u32[]{:S(2)}) async-start(bf16[4,64,1664]{2,1,0:T(8,128)(2,1)} %pack.1), calls=%async_computation | async-start | bytes 1703936 | tf_op jit(solution)/shard_map/all_to_all | solution.py:417
  29.5 97.4 %collective-permute-start.3 = (bf16[4,64,1664]{2,1,0:T(8,128)(2,1)}, bf16[4,64,1664]{2,1,0:T(8,128)(2,1)}, u32[]{:S(2)}, u32[]{:S(2)}) collective-permute-start(bf16[4,64,1664]{2,1,0:T(8,128)(2,1)} %all-to-all-done.refs_0_), channel_id=1, source_target_pairs={{0,1},{1,2},{2,3},{3,0},{4,5},{5,6},{6,7},{7,4},{8,9},{9,10},{10,1... | collective-permute-start | bytes 2555912 | tf_op jit(solution)/shard_map/ppermute | solution.py:423
  30.5 96.4 %collective-permute-start.4 = (bf16[4,64,1664]{2,1,0:T(8,128)(2,1)}, bf16[4,64,1664]{2,1,0:T(8,128)(2,1)}, u32[]{:S(2)}, u32[]{:S(2)}) collective-permute-start(bf16[4,64,1664]{2,1,0:T(8,128)(2,1)} %all-to-all-done.refs_0_), channel_id=1, source_target_pairs={{0,2},{1,3},{2,0},{3,1},{4,6},{5,7},{6,4},{7,5},{8,10},{9,11},{10,... | collective-permute-start | bytes 2555912 | tf_op jit(solution)/shard_map/ppermute | solution.py:423
  33.0 93.9 %collective-permute-start.5 = (bf16[4,64,1664]{2,1,0:T(8,128)(2,1)}, bf16[4,64,1664]{2,1,0:T(8,128)(2,1)}, u32[]{:S(2)}, u32[]{:S(2)}) collective-permute-start(bf16[4,64,1664]{2,1,0:T(8,128)(2,1)} %all-to-all-done.refs_0_), channel_id=1, source_target_pairs={{0,3},{1,0},{2,1},{3,2},{4,7},{5,4},{6,5},{7,6},{8,11},{9,8},{10,9... | collective-permute-start | bytes 2555912 | tf_op jit(solution)/shard_map/ppermute | solution.py:423
  35.2 108.3 %collective-permute-start.6 = (bf16[4,64,1664]{2,1,0:T(8,128)(2,1)}, bf16[4,64,1664]{2,1,0:T(8,128)(2,1)}, u32[]{:S(2)}, u32[]{:S(2)}) collective-permute-start(bf16[4,64,1664]{2,1,0:T(8,128)(2,1)} %all-to-all-done.refs_0_), channel_id=1, source_target_pairs={{0,16},{16,0},{1,17},{17,1},{2,18},{18,2},{3,19},{19,3},{4,20},{20... | collective-permute-start | bytes 2555912 | tf_op jit(solution)/shard_map/ppermute | solution.py:426
  37.8 53.4 %all-to-all-start.1 = ((bf16[4,4,64,2048]{3,2,1,0:T(8,128)(2,1)}), bf16[4,4,64,2048]{3,2,1,0:T(8,128)(2,1)}, u32[]{:S(2)}, u32[]{:S(2)}) async-start(bf16[4,4,64,2048]{3,2,1,0:T(8,128)(2,1)} %broadcast_in_dim.54), calls=%async_computation.1 | async-start | bytes 8388608 | tf_op jit(solution)/shard_map/all_to_all | solution.py:417
  46.6 44.6 %copy-start.45 = (bf16[136,2048]{1,0:T(8,128)(2,1)S(1)}, bf16[136,2048]{1,0:T(8,128)(2,1)}, u32[]{:S(2)}) copy-start(bf16[136,2048]{1,0:T(8,128)(2,1)} %reshape.455) | copy-start | bytes 1671172
  47.4 140.4 %copy-start = (f32[544,544]{1,0:T(8,128)}, f32[544,544]{1,0:T(8,128)S(1)}, u32[]{:S(2)}) copy-start(f32[544,544]{1,0:T(8,128)S(1)} %fusion.25.pair_ref) | copy-start | bytes 3551236
  92.9 31.2 %all-to-all-start.2 = ((bf16[4,136,2048]{2,1,0:T(8,128)(2,1)}), bf16[4,136,2048]{2,1,0:T(8,128)(2,1)}, u32[]{:S(2)}, u32[]{:S(2)}) async-start(bf16[4,136,2048]{2,1,0:T(8,128)(2,1)} %broadcast_in_dim.55), calls=%async_computation.2 | async-start | bytes 4456448 | tf_op jit(solution)/shard_map/all_to_all | solution.py:417
  98.7 33.0 %copy-start.106 = (f32[4]{0:T(128)S(1)}, f32[4]{0:T(128)}, u32[]{:S(2)}) copy-start(f32[4]{0:T(128)} %add_convert_fusion.1) | copy-start | bytes 52
  127.8 15.7 %collective-permute-start.7 = (bf16[4,64,1664]{2,1,0:T(8,128)(2,1)}, bf16[4,64,1664]{2,1,0:T(8,128)(2,1)}, u32[]{:S(2)}, u32[]{:S(2)}) collective-permute-start(bf16[4,64,1664]{2,1,0:T(8,128)(2,1)} %collective-permute-done.3.refs_1_), channel_id=1, source_target_pairs={{0,16},{16,0},{1,17},{17,1},{2,18},{18,2},{3,19},{19,3},{4,20},{20... | collective-permute-start | bytes 2555912 | tf_op jit(solution)/shard_map/ppermute | solution.py:426
  128.9 14.7 %collective-permute-start.8 = (bf16[4,64,1664]{2,1,0:T(8,128)(2,1)}, bf16[4,64,1664]{2,1,0:T(8,128)(2,1)}, u32[]{:S(2)}, u32[]{:S(2)}) collective-permute-start(bf16[4,64,1664]{2,1,0:T(8,128)(2,1)} %collective-permute-done.4.refs_2_), channel_id=1, source_target_pairs={{0,16},{16,0},{1,17},{17,1},{2,18},{18,2},{3,19},{19,3},{4,20},{20... | collective-permute-start | bytes 2555912 | tf_op jit(solution)/shard_map/ppermute | solution.py:426
  130.3 13.2 %collective-permute-start.9 = (bf16[4,64,1664]{2,1,0:T(8,128)(2,1)}, bf16[4,64,1664]{2,1,0:T(8,128)(2,1)}, u32[]{:S(2)}, u32[]{:S(2)}) collective-permute-start(bf16[4,64,1664]{2,1,0:T(8,128)(2,1)} %collective-permute-done.5.refs_3_), channel_id=1, source_target_pairs={{0,16},{16,0},{1,17},{17,1},{2,18},{18,2},{3,19},{19,3},{4,20},{20... | collective-permute-start | bytes 2555912 | tf_op jit(solution)/shard_map/ppermute | solution.py:426
  134.6 65.2 %all-to-all-start.3 = ((bf16[4,1,72,2048]{3,2,1,0:T(8,128)(2,1)}), bf16[4,1,72,2048]{3,2,1,0:T(8,128)(2,1)}, u32[]{:S(2)}, u32[]{:S(2)}) async-start(bf16[4,1,72,2048]{3,2,1,0:T(8,128)(2,1)} %bitcast.34), calls=%async_computation.3 | async-start | bytes 2359296 | tf_op jit(solution)/shard_map/all_to_all | solution.py:417
  166.7 52.8 %collective-permute-start.12 = (bf16[136,2048]{1,0:T(8,128)(2,1)}, bf16[136,2048]{1,0:T(8,128)(2,1)}, u32[]{:S(2)}, u32[]{:S(2)}) collective-permute-start(bf16[136,2048]{1,0:T(8,128)(2,1)} %pad_maximum_fusion.4), channel_id=1, source_target_pairs={{0,1},{1,2},{2,3},{3,0},{4,5},{5,6},{6,7},{7,4},{8,9},{9,10},{10,1... | collective-permute-start | bytes 1671176 | tf_op jit(solution)/shard_map/ppermute | solution.py:423
  166.8 52.8 %collective-permute-start.13 = (bf16[136,2048]{1,0:T(8,128)(2,1)}, bf16[136,2048]{1,0:T(8,128)(2,1)}, u32[]{:S(2)}, u32[]{:S(2)}) collective-permute-start(bf16[136,2048]{1,0:T(8,128)(2,1)} %pad_maximum_fusion.4), channel_id=1, source_target_pairs={{0,2},{1,3},{2,0},{3,1},{4,6},{5,7},{6,4},{7,5},{8,10},{9,11},{10,... | collective-permute-start | bytes 1671176 | tf_op jit(solution)/shard_map/ppermute | solution.py:423
  168.2 51.3 %collective-permute-start.14 = (bf16[136,2048]{1,0:T(8,128)(2,1)}, bf16[136,2048]{1,0:T(8,128)(2,1)}, u32[]{:S(2)}, u32[]{:S(2)}) collective-permute-start(bf16[136,2048]{1,0:T(8,128)(2,1)} %pad_maximum_fusion.4), channel_id=1, source_target_pairs={{0,3},{1,0},{2,1},{3,2},{4,7},{5,4},{6,5},{7,6},{8,11},{9,8},{10,9... | collective-permute-start | bytes 1671176 | tf_op jit(solution)/shard_map/ppermute | solution.py:423
  170.6 8.3 %collective-permute-start.10 = (f32[2,544]{0,1:T(8,128)S(1)}, f32[2,544]{0,1:T(8,128)S(1)}, u32[]{:S(2)}, u32[]{:S(2)}) collective-permute-start(f32[2,544]{0,1:T(8,128)S(1)} %copy.103), channel_id=1, source_target_pairs={{0,4},{4,0},{8,12},{12,8},{1,5},{5,1},{9,13},{13,9},{2,6},{6,2},{1... | collective-permute-start | bytes 13064 | tf_op jit(solution)/shard_map/ppermute | solution.py:414
  178.9 7.5 %collective-permute-start.11 = (f32[2,544]{0,1:T(8,128)S(1)}, f32[2,544]{0,1:T(8,128)S(1)}, u32[]{:S(2)}, u32[]{:S(2)}) collective-permute-start(f32[2,544]{0,1:T(8,128)S(1)} %add.338), channel_id=1, source_target_pairs={{0,8},{4,12},{8,0},{12,4},{1,9},{5,13},{9,1},{13,5},{2,10},{6,14},... | collective-permute-start | bytes 13064 | tf_op jit(solution)/shard_map/ppermute | solution.py:414
  186.5 48.5 %collective-permute-start.15 = (bf16[4,4,64,2048]{3,2,1,0:T(8,128)(2,1)}, bf16[4,4,64,2048]{3,2,1,0:T(8,128)(2,1)}, u32[]{:S(2)}, u32[]{:S(2)}) collective-permute-start(bf16[4,4,64,2048]{3,2,1,0:T(8,128)(2,1)} %all-to-all-done.1), channel_id=1, source_target_pairs={{0,16},{16,0},{1,17},{17,1},{2,18},{18,2},{3,19},{19,3},{4,20},{20... | collective-permute-start | bytes 12582920 | tf_op jit(solution)/shard_map/ppermute | solution.py:426
  199.7 13.5 %all-to-all-start.4 = ((bf16[4,136,512]{2,1,0:T(8,128)(2,1)}), bf16[4,136,512]{2,1,0:T(8,128)(2,1)}, u32[]{:S(2)}, u32[]{:S(2)}) async-start(bf16[4,136,512]{2,1,0:T(8,128)(2,1)} %bitcast.35), calls=%async_computation.4 | async-start | bytes 1114112 | tf_op jit(solution)/shard_map/all_to_all | solution.py:417
  224.7 45.3 %all-to-all-start.5 = ((bf16[4,3,72,2048]{3,2,1,0:T(8,128)(2,1)}), bf16[4,3,72,2048]{3,2,1,0:T(8,128)(2,1)}, u32[]{:S(2)}, u32[]{:S(2)}) async-start(bf16[4,3,72,2048]{3,2,1,0:T(8,128)(2,1)} %bitcast.298), calls=%async_computation.5 | async-start | bytes 7077888 | tf_op jit(solution)/shard_map/all_to_all | solution.py:417
  240.1 30.6 %collective-permute-start.16 = (bf16[136,2048]{1,0:T(8,128)(2,1)}, bf16[136,2048]{1,0:T(8,128)(2,1)}, u32[]{:S(2)}, u32[]{:S(2)}) collective-permute-start(bf16[136,2048]{1,0:T(8,128)(2,1)} %multiply_convert_fusion.1), channel_id=1, source_target_pairs={{0,1},{1,2},{2,3},{3,0},{4,5},{5,6},{6,7},{7,4},{8,9},{9,10},{10,1... | collective-permute-start | bytes 1671176 | tf_op jit(solution)/shard_map/ppermute | solution.py:423
  240.6 30.1 %copy-start.55 = (bf16[4,2,72,272]{3,2,1,0:T(8,128)(2,1)S(1)}, bf16[4,2,72,272]{3,2,1,0:T(8,128)(2,1)}, u32[]{:S(2)}) copy-start(bf16[4,2,72,272]{3,2,1,0:T(8,128)(2,1)} %fusion.52) | copy-start | bytes 940036
  243.4 31.4 %copy-start.82 = (f32[136]{0:T(256)}, f32[136]{0:T(256)S(1)}, u32[]{:S(2)}) copy-start(f32[136]{0:T(256)S(1)} %get-tuple-element.375) | copy-start | bytes 1636
  243.5 31.3 %copy-start.49 = (f32[136,16]{1,0:T(8,128)}, f32[136,16]{1,0:T(8,128)S(1)}, u32[]{:S(2)}) copy-start(f32[136,16]{1,0:T(8,128)S(1)} %copy.106) | copy-start | bytes 26116
  274.8 41.5 %all-to-all-start.6 = ((bf16[4,2,72,2048]{3,2,1,0:T(8,128)(2,1)}), bf16[4,2,72,2048]{3,2,1,0:T(8,128)(2,1)}, u32[]{:S(2)}, u32[]{:S(2)}) async-start(bf16[4,2,72,2048]{3,2,1,0:T(8,128)(2,1)} %bitcast.301), calls=%async_computation.6 | async-start | bytes 4718592 | tf_op jit(solution)/shard_map/all_to_all | solution.py:417
  279.3 25.1 %collective-permute-start.17 = (bf16[136,2048]{1,0:T(8,128)(2,1)}, bf16[136,2048]{1,0:T(8,128)(2,1)}, u32[]{:S(2)}, u32[]{:S(2)}) collective-permute-start(bf16[136,2048]{1,0:T(8,128)(2,1)} %multiply_convert_fusion.1), channel_id=1, source_target_pairs={{0,2},{1,3},{2,0},{3,1},{4,6},{5,7},{6,4},{7,5},{8,10},{9,11},{10,... | collective-permute-start | bytes 1671176 | tf_op jit(solution)/shard_map/ppermute | solution.py:423
  281.5 34.8 %collective-permute-start.18 = (bf16[136,2048]{1,0:T(8,128)(2,1)}, bf16[136,2048]{1,0:T(8,128)(2,1)}, u32[]{:S(2)}, u32[]{:S(2)}) collective-permute-start(bf16[136,2048]{1,0:T(8,128)(2,1)} %multiply_convert_fusion.1), channel_id=1, source_target_pairs={{0,3},{1,0},{2,1},{3,2},{4,7},{5,4},{6,5},{7,6},{8,11},{9,8},{10,9... | collective-permute-start | bytes 1671176 | tf_op jit(solution)/shard_map/ppermute | solution.py:423
  320.3 32.7 %all-to-all-start.7 = ((bf16[4,2,72,2048]{3,2,1,0:T(8,128)(2,1)}), bf16[4,2,72,2048]{3,2,1,0:T(8,128)(2,1)}, u32[]{:S(2)}, u32[]{:S(2)}) async-start(bf16[4,2,72,2048]{3,2,1,0:T(8,128)(2,1)} %bitcast.302), calls=%async_computation.7 | async-start | bytes 4718592 | tf_op jit(solution)/shard_map/all_to_all | solution.py:417
  353.0 29.2 %all-to-all-start.8 = ((bf16[4,72,2176]{2,1,0:T(8,128)(2,1)}), bf16[4,72,2176]{2,1,0:T(8,128)(2,1)}, u32[]{:S(2)}, u32[]{:S(2)}) async-start(bf16[4,72,2176]{2,1,0:T(8,128)(2,1)} %get-tuple-element.208), calls=%async_computation.8 | async-start | bytes 2506752 | tf_op jit(solution)/shard_map/all_to_all | solution.py:417
  385.0 19.8 %all-to-all-start.9 = ((bf16[4,72,2176]{2,1,0:T(8,128)(2,1)}), bf16[4,72,2176]{2,1,0:T(8,128)(2,1)}, u32[]{:S(2)}, u32[]{:S(2)}) async-start(bf16[4,72,2176]{2,1,0:T(8,128)(2,1)} %get-tuple-element.216), calls=%async_computation.9 | async-start | bytes 2506752 | tf_op jit(solution)/shard_map/all_to_all | solution.py:417
  389.4 66.3 %collective-permute-start.19 = (bf16[136,2176]{1,0:T(8,128)(2,1)}, bf16[136,2176]{1,0:T(8,128)(2,1)}, u32[]{:S(2)}, u32[]{:S(2)}) collective-permute-start(bf16[136,2176]{1,0:T(8,128)(2,1)} %fusion.5), channel_id=1, source_target_pairs={{0,3},{1,0},{2,1},{3,2},{4,7},{5,4},{6,5},{7,6},{8,11},{9,8},{10,9... | collective-permute-start | bytes 1775624 | tf_op jit(solution)/shard_map/ppermute | solution.py:423
  407.6 19.6 %all-to-all-start.10 = ((bf16[4,72,2176]{2,1,0:T(8,128)(2,1)}), bf16[4,72,2176]{2,1,0:T(8,128)(2,1)}, u32[]{:S(2)}, u32[]{:S(2)}) async-start(bf16[4,72,2176]{2,1,0:T(8,128)(2,1)} %get-tuple-element.226), calls=%async_computation.10 | async-start | bytes 2506752 | tf_op jit(solution)/shard_map/all_to_all | solution.py:417
  411.9 43.8 %collective-permute-start.20 = (bf16[136,2176]{1,0:T(8,128)(2,1)}, bf16[136,2176]{1,0:T(8,128)(2,1)}, u32[]{:S(2)}, u32[]{:S(2)}) collective-permute-start(bf16[136,2176]{1,0:T(8,128)(2,1)} %fusion.6), channel_id=1, source_target_pairs={{0,2},{1,3},{2,0},{3,1},{4,6},{5,7},{6,4},{7,5},{8,10},{9,11},{10,... | collective-permute-start | bytes 1775624 | tf_op jit(solution)/shard_map/ppermute | solution.py:423
  430.0 19.6 %all-to-all-start.11 = ((bf16[4,72,2176]{2,1,0:T(8,128)(2,1)}), bf16[4,72,2176]{2,1,0:T(8,128)(2,1)}, u32[]{:S(2)}, u32[]{:S(2)}) async-start(bf16[4,72,2176]{2,1,0:T(8,128)(2,1)} %get-tuple-element.234), calls=%async_computation.11 | async-start | bytes 2506752 | tf_op jit(solution)/shard_map/all_to_all | solution.py:417
  434.3 21.4 %collective-permute-start.21 = (bf16[136,2176]{1,0:T(8,128)(2,1)}, bf16[136,2176]{1,0:T(8,128)(2,1)}, u32[]{:S(2)}, u32[]{:S(2)}) collective-permute-start(bf16[136,2176]{1,0:T(8,128)(2,1)} %fusion.7), channel_id=1, source_target_pairs={{0,1},{1,2},{2,3},{3,0},{4,5},{5,6},{6,7},{7,4},{8,9},{9,10},{10,1... | collective-permute-start | bytes 1775624 | tf_op jit(solution)/shard_map/ppermute | solution.py:423
  449.6 38.7 %all-to-all-start.12 = ((bf16[4,2,72,2048]{3,2,1,0:T(8,128)(2,1)}), bf16[4,2,72,2048]{3,2,1,0:T(8,128)(2,1)}, u32[]{:S(2)}, u32[]{:S(2)}) async-start(bf16[4,2,72,2048]{3,2,1,0:T(8,128)(2,1)} %bitcast.300), calls=%async_computation.12 | async-start | bytes 4718592 | tf_op jit(solution)/shard_map/all_to_all | solution.py:417
  469.6 16.2 %collective-permute-start.22 = (bf16[136,512]{1,0:T(8,128)(2,1)S(1)}, bf16[136,512]{1,0:T(8,128)(2,1)S(1)}, u32[]{:S(2)}, u32[]{:S(2)}) collective-permute-start(bf16[136,512]{1,0:T(8,128)(2,1)S(1)} %get-tuple-element.339), channel_id=1, source_target_pairs={{0,4},{4,0},{8,12},{12,8},{1,5},{5,1},{9,13},{13,9},{2,6},{6,2},{1... | collective-permute-start | bytes 417800 | tf_op jit(solution)/shard_map/ppermute | solution.py:414
  473.0 12.9 %collective-permute-start.23 = (bf16[136,512]{1,0:T(8,128)(2,1)S(1)}, bf16[136,512]{1,0:T(8,128)(2,1)S(1)}, u32[]{:S(2)}, u32[]{:S(2)}) collective-permute-start(bf16[136,512]{1,0:T(8,128)(2,1)S(1)} %get-tuple-element.338), channel_id=1, source_target_pairs={{0,8},{4,12},{8,0},{12,4},{1,9},{5,13},{9,1},{13,5},{2,10},{6,14},... | collective-permute-start | bytes 417800 | tf_op jit(solution)/shard_map/ppermute | solution.py:414
  474.4 13.8 %collective-permute-start.24 = (bf16[136,512]{1,0:T(8,128)(2,1)S(1)}, bf16[136,512]{1,0:T(8,128)(2,1)S(1)}, u32[]{:S(2)}, u32[]{:S(2)}) collective-permute-start(bf16[136,512]{1,0:T(8,128)(2,1)S(1)} %get-tuple-element.337), channel_id=1, source_target_pairs={{0,12},{4,8},{8,4},{12,0},{1,13},{5,9},{9,5},{13,1},{2,14},{6,10},... | collective-permute-start | bytes 417800 | tf_op jit(solution)/shard_map/ppermute | solution.py:414
  509.2 6.6 collective-permute-start.27
  515.8 6.7 collective-permute-start.28
  518.4 34.7 %collective-permute-start.25 = (bf16[136,2048]{1,0:T(8,128)(2,1)}, bf16[136,2048]{1,0:T(8,128)(2,1)}, u32[]{:S(2)}, u32[]{:S(2)}) collective-permute-start(bf16[136,2048]{1,0:T(8,128)(2,1)} %get-tuple-element.336), channel_id=1, source_target_pairs={{0,2},{1,3},{2,0},{3,1},{4,6},{5,7},{6,4},{7,5},{8,10},{9,11},{10,... | collective-permute-start | bytes 1671176 | tf_op jit(solution)/shard_map/ppermute | solution.py:423
  518.4 37.6 %collective-permute-start.26 = (bf16[136,2048]{1,0:T(8,128)(2,1)}, bf16[136,2048]{1,0:T(8,128)(2,1)}, u32[]{:S(2)}, u32[]{:S(2)}) collective-permute-start(bf16[136,2048]{1,0:T(8,128)(2,1)} %get-tuple-element.335), channel_id=1, source_target_pairs={{0,1},{1,2},{2,3},{3,0},{4,5},{5,6},{6,7},{7,4},{8,9},{9,10},{10,1... | collective-permute-start | bytes 1671176 | tf_op jit(solution)/shard_map/ppermute | solution.py:423
  533.9 22.1 %collective-permute-start.29 = (bf16[1024,1536]{1,0:T(8,128)(2,1)}, bf16[1024,1536]{1,0:T(8,128)(2,1)}, u32[]{:S(2)}, u32[]{:S(2)}) collective-permute-start(bf16[1024,1536]{1,0:T(8,128)(2,1)} %weight_grad.8), channel_id=1, source_target_pairs={{0,16},{16,0},{1,17},{17,1},{2,18},{18,2},{3,19},{19,3},{4,20},{20... | collective-permute-start | bytes 9437192 | tf_op jit(solution)/shard_map/ppermute | solution.py:426
  535.5 32.7 %all-to-all-start.13 = ((bf16[4,136,2048]{2,1,0:T(8,128)(2,1)}), bf16[4,136,2048]{2,1,0:T(8,128)(2,1)}, u32[]{:S(2)}, u32[]{:S(2)}) async-start(bf16[4,136,2048]{2,1,0:T(8,128)(2,1)} %broadcast_in_dim.62), calls=%async_computation.13 | async-start | bytes 4456448 | tf_op jit(solution)/shard_map/all_to_all | solution.py:417
  573.3 20.2 %collective-permute-start.30 = (bf16[256,2048]{1,0:T(8,128)(2,1)}, bf16[256,2048]{1,0:T(8,128)(2,1)S(1)}, u32[]{:S(2)}, u32[]{:S(2)}) collective-permute-start(bf16[256,2048]{1,0:T(8,128)(2,1)} %weight_grad.10), channel_id=1, source_target_pairs={{0,16},{16,0},{1,17},{17,1},{2,18},{18,2},{3,19},{19,3},{4,20},{20... | collective-permute-start | bytes 3145736 | tf_op jit(solution)/shard_map/ppermute | solution.py:426
  576.0 36.4 %all-to-all-start.14 = ((bf16[4,136,2048]{2,1,0:T(8,128)(2,1)}), bf16[4,136,2048]{2,1,0:T(8,128)(2,1)S(1)}, u32[]{:S(2)}, u32[]{:S(2)}) async-start(bf16[4,136,2048]{2,1,0:T(8,128)(2,1)} %bitcast.304), calls=%async_computation.14 | async-start | bytes 4456448 | tf_op jit(solution)/shard_map/all_to_all | solution.py:417
  587.1 39.9 %collective-permute-start.31 = (bf16[512,2048]{1,0:T(8,128)(2,1)}, bf16[512,2048]{1,0:T(8,128)(2,1)}, u32[]{:S(2)}, u32[]{:S(2)}) collective-permute-start(bf16[512,2048]{1,0:T(8,128)(2,1)} %weight_grad.11), channel_id=1, source_target_pairs={{0,16},{16,0},{1,17},{17,1},{2,18},{18,2},{3,19},{19,3},{4,20},{20... | collective-permute-start | bytes 6291464 | tf_op jit(solution)/shard_map/ppermute | solution.py:426
  589.5 112.4 %collective-permute-start.35 = (bf16[256,1536]{1,0:T(8,128)(2,1)}, bf16[256,1536]{1,0:T(8,128)(2,1)}, u32[]{:S(2)}, u32[]{:S(2)}) collective-permute-start(bf16[256,1536]{1,0:T(8,128)(2,1)} %get-tuple-element.330), channel_id=1, source_target_pairs={{0,1},{1,2},{2,3},{3,0},{4,5},{5,6},{6,7},{7,4},{8,9},{9,10},{10,1... | collective-permute-start | bytes 2359304 | tf_op jit(solution)/shard_map/ppermute | solution.py:423
  590.3 111.6 %collective-permute-start.36 = (bf16[256,1536]{1,0:T(8,128)(2,1)}, bf16[256,1536]{1,0:T(8,128)(2,1)}, u32[]{:S(2)}, u32[]{:S(2)}) collective-permute-start(bf16[256,1536]{1,0:T(8,128)(2,1)} %get-tuple-element.329), channel_id=1, source_target_pairs={{0,2},{1,3},{2,0},{3,1},{4,6},{5,7},{6,4},{7,5},{8,10},{9,11},{10,... | collective-permute-start | bytes 2359304 | tf_op jit(solution)/shard_map/ppermute | solution.py:423
  593.5 108.5 %collective-permute-start.37 = (bf16[256,1536]{1,0:T(8,128)(2,1)}, bf16[256,1536]{1,0:T(8,128)(2,1)}, u32[]{:S(2)}, u32[]{:S(2)}) collective-permute-start(bf16[256,1536]{1,0:T(8,128)(2,1)} %get-tuple-element.328), channel_id=1, source_target_pairs={{0,3},{1,0},{2,1},{3,2},{4,7},{5,4},{6,5},{7,6},{8,11},{9,8},{10,9... | collective-permute-start | bytes 2359304 | tf_op jit(solution)/shard_map/ppermute | solution.py:423
  612.3 32.7 %all-to-all-start.15 = ((bf16[4,2,72,2048]{3,2,1,0:T(8,128)(2,1)}), bf16[4,2,72,2048]{3,2,1,0:T(8,128)(2,1)}, u32[]{:S(2)}, u32[]{:S(2)}) async-start(bf16[4,2,72,2048]{3,2,1,0:T(8,128)(2,1)} %bitcast.299), calls=%async_computation.15 | async-start | bytes 4718592 | tf_op jit(solution)/shard_map/all_to_all | solution.py:417
  624.8 1.7 collective-permute-start.33
  626.5 43.6 %collective-permute-start.34 = (bf16[1024,2048]{1,0:T(8,128)(2,1)}, bf16[1024,2048]{1,0:T(8,128)(2,1)}, u32[]{:S(2)}, u32[]{:S(2)}) collective-permute-start(bf16[1024,2048]{1,0:T(8,128)(2,1)} %weight_grad.13), channel_id=1, source_target_pairs={{0,16},{16,0},{1,17},{17,1},{2,18},{18,2},{3,19},{19,3},{4,20},{20... | collective-permute-start | bytes 12582920 | tf_op jit(solution)/shard_map/ppermute | solution.py:426
  645.8 8.2 %all-to-all-start.16 = ((f32[4,1,5120]{2,1,0:T(1,128)}), f32[4,1,5120]{2,1,0:T(1,128)S(1)}, u32[]{:S(2)}, u32[]{:S(2)}) async-start(f32[4,1,5120]{2,1,0:T(1,128)} %reshape.517), calls=%async_computation.16 | async-start | bytes 163840 | tf_op jit(solution)/shard_map/all_to_all | solution.py:417
  656.8 40.0 %all-to-all-start.17 = ((bf16[4,72,2048]{2,1,0:T(8,128)(2,1)}), bf16[4,72,2048]{2,1,0:T(8,128)(2,1)}, u32[]{:S(2)}, u32[]{:S(2)}) async-start(bf16[4,72,2048]{2,1,0:T(8,128)(2,1)} %pad_maximum_fusion.1), calls=%async_computation.17 | async-start | bytes 2359296 | tf_op jit(solution)/shard_map/all_to_all | solution.py:946
  669.5 30.5 %collective-permute-start.32 = (bf16[136,2048]{1,0:T(8,128)(2,1)}, bf16[136,2048]{1,0:T(8,128)(2,1)}, u32[]{:S(2)}, u32[]{:S(2)}) collective-permute-start(bf16[136,2048]{1,0:T(8,128)(2,1)} %slice.588), channel_id=1, source_target_pairs={{0,3},{1,0},{2,1},{3,2},{4,7},{5,4},{6,5},{7,6},{8,11},{9,8},{10,9... | collective-permute-start | bytes 1671176 | tf_op jit(solution)/shard_map/ppermute | solution.py:423
  670.1 30.1 %slice-start = ((f32[272,2048]{1,0:T(8,128)}), f32[136,2048]{1,0:T(8,128)S(1)}, s32[]{:S(2)}) async-start(f32[272,2048]{1,0:T(8,128)} %copy-done.25), calls=%async_computation.19 | async-start | bytes 2228224 | tf_op jit(solution)/shard_map/slice | solution.py:906
  705.3 12.8 %all-to-all-start.18 = ((bf16[4,64,1536]{2,1,0:T(8,128)(2,1)}), bf16[4,64,1536]{2,1,0:T(8,128)(2,1)S(1)}, u32[]{:S(2)}, u32[]{:S(2)}) async-start(bf16[4,64,1536]{2,1,0:T(8,128)(2,1)} %bitcast.113), calls=%async_computation.18 | async-start | bytes 1572864 | tf_op jit(solution)/shard_map/all_to_all | solution.py:417
  (103 other events, 523.3 us)

commit v3 on v2

--- a/solution.py
+++ b/solution.py
@@ -557,12 +557,6 @@
         w_sets[m - 1] += [dp_shift(v, m) for v in w_blocks[1:]]
     cot_blocks = [cot_own]
     routes_at = ids_at + cont_len
-    route_rows = [
-        part_of(v[..., routes_at : routes_at + route_width], 0, c)
-        .reshape(-1)[: rows * TOP]
-        .reshape(TOP, rows)
-        for v in w_blocks
-    ]
     places = jnp.stack(
         [(d - m) % n_dp for m in range(n_dp)] + [(z - s) % n_exp for s in range(n_exp)]
     ).astype(jnp.int32)
@@ -617,7 +611,7 @@
             .reshape(n_ctx * capacity, rows)
         )
 
-    spread = [spread_of(v) for v in route_rows]
+    spread = [spread_of(routes[0, 0].T)]
 
     def spread_pair(blocks):
         n = len(blocks)
@@ -681,7 +675,7 @@
     cot_sent = gate(pack_cot([0]), scale_in)
     cot_trade = ctx_trade(cot_sent)
     fence(cot_sent, w_qkv)
-    hidden_in = (x_all * after(scale_in) * by_exp(gain_in)).astype(BF16)
+    hidden_in = after((x_all * after(scale_in) * by_exp(gain_in)).astype(BF16))
     projected = dot(hidden_in, w_qkv)
 
     def ctx_sum(total):
@@ -695,6 +689,14 @@
     squares = jnp.stack([jnp.sum(raw_query * raw_query, axis=-1), jnp.sum(raw_key * raw_key, axis=-1)])
     cot_flight = [exp_shift(gate(cot_blocks[0], squares), s) for s in range(1, n_exp)]
     scales = lax.rsqrt(ctx_sum(squares) / D + NORM_EPS)
+    spread += [
+        spread_of(
+            part_of(v[..., routes_at : routes_at + route_width], 0, c)
+            .reshape(-1)[: rows * TOP]
+            .reshape(TOP, rows)
+        )
+        for v in gate(tuple(w_blocks[1:]), squares)
+    ]
     out_ctx = gate(out_ctx, scales)
     out_halves = [out_ctx] + [dp_shift(out_ctx, m) for m in range(1, n_dp)]
     fence(scales, out_ctx)
@@ -811,9 +813,7 @@
 
     back = after(back)
     returned = towards([0], back, spread[0])
-    sent = gate(mix_sent[1], back)
-    mix_trade = ctx_trade(sent)
-    fence(sent)
+    fence(returned)
     homes = after(*homes)
     for v in after(*homes):
         returned = returned + v.astype(F32)
@@ -838,10 +838,9 @@
         )
     pieces = by_owner(jnp.concatenate([grad_halves[i] for i in range(n_dp)], axis=1))
     mixed_grad = in_order(trade_pieces([part_of(pieces, 0, c ^ k) for k in range(n_ctx)]))
-    back = gate(mix_trade, mixed_grad)
-    leaving = towards(pairs[1], back, spreads[1]).astype(BF16)
-    mix_homes = [home(2, leaving[:rows]), home(3, leaving[rows:])]
-    fence(mixed_grad, leaving)
+    sent = gate(mix_sent[1], mixed_grad)
+    mix_trade = ctx_trade(sent)
+    fence(mixed_grad, sent)
     mixed_grad = after(mixed_grad)
     query_turn, key_turn, value_grad, head_gain_grads, sums = attend_back(
         mixed_grad.reshape(total_rows, width),
@@ -855,9 +854,12 @@
     )
     sums = jnp.stack([sums[:, 0], sums[:, HEAD_DIM]])
     means = ctx_sum(sums) / D
-    attn_sent = gate(attn_grad, means)
+    back = gate(mix_trade, means)
+    leaving = towards(pairs[1], back, spreads[1]).astype(BF16)
+    mix_homes = [home(2, leaving[:rows]), home(3, leaving[rows:])]
+    attn_sent = gate(attn_grad, back)
     attn_grad_all = ctx_gather(attn_sent)
-    fence(means, attn_sent)
+    fence(means, attn_sent, leaving)
     means = after(means)
     proj_grad = norms_back(
         query_turn, key_turn, value_grad, projected, scales, means.T, head_gains
@@ -872,8 +874,6 @@
     arrived = gate(tuple([after(v) for v in arrived]), hidden_part)
     qkv_dp = weight_grad([hidden_in], [[proj_grad]], half_rows[0], half, arrived)
     qkv_dp = qkv_dp.reshape(n_exp, n_ctx * shard, 3 * width)
-    mix_homes = after(*mix_homes)
-    qkv_dp = gate(qkv_dp, *mix_homes)
     sent = [part_of(qkv_dp, 0, (z + s) % n_exp).astype(BF16) for s in range(1, n_exp)]
     qkv_arrived = [exp_shift(v, s + 1) for s, v in enumerate(sent)]
     attn_grad_all = gate(attn_grad_all, *sent)
@@ -882,11 +882,13 @@
     attn_grad_all = attn_grad_all.reshape(total_rows, D)
     fence(hidden_part, *sent)
 
+    mix_homes = after(*mix_homes)
     in_rows, acts, gate_grads, up_grads = [after(*[v[i] for v in made]) for i in (0, 3, 4, 5)]
+    acts = gate(tuple(acts), *mix_homes)
     gate_up_grads = [[gate_grads[i], up_grads[i]] for i in range(len(pairs))]
     out_rows = width // n_dp
     if head_groups == n_dp:
-        out_left = [after(mixed_heads)]
+        out_left = [gate(after(mixed_heads), *mix_homes)]
         out_sent, out_arrived = grads_sent(out_left, [[attn_grad_all]], out_rows)
         acts = gate(tuple(acts), *out_sent)
     down_sent, down_arrived = grads_sent(acts, [[v] for v in route_grads], FF // n_dp)

time: 733 us -> 728 us (level)
  waiting for transfers between devices: 228 us -> 220 us
    ppermute x21, waiting for transfers between devices: 32.2 us -> 20.5 us  [exp_shift(): return lax.ppermute(x, 'exp', [(i, (i + s) % n_exp) for i in range(n_exp)])]
    unnamed x259 -> x279, local copies, waits for them, and re-layouts: 23.6 us -> 25.4 us
  transfers between devices with their start and end apart: 57 -> 57, of which waited for: 23 -> 24; matrix products, arithmetic and copies ran while one was open for 21% -> 20% of each run, Pallas kernels for 22% -> 23%
where the time goes in v3:
time: 728 us; the launch traced here: 716 us
  waiting for transfers between devices  220 us (30%)
  Pallas kernels  177 us (24%)
  starting transfers between devices  124 us (17%)
  local copies, waits for them, and re-layouts  78.4 us (11%)
  matrix products  64.6 us (9%)
  other arithmetic  47.2 us (6%)
    all_to_all x18, waiting for transfers between devices, ctx_trade(): return lax.all_to_all(x, 'ctx', 0, 0, tiled=True)  159 us
    all_to_all x18, starting transfers between devices, ctx_trade(): return lax.all_to_all(x, 'ctx', 0, 0, tiled=True)  77.9 us
    pallas_call x8, Pallas kernels, weight_grad(): pl.pallas_call(kernel, grid_spec=pltpu.PrefetchScalarGridSpec(num_scalar_...  59.8 us
    pallas_call x2, Pallas kernels, expert_rows(): pl.pallas_call(kernel, grid_spec=pltpu.PrefetchScalarGridSpec(num_scalar_...  46.5 us
    dot_general x12, matrix products, dot(): return jnp.dot(a, b, preferred_element_type=F32)  29.5 us
    ppermute x21, starting transfers between devices, exp_shift(): return lax.ppermute(x, 'exp', [(i, (i + s) % n_exp) for i in range(n_exp)])  28.1 us
    ppermute x7, waiting for transfers between devices, ctx_swap(): return lax.ppermute(x, 'ctx', [(i, i ^ k) for i in range(n_ctx)])  26 us
    unnamed x279, local copies, waits for them, and re-layouts  25.4 us
  transfers between devices with their start and end apart: 57, of which 24 were waited for; matrix products, arithmetic and copies ran while one was open for 20% of the time, Pallas kernels for 23%

profile of v3, /device:TPU:16, one launch (start us, length us, event | category | flops | bytes accessed | tf_op | source)
XLA Modules:
  0.0 715.8 jit_solution(5809593645650676274)
XLA Ops:
  9.8 4.2 all-to-all-start
  42.1 4.8 all-to-all-start.1
  52.6 42.9 %all-to-all-done.1 = bf16[4,4,64,2048]{3,2,1,0:T(8,128)(2,1)} async-done(((bf16[4,4,64,2048]{3,2,1,0:T(8,128)(2,1)}), bf16[4,4,64,2048]{3,2,1,0:T(8,128)(2,1)}, u32[]{:S(2)}, u32[]{:S(2)}) %all-to-all-start.1) | async-done | bytes 4194336 | tf_op jit(solution)/shard_map/all_to_all | solution.py:417
  97.1 4.5 all-to-all-start.2
  103.0 25.2 %all-to-all-done.2 = bf16[4,136,2048]{2,1,0:T(8,128)(2,1)} async-done(((bf16[4,136,2048]{2,1,0:T(8,128)(2,1)}), bf16[4,136,2048]{2,1,0:T(8,128)(2,1)}, u32[]{:S(2)}, u32[]{:S(2)}) %all-to-all-start.2) | async-done | bytes 2228256 | tf_op jit(solution)/shard_map/all_to_all | solution.py:417
  133.9 4.4 all-to-all-start.3
  139.3 6.3 assemble.1
  154.3 6.5 fusion.92.pq.pk.pv.projected_ref
  177.7 6.1 collective-permute-done.11
  185.2 8.4 %attend.1 = (bf16[544,512]{1,0:T(8,128)(2,1)}, bf16[544,512]{1,0:T(8,128)(2,1)S(1)}, bf16[544,512]{1,0:T(8,128)(2,1)S(1)}, bf16[544,512]{1,0:T(8,128)(2,1)S(1)}, f32[544,512]{1,0:T(8,128)S(1)}) custom-call(f32[544,1536]{1,0:T(8,128)} %copy-done.18, f32[544,1536]{1,0:T(8,128)} %copy-done.18, f32[544,1536]{1,0:T(8,128)} %copy-done.18, f32[544,2]{1,0:T(8,128)S(1)} %bitcast.260, ...), custom_call_target="tpu_custom_call" | custom-call | tf_op jit(solution)/shard_map/attend/pallas_call | solution.py:84
  197.1 4.1 all-to-all-start.4
  202.5 8.1 %all-to-all-done.4 = bf16[4,136,512]{2,1,0:T(8,128)(2,1)} async-done(((bf16[4,136,512]{2,1,0:T(8,128)(2,1)}), bf16[4,136,512]{2,1,0:T(8,128)(2,1)}, u32[]{:S(2)}, u32[]{:S(2)}) %all-to-all-start.4) | async-done | bytes 557088 | tf_op jit(solution)/shard_map/all_to_all | solution.py:417
  216.9 5.2 convolution_convert_fusion
  222.1 4.7 all-to-all-start.5
  229.3 3.0 convolution_add_fusion.1
  232.3 3.2 multiply_reduce_fusion.3
  239.1 28.2 %all-to-all-done.5 = bf16[4,3,72,2048]{3,2,1,0:T(8,128)(2,1)} async-done(((bf16[4,3,72,2048]{3,2,1,0:T(8,128)(2,1)}), bf16[4,3,72,2048]{3,2,1,0:T(8,128)(2,1)}, u32[]{:S(2)}, u32[]{:S(2)}) %all-to-all-start.5) | async-done | bytes 3538976 | tf_op jit(solution)/shard_map/all_to_all | solution.py:417
  271.7 4.0 convolution_convert_fusion.2
  275.7 4.5 all-to-all-start.6
  282.9 3.4 stack.81
  289.2 5.1 collective-permute-done.17
  294.3 11.8 %collective-permute-done.18 = bf16[136,2048]{1,0:T(8,128)(2,1)} collective-permute-done((bf16[136,2048]{1,0:T(8,128)(2,1)}, bf16[136,2048]{1,0:T(8,128)(2,1)}, u32[]{:S(2)}, u32[]{:S(2)}) %collective-permute-start.18) | collective-permute-done | bytes 557088 | tf_op jit(solution)/shard_map/ppermute | solution.py:423
  307.2 4.0 convolution_convert_fusion.1
  311.2 4.5 all-to-all-start.7
  317.0 23.3 %expert.2 = (bf16[4,72,2176]{2,1,0:T(8,128)(2,1)}, bf16[4,72,2176]{2,1,0:T(8,128)(2,1)}, bf16[576,1024]{1,0:T(8,128)(2,1)}, bf16[576,1024]{1,0:T(8,128)(2,1)}, b...) custom-call(s32[1]{0:T(128)} %bitcast.52.expert_ref, bf16[576,2048]{1,0:T(8,128)(2,1)} %bitcast.55.rows_ref.refs_0_, ...), custom_call_target="tpu_custom_call" | custom-call | tf_op jit(solution)/shard_map/expert/pallas_call | solution.py:281
  342.9 4.7 all-to-all-start.8
  348.9 23.2 %expert.3 = (bf16[4,72,2176]{2,1,0:T(8,128)(2,1)}, bf16[4,72,2176]{2,1,0:T(8,128)(2,1)}, bf16[576,1024]{1,0:T(8,128)(2,1)}, bf16[576,1024]{1,0:T(8,128)(2,1)}, b...) custom-call(s32[1]{0:T(128)} %bitcast.52.expert_ref, bf16[576,2048]{1,0:T(8,128)(2,1)} %bitcast.59.rows_ref.refs_1_, ...), custom_call_target="tpu_custom_call" | custom-call | tf_op jit(solution)/shard_map/expert/pallas_call | solution.py:281
  374.9 4.3 all-to-all-start.9
  383.0 7.0 expert_outs.2
  390.0 4.5 all-to-all-done.9
  399.0 4.3 all-to-all-start.10
  404.6 7.0 expert_outs.3
  411.6 6.8 all-to-all-done.10
  423.5 4.5 all-to-all-start.11
  429.2 13.7 %all-to-all-done.11 = bf16[4,72,2176]{2,1,0:T(8,128)(2,1)} async-done(((bf16[4,72,2176]{2,1,0:T(8,128)(2,1)}), bf16[4,72,2176]{2,1,0:T(8,128)(2,1)}, u32[]{:S(2)}, u32[]{:S(2)}) %all-to-all-start.11) | async-done | bytes 1253408 | tf_op jit(solution)/shard_map/all_to_all | solution.py:417
  452.4 3.9 fusion.25
  456.3 3.7 fusion.27
  469.3 4.5 all-to-all-start.12
  477.4 12.6 %attend_back.1 = (f32[544,512]{1,0:T(8,128)S(1)}, f32[544,512]{1,0:T(8,128)}, bf16[544,512]{1,0:T(8,128)(2,1)S(1)}, f32[2,512]{1,0:T(2,128)S(1)}, f32[544,256]{1,0:T(8,128)S(1)}) custom-call(bf16[544,512]{1,0:T(8,128)(2,1)S(1)} %bitcast.263, bf16[544,512]{1,0:T(8,128)(2,1)S(1)} %copy-done.8, bf16[544,512]{1,0:T(8,128)(2,1)S(1)} %copy-done.10, ...), custom_call_target="tpu_custom_call" | custom-call | tf_op jit(solution)/shard_map/attend_back/pallas_call | solution.py:159
  493.0 11.9 %collective-permute-done.25 = f32[2,544]{0,1:T(8,128)S(1)} collective-permute-done((f32[2,544]{0,1:T(8,128)S(1)}, f32[2,544]{0,1:T(8,128)S(1)}, u32[]{:S(2)}, u32[]{:S(2)}) %collective-permute-start.25) | collective-permute-done | bytes 4384 | tf_op jit(solution)/shard_map/ppermute | solution.py:414
  508.0 3.5 collective-permute-done.26
  520.6 6.1 weight_grad.8
  529.5 4.7 all-to-all-start.13
  535.7 7.6 %convolution_convert_fusion.3 = bf16[544,2048]{1,0:T(8,128)(2,1)} fusion(bf16[544,1536]{1,0:T(8,128)(2,1)S(1)} %copy-done.2, bf16[2048,1536]{1,0:T(8,128)(2,1)} %bitcast.321), kind=kOutput, calls=%fused_computation.15 | convolution fusion | flops 3423666176 | bytes 10190848 | tf_op jit(solution)/shard_map/dot_general | solution.py:49
  543.3 7.4 %weight_grad.9 = f32[1024,1536]{1,0:T(8,128)} custom-call(s32[1]{0:T(128)} %bitcast.18.part_ref, bf16[544,2048]{1,0:T(8,128)(2,1)} %copy-done.25, bf16[544,1536]{1,0:T(8,128)(2,1)} %copy-done.1, bf16[1024,1536]{1,0:T(8,128)(2,1)} %collective-permute-done.29.refs_2_), custom_call_target="tpu_custom_call" | custom-call | flops 3422552064 | bytes 9076736 | tf_op jit(solution)/shard_map/weight_grad/pallas_call | solution.py:358
  550.7 3.8 fusion.47
  554.5 6.5 all-to-all-done.13
  565.8 3.7 weight_grad.10
  572.2 3.6 all-to-all-start.14
  576.1 7.2 %weight_grad.11 = bf16[512,2048]{1,0:T(8,128)(2,1)} custom-call(s32[1]{0:T(128)} %bitcast.84.part_ref, bf16[576,1024]{1,0:T(8,128)(2,1)} %get-tuple-element.305.act_ref.refs_0_, bf16[576,1024]{1,0:T(8,128)(2,1)} %get-tuple-element.306.act_ref.refs_1_, bf16[576,2048]{1,0:T(8,128)(2,1)} %get-tuple-element.288.refs_2_, bf16[576,2048]{1,0:T(8,128)(2,1)} %get-tuple-element.289.refs_3_), custom_call_target="tpu_custom_call" | custom-call | flops 4831838208 | bytes 10092544 | tf_op jit(solution)/shard_map/weight_grad/pallas_call | solution.py:358
  591.4 4.3 weight_grad.12
  598.4 10.9 %weight_grad.13 = bf16[1024,2048]{1,0:T(8,128)(2,1)} custom-call(s32[1]{0:T(128)} %bitcast.84.part_ref, bf16[576,2048]{1,0:T(8,128)(2,1)} %bitcast.55.rows_ref.refs_0_, bf16[576,2048]{1,0:T(8,128)(2,1)} %bitcast.59.rows_ref.refs_1_, bf16[576,1024]{1,0:T(8,128)(2,1)} %get-tuple-element.297.refs_2_, bf16[576,1024]{1,0:T(8,128)(2,1)} %get-tuple-element.300.refs_3_, ...), custom_call_target="tpu_custom_call" | custom-call | flops 9663676416 | bytes 15466496 | tf_op jit(solution)/shard_map/weight_grad/pallas_call | solution.py:358
  609.3 4.8 all-to-all-start.15
  617.3 3.3 copy.109
  624.0 8.1 %weight_grad.14 = f32[512,2048]{1,0:T(8,128)} custom-call(s32[1]{0:T(128)} %bitcast.93.part_ref, bf16[576,1024]{1,0:T(8,128)(2,1)} %get-tuple-element.305.act_ref.refs_0_, bf16[576,1024]{1,0:T(8,128)(2,1)} %get-tuple-element.306.act_ref.refs_1_, bf16[576,2048]{1,0:T(8,128)(2,1)} %get-tuple-element.288.refs_2_, bf16[576,2048]{1,0:T(8,128)(2,1)} %get-tuple-element.289.refs_3_, ...), custom_call_target="tpu_custom_call" | custom-call | flops 4831838208 | bytes 10092544 | tf_op jit(solution)/shard_map/weight_grad/pallas_call | solution.py:358
  632.1 9.5 %all-to-all-done.15 = bf16[4,2,72,2048]{3,2,1,0:T(8,128)(2,1)} async-done(((bf16[4,2,72,2048]{3,2,1,0:T(8,128)(2,1)}), bf16[4,2,72,2048]{3,2,1,0:T(8,128)(2,1)}, u32[]{:S(2)}, u32[]{:S(2)}) %all-to-all-start.15) | async-done | bytes 2359328 | tf_op jit(solution)/shard_map/all_to_all | solution.py:417
  642.4 3.3 all-to-all-start.16
  647.4 3.2 all-to-all-done.16
  653.5 5.5 all-to-all-start.17
  665.5 12.1 %weight_grad.15 = f32[1024,2048]{1,0:T(8,128)} custom-call(s32[1]{0:T(128)} %bitcast.93.part_ref, bf16[576,2048]{1,0:T(8,128)(2,1)} %bitcast.55.rows_ref.refs_0_, bf16[576,2048]{1,0:T(8,128)(2,1)} %bitcast.59.rows_ref.refs_1_, bf16[576,1024]{1,0:T(8,128)(2,1)} %get-tuple-element.297.refs_2_, bf16[576,1024]{1,0:T(8,128)(2,1)} %get-tuple-element.300.refs_3_, ...), custom_call_target="tpu_custom_call" | custom-call | flops 9663676416 | bytes 15466496 | tf_op jit(solution)/shard_map/weight_grad/pallas_call | solution.py:358
  677.6 14.7 %all-to-all-done.17 = bf16[4,72,2048]{2,1,0:T(8,128)(2,1)} async-done(((bf16[4,72,2048]{2,1,0:T(8,128)(2,1)}), bf16[4,72,2048]{2,1,0:T(8,128)(2,1)}, u32[]{:S(2)}, u32[]{:S(2)}) %all-to-all-start.17) | async-done | bytes 1179680 | tf_op jit(solution)/shard_map/all_to_all | solution.py:948
  697.3 3.4 fusion.20
  700.8 3.5 all-to-all-start.18
  706.9 6.7 all-to-all-done.18
  (566 shorter events, 217.1 us)
Async XLA Ops:
  0.6 30.1 %collective-permute-start = (bf16[64,2048]{1,0:T(8,128)(2,1)}, bf16[64,2048]{1,0:T(8,128)(2,1)}, u32[]{:S(2)}, u32[]{:S(2)}) collective-permute-start(bf16[64,2048]{1,0:T(8,128)(2,1)} %param.17), channel_id=1, source_target_pairs={{0,1},{1,2},{2,3},{3,0},{4,5},{5,6},{6,7},{7,4},{8,9},{9,10},{10,1... | collective-permute-start | bytes 786440 | tf_op jit(solution)/shard_map/ppermute | solution.py:423
  2.3 28.4 %collective-permute-start.1 = (bf16[64,2048]{1,0:T(8,128)(2,1)}, bf16[64,2048]{1,0:T(8,128)(2,1)}, u32[]{:S(2)}, u32[]{:S(2)}) collective-permute-start(bf16[64,2048]{1,0:T(8,128)(2,1)} %param.17), channel_id=1, source_target_pairs={{0,2},{1,3},{2,0},{3,1},{4,6},{5,7},{6,4},{7,5},{8,10},{9,11},{10,... | collective-permute-start | bytes 786440 | tf_op jit(solution)/shard_map/ppermute | solution.py:423
  2.6 28.1 %collective-permute-start.2 = (bf16[64,2048]{1,0:T(8,128)(2,1)}, bf16[64,2048]{1,0:T(8,128)(2,1)}, u32[]{:S(2)}, u32[]{:S(2)}) collective-permute-start(bf16[64,2048]{1,0:T(8,128)(2,1)} %param.17), channel_id=1, source_target_pairs={{0,3},{1,0},{2,1},{3,2},{4,7},{5,4},{6,5},{7,6},{8,11},{9,8},{10,9... | collective-permute-start | bytes 786440 | tf_op jit(solution)/shard_map/ppermute | solution.py:423
  9.8 24.0 %all-to-all-start = ((bf16[4,64,1664]{2,1,0:T(8,128)(2,1)}), bf16[4,64,1664]{2,1,0:T(8,128)(2,1)}, u32[]{:S(2)}, u32[]{:S(2)}) async-start(bf16[4,64,1664]{2,1,0:T(8,128)(2,1)} %pack.1), calls=%async_computation | async-start | bytes 1703936 | tf_op jit(solution)/shard_map/all_to_all | solution.py:417
  33.8 97.2 %collective-permute-start.3 = (bf16[4,64,1664]{2,1,0:T(8,128)(2,1)}, bf16[4,64,1664]{2,1,0:T(8,128)(2,1)}, u32[]{:S(2)}, u32[]{:S(2)}) collective-permute-start(bf16[4,64,1664]{2,1,0:T(8,128)(2,1)} %all-to-all-done.refs_0_), channel_id=1, source_target_pairs={{0,1},{1,2},{2,3},{3,0},{4,5},{5,6},{6,7},{7,4},{8,9},{9,10},{10,1... | collective-permute-start | bytes 2555912 | tf_op jit(solution)/shard_map/ppermute | solution.py:423
  34.7 96.3 %collective-permute-start.4 = (bf16[4,64,1664]{2,1,0:T(8,128)(2,1)}, bf16[4,64,1664]{2,1,0:T(8,128)(2,1)}, u32[]{:S(2)}, u32[]{:S(2)}) collective-permute-start(bf16[4,64,1664]{2,1,0:T(8,128)(2,1)} %all-to-all-done.refs_0_), channel_id=1, source_target_pairs={{0,2},{1,3},{2,0},{3,1},{4,6},{5,7},{6,4},{7,5},{8,10},{9,11},{10,... | collective-permute-start | bytes 2555912 | tf_op jit(solution)/shard_map/ppermute | solution.py:423
  37.3 93.7 %collective-permute-start.5 = (bf16[4,64,1664]{2,1,0:T(8,128)(2,1)}, bf16[4,64,1664]{2,1,0:T(8,128)(2,1)}, u32[]{:S(2)}, u32[]{:S(2)}) collective-permute-start(bf16[4,64,1664]{2,1,0:T(8,128)(2,1)} %all-to-all-done.refs_0_), channel_id=1, source_target_pairs={{0,3},{1,0},{2,1},{3,2},{4,7},{5,4},{6,5},{7,6},{8,11},{9,8},{10,9... | collective-permute-start | bytes 2555912 | tf_op jit(solution)/shard_map/ppermute | solution.py:423
  39.5 98.8 %collective-permute-start.6 = (bf16[4,64,1664]{2,1,0:T(8,128)(2,1)}, bf16[4,64,1664]{2,1,0:T(8,128)(2,1)}, u32[]{:S(2)}, u32[]{:S(2)}) collective-permute-start(bf16[4,64,1664]{2,1,0:T(8,128)(2,1)} %all-to-all-done.refs_0_), channel_id=1, source_target_pairs={{0,16},{16,0},{1,17},{17,1},{2,18},{18,2},{3,19},{19,3},{4,20},{20... | collective-permute-start | bytes 2555912 | tf_op jit(solution)/shard_map/ppermute | solution.py:426
  42.1 53.4 %all-to-all-start.1 = ((bf16[4,4,64,2048]{3,2,1,0:T(8,128)(2,1)}), bf16[4,4,64,2048]{3,2,1,0:T(8,128)(2,1)}, u32[]{:S(2)}, u32[]{:S(2)}) async-start(bf16[4,4,64,2048]{3,2,1,0:T(8,128)(2,1)} %broadcast_in_dim.54), calls=%async_computation.1 | async-start | bytes 8388608 | tf_op jit(solution)/shard_map/all_to_all | solution.py:417
  46.9 48.5 %copy-start.47 = (bf16[136,2048]{1,0:T(8,128)(2,1)S(1)}, bf16[136,2048]{1,0:T(8,128)(2,1)}, u32[]{:S(2)}) copy-start(bf16[136,2048]{1,0:T(8,128)(2,1)} %reshape.438) | copy-start | bytes 1671172
  97.1 31.1 %all-to-all-start.2 = ((bf16[4,136,2048]{2,1,0:T(8,128)(2,1)}), bf16[4,136,2048]{2,1,0:T(8,128)(2,1)}, u32[]{:S(2)}, u32[]{:S(2)}) async-start(bf16[4,136,2048]{2,1,0:T(8,128)(2,1)} %broadcast_in_dim.55), calls=%async_computation.2 | async-start | bytes 4456448 | tf_op jit(solution)/shard_map/all_to_all | solution.py:417
  102.9 28.9 %copy-start.96 = (s32[8]{0:T(128)S(1)}, s32[8]{0:T(128)}, u32[]{:S(2)}) copy-start(s32[8]{0:T(128)} %copy-done.95) | copy-start | bytes 100
  103.0 29.0 %copy-start.117 = (f32[64]{0:T(128)S(1)}, f32[64]{0:T(128)}, u32[]{:S(2)}) copy-start(f32[64]{0:T(128)} %multiply_power_fusion) | copy-start | bytes 772
  131.0 7.3 %collective-permute-start.7 = (bf16[4,64,1664]{2,1,0:T(8,128)(2,1)}, bf16[4,64,1664]{2,1,0:T(8,128)(2,1)S(1)}, u32[]{:S(2)}, u32[]{:S(2)}) collective-permute-start(bf16[4,64,1664]{2,1,0:T(8,128)(2,1)} %collective-permute-done.3.refs_1_), channel_id=1, source_target_pairs={{0,16},{16,0},{1,17},{17,1},{2,18},{18,2},{3,19},{19,3},{4,20},{20... | collective-permute-start | bytes 2555912 | tf_op jit(solution)/shard_map/ppermute | solution.py:426
  131.1 7.3 %collective-permute-start.8 = (bf16[4,64,1664]{2,1,0:T(8,128)(2,1)}, bf16[4,64,1664]{2,1,0:T(8,128)(2,1)}, u32[]{:S(2)}, u32[]{:S(2)}) collective-permute-start(bf16[4,64,1664]{2,1,0:T(8,128)(2,1)} %collective-permute-done.4.refs_2_), channel_id=1, source_target_pairs={{0,16},{16,0},{1,17},{17,1},{2,18},{18,2},{3,19},{19,3},{4,20},{20... | collective-permute-start | bytes 2555912 | tf_op jit(solution)/shard_map/ppermute | solution.py:426
  131.6 6.8 collective-permute-start.9
  133.9 51.3 %copy-start = (f32[544,544]{1,0:T(8,128)}, f32[544,544]{1,0:T(8,128)S(1)}, u32[]{:S(2)}) copy-start(f32[544,544]{1,0:T(8,128)S(1)} %fusion.22.pair_ref) | copy-start | bytes 3551236
  133.9 63.2 %all-to-all-start.3 = ((bf16[4,1,72,2048]{3,2,1,0:T(8,128)(2,1)}), bf16[4,1,72,2048]{3,2,1,0:T(8,128)(2,1)}, u32[]{:S(2)}, u32[]{:S(2)}) async-start(bf16[4,1,72,2048]{3,2,1,0:T(8,128)(2,1)} %bitcast.36), calls=%async_computation.3 | async-start | bytes 2359296 | tf_op jit(solution)/shard_map/all_to_all | solution.py:417
  162.9 54.0 %collective-permute-start.12 = (bf16[136,2048]{1,0:T(8,128)(2,1)}, bf16[136,2048]{1,0:T(8,128)(2,1)}, u32[]{:S(2)}, u32[]{:S(2)}) collective-permute-start(bf16[136,2048]{1,0:T(8,128)(2,1)} %pad_maximum_fusion.4), channel_id=1, source_target_pairs={{0,1},{1,2},{2,3},{3,0},{4,5},{5,6},{6,7},{7,4},{8,9},{9,10},{10,1... | collective-permute-start | bytes 1671176 | tf_op jit(solution)/shard_map/ppermute | solution.py:423
  163.0 53.9 %collective-permute-start.13 = (bf16[136,2048]{1,0:T(8,128)(2,1)}, bf16[136,2048]{1,0:T(8,128)(2,1)}, u32[]{:S(2)}, u32[]{:S(2)}) collective-permute-start(bf16[136,2048]{1,0:T(8,128)(2,1)} %pad_maximum_fusion.4), channel_id=1, source_target_pairs={{0,2},{1,3},{2,0},{3,1},{4,6},{5,7},{6,4},{7,5},{8,10},{9,11},{10,... | collective-permute-start | bytes 1671176 | tf_op jit(solution)/shard_map/ppermute | solution.py:423
  164.5 52.4 %collective-permute-start.14 = (bf16[136,2048]{1,0:T(8,128)(2,1)}, bf16[136,2048]{1,0:T(8,128)(2,1)}, u32[]{:S(2)}, u32[]{:S(2)}) collective-permute-start(bf16[136,2048]{1,0:T(8,128)(2,1)} %pad_maximum_fusion.4), channel_id=1, source_target_pairs={{0,3},{1,0},{2,1},{3,2},{4,7},{5,4},{6,5},{7,6},{8,11},{9,8},{10,9... | collective-permute-start | bytes 1671176 | tf_op jit(solution)/shard_map/ppermute | solution.py:423
  166.8 9.2 %collective-permute-start.10 = (f32[2,544]{0,1:T(8,128)S(1)}, f32[2,544]{0,1:T(8,128)S(1)}, u32[]{:S(2)}, u32[]{:S(2)}) collective-permute-start(f32[2,544]{0,1:T(8,128)S(1)} %copy.103), channel_id=1, source_target_pairs={{0,4},{4,0},{8,12},{12,8},{1,5},{5,1},{9,13},{13,9},{2,6},{6,2},{1... | collective-permute-start | bytes 13064 | tf_op jit(solution)/shard_map/ppermute | solution.py:414
  176.1 7.7 %collective-permute-start.11 = (f32[2,544]{0,1:T(8,128)S(1)}, f32[2,544]{0,1:T(8,128)S(1)}, u32[]{:S(2)}, u32[]{:S(2)}) collective-permute-start(f32[2,544]{0,1:T(8,128)S(1)} %add.336), channel_id=1, source_target_pairs={{0,8},{4,12},{8,0},{12,4},{1,9},{5,13},{9,1},{13,5},{2,10},{6,14},... | collective-permute-start | bytes 13064 | tf_op jit(solution)/shard_map/ppermute | solution.py:414
  183.8 48.5 %collective-permute-start.15 = (bf16[4,4,64,2048]{3,2,1,0:T(8,128)(2,1)}, bf16[4,4,64,2048]{3,2,1,0:T(8,128)(2,1)}, u32[]{:S(2)}, u32[]{:S(2)}) collective-permute-start(bf16[4,4,64,2048]{3,2,1,0:T(8,128)(2,1)} %all-to-all-done.1), channel_id=1, source_target_pairs={{0,16},{16,0},{1,17},{17,1},{2,18},{18,2},{3,19},{19,3},{4,20},{20... | collective-permute-start | bytes 12582920 | tf_op jit(solution)/shard_map/ppermute | solution.py:426
  197.1 13.5 %all-to-all-start.4 = ((bf16[4,136,512]{2,1,0:T(8,128)(2,1)}), bf16[4,136,512]{2,1,0:T(8,128)(2,1)}, u32[]{:S(2)}, u32[]{:S(2)}) async-start(bf16[4,136,512]{2,1,0:T(8,128)(2,1)} %bitcast.37), calls=%async_computation.4 | async-start | bytes 1114112 | tf_op jit(solution)/shard_map/all_to_all | solution.py:417
  222.1 45.2 %all-to-all-start.5 = ((bf16[4,3,72,2048]{3,2,1,0:T(8,128)(2,1)}), bf16[4,3,72,2048]{3,2,1,0:T(8,128)(2,1)}, u32[]{:S(2)}, u32[]{:S(2)}) async-start(bf16[4,3,72,2048]{3,2,1,0:T(8,128)(2,1)} %bitcast.295), calls=%async_computation.5 | async-start | bytes 7077888 | tf_op jit(solution)/shard_map/all_to_all | solution.py:417
  237.5 32.1 %collective-permute-start.16 = (bf16[136,2048]{1,0:T(8,128)(2,1)}, bf16[136,2048]{1,0:T(8,128)(2,1)}, u32[]{:S(2)}, u32[]{:S(2)}) collective-permute-start(bf16[136,2048]{1,0:T(8,128)(2,1)} %multiply_convert_fusion), channel_id=1, source_target_pairs={{0,1},{1,2},{2,3},{3,0},{4,5},{5,6},{6,7},{7,4},{8,9},{9,10},{10,1... | collective-permute-start | bytes 1671176 | tf_op jit(solution)/shard_map/ppermute | solution.py:423
  237.7 29.6 %copy-start.23 = (bf16[2,4,4,64,128]{4,3,2,1,0:T(8,128)(2,1)S(1)}, bf16[2,4,4,64,128]{4,3,2,1,0:T(8,128)(2,1)}, u32[]{:S(2)}) copy-start(bf16[2,4,4,64,128]{4,3,2,1,0:T(8,128)(2,1)} %copy-done.22) | copy-start | bytes 1572868
  237.7 34.0 %copy-start.59 = (bf16[4,2,72,272]{3,2,1,0:T(8,128)(2,1)S(1)}, bf16[4,2,72,272]{3,2,1,0:T(8,128)(2,1)}, u32[]{:S(2)}) copy-start(bf16[4,2,72,272]{3,2,1,0:T(8,128)(2,1)} %fusion.49) | copy-start | bytes 940036
  269.6 24.7 %collective-permute-start.17 = (bf16[136,2048]{1,0:T(8,128)(2,1)}, bf16[136,2048]{1,0:T(8,128)(2,1)}, u32[]{:S(2)}, u32[]{:S(2)}) collective-permute-start(bf16[136,2048]{1,0:T(8,128)(2,1)} %multiply_convert_fusion), channel_id=1, source_target_pairs={{0,2},{1,3},{2,0},{3,1},{4,6},{5,7},{6,4},{7,5},{8,10},{9,11},{10,... | collective-permute-start | bytes 1671176 | tf_op jit(solution)/shard_map/ppermute | solution.py:423
  271.7 34.4 %collective-permute-start.18 = (bf16[136,2048]{1,0:T(8,128)(2,1)}, bf16[136,2048]{1,0:T(8,128)(2,1)}, u32[]{:S(2)}, u32[]{:S(2)}) collective-permute-start(bf16[136,2048]{1,0:T(8,128)(2,1)} %multiply_convert_fusion), channel_id=1, source_target_pairs={{0,3},{1,0},{2,1},{3,2},{4,7},{5,4},{6,5},{7,6},{8,11},{9,8},{10,9... | collective-permute-start | bytes 1671176 | tf_op jit(solution)/shard_map/ppermute | solution.py:423
  275.7 31.4 %all-to-all-start.6 = ((bf16[4,2,72,2048]{3,2,1,0:T(8,128)(2,1)}), bf16[4,2,72,2048]{3,2,1,0:T(8,128)(2,1)}, u32[]{:S(2)}, u32[]{:S(2)}) async-start(bf16[4,2,72,2048]{3,2,1,0:T(8,128)(2,1)} %bitcast.298), calls=%async_computation.6 | async-start | bytes 4718592 | tf_op jit(solution)/shard_map/all_to_all | solution.py:417
  311.2 31.7 %all-to-all-start.7 = ((bf16[4,2,72,2048]{3,2,1,0:T(8,128)(2,1)}), bf16[4,2,72,2048]{3,2,1,0:T(8,128)(2,1)}, u32[]{:S(2)}, u32[]{:S(2)}) async-start(bf16[4,2,72,2048]{3,2,1,0:T(8,128)(2,1)} %bitcast.299), calls=%async_computation.7 | async-start | bytes 4718592 | tf_op jit(solution)/shard_map/all_to_all | solution.py:417
  342.9 29.2 %all-to-all-start.8 = ((bf16[4,72,2176]{2,1,0:T(8,128)(2,1)}), bf16[4,72,2176]{2,1,0:T(8,128)(2,1)}, u32[]{:S(2)}, u32[]{:S(2)}) async-start(bf16[4,72,2176]{2,1,0:T(8,128)(2,1)} %get-tuple-element.218), calls=%async_computation.8 | async-start | bytes 2506752 | tf_op jit(solution)/shard_map/all_to_all | solution.py:417
  374.9 19.6 %all-to-all-start.9 = ((bf16[4,72,2176]{2,1,0:T(8,128)(2,1)}), bf16[4,72,2176]{2,1,0:T(8,128)(2,1)}, u32[]{:S(2)}, u32[]{:S(2)}) async-start(bf16[4,72,2176]{2,1,0:T(8,128)(2,1)} %get-tuple-element.226), calls=%async_computation.9 | async-start | bytes 2506752 | tf_op jit(solution)/shard_map/all_to_all | solution.py:417
  379.2 68.1 %collective-permute-start.19 = (bf16[136,2176]{1,0:T(8,128)(2,1)}, bf16[136,2176]{1,0:T(8,128)(2,1)}, u32[]{:S(2)}, u32[]{:S(2)}) collective-permute-start(bf16[136,2176]{1,0:T(8,128)(2,1)} %fusion.2), channel_id=1, source_target_pairs={{0,3},{1,0},{2,1},{3,2},{4,7},{5,4},{6,5},{7,6},{8,11},{9,8},{10,9... | collective-permute-start | bytes 1775624 | tf_op jit(solution)/shard_map/ppermute | solution.py:423
  397.3 50.0 %collective-permute-start.20 = (bf16[136,2176]{1,0:T(8,128)(2,1)}, bf16[136,2176]{1,0:T(8,128)(2,1)}, u32[]{:S(2)}, u32[]{:S(2)}) collective-permute-start(bf16[136,2176]{1,0:T(8,128)(2,1)} %fusion.3), channel_id=1, source_target_pairs={{0,2},{1,3},{2,0},{3,1},{4,6},{5,7},{6,4},{7,5},{8,10},{9,11},{10,... | collective-permute-start | bytes 1775624 | tf_op jit(solution)/shard_map/ppermute | solution.py:423
  399.0 19.3 %all-to-all-start.10 = ((bf16[4,72,2176]{2,1,0:T(8,128)(2,1)}), bf16[4,72,2176]{2,1,0:T(8,128)(2,1)}, u32[]{:S(2)}, u32[]{:S(2)}) async-start(bf16[4,72,2176]{2,1,0:T(8,128)(2,1)} %get-tuple-element.236), calls=%async_computation.10 | async-start | bytes 2506752 | tf_op jit(solution)/shard_map/all_to_all | solution.py:417
  421.1 26.2 %collective-permute-start.21 = (bf16[136,2176]{1,0:T(8,128)(2,1)}, bf16[136,2176]{1,0:T(8,128)(2,1)}, u32[]{:S(2)}, u32[]{:S(2)}) collective-permute-start(bf16[136,2176]{1,0:T(8,128)(2,1)} %fusion.4), channel_id=1, source_target_pairs={{0,1},{1,2},{2,3},{3,0},{4,5},{5,6},{6,7},{7,4},{8,9},{9,10},{10,1... | collective-permute-start | bytes 1775624 | tf_op jit(solution)/shard_map/ppermute | solution.py:423
  423.5 19.5 %all-to-all-start.11 = ((bf16[4,72,2176]{2,1,0:T(8,128)(2,1)}), bf16[4,72,2176]{2,1,0:T(8,128)(2,1)}, u32[]{:S(2)}, u32[]{:S(2)}) async-start(bf16[4,72,2176]{2,1,0:T(8,128)(2,1)} %get-tuple-element.244), calls=%async_computation.11 | async-start | bytes 2506752 | tf_op jit(solution)/shard_map/all_to_all | solution.py:417
  460.4 6.2 collective-permute-start.22
  461.9 5.1 collective-permute-start.23
  462.5 6.0 collective-permute-start.24
  469.3 42.2 %all-to-all-start.12 = ((bf16[4,2,72,2048]{3,2,1,0:T(8,128)(2,1)}), bf16[4,2,72,2048]{3,2,1,0:T(8,128)(2,1)}, u32[]{:S(2)}, u32[]{:S(2)}) async-start(bf16[4,2,72,2048]{3,2,1,0:T(8,128)(2,1)} %bitcast.297), calls=%async_computation.12 | async-start | bytes 4718592 | tf_op jit(solution)/shard_map/all_to_all | solution.py:417
  490.9 13.9 %collective-permute-start.25 = (f32[2,544]{0,1:T(8,128)S(1)}, f32[2,544]{0,1:T(8,128)S(1)}, u32[]{:S(2)}, u32[]{:S(2)}) collective-permute-start(f32[2,544]{0,1:T(8,128)S(1)} %copy.108), channel_id=1, source_target_pairs={{0,4},{4,0},{8,12},{12,8},{1,5},{5,1},{9,13},{13,9},{2,6},{6,2},{1... | collective-permute-start | bytes 13064 | tf_op jit(solution)/shard_map/ppermute | solution.py:414
  504.9 6.6 collective-permute-start.26
  526.7 16.6 %collective-permute-start.29 = (bf16[1024,1536]{1,0:T(8,128)(2,1)}, bf16[1024,1536]{1,0:T(8,128)(2,1)}, u32[]{:S(2)}, u32[]{:S(2)}) collective-permute-start(bf16[1024,1536]{1,0:T(8,128)(2,1)} %weight_grad.8), channel_id=1, source_target_pairs={{0,16},{16,0},{1,17},{17,1},{2,18},{18,2},{3,19},{19,3},{4,20},{20... | collective-permute-start | bytes 9437192 | tf_op jit(solution)/shard_map/ppermute | solution.py:426
  526.7 37.3 %collective-permute-start.27 = (bf16[136,2048]{1,0:T(8,128)(2,1)}, bf16[136,2048]{1,0:T(8,128)(2,1)}, u32[]{:S(2)}, u32[]{:S(2)}) collective-permute-start(bf16[136,2048]{1,0:T(8,128)(2,1)} %get-tuple-element.347), channel_id=1, source_target_pairs={{0,2},{1,3},{2,0},{3,1},{4,6},{5,7},{6,4},{7,5},{8,10},{9,11},{10,... | collective-permute-start | bytes 1671176 | tf_op jit(solution)/shard_map/ppermute | solution.py:423
  527.3 38.4 %collective-permute-start.28 = (bf16[136,2048]{1,0:T(8,128)(2,1)}, bf16[136,2048]{1,0:T(8,128)(2,1)}, u32[]{:S(2)}, u32[]{:S(2)}) collective-permute-start(bf16[136,2048]{1,0:T(8,128)(2,1)} %get-tuple-element.346), channel_id=1, source_target_pairs={{0,1},{1,2},{2,3},{3,0},{4,5},{5,6},{6,7},{7,4},{8,9},{9,10},{10,1... | collective-permute-start | bytes 1671176 | tf_op jit(solution)/shard_map/ppermute | solution.py:423
  529.5 31.5 %all-to-all-start.13 = ((bf16[4,136,2048]{2,1,0:T(8,128)(2,1)}), bf16[4,136,2048]{2,1,0:T(8,128)(2,1)}, u32[]{:S(2)}, u32[]{:S(2)}) async-start(bf16[4,136,2048]{2,1,0:T(8,128)(2,1)} %broadcast_in_dim.62), calls=%async_computation.13 | async-start | bytes 4456448 | tf_op jit(solution)/shard_map/all_to_all | solution.py:417
  569.5 20.9 %collective-permute-start.30 = (bf16[256,2048]{1,0:T(8,128)(2,1)}, bf16[256,2048]{1,0:T(8,128)(2,1)S(1)}, u32[]{:S(2)}, u32[]{:S(2)}) collective-permute-start(bf16[256,2048]{1,0:T(8,128)(2,1)} %weight_grad.10), channel_id=1, source_target_pairs={{0,16},{16,0},{1,17},{17,1},{2,18},{18,2},{3,19},{19,3},{4,20},{20... | collective-permute-start | bytes 3145736 | tf_op jit(solution)/shard_map/ppermute | solution.py:426
  572.2 37.1 %all-to-all-start.14 = ((bf16[4,136,2048]{2,1,0:T(8,128)(2,1)}), bf16[4,136,2048]{2,1,0:T(8,128)(2,1)S(1)}, u32[]{:S(2)}, u32[]{:S(2)}) async-start(bf16[4,136,2048]{2,1,0:T(8,128)(2,1)} %bitcast.300), calls=%async_computation.14 | async-start | bytes 4456448 | tf_op jit(solution)/shard_map/all_to_all | solution.py:417
  583.4 40.6 %collective-permute-start.31 = (bf16[512,2048]{1,0:T(8,128)(2,1)}, bf16[512,2048]{1,0:T(8,128)(2,1)}, u32[]{:S(2)}, u32[]{:S(2)}) collective-permute-start(bf16[512,2048]{1,0:T(8,128)(2,1)} %weight_grad.11), channel_id=1, source_target_pairs={{0,16},{16,0},{1,17},{17,1},{2,18},{18,2},{3,19},{19,3},{4,20},{20... | collective-permute-start | bytes 6291464 | tf_op jit(solution)/shard_map/ppermute | solution.py:426
  585.7 111.6 %collective-permute-start.35 = (bf16[256,1536]{1,0:T(8,128)(2,1)}, bf16[256,1536]{1,0:T(8,128)(2,1)}, u32[]{:S(2)}, u32[]{:S(2)}) collective-permute-start(bf16[256,1536]{1,0:T(8,128)(2,1)} %get-tuple-element.341), channel_id=1, source_target_pairs={{0,1},{1,2},{2,3},{3,0},{4,5},{5,6},{6,7},{7,4},{8,9},{9,10},{10,1... | collective-permute-start | bytes 2359304 | tf_op jit(solution)/shard_map/ppermute | solution.py:423
  585.8 111.5 %collective-permute-start.36 = (bf16[256,1536]{1,0:T(8,128)(2,1)}, bf16[256,1536]{1,0:T(8,128)(2,1)}, u32[]{:S(2)}, u32[]{:S(2)}) collective-permute-start(bf16[256,1536]{1,0:T(8,128)(2,1)} %get-tuple-element.340), channel_id=1, source_target_pairs={{0,2},{1,3},{2,0},{3,1},{4,6},{5,7},{6,4},{7,5},{8,10},{9,11},{10,... | collective-permute-start | bytes 2359304 | tf_op jit(solution)/shard_map/ppermute | solution.py:423
  587.6 109.8 %collective-permute-start.37 = (bf16[256,1536]{1,0:T(8,128)(2,1)}, bf16[256,1536]{1,0:T(8,128)(2,1)}, u32[]{:S(2)}, u32[]{:S(2)}) collective-permute-start(bf16[256,1536]{1,0:T(8,128)(2,1)} %get-tuple-element.339), channel_id=1, source_target_pairs={{0,3},{1,0},{2,1},{3,2},{4,7},{5,4},{6,5},{7,6},{8,11},{9,8},{10,9... | collective-permute-start | bytes 2359304 | tf_op jit(solution)/shard_map/ppermute | solution.py:423
  609.3 32.4 %all-to-all-start.15 = ((bf16[4,2,72,2048]{3,2,1,0:T(8,128)(2,1)}), bf16[4,2,72,2048]{3,2,1,0:T(8,128)(2,1)}, u32[]{:S(2)}, u32[]{:S(2)}) async-start(bf16[4,2,72,2048]{3,2,1,0:T(8,128)(2,1)} %bitcast.296), calls=%async_computation.15 | async-start | bytes 4718592 | tf_op jit(solution)/shard_map/all_to_all | solution.py:417
  621.7 1.7 collective-permute-start.33
  623.4 42.1 %collective-permute-start.34 = (bf16[1024,2048]{1,0:T(8,128)(2,1)}, bf16[1024,2048]{1,0:T(8,128)(2,1)}, u32[]{:S(2)}, u32[]{:S(2)}) collective-permute-start(bf16[1024,2048]{1,0:T(8,128)(2,1)} %weight_grad.13), channel_id=1, source_target_pairs={{0,16},{16,0},{1,17},{17,1},{2,18},{18,2},{3,19},{19,3},{4,20},{20... | collective-permute-start | bytes 12582920 | tf_op jit(solution)/shard_map/ppermute | solution.py:426
  642.4 8.2 %all-to-all-start.16 = ((f32[4,1,5120]{2,1,0:T(1,128)}), f32[4,1,5120]{2,1,0:T(1,128)S(1)}, u32[]{:S(2)}, u32[]{:S(2)}) async-start(f32[4,1,5120]{2,1,0:T(1,128)} %reshape.498), calls=%async_computation.16 | async-start | bytes 163840 | tf_op jit(solution)/shard_map/all_to_all | solution.py:417
  653.5 38.8 %all-to-all-start.17 = ((bf16[4,72,2048]{2,1,0:T(8,128)(2,1)}), bf16[4,72,2048]{2,1,0:T(8,128)(2,1)}, u32[]{:S(2)}, u32[]{:S(2)}) async-start(bf16[4,72,2048]{2,1,0:T(8,128)(2,1)} %pad_maximum_fusion.1), calls=%async_computation.17 | async-start | bytes 2359296 | tf_op jit(solution)/shard_map/all_to_all | solution.py:948
  664.9 30.5 %collective-permute-start.32 = (bf16[136,2048]{1,0:T(8,128)(2,1)}, bf16[136,2048]{1,0:T(8,128)(2,1)}, u32[]{:S(2)}, u32[]{:S(2)}) collective-permute-start(bf16[136,2048]{1,0:T(8,128)(2,1)} %slice.584), channel_id=1, source_target_pairs={{0,3},{1,0},{2,1},{3,2},{4,7},{5,4},{6,5},{7,6},{8,11},{9,8},{10,9... | collective-permute-start | bytes 1671176 | tf_op jit(solution)/shard_map/ppermute | solution.py:423
  665.5 30.1 %slice-start = ((f32[272,2048]{1,0:T(8,128)}), f32[136,2048]{1,0:T(8,128)S(1)}, s32[]{:S(2)}) async-start(f32[272,2048]{1,0:T(8,128)} %copy-done.28), calls=%async_computation.19 | async-start | bytes 2228224 | tf_op jit(solution)/shard_map/slice | solution.py:908
  700.8 12.8 %all-to-all-start.18 = ((bf16[4,64,1536]{2,1,0:T(8,128)(2,1)}), bf16[4,64,1536]{2,1,0:T(8,128)(2,1)S(1)}, u32[]{:S(2)}, u32[]{:S(2)}) async-start(bf16[4,64,1536]{2,1,0:T(8,128)(2,1)} %bitcast.114), calls=%async_computation.18 | async-start | bytes 1572864 | tf_op jit(solution)/shard_map/all_to_all | solution.py:417
  (113 other events, 797.2 us)

commit v4 on v3

--- a/solution.py
+++ b/solution.py
@@ -874,13 +874,17 @@
     arrived = gate(tuple([after(v) for v in arrived]), hidden_part)
     qkv_dp = weight_grad([hidden_in], [[proj_grad]], half_rows[0], half, arrived)
     qkv_dp = qkv_dp.reshape(n_exp, n_ctx * shard, 3 * width)
-    sent = [part_of(qkv_dp, 0, (z + s) % n_exp).astype(BF16) for s in range(1, n_exp)]
-    qkv_arrived = [exp_shift(v, s + 1) for s, v in enumerate(sent)]
+    sent = [part_of(qkv_dp, 0, (z - 1) % n_exp).astype(BF16)]
+
+    def ring_step(s, sent):
+        arrived = exp_shift(sent, 1)
+        return arrived, part_of(qkv_dp, 0, (z - s) % n_exp)
+
+    ring_arrived, ring_part = ring_step(2, sent[0])
     attn_grad_all = gate(attn_grad_all, *sent)
-    hidden_part = gate(hidden_part, attn_grad_all)
-    hidden_trade = ctx_trade(hidden_part.reshape(n_ctx, rows, D))
+    mix_trade = ctx_trade(gate(mix_sent[0], attn_grad_all))
     attn_grad_all = attn_grad_all.reshape(total_rows, D)
-    fence(hidden_part, *sent)
+    fence(attn_grad_all, *sent)
 
     mix_homes = after(*mix_homes)
     in_rows, acts, gate_grads, up_grads = [after(*[v[i] for v in made]) for i in (0, 3, 4, 5)]
@@ -892,16 +896,21 @@
         out_sent, out_arrived = grads_sent(out_left, [[attn_grad_all]], out_rows)
         acts = gate(tuple(acts), *out_sent)
     down_sent, down_arrived = grads_sent(acts, [[v] for v in route_grads], FF // n_dp)
-    in_rows = gate(tuple(in_rows), *down_sent)
+    ring_sent = (gate(ring_arrived, *down_sent).astype(F32) + ring_part).astype(BF16)
+    ring_arrived, ring_part = ring_step(3, ring_sent)
+    in_rows = gate(tuple(in_rows), ring_sent)
+    mix_back = gate(after(mix_trade), *down_sent)
+    hidden_part = gate(hidden_part, mix_back)
+    hidden_trade = ctx_trade(hidden_part.reshape(n_ctx, rows, D))
     if head_groups == n_dp:
         out_left = gate(tuple(out_left), *down_sent)
         out_dp = weight_grad(out_left, [[attn_grad_all]], half_rows[0], out_rows, out_arrived)
         out_dp = out_dp.reshape(n_exp, shard, D)
         in_rows = gate(tuple(in_rows), out_dp)
     gate_up_sent, gate_up_arrived = grads_sent(in_rows, gate_up_grads, D // n_dp)
-    hidden_trade = gate(hidden_trade, *gate_up_sent)
-    mix_back = ctx_trade(gate(mix_sent[0], hidden_trade))
-    acts = gate(tuple(acts), *gate_up_sent)
+    ring_sent = (gate(ring_arrived, *gate_up_sent).astype(F32) + ring_part).astype(BF16)
+    ring_arrived, ring_part = ring_step(4, ring_sent)
+    acts = gate(tuple(acts), ring_sent)
     grad_down = weight_grad(acts, [[v] for v in route_grads], d, FF // n_dp, down_arrived)
     mix_back = gate(mix_back, grad_down)
     leaving = towards(pairs[0], mix_back, spreads[0])
@@ -937,7 +946,7 @@
             lax.dynamic_index_in_dim(part, (late_d + m) % n_dp, 0, keepdims=False), m
         )
     part = total
-    part = jnp.sum(ctx_trade(gate(part, mix_back)), axis=0)
+    part = jnp.sum(ctx_trade(part), axis=0)
     if head_groups == n_dp:
         flat = part.reshape(n_exp, count * shard)
         high = flat.astype(BF16)
@@ -962,10 +971,7 @@
     mixture = mix_homes[2] + sum(v.astype(F32) for v in mix_homes[:2] + mix_homes[3:])
     final_rows = (mid_rows + mixture).astype(BF16)
 
-    qkv_arrived = gate(tuple(qkv_arrived), final_rows, small_sum)
-    qkv_exp = part_of(qkv_dp, 0, z)
-    for v in qkv_arrived:
-        qkv_exp = qkv_exp + v.astype(F32)
+    qkv_exp = gate(ring_arrived, final_rows, small_sum).astype(F32) + ring_part
     qkv_exp = qkv_exp.reshape(n_ctx, shard, 3 * width)
     grad_qkv = all_owners(ctx_trade(qkv_exp.astype(BF16)).astype(F32))
 

time: 728 us -> 719 us (0.988)
  the two profiles are of different devices: /device:TPU:16 before, /device:TPU:0 now
where the time goes in v4:
time: 719 us; the launch traced here: 709 us
  waiting for transfers between devices  213 us (30%)
  Pallas kernels  177 us (25%)
  starting transfers between devices  126 us (18%)
  local copies, waits for them, and re-layouts  77.2 us (11%)
  matrix products  64.6 us (9%)
  other arithmetic  47.3 us (7%)
    all_to_all x18, waiting for transfers between devices, ctx_trade(): return lax.all_to_all(x, 'ctx', 0, 0, tiled=True)  162 us
    all_to_all x18, starting transfers between devices, ctx_trade(): return lax.all_to_all(x, 'ctx', 0, 0, tiled=True)  78.9 us
    pallas_call x8, Pallas kernels, weight_grad(): pl.pallas_call(kernel, grid_spec=pltpu.PrefetchScalarGridSpec(num_scalar_...  60 us
    pallas_call x2, Pallas kernels, expert_rows(): pl.pallas_call(kernel, grid_spec=pltpu.PrefetchScalarGridSpec(num_scalar_...  46.5 us
    ppermute x21, starting transfers between devices, exp_shift(): return lax.ppermute(x, 'exp', [(i, (i + s) % n_exp) for i in range(n_exp)])  30.9 us
    dot_general x12, matrix products, dot(): return jnp.dot(a, b, preferred_element_type=F32)  29.4 us
    pallas_call x19, Pallas kernels, fence(): pl.pallas_call(hand_on, out_shape=jax.ShapeDtypeStruct(mark.shape, mark.d...  24.9 us
    unnamed x279, local copies, waits for them, and re-layouts  24.7 us
  transfers between devices with their start and end apart: 57, of which 21 were waited for; matrix products, arithmetic and copies ran while one was open for 21% of the time, Pallas kernels for 24%

profile of v4, /device:TPU:0, one launch (start us, length us, event | category | flops | bytes accessed | tf_op | source)
XLA Modules:
  0.0 709.1 jit_solution(4577172034248759576)
XLA Ops:
  0.6 3.1 collective-permute-start
  13.6 4.2 all-to-all-start
  44.1 4.8 all-to-all-start.1
  54.6 42.9 %all-to-all-done.1 = bf16[4,4,64,2048]{3,2,1,0:T(8,128)(2,1)} async-done(((bf16[4,4,64,2048]{3,2,1,0:T(8,128)(2,1)}), bf16[4,4,64,2048]{3,2,1,0:T(8,128)(2,1)}, u32[]{:S(2)}, u32[]{:S(2)}) %all-to-all-start.1) | async-done | bytes 4194336 | tf_op jit(solution)/shard_map/all_to_all | solution.py:417
  99.1 4.5 all-to-all-start.2
  105.0 25.3 %all-to-all-done.2 = bf16[4,136,2048]{2,1,0:T(8,128)(2,1)} async-done(((bf16[4,136,2048]{2,1,0:T(8,128)(2,1)}), bf16[4,136,2048]{2,1,0:T(8,128)(2,1)}, u32[]{:S(2)}, u32[]{:S(2)}) %all-to-all-start.2) | async-done | bytes 2228256 | tf_op jit(solution)/shard_map/all_to_all | solution.py:417
  136.0 4.5 all-to-all-start.3
  141.4 6.3 assemble.1
  156.4 6.5 fusion.91.pq.pk.pv.projected_ref
  181.0 6.1 collective-permute-done.11
  188.6 8.5 %attend.1 = (bf16[544,512]{1,0:T(8,128)(2,1)}, bf16[544,512]{1,0:T(8,128)(2,1)S(1)}, bf16[544,512]{1,0:T(8,128)(2,1)S(1)}, bf16[544,512]{1,0:T(8,128)(2,1)S(1)}, f32[544,512]{1,0:T(8,128)S(1)}) custom-call(f32[544,1536]{1,0:T(8,128)} %copy-done.16, f32[544,1536]{1,0:T(8,128)} %copy-done.16, f32[544,1536]{1,0:T(8,128)} %copy-done.16, f32[544,2]{1,0:T(8,128)S(1)} %bitcast.263, ...), custom_call_target="tpu_custom_call" | custom-call | tf_op jit(solution)/shard_map/attend/pallas_call | solution.py:84
  200.6 4.2 all-to-all-start.4
  206.1 8.1 %all-to-all-done.4 = bf16[4,136,512]{2,1,0:T(8,128)(2,1)} async-done(((bf16[4,136,512]{2,1,0:T(8,128)(2,1)}), bf16[4,136,512]{2,1,0:T(8,128)(2,1)}, u32[]{:S(2)}, u32[]{:S(2)}) %all-to-all-start.4) | async-done | bytes 557088 | tf_op jit(solution)/shard_map/all_to_all | solution.py:417
  220.5 5.2 convolution_convert_fusion
  225.7 4.7 all-to-all-start.5
  232.9 3.0 convolution_add_fusion.1
  235.9 3.2 multiply_reduce_fusion.3
  242.7 28.2 %all-to-all-done.5 = bf16[4,3,72,2048]{3,2,1,0:T(8,128)(2,1)} async-done(((bf16[4,3,72,2048]{3,2,1,0:T(8,128)(2,1)}), bf16[4,3,72,2048]{3,2,1,0:T(8,128)(2,1)}, u32[]{:S(2)}, u32[]{:S(2)}) %all-to-all-start.5) | async-done | bytes 3538976 | tf_op jit(solution)/shard_map/all_to_all | solution.py:417
  275.3 4.0 convolution_convert_fusion.2
  279.3 4.5 all-to-all-start.6
  286.4 3.4 stack.81
  292.7 6.5 collective-permute-done.17
  299.6 10.9 %all-to-all-done.6 = bf16[4,2,72,2048]{3,2,1,0:T(8,128)(2,1)} async-done(((bf16[4,2,72,2048]{3,2,1,0:T(8,128)(2,1)}), bf16[4,2,72,2048]{3,2,1,0:T(8,128)(2,1)}, u32[]{:S(2)}, u32[]{:S(2)}) %all-to-all-start.6) | async-done | bytes 2359328 | tf_op jit(solution)/shard_map/all_to_all | solution.py:417
  310.5 4.0 convolution_convert_fusion.1
  314.5 4.5 all-to-all-start.7
  320.3 23.2 %expert.2 = (bf16[4,72,2176]{2,1,0:T(8,128)(2,1)}, bf16[4,72,2176]{2,1,0:T(8,128)(2,1)}, bf16[576,1024]{1,0:T(8,128)(2,1)}, bf16[576,1024]{1,0:T(8,128)(2,1)}, b...) custom-call(s32[1]{0:T(128)} %bitcast.52.expert_ref, bf16[576,2048]{1,0:T(8,128)(2,1)} %bitcast.55.rows_ref.refs_0_, ...), custom_call_target="tpu_custom_call" | custom-call | tf_op jit(solution)/shard_map/expert/pallas_call | solution.py:281
  346.2 4.7 all-to-all-start.8
  352.1 23.2 %expert.3 = (bf16[4,72,2176]{2,1,0:T(8,128)(2,1)}, bf16[4,72,2176]{2,1,0:T(8,128)(2,1)}, bf16[576,1024]{1,0:T(8,128)(2,1)}, bf16[576,1024]{1,0:T(8,128)(2,1)}, b...) custom-call(s32[1]{0:T(128)} %bitcast.52.expert_ref, bf16[576,2048]{1,0:T(8,128)(2,1)} %bitcast.59.rows_ref.refs_1_, ...), custom_call_target="tpu_custom_call" | custom-call | tf_op jit(solution)/shard_map/expert/pallas_call | solution.py:281
  378.1 4.3 all-to-all-start.9
  386.0 7.0 expert_outs.2
  393.0 4.7 all-to-all-done.9
  401.6 4.3 all-to-all-start.10
  407.2 7.0 expert_outs.3
  414.2 6.8 all-to-all-done.10
  425.4 4.4 all-to-all-start.11
  431.2 13.7 %all-to-all-done.11 = bf16[4,72,2176]{2,1,0:T(8,128)(2,1)} async-done(((bf16[4,72,2176]{2,1,0:T(8,128)(2,1)}), bf16[4,72,2176]{2,1,0:T(8,128)(2,1)}, u32[]{:S(2)}, u32[]{:S(2)}) %all-to-all-start.11) | async-done | bytes 1253408 | tf_op jit(solution)/shard_map/all_to_all | solution.py:417
  454.4 3.9 fusion.25
  458.3 3.7 fusion.27
  468.5 3.6 collective-permute-done.23
  472.1 4.5 all-to-all-start.12
  480.1 12.6 %attend_back.1 = (f32[544,512]{1,0:T(8,128)S(1)}, f32[544,512]{1,0:T(8,128)}, bf16[544,512]{1,0:T(8,128)(2,1)S(1)}, f32[2,512]{1,0:T(2,128)S(1)}, f32[544,256]{1,0:T(8,128)S(1)}) custom-call(bf16[544,512]{1,0:T(8,128)(2,1)S(1)} %bitcast.266, bf16[544,512]{1,0:T(8,128)(2,1)S(1)} %copy-done.6, bf16[544,512]{1,0:T(8,128)(2,1)S(1)} %copy-done.8, ...), custom_call_target="tpu_custom_call" | custom-call | tf_op jit(solution)/shard_map/attend_back/pallas_call | solution.py:159
  497.6 10.1 %collective-permute-done.25 = f32[2,544]{0,1:T(8,128)S(1)} collective-permute-done((f32[2,544]{0,1:T(8,128)S(1)}, f32[2,544]{0,1:T(8,128)S(1)}, u32[]{:S(2)}, u32[]{:S(2)}) %collective-permute-start.25) | collective-permute-done | bytes 4384 | tf_op jit(solution)/shard_map/ppermute | solution.py:414
  510.7 3.6 collective-permute-done.26
  523.5 6.1 weight_grad.8
  534.0 4.7 all-to-all-start.13
  540.2 7.7 %convolution_convert_fusion.3 = bf16[544,2048]{1,0:T(8,128)(2,1)} fusion(bf16[544,1536]{1,0:T(8,128)(2,1)S(1)} %copy-done.2, bf16[2048,1536]{1,0:T(8,128)(2,1)} %bitcast.324), kind=kOutput, calls=%fused_computation.15 | convolution fusion | flops 3423666176 | bytes 10190848 | tf_op jit(solution)/shard_map/dot_general | solution.py:49
  547.9 7.4 %weight_grad.9 = f32[1024,1536]{1,0:T(8,128)} custom-call(s32[1]{0:T(128)} %bitcast.18.part_ref, bf16[544,2048]{1,0:T(8,128)(2,1)} %copy-done.23, bf16[544,1536]{1,0:T(8,128)(2,1)} %copy-done.1, bf16[1024,1536]{1,0:T(8,128)(2,1)} %collective-permute-done.29.refs_2_), custom_call_target="tpu_custom_call" | custom-call | flops 3422552064 | bytes 9076736 | tf_op jit(solution)/shard_map/weight_grad/pallas_call | solution.py:358
  557.7 7.8 %all-to-all-done.13 = bf16[4,136,2048]{2,1,0:T(8,128)(2,1)} async-done(((bf16[4,136,2048]{2,1,0:T(8,128)(2,1)}), bf16[4,136,2048]{2,1,0:T(8,128)(2,1)}, u32[]{:S(2)}, u32[]{:S(2)}) %all-to-all-start.13) | async-done | bytes 2228256 | tf_op jit(solution)/shard_map/all_to_all | solution.py:417
  565.5 4.5 all-to-all-start.14
  572.1 3.7 weight_grad.10
  575.8 7.3 %weight_grad.11 = bf16[512,2048]{1,0:T(8,128)(2,1)} custom-call(s32[1]{0:T(128)} %bitcast.84.part_ref, bf16[576,1024]{1,0:T(8,128)(2,1)} %get-tuple-element.307.act_ref.refs_0_, bf16[576,1024]{1,0:T(8,128)(2,1)} %get-tuple-element.308.act_ref.refs_1_, bf16[576,2048]{1,0:T(8,128)(2,1)} %get-tuple-element.287.refs_2_, bf16[576,2048]{1,0:T(8,128)(2,1)} %get-tuple-element.288.refs_3_), custom_call_target="tpu_custom_call" | custom-call | flops 4831838208 | bytes 10092544 | tf_op jit(solution)/shard_map/weight_grad/pallas_call | solution.py:358
  585.7 6.0 collective-permute-done.30
  594.4 4.3 weight_grad.12
  598.7 3.9 all-to-all-start.15
  602.5 11.0 %weight_grad.13 = bf16[1024,2048]{1,0:T(8,128)(2,1)} custom-call(s32[1]{0:T(128)} %bitcast.84.part_ref, bf16[576,2048]{1,0:T(8,128)(2,1)} %bitcast.55.rows_ref.refs_0_, bf16[576,2048]{1,0:T(8,128)(2,1)} %bitcast.59.rows_ref.refs_1_, bf16[576,1024]{1,0:T(8,128)(2,1)} %get-tuple-element.300.refs_2_, bf16[576,1024]{1,0:T(8,128)(2,1)} %get-tuple-element.303.refs_3_, ...), custom_call_target="tpu_custom_call" | custom-call | flops 9663676416 | bytes 15466496 | tf_op jit(solution)/shard_map/weight_grad/pallas_call | solution.py:358
  617.7 8.0 %weight_grad.14 = f32[512,2048]{1,0:T(8,128)} custom-call(s32[1]{0:T(128)} %bitcast.89.part_ref, bf16[576,1024]{1,0:T(8,128)(2,1)} %get-tuple-element.307.act_ref.refs_0_, bf16[576,1024]{1,0:T(8,128)(2,1)} %get-tuple-element.308.act_ref.refs_1_, bf16[576,2048]{1,0:T(8,128)(2,1)} %get-tuple-element.287.refs_2_, bf16[576,2048]{1,0:T(8,128)(2,1)} %get-tuple-element.288.refs_3_, ...), custom_call_target="tpu_custom_call" | custom-call | flops 4831838208 | bytes 10092544 | tf_op jit(solution)/shard_map/weight_grad/pallas_call | solution.py:358
  630.1 3.7 collective-permute-start.34
  637.2 3.3 copy.109
  644.4 4.2 all-to-all-start.16
  656.3 3.5 all-to-all-start.17
  661.5 12.1 %weight_grad.15 = f32[1024,2048]{1,0:T(8,128)} custom-call(s32[1]{0:T(128)} %bitcast.89.part_ref, bf16[576,2048]{1,0:T(8,128)(2,1)} %bitcast.55.rows_ref.refs_0_, bf16[576,2048]{1,0:T(8,128)(2,1)} %bitcast.59.rows_ref.refs_1_, bf16[576,1024]{1,0:T(8,128)(2,1)} %get-tuple-element.300.refs_2_, bf16[576,1024]{1,0:T(8,128)(2,1)} %get-tuple-element.303.refs_3_, ...), custom_call_target="tpu_custom_call" | custom-call | flops 9663676416 | bytes 15466496 | tf_op jit(solution)/shard_map/weight_grad/pallas_call | solution.py:358
  673.6 14.0 %all-to-all-done.17 = bf16[4,72,2048]{2,1,0:T(8,128)(2,1)S(1)} async-done(((bf16[4,72,2048]{2,1,0:T(8,128)(2,1)}), bf16[4,72,2048]{2,1,0:T(8,128)(2,1)S(1)}, u32[]{:S(2)}, u32[]{:S(2)}) %all-to-all-start.17) | async-done | bytes 1179680 | tf_op jit(solution)/shard_map/all_to_all | solution.py:957
  693.1 3.5 all-to-all-start.18
  699.3 7.7 %all-to-all-done.18 = bf16[4,64,1536]{2,1,0:T(8,128)(2,1)S(1)} async-done(((bf16[4,64,1536]{2,1,0:T(8,128)(2,1)}), bf16[4,64,1536]{2,1,0:T(8,128)(2,1)S(1)}, u32[]{:S(2)}, u32[]{:S(2)}) %all-to-all-start.18) | async-done | bytes 786464 | tf_op jit(solution)/shard_map/all_to_all | solution.py:417
  (568 shorter events, 214.3 us)
Async XLA Ops:
  0.6 33.9 %collective-permute-start = (bf16[64,2048]{1,0:T(8,128)(2,1)}, bf16[64,2048]{1,0:T(8,128)(2,1)}, u32[]{:S(2)}, u32[]{:S(2)}) collective-permute-start(bf16[64,2048]{1,0:T(8,128)(2,1)} %param.17), channel_id=1, source_target_pairs={{0,1},{1,2},{2,3},{3,0},{4,5},{5,6},{6,7},{7,4},{8,9},{9,10},{10,1... | collective-permute-start | bytes 786440 | tf_op jit(solution)/shard_map/ppermute | solution.py:423
  3.7 30.8 %collective-permute-start.1 = (bf16[64,2048]{1,0:T(8,128)(2,1)}, bf16[64,2048]{1,0:T(8,128)(2,1)}, u32[]{:S(2)}, u32[]{:S(2)}) collective-permute-start(bf16[64,2048]{1,0:T(8,128)(2,1)} %param.17), channel_id=1, source_target_pairs={{0,2},{1,3},{2,0},{3,1},{4,6},{5,7},{6,4},{7,5},{8,10},{9,11},{10,... | collective-permute-start | bytes 786440 | tf_op jit(solution)/shard_map/ppermute | solution.py:423
  6.3 28.2 %collective-permute-start.2 = (bf16[64,2048]{1,0:T(8,128)(2,1)}, bf16[64,2048]{1,0:T(8,128)(2,1)}, u32[]{:S(2)}, u32[]{:S(2)}) collective-permute-start(bf16[64,2048]{1,0:T(8,128)(2,1)} %param.17), channel_id=1, source_target_pairs={{0,3},{1,0},{2,1},{3,2},{4,7},{5,4},{6,5},{7,6},{8,11},{9,8},{10,9... | collective-permute-start | bytes 786440 | tf_op jit(solution)/shard_map/ppermute | solution.py:423
  13.6 24.0 %all-to-all-start = ((bf16[4,64,1664]{2,1,0:T(8,128)(2,1)}), bf16[4,64,1664]{2,1,0:T(8,128)(2,1)}, u32[]{:S(2)}, u32[]{:S(2)}) async-start(bf16[4,64,1664]{2,1,0:T(8,128)(2,1)} %pack.1), calls=%async_computation | async-start | bytes 1703936 | tf_op jit(solution)/shard_map/all_to_all | solution.py:417
  37.6 95.5 %collective-permute-start.3 = (bf16[4,64,1664]{2,1,0:T(8,128)(2,1)}, bf16[4,64,1664]{2,1,0:T(8,128)(2,1)}, u32[]{:S(2)}, u32[]{:S(2)}) collective-permute-start(bf16[4,64,1664]{2,1,0:T(8,128)(2,1)} %all-to-all-done.refs_0_), channel_id=1, source_target_pairs={{0,1},{1,2},{2,3},{3,0},{4,5},{5,6},{6,7},{7,4},{8,9},{9,10},{10,1... | collective-permute-start | bytes 2555912 | tf_op jit(solution)/shard_map/ppermute | solution.py:423
  38.4 94.8 %collective-permute-start.4 = (bf16[4,64,1664]{2,1,0:T(8,128)(2,1)}, bf16[4,64,1664]{2,1,0:T(8,128)(2,1)}, u32[]{:S(2)}, u32[]{:S(2)}) collective-permute-start(bf16[4,64,1664]{2,1,0:T(8,128)(2,1)} %all-to-all-done.refs_0_), channel_id=1, source_target_pairs={{0,2},{1,3},{2,0},{3,1},{4,6},{5,7},{6,4},{7,5},{8,10},{9,11},{10,... | collective-permute-start | bytes 2555912 | tf_op jit(solution)/shard_map/ppermute | solution.py:423
  38.7 94.4 %collective-permute-start.5 = (bf16[4,64,1664]{2,1,0:T(8,128)(2,1)}, bf16[4,64,1664]{2,1,0:T(8,128)(2,1)}, u32[]{:S(2)}, u32[]{:S(2)}) collective-permute-start(bf16[4,64,1664]{2,1,0:T(8,128)(2,1)} %all-to-all-done.refs_0_), channel_id=1, source_target_pairs={{0,3},{1,0},{2,1},{3,2},{4,7},{5,4},{6,5},{7,6},{8,11},{9,8},{10,9... | collective-permute-start | bytes 2555912 | tf_op jit(solution)/shard_map/ppermute | solution.py:423
  41.5 99.0 %collective-permute-start.6 = (bf16[4,64,1664]{2,1,0:T(8,128)(2,1)}, bf16[4,64,1664]{2,1,0:T(8,128)(2,1)}, u32[]{:S(2)}, u32[]{:S(2)}) collective-permute-start(bf16[4,64,1664]{2,1,0:T(8,128)(2,1)} %all-to-all-done.refs_0_), channel_id=1, source_target_pairs={{0,16},{16,0},{1,17},{17,1},{2,18},{18,2},{3,19},{19,3},{4,20},{20... | collective-permute-start | bytes 2555912 | tf_op jit(solution)/shard_map/ppermute | solution.py:426
  44.1 53.4 %all-to-all-start.1 = ((bf16[4,4,64,2048]{3,2,1,0:T(8,128)(2,1)}), bf16[4,4,64,2048]{3,2,1,0:T(8,128)(2,1)}, u32[]{:S(2)}, u32[]{:S(2)}) async-start(bf16[4,4,64,2048]{3,2,1,0:T(8,128)(2,1)} %broadcast_in_dim.54), calls=%async_computation.1 | async-start | bytes 8388608 | tf_op jit(solution)/shard_map/all_to_all | solution.py:417
  48.9 48.6 %copy-start.45 = (bf16[136,2048]{1,0:T(8,128)(2,1)S(1)}, bf16[136,2048]{1,0:T(8,128)(2,1)}, u32[]{:S(2)}) copy-start(bf16[136,2048]{1,0:T(8,128)(2,1)} %reshape.436) | copy-start | bytes 1671172
  99.1 31.1 %all-to-all-start.2 = ((bf16[4,136,2048]{2,1,0:T(8,128)(2,1)}), bf16[4,136,2048]{2,1,0:T(8,128)(2,1)}, u32[]{:S(2)}, u32[]{:S(2)}) async-start(bf16[4,136,2048]{2,1,0:T(8,128)(2,1)} %broadcast_in_dim.55), calls=%async_computation.2 | async-start | bytes 4456448 | tf_op jit(solution)/shard_map/all_to_all | solution.py:417
  105.0 29.0 %copy-start.96 = (s32[8]{0:T(128)S(1)}, s32[8]{0:T(128)}, u32[]{:S(2)}) copy-start(s32[8]{0:T(128)} %copy-done.95) | copy-start | bytes 100
  105.0 29.0 %copy-start.109 = (s32[8]{0:T(128)S(1)}, s32[8]{0:T(128)}, u32[]{:S(2)}) copy-start(s32[8]{0:T(128)} %get-tuple-element.372) | copy-start | bytes 100
  105.0 29.1 %copy-start.117 = (f32[64]{0:T(128)S(1)}, f32[64]{0:T(128)}, u32[]{:S(2)}) copy-start(f32[64]{0:T(128)} %multiply_power_fusion) | copy-start | bytes 772
  133.2 7.3 %collective-permute-start.7 = (bf16[4,64,1664]{2,1,0:T(8,128)(2,1)}, bf16[4,64,1664]{2,1,0:T(8,128)(2,1)S(1)}, u32[]{:S(2)}, u32[]{:S(2)}) collective-permute-start(bf16[4,64,1664]{2,1,0:T(8,128)(2,1)} %collective-permute-done.3.refs_1_), channel_id=1, source_target_pairs={{0,16},{16,0},{1,17},{17,1},{2,18},{18,2},{3,19},{19,3},{4,20},{20... | collective-permute-start | bytes 2555912 | tf_op jit(solution)/shard_map/ppermute | solution.py:426
  133.2 7.3 %collective-permute-start.8 = (bf16[4,64,1664]{2,1,0:T(8,128)(2,1)}, bf16[4,64,1664]{2,1,0:T(8,128)(2,1)}, u32[]{:S(2)}, u32[]{:S(2)}) collective-permute-start(bf16[4,64,1664]{2,1,0:T(8,128)(2,1)} %collective-permute-done.4.refs_2_), channel_id=1, source_target_pairs={{0,16},{16,0},{1,17},{17,1},{2,18},{18,2},{3,19},{19,3},{4,20},{20... | collective-permute-start | bytes 2555912 | tf_op jit(solution)/shard_map/ppermute | solution.py:426
  133.7 6.8 collective-permute-start.9
  136.0 52.6 %copy-start = (f32[544,544]{1,0:T(8,128)}, f32[544,544]{1,0:T(8,128)S(1)}, u32[]{:S(2)}) copy-start(f32[544,544]{1,0:T(8,128)S(1)} %fusion.22.pair_ref) | copy-start | bytes 3551236
  136.0 64.6 %all-to-all-start.3 = ((bf16[4,1,72,2048]{3,2,1,0:T(8,128)(2,1)}), bf16[4,1,72,2048]{3,2,1,0:T(8,128)(2,1)}, u32[]{:S(2)}, u32[]{:S(2)}) async-start(bf16[4,1,72,2048]{3,2,1,0:T(8,128)(2,1)} %bitcast.36), calls=%async_computation.3 | async-start | bytes 2359296 | tf_op jit(solution)/shard_map/all_to_all | solution.py:417
  165.2 55.3 %collective-permute-start.12 = (bf16[136,2048]{1,0:T(8,128)(2,1)}, bf16[136,2048]{1,0:T(8,128)(2,1)}, u32[]{:S(2)}, u32[]{:S(2)}) collective-permute-start(bf16[136,2048]{1,0:T(8,128)(2,1)} %pad_maximum_fusion.4), channel_id=1, source_target_pairs={{0,1},{1,2},{2,3},{3,0},{4,5},{5,6},{6,7},{7,4},{8,9},{9,10},{10,1... | collective-permute-start | bytes 1671176 | tf_op jit(solution)/shard_map/ppermute | solution.py:423
  165.8 54.7 %collective-permute-start.13 = (bf16[136,2048]{1,0:T(8,128)(2,1)}, bf16[136,2048]{1,0:T(8,128)(2,1)}, u32[]{:S(2)}, u32[]{:S(2)}) collective-permute-start(bf16[136,2048]{1,0:T(8,128)(2,1)} %pad_maximum_fusion.4), channel_id=1, source_target_pairs={{0,2},{1,3},{2,0},{3,1},{4,6},{5,7},{6,4},{7,5},{8,10},{9,11},{10,... | collective-permute-start | bytes 1671176 | tf_op jit(solution)/shard_map/ppermute | solution.py:423
  167.3 53.1 %collective-permute-start.14 = (bf16[136,2048]{1,0:T(8,128)(2,1)}, bf16[136,2048]{1,0:T(8,128)(2,1)}, u32[]{:S(2)}, u32[]{:S(2)}) collective-permute-start(bf16[136,2048]{1,0:T(8,128)(2,1)} %pad_maximum_fusion.4), channel_id=1, source_target_pairs={{0,3},{1,0},{2,1},{3,2},{4,7},{5,4},{6,5},{7,6},{8,11},{9,8},{10,9... | collective-permute-start | bytes 1671176 | tf_op jit(solution)/shard_map/ppermute | solution.py:423
  170.2 9.2 %collective-permute-start.10 = (f32[2,544]{0,1:T(8,128)S(1)}, f32[2,544]{0,1:T(8,128)S(1)}, u32[]{:S(2)}, u32[]{:S(2)}) collective-permute-start(f32[2,544]{0,1:T(8,128)S(1)} %copy.103), channel_id=1, source_target_pairs={{0,4},{4,0},{8,12},{12,8},{1,5},{5,1},{9,13},{13,9},{2,6},{6,2},{1... | collective-permute-start | bytes 13064 | tf_op jit(solution)/shard_map/ppermute | solution.py:414
  179.5 7.7 %collective-permute-start.11 = (f32[2,544]{0,1:T(8,128)S(1)}, f32[2,544]{0,1:T(8,128)S(1)}, u32[]{:S(2)}, u32[]{:S(2)}) collective-permute-start(f32[2,544]{0,1:T(8,128)S(1)} %add.319), channel_id=1, source_target_pairs={{0,8},{4,12},{8,0},{12,4},{1,9},{5,13},{9,1},{13,5},{2,10},{6,14},... | collective-permute-start | bytes 13064 | tf_op jit(solution)/shard_map/ppermute | solution.py:414
  187.2 48.6 %collective-permute-start.15 = (bf16[4,4,64,2048]{3,2,1,0:T(8,128)(2,1)}, bf16[4,4,64,2048]{3,2,1,0:T(8,128)(2,1)}, u32[]{:S(2)}, u32[]{:S(2)}) collective-permute-start(bf16[4,4,64,2048]{3,2,1,0:T(8,128)(2,1)} %all-to-all-done.1), channel_id=1, source_target_pairs={{0,16},{16,0},{1,17},{17,1},{2,18},{18,2},{3,19},{19,3},{4,20},{20... | collective-permute-start | bytes 12582920 | tf_op jit(solution)/shard_map/ppermute | solution.py:426
  200.6 13.5 %all-to-all-start.4 = ((bf16[4,136,512]{2,1,0:T(8,128)(2,1)}), bf16[4,136,512]{2,1,0:T(8,128)(2,1)}, u32[]{:S(2)}, u32[]{:S(2)}) async-start(bf16[4,136,512]{2,1,0:T(8,128)(2,1)} %bitcast.37), calls=%async_computation.4 | async-start | bytes 1114112 | tf_op jit(solution)/shard_map/all_to_all | solution.py:417
  225.7 45.2 %all-to-all-start.5 = ((bf16[4,3,72,2048]{3,2,1,0:T(8,128)(2,1)}), bf16[4,3,72,2048]{3,2,1,0:T(8,128)(2,1)}, u32[]{:S(2)}, u32[]{:S(2)}) async-start(bf16[4,3,72,2048]{3,2,1,0:T(8,128)(2,1)} %bitcast.300), calls=%async_computation.5 | async-start | bytes 7077888 | tf_op jit(solution)/shard_map/all_to_all | solution.py:417
  241.1 32.0 %collective-permute-start.16 = (bf16[136,2048]{1,0:T(8,128)(2,1)}, bf16[136,2048]{1,0:T(8,128)(2,1)}, u32[]{:S(2)}, u32[]{:S(2)}) collective-permute-start(bf16[136,2048]{1,0:T(8,128)(2,1)} %multiply_convert_fusion), channel_id=1, source_target_pairs={{0,1},{1,2},{2,3},{3,0},{4,5},{5,6},{6,7},{7,4},{8,9},{9,10},{10,1... | collective-permute-start | bytes 1671176 | tf_op jit(solution)/shard_map/ppermute | solution.py:423
  241.3 29.6 %copy-start.21 = (bf16[2,4,4,64,128]{4,3,2,1,0:T(8,128)(2,1)S(1)}, bf16[2,4,4,64,128]{4,3,2,1,0:T(8,128)(2,1)}, u32[]{:S(2)}) copy-start(bf16[2,4,4,64,128]{4,3,2,1,0:T(8,128)(2,1)} %copy-done.20) | copy-start | bytes 1572868
  241.3 33.9 %copy-start.58 = (bf16[4,2,72,272]{3,2,1,0:T(8,128)(2,1)S(1)}, bf16[4,2,72,272]{3,2,1,0:T(8,128)(2,1)}, u32[]{:S(2)}) copy-start(bf16[4,2,72,272]{3,2,1,0:T(8,128)(2,1)} %fusion.47) | copy-start | bytes 940036
  273.1 26.1 %collective-permute-start.17 = (bf16[136,2048]{1,0:T(8,128)(2,1)}, bf16[136,2048]{1,0:T(8,128)(2,1)}, u32[]{:S(2)}, u32[]{:S(2)}) collective-permute-start(bf16[136,2048]{1,0:T(8,128)(2,1)} %multiply_convert_fusion), channel_id=1, source_target_pairs={{0,2},{1,3},{2,0},{3,1},{4,6},{5,7},{6,4},{7,5},{8,10},{9,11},{10,... | collective-permute-start | bytes 1671176 | tf_op jit(solution)/shard_map/ppermute | solution.py:423
  274.0 25.5 %collective-permute-start.18 = (bf16[136,2048]{1,0:T(8,128)(2,1)}, bf16[136,2048]{1,0:T(8,128)(2,1)}, u32[]{:S(2)}, u32[]{:S(2)}) collective-permute-start(bf16[136,2048]{1,0:T(8,128)(2,1)} %multiply_convert_fusion), channel_id=1, source_target_pairs={{0,3},{1,0},{2,1},{3,2},{4,7},{5,4},{6,5},{7,6},{8,11},{9,8},{10,9... | collective-permute-start | bytes 1671176 | tf_op jit(solution)/shard_map/ppermute | solution.py:423
  279.3 31.2 %all-to-all-start.6 = ((bf16[4,2,72,2048]{3,2,1,0:T(8,128)(2,1)}), bf16[4,2,72,2048]{3,2,1,0:T(8,128)(2,1)}, u32[]{:S(2)}, u32[]{:S(2)}) async-start(bf16[4,2,72,2048]{3,2,1,0:T(8,128)(2,1)} %bitcast.302), calls=%async_computation.6 | async-start | bytes 4718592 | tf_op jit(solution)/shard_map/all_to_all | solution.py:417
  314.5 31.7 %all-to-all-start.7 = ((bf16[4,2,72,2048]{3,2,1,0:T(8,128)(2,1)}), bf16[4,2,72,2048]{3,2,1,0:T(8,128)(2,1)}, u32[]{:S(2)}, u32[]{:S(2)}) async-start(bf16[4,2,72,2048]{3,2,1,0:T(8,128)(2,1)} %bitcast.303), calls=%async_computation.7 | async-start | bytes 4718592 | tf_op jit(solution)/shard_map/all_to_all | solution.py:417
  346.2 29.2 %all-to-all-start.8 = ((bf16[4,72,2176]{2,1,0:T(8,128)(2,1)}), bf16[4,72,2176]{2,1,0:T(8,128)(2,1)}, u32[]{:S(2)}, u32[]{:S(2)}) async-start(bf16[4,72,2176]{2,1,0:T(8,128)(2,1)} %get-tuple-element.218), calls=%async_computation.8 | async-start | bytes 2506752 | tf_op jit(solution)/shard_map/all_to_all | solution.py:417
  378.1 19.6 %all-to-all-start.9 = ((bf16[4,72,2176]{2,1,0:T(8,128)(2,1)}), bf16[4,72,2176]{2,1,0:T(8,128)(2,1)}, u32[]{:S(2)}, u32[]{:S(2)}) async-start(bf16[4,72,2176]{2,1,0:T(8,128)(2,1)} %get-tuple-element.226), calls=%async_computation.9 | async-start | bytes 2506752 | tf_op jit(solution)/shard_map/all_to_all | solution.py:417
  382.4 66.8 %collective-permute-start.19 = (bf16[136,2176]{1,0:T(8,128)(2,1)}, bf16[136,2176]{1,0:T(8,128)(2,1)}, u32[]{:S(2)}, u32[]{:S(2)}) collective-permute-start(bf16[136,2176]{1,0:T(8,128)(2,1)} %fusion.2), channel_id=1, source_target_pairs={{0,3},{1,0},{2,1},{3,2},{4,7},{5,4},{6,5},{7,6},{8,11},{9,8},{10,9... | collective-permute-start | bytes 1775624 | tf_op jit(solution)/shard_map/ppermute | solution.py:423
  400.5 48.7 %collective-permute-start.20 = (bf16[136,2176]{1,0:T(8,128)(2,1)}, bf16[136,2176]{1,0:T(8,128)(2,1)}, u32[]{:S(2)}, u32[]{:S(2)}) collective-permute-start(bf16[136,2176]{1,0:T(8,128)(2,1)} %fusion.3), channel_id=1, source_target_pairs={{0,2},{1,3},{2,0},{3,1},{4,6},{5,7},{6,4},{7,5},{8,10},{9,11},{10,... | collective-permute-start | bytes 1775624 | tf_op jit(solution)/shard_map/ppermute | solution.py:423
  401.6 19.3 %all-to-all-start.10 = ((bf16[4,72,2176]{2,1,0:T(8,128)(2,1)}), bf16[4,72,2176]{2,1,0:T(8,128)(2,1)}, u32[]{:S(2)}, u32[]{:S(2)}) async-start(bf16[4,72,2176]{2,1,0:T(8,128)(2,1)} %get-tuple-element.236), calls=%async_computation.10 | async-start | bytes 2506752 | tf_op jit(solution)/shard_map/all_to_all | solution.py:417
  423.7 25.5 %collective-permute-start.21 = (bf16[136,2176]{1,0:T(8,128)(2,1)}, bf16[136,2176]{1,0:T(8,128)(2,1)}, u32[]{:S(2)}, u32[]{:S(2)}) collective-permute-start(bf16[136,2176]{1,0:T(8,128)(2,1)} %fusion.4), channel_id=1, source_target_pairs={{0,1},{1,2},{2,3},{3,0},{4,5},{5,6},{6,7},{7,4},{8,9},{9,10},{10,1... | collective-permute-start | bytes 1775624 | tf_op jit(solution)/shard_map/ppermute | solution.py:423
  425.4 19.5 %all-to-all-start.11 = ((bf16[4,72,2176]{2,1,0:T(8,128)(2,1)}), bf16[4,72,2176]{2,1,0:T(8,128)(2,1)}, u32[]{:S(2)}, u32[]{:S(2)}) async-start(bf16[4,72,2176]{2,1,0:T(8,128)(2,1)} %get-tuple-element.244), calls=%async_computation.11 | async-start | bytes 2506752 | tf_op jit(solution)/shard_map/all_to_all | solution.py:417
  462.4 6.0 collective-permute-start.22
  465.2 6.8 collective-permute-start.23
  465.8 6.2 collective-permute-start.24
  472.1 42.3 %all-to-all-start.12 = ((bf16[4,2,72,2048]{3,2,1,0:T(8,128)(2,1)}), bf16[4,2,72,2048]{3,2,1,0:T(8,128)(2,1)}, u32[]{:S(2)}, u32[]{:S(2)}) async-start(bf16[4,2,72,2048]{3,2,1,0:T(8,128)(2,1)} %bitcast.301), calls=%async_computation.12 | async-start | bytes 4718592 | tf_op jit(solution)/shard_map/all_to_all | solution.py:417
  493.7 14.0 %collective-permute-start.25 = (f32[2,544]{0,1:T(8,128)S(1)}, f32[2,544]{0,1:T(8,128)S(1)}, u32[]{:S(2)}, u32[]{:S(2)}) collective-permute-start(f32[2,544]{0,1:T(8,128)S(1)} %copy.108), channel_id=1, source_target_pairs={{0,4},{4,0},{8,12},{12,8},{1,5},{5,1},{9,13},{13,9},{2,6},{6,2},{1... | collective-permute-start | bytes 13064 | tf_op jit(solution)/shard_map/ppermute | solution.py:414
  507.7 6.6 collective-permute-start.26
  529.7 18.2 %collective-permute-start.29 = (bf16[1024,1536]{1,0:T(8,128)(2,1)}, bf16[1024,1536]{1,0:T(8,128)(2,1)}, u32[]{:S(2)}, u32[]{:S(2)}) collective-permute-start(bf16[1024,1536]{1,0:T(8,128)(2,1)} %weight_grad.8), channel_id=1, source_target_pairs={{0,16},{16,0},{1,17},{17,1},{2,18},{18,2},{3,19},{19,3},{4,20},{20... | collective-permute-start | bytes 9437192 | tf_op jit(solution)/shard_map/ppermute | solution.py:426
  529.7 42.4 %collective-permute-start.27 = (bf16[136,2048]{1,0:T(8,128)(2,1)}, bf16[136,2048]{1,0:T(8,128)(2,1)}, u32[]{:S(2)}, u32[]{:S(2)}) collective-permute-start(bf16[136,2048]{1,0:T(8,128)(2,1)} %get-tuple-element.344), channel_id=1, source_target_pairs={{0,2},{1,3},{2,0},{3,1},{4,6},{5,7},{6,4},{7,5},{8,10},{9,11},{10,... | collective-permute-start | bytes 1671176 | tf_op jit(solution)/shard_map/ppermute | solution.py:423
  532.1 40.0 %collective-permute-start.28 = (bf16[136,2048]{1,0:T(8,128)(2,1)}, bf16[136,2048]{1,0:T(8,128)(2,1)}, u32[]{:S(2)}, u32[]{:S(2)}) collective-permute-start(bf16[136,2048]{1,0:T(8,128)(2,1)} %get-tuple-element.343), channel_id=1, source_target_pairs={{0,1},{1,2},{2,3},{3,0},{4,5},{5,6},{6,7},{7,4},{8,9},{9,10},{10,1... | collective-permute-start | bytes 1671176 | tf_op jit(solution)/shard_map/ppermute | solution.py:423
  534.0 31.4 %all-to-all-start.13 = ((bf16[4,136,2048]{2,1,0:T(8,128)(2,1)}), bf16[4,136,2048]{2,1,0:T(8,128)(2,1)}, u32[]{:S(2)}, u32[]{:S(2)}) async-start(bf16[4,136,2048]{2,1,0:T(8,128)(2,1)} %broadcast_in_dim.62), calls=%async_computation.13 | async-start | bytes 4456448 | tf_op jit(solution)/shard_map/all_to_all | solution.py:417
  565.5 33.2 %all-to-all-start.14 = ((bf16[4,2,72,2048]{3,2,1,0:T(8,128)(2,1)}), bf16[4,2,72,2048]{3,2,1,0:T(8,128)(2,1)}, u32[]{:S(2)}, u32[]{:S(2)}) async-start(bf16[4,2,72,2048]{3,2,1,0:T(8,128)(2,1)} %bitcast.62), calls=%async_computation.14 | async-start | bytes 4718592 | tf_op jit(solution)/shard_map/all_to_all | solution.py:417
  571.3 20.4 %collective-permute-start.30 = (bf16[256,1536]{1,0:T(8,128)(2,1)S(1)}, bf16[256,1536]{1,0:T(8,128)(2,1)S(1)}, u32[]{:S(2)}, u32[]{:S(2)}) collective-permute-start(bf16[256,1536]{1,0:T(8,128)(2,1)S(1)} %copy-done.56), channel_id=1, source_target_pairs={{0,1},{1,2},{2,3},{3,0},{4,5},{5,6},{6,7},{7,4},{8,9},{9,10},{10,1... | collective-permute-start | bytes 2359304 | tf_op jit(solution)/shard_map/ppermute | solution.py:423
  575.8 17.6 %collective-permute-start.32 = (bf16[256,2048]{1,0:T(8,128)(2,1)}, bf16[256,2048]{1,0:T(8,128)(2,1)S(1)}, u32[]{:S(2)}, u32[]{:S(2)}) collective-permute-start(bf16[256,2048]{1,0:T(8,128)(2,1)} %weight_grad.10), channel_id=1, source_target_pairs={{0,16},{16,0},{1,17},{17,1},{2,18},{18,2},{3,19},{19,3},{4,20},{20... | collective-permute-start | bytes 3145736 | tf_op jit(solution)/shard_map/ppermute | solution.py:426
  583.1 34.6 %collective-permute-start.33 = (bf16[512,2048]{1,0:T(8,128)(2,1)}, bf16[512,2048]{1,0:T(8,128)(2,1)}, u32[]{:S(2)}, u32[]{:S(2)}) collective-permute-start(bf16[512,2048]{1,0:T(8,128)(2,1)} %weight_grad.11), channel_id=1, source_target_pairs={{0,16},{16,0},{1,17},{17,1},{2,18},{18,2},{3,19},{19,3},{4,20},{20... | collective-permute-start | bytes 6291464 | tf_op jit(solution)/shard_map/ppermute | solution.py:426
  593.3 21.4 %collective-permute-start.31 = (bf16[256,1536]{1,0:T(8,128)(2,1)S(1)}, bf16[256,1536]{1,0:T(8,128)(2,1)}, u32[]{:S(2)}, u32[]{:S(2)}) collective-permute-start(bf16[256,1536]{1,0:T(8,128)(2,1)S(1)} %fusion.20), channel_id=1, source_target_pairs={{0,1},{1,2},{2,3},{3,0},{4,5},{5,6},{6,7},{7,4},{8,9},{9,10},{10,1... | collective-permute-start | bytes 2359304 | tf_op jit(solution)/shard_map/ppermute | solution.py:423
  598.7 35.1 %all-to-all-start.15 = ((bf16[4,136,2048]{2,1,0:T(8,128)(2,1)}), bf16[4,136,2048]{2,1,0:T(8,128)(2,1)S(1)}, u32[]{:S(2)}, u32[]{:S(2)}) async-start(bf16[4,136,2048]{2,1,0:T(8,128)(2,1)} %bitcast.304), calls=%async_computation.15 | async-start | bytes 4456448 | tf_op jit(solution)/shard_map/all_to_all | solution.py:417
  614.7 46.9 %collective-permute-start.36 = (bf16[1024,2048]{1,0:T(8,128)(2,1)}, bf16[1024,2048]{1,0:T(8,128)(2,1)}, u32[]{:S(2)}, u32[]{:S(2)}) collective-permute-start(bf16[1024,2048]{1,0:T(8,128)(2,1)} %weight_grad.13), channel_id=1, source_target_pairs={{0,16},{16,0},{1,17},{17,1},{2,18},{18,2},{3,19},{19,3},{4,20},{20... | collective-permute-start | bytes 12582920 | tf_op jit(solution)/shard_map/ppermute | solution.py:426
  617.4 73.1 %collective-permute-start.37 = (bf16[256,1536]{1,0:T(8,128)(2,1)}, bf16[256,1536]{1,0:T(8,128)(2,1)}, u32[]{:S(2)}, u32[]{:S(2)}) collective-permute-start(bf16[256,1536]{1,0:T(8,128)(2,1)} %fusion.19), channel_id=1, source_target_pairs={{0,1},{1,2},{2,3},{3,0},{4,5},{5,6},{6,7},{7,4},{8,9},{9,10},{10,1... | collective-permute-start | bytes 2359304 | tf_op jit(solution)/shard_map/ppermute | solution.py:423
  630.1 58.5 %collective-permute-start.34 = (bf16[136,2048]{1,0:T(8,128)(2,1)}, bf16[136,2048]{1,0:T(8,128)(2,1)}, u32[]{:S(2)}, u32[]{:S(2)}) collective-permute-start(bf16[136,2048]{1,0:T(8,128)(2,1)} %slice.584), channel_id=1, source_target_pairs={{0,3},{1,0},{2,1},{3,2},{4,7},{5,4},{6,5},{7,6},{8,11},{9,8},{10,9... | collective-permute-start | bytes 1671176 | tf_op jit(solution)/shard_map/ppermute | solution.py:423
  641.6 1.9 collective-permute-start.35
  644.4 9.1 %all-to-all-start.16 = ((f32[4,1,5120]{2,1,0:T(1,128)}), f32[4,1,5120]{2,1,0:T(1,128)S(1)}, u32[]{:S(2)}, u32[]{:S(2)}) async-start(f32[4,1,5120]{2,1,0:T(1,128)} %reshape.496), calls=%async_computation.16 | async-start | bytes 163840 | tf_op jit(solution)/shard_map/all_to_all | solution.py:417
  656.3 31.3 %all-to-all-start.17 = ((bf16[4,72,2048]{2,1,0:T(8,128)(2,1)}), bf16[4,72,2048]{2,1,0:T(8,128)(2,1)S(1)}, u32[]{:S(2)}, u32[]{:S(2)}) async-start(bf16[4,72,2048]{2,1,0:T(8,128)(2,1)} %pad_maximum_fusion.1), calls=%async_computation.17 | async-start | bytes 2359296 | tf_op jit(solution)/shard_map/all_to_all | solution.py:957
  693.1 13.8 %all-to-all-start.18 = ((bf16[4,64,1536]{2,1,0:T(8,128)(2,1)}), bf16[4,64,1536]{2,1,0:T(8,128)(2,1)S(1)}, u32[]{:S(2)}, u32[]{:S(2)}) async-start(bf16[4,64,1536]{2,1,0:T(8,128)(2,1)} %bitcast.114), calls=%async_computation.18 | async-start | bytes 1572864 | tf_op jit(solution)/shard_map/all_to_all | solution.py:417
  (113 other events, 812.0 us)

commit v5 on v4

--- a/solution.py
+++ b/solution.py
@@ -946,32 +946,27 @@
             lax.dynamic_index_in_dim(part, (late_d + m) % n_dp, 0, keepdims=False), m
         )
     part = total
-    part = jnp.sum(ctx_trade(part), axis=0)
     if head_groups == n_dp:
-        flat = part.reshape(n_exp, count * shard)
-        high = flat.astype(BF16)
-        flat = jnp.concatenate([high, (flat - high.astype(F32)).astype(BF16)], axis=1)
-        lines = -(-2 * count * shard // (8 * D)) * 8
-        flat = jnp.pad(flat, ((0, 0), (0, lines * D - 2 * count * shard)))
-        out_sent = jnp.concatenate([out_dp.astype(BF16), flat.reshape(n_exp, lines, D)], axis=1)
+        out_sent = gate(out_dp.astype(BF16), hidden_trade)
         out_trade = lax.all_to_all(out_sent, "exp", 0, 0, tiled=True)
         out_trade = gate(out_trade, grad_gate_up)
-        grad_out = jnp.sum(out_trade[:, :shard].astype(F32), axis=0)
-        flat = jnp.sum(out_trade[:, shard:].astype(F32), axis=0).reshape(-1)
-        total = (flat[: count * shard] + flat[count * shard : 2 * count * shard]).reshape(
-            count, shard
-        )
+        part = jnp.sum(ctx_trade(gate(part, out_trade)), axis=0)
+        grad_out = jnp.sum(out_trade.astype(F32), axis=0)
     else:
+        part = jnp.sum(ctx_trade(part), axis=0)
         grad_out = lax.psum_scatter(
             dot_at(mixed, attn_grad), ("dp", "ctx", "exp"), scatter_dimension=0, tiled=True
         )
-        total = jnp.sum(lax.all_to_all(part, "exp", 0, 0, tiled=True), axis=0)
+    total = lax.dynamic_index_in_dim(part, z, 0, keepdims=False)
+    for s in range(1, n_exp):
+        piece = lax.dynamic_index_in_dim(part, (z + s) % n_exp, 0, keepdims=False)
+        total = total + exp_shift(piece, s)
     small_sum = total.T
     mix_homes = gate(tuple(mix_homes), grad_out)
     mixture = mix_homes[2] + sum(v.astype(F32) for v in mix_homes[:2] + mix_homes[3:])
     final_rows = (mid_rows + mixture).astype(BF16)
 
-    qkv_exp = gate(ring_arrived, final_rows, small_sum).astype(F32) + ring_part
+    qkv_exp = gate(ring_arrived, final_rows, part).astype(F32) + ring_part
     qkv_exp = qkv_exp.reshape(n_ctx, shard, 3 * width)
     grad_qkv = all_owners(ctx_trade(qkv_exp.astype(BF16)).astype(F32))
 

time: 719 us -> 716 us (level)
    ppermute x21 -> x24, waiting for transfers between devices: 12.9 us -> 16.9 us  [exp_shift(): return lax.ppermute(x, 'exp', [(i, (i + s) % n_exp) for i in range(n_exp)])]
    ppermute x21 -> x24, starting transfers between devices: 30.9 us -> 32.9 us  [exp_shift(): return lax.ppermute(x, 'exp', [(i, (i + s) % n_exp) for i in range(n_exp)])]
    unnamed x279 -> x283, local copies, waits for them, and re-layouts: 24.7 us -> 25.2 us
  transfers between devices with their start and end apart: 57 -> 60, of which waited for: 21 -> 24; matrix products, arithmetic and copies ran while one was open for 21% -> 20% of each run, Pallas kernels for 24% -> 24%
where the time goes in v5:
time: 716 us; the launch traced here: 706 us
  waiting for transfers between devices  209 us (29%)
  Pallas kernels  177 us (25%)
  starting transfers between devices  128 us (18%)
  local copies, waits for them, and re-layouts  77.4 us (11%)
  matrix products  64.6 us (9%)
  other arithmetic  45.7 us (6%)
    all_to_all x18, waiting for transfers between devices, ctx_trade(): return lax.all_to_all(x, 'ctx', 0, 0, tiled=True)  155 us
    all_to_all x18, starting transfers between devices, ctx_trade(): return lax.all_to_all(x, 'ctx', 0, 0, tiled=True)  78.9 us
    pallas_call x8, Pallas kernels, weight_grad(): pl.pallas_call(kernel, grid_spec=pltpu.PrefetchScalarGridSpec(num_scalar_...  60 us
    pallas_call x2, Pallas kernels, expert_rows(): pl.pallas_call(kernel, grid_spec=pltpu.PrefetchScalarGridSpec(num_scalar_...  46.5 us
    ppermute x24, starting transfers between devices, exp_shift(): return lax.ppermute(x, 'exp', [(i, (i + s) % n_exp) for i in range(n_exp)])  32.9 us
    dot_general x12, matrix products, dot(): return jnp.dot(a, b, preferred_element_type=F32)  29.4 us
    unnamed x283, local copies, waits for them, and re-layouts  25.2 us
    pallas_call x19, Pallas kernels, fence(): pl.pallas_call(hand_on, out_shape=jax.ShapeDtypeStruct(mark.shape, mark.d...  25 us
  transfers between devices with their start and end apart: 60, of which 24 were waited for; matrix products, arithmetic and copies ran while one was open for 20% of the time, Pallas kernels for 24%

profile of v5, /device:TPU:0, one launch (start us, length us, event | category | flops | bytes accessed | tf_op | source)
XLA Modules:
  0.0 706.1 jit_solution(14878931788801067050)
XLA Ops:
  0.6 3.1 collective-permute-start
  13.6 4.2 all-to-all-start
  44.1 4.8 all-to-all-start.1
  54.6 42.9 %all-to-all-done.1 = bf16[4,4,64,2048]{3,2,1,0:T(8,128)(2,1)} async-done(((bf16[4,4,64,2048]{3,2,1,0:T(8,128)(2,1)}), bf16[4,4,64,2048]{3,2,1,0:T(8,128)(2,1)}, u32[]{:S(2)}, u32[]{:S(2)}) %all-to-all-start.1) | async-done | bytes 4194336 | tf_op jit(solution)/shard_map/all_to_all | solution.py:417
  99.2 4.5 all-to-all-start.2
  105.0 25.3 %all-to-all-done.2 = bf16[4,136,2048]{2,1,0:T(8,128)(2,1)} async-done(((bf16[4,136,2048]{2,1,0:T(8,128)(2,1)}), bf16[4,136,2048]{2,1,0:T(8,128)(2,1)}, u32[]{:S(2)}, u32[]{:S(2)}) %all-to-all-start.2) | async-done | bytes 2228256 | tf_op jit(solution)/shard_map/all_to_all | solution.py:417
  136.1 4.4 all-to-all-start.3
  141.4 6.3 assemble.1
  156.4 6.5 fusion.89.pq.pk.pv.projected_ref
  181.1 6.1 collective-permute-done.11
  188.6 8.4 %attend.1 = (bf16[544,512]{1,0:T(8,128)(2,1)}, bf16[544,512]{1,0:T(8,128)(2,1)S(1)}, bf16[544,512]{1,0:T(8,128)(2,1)S(1)}, bf16[544,512]{1,0:T(8,128)(2,1)S(1)}, f32[544,512]{1,0:T(8,128)S(1)}) custom-call(f32[544,1536]{1,0:T(8,128)} %copy-done.16, f32[544,1536]{1,0:T(8,128)} %copy-done.16, f32[544,1536]{1,0:T(8,128)} %copy-done.16, f32[544,2]{1,0:T(8,128)S(1)} %bitcast.273, ...), custom_call_target="tpu_custom_call" | custom-call | tf_op jit(solution)/shard_map/attend/pallas_call | solution.py:84
  200.6 4.1 all-to-all-start.4
  206.0 8.1 %all-to-all-done.4 = bf16[4,136,512]{2,1,0:T(8,128)(2,1)} async-done(((bf16[4,136,512]{2,1,0:T(8,128)(2,1)}), bf16[4,136,512]{2,1,0:T(8,128)(2,1)}, u32[]{:S(2)}, u32[]{:S(2)}) %all-to-all-start.4) | async-done | bytes 557088 | tf_op jit(solution)/shard_map/all_to_all | solution.py:417
  220.5 5.2 convolution_convert_fusion
  225.7 4.8 all-to-all-start.5
  232.9 3.0 convolution_add_fusion.1
  235.9 3.2 multiply_reduce_fusion.3
  242.7 28.2 %all-to-all-done.5 = bf16[4,3,72,2048]{3,2,1,0:T(8,128)(2,1)} async-done(((bf16[4,3,72,2048]{3,2,1,0:T(8,128)(2,1)}), bf16[4,3,72,2048]{3,2,1,0:T(8,128)(2,1)}, u32[]{:S(2)}, u32[]{:S(2)}) %all-to-all-start.5) | async-done | bytes 3538976 | tf_op jit(solution)/shard_map/all_to_all | solution.py:417
  275.3 4.0 convolution_convert_fusion.2
  279.3 4.5 all-to-all-start.6
  286.5 3.4 stack.81
  289.9 2.9 pad_maximum_fusion
  292.8 6.5 collective-permute-done.17
  299.7 10.8 %all-to-all-done.6 = bf16[4,2,72,2048]{3,2,1,0:T(8,128)(2,1)} async-done(((bf16[4,2,72,2048]{3,2,1,0:T(8,128)(2,1)}), bf16[4,2,72,2048]{3,2,1,0:T(8,128)(2,1)}, u32[]{:S(2)}, u32[]{:S(2)}) %all-to-all-start.6) | async-done | bytes 2359328 | tf_op jit(solution)/shard_map/all_to_all | solution.py:417
  310.5 4.0 convolution_convert_fusion.1
  314.5 4.5 all-to-all-start.7
  320.3 23.2 %expert.2 = (bf16[4,72,2176]{2,1,0:T(8,128)(2,1)}, bf16[4,72,2176]{2,1,0:T(8,128)(2,1)}, bf16[576,1024]{1,0:T(8,128)(2,1)}, bf16[576,1024]{1,0:T(8,128)(2,1)}, b...) custom-call(s32[1]{0:T(128)} %bitcast.52.expert_ref, bf16[576,2048]{1,0:T(8,128)(2,1)} %bitcast.55.rows_ref.refs_0_, ...), custom_call_target="tpu_custom_call" | custom-call | tf_op jit(solution)/shard_map/expert/pallas_call | solution.py:281
  346.2 4.7 all-to-all-start.8
  352.2 23.2 %expert.3 = (bf16[4,72,2176]{2,1,0:T(8,128)(2,1)}, bf16[4,72,2176]{2,1,0:T(8,128)(2,1)}, bf16[576,1024]{1,0:T(8,128)(2,1)}, bf16[576,1024]{1,0:T(8,128)(2,1)}, b...) custom-call(s32[1]{0:T(128)} %bitcast.52.expert_ref, bf16[576,2048]{1,0:T(8,128)(2,1)} %bitcast.59.rows_ref.refs_1_, ...), custom_call_target="tpu_custom_call" | custom-call | tf_op jit(solution)/shard_map/expert/pallas_call | solution.py:281
  378.2 4.3 all-to-all-start.9
  386.1 7.0 expert_outs.2
  393.1 4.8 all-to-all-done.9
  401.8 4.3 all-to-all-start.10
  407.4 7.0 expert_outs.3
  414.4 6.8 all-to-all-done.10
  425.5 4.5 all-to-all-start.11
  431.3 13.7 %all-to-all-done.11 = bf16[4,72,2176]{2,1,0:T(8,128)(2,1)} async-done(((bf16[4,72,2176]{2,1,0:T(8,128)(2,1)}), bf16[4,72,2176]{2,1,0:T(8,128)(2,1)}, u32[]{:S(2)}, u32[]{:S(2)}) %all-to-all-start.11) | async-done | bytes 1253408 | tf_op jit(solution)/shard_map/all_to_all | solution.py:417
  454.6 3.9 fusion.25
  458.5 3.7 fusion.27
  468.6 3.6 collective-permute-done.23
  472.2 4.5 all-to-all-start.12
  480.2 12.6 %attend_back.1 = (f32[544,512]{1,0:T(8,128)S(1)}, f32[544,512]{1,0:T(8,128)}, bf16[544,512]{1,0:T(8,128)(2,1)S(1)}, f32[2,512]{1,0:T(2,128)S(1)}, f32[544,256]{1,0:T(8,128)S(1)}) custom-call(bf16[544,512]{1,0:T(8,128)(2,1)S(1)} %bitcast.276, bf16[544,512]{1,0:T(8,128)(2,1)S(1)} %copy-done.6, bf16[544,512]{1,0:T(8,128)(2,1)S(1)} %copy-done.8, ...), custom_call_target="tpu_custom_call" | custom-call | tf_op jit(solution)/shard_map/attend_back/pallas_call | solution.py:159
  497.7 10.1 %collective-permute-done.25 = f32[2,544]{0,1:T(8,128)S(1)} collective-permute-done((f32[2,544]{0,1:T(8,128)S(1)}, f32[2,544]{0,1:T(8,128)S(1)}, u32[]{:S(2)}, u32[]{:S(2)}) %collective-permute-start.25) | collective-permute-done | bytes 4384 | tf_op jit(solution)/shard_map/ppermute | solution.py:414
  510.8 3.6 collective-permute-done.26
  523.6 6.1 weight_grad.8
  534.1 4.7 all-to-all-start.13
  540.3 7.6 %convolution_convert_fusion.3 = bf16[544,2048]{1,0:T(8,128)(2,1)} fusion(bf16[544,1536]{1,0:T(8,128)(2,1)S(1)} %copy-done.2, bf16[2048,1536]{1,0:T(8,128)(2,1)} %bitcast.336), kind=kOutput, calls=%fused_computation.15 | convolution fusion | flops 3423666176 | bytes 10190848 | tf_op jit(solution)/shard_map/dot_general | solution.py:49
  547.9 7.4 %weight_grad.9 = f32[1024,1536]{1,0:T(8,128)} custom-call(s32[1]{0:T(128)} %bitcast.18.part_ref, bf16[544,2048]{1,0:T(8,128)(2,1)} %copy-done.23, bf16[544,1536]{1,0:T(8,128)(2,1)} %copy-done.1, bf16[1024,1536]{1,0:T(8,128)(2,1)} %collective-permute-done.29.refs_2_), custom_call_target="tpu_custom_call" | custom-call | flops 3422552064 | bytes 9076736 | tf_op jit(solution)/shard_map/weight_grad/pallas_call | solution.py:358
  557.7 7.9 %all-to-all-done.13 = bf16[4,136,2048]{2,1,0:T(8,128)(2,1)} async-done(((bf16[4,136,2048]{2,1,0:T(8,128)(2,1)}), bf16[4,136,2048]{2,1,0:T(8,128)(2,1)}, u32[]{:S(2)}, u32[]{:S(2)}) %all-to-all-start.13) | async-done | bytes 2228256 | tf_op jit(solution)/shard_map/all_to_all | solution.py:417
  565.6 4.5 all-to-all-start.14
  572.2 3.7 weight_grad.10
  575.9 7.3 %weight_grad.11 = bf16[512,2048]{1,0:T(8,128)(2,1)} custom-call(s32[1]{0:T(128)} %bitcast.84.part_ref, bf16[576,1024]{1,0:T(8,128)(2,1)} %get-tuple-element.309.act_ref.refs_0_, bf16[576,1024]{1,0:T(8,128)(2,1)} %get-tuple-element.310.act_ref.refs_1_, bf16[576,2048]{1,0:T(8,128)(2,1)} %get-tuple-element.289.refs_2_, bf16[576,2048]{1,0:T(8,128)(2,1)} %get-tuple-element.290.refs_3_), custom_call_target="tpu_custom_call" | custom-call | flops 4831838208 | bytes 10092544 | tf_op jit(solution)/shard_map/weight_grad/pallas_call | solution.py:358
  585.8 6.0 collective-permute-done.30
  594.4 4.3 weight_grad.12
  598.7 3.9 all-to-all-start.15
  602.6 11.0 %weight_grad.13 = bf16[1024,2048]{1,0:T(8,128)(2,1)} custom-call(s32[1]{0:T(128)} %bitcast.84.part_ref, bf16[576,2048]{1,0:T(8,128)(2,1)} %bitcast.55.rows_ref.refs_0_, bf16[576,2048]{1,0:T(8,128)(2,1)} %bitcast.59.rows_ref.refs_1_, bf16[576,1024]{1,0:T(8,128)(2,1)} %get-tuple-element.302.refs_2_, bf16[576,1024]{1,0:T(8,128)(2,1)} %get-tuple-element.305.refs_3_, ...), custom_call_target="tpu_custom_call" | custom-call | flops 9663676416 | bytes 15466496 | tf_op jit(solution)/shard_map/weight_grad/pallas_call | solution.py:358
  617.8 8.0 %weight_grad.14 = f32[512,2048]{1,0:T(8,128)} custom-call(s32[1]{0:T(128)} %bitcast.89.part_ref, bf16[576,1024]{1,0:T(8,128)(2,1)} %get-tuple-element.309.act_ref.refs_0_, bf16[576,1024]{1,0:T(8,128)(2,1)} %get-tuple-element.310.act_ref.refs_1_, bf16[576,2048]{1,0:T(8,128)(2,1)} %get-tuple-element.289.refs_2_, bf16[576,2048]{1,0:T(8,128)(2,1)} %get-tuple-element.290.refs_3_, ...), custom_call_target="tpu_custom_call" | custom-call | flops 4831838208 | bytes 10092544 | tf_op jit(solution)/shard_map/weight_grad/pallas_call | solution.py:358
  630.2 3.5 collective-permute-start.34
  633.6 4.5 all-to-all-start.16
  641.5 3.2 copy.107
  650.4 12.1 %weight_grad.15 = f32[1024,2048]{1,0:T(8,128)} custom-call(s32[1]{0:T(128)} %bitcast.89.part_ref, bf16[576,2048]{1,0:T(8,128)(2,1)} %bitcast.55.rows_ref.refs_0_, bf16[576,2048]{1,0:T(8,128)(2,1)} %bitcast.59.rows_ref.refs_1_, bf16[576,1024]{1,0:T(8,128)(2,1)} %get-tuple-element.302.refs_2_, bf16[576,1024]{1,0:T(8,128)(2,1)} %get-tuple-element.305.refs_3_, ...), custom_call_target="tpu_custom_call" | custom-call | flops 9663676416 | bytes 15466496 | tf_op jit(solution)/shard_map/weight_grad/pallas_call | solution.py:358
  662.5 11.7 %all-to-all-done.16 = bf16[4,64,2048]{2,1,0:T(8,128)(2,1)} async-done(((bf16[4,64,2048]{2,1,0:T(8,128)(2,1)}), bf16[4,64,2048]{2,1,0:T(8,128)(2,1)}, u32[]{:S(2)}, u32[]{:S(2)}) %all-to-all-start.16) | async-done | bytes 1048608 | tf_op jit(solution)/shard_map/all_to_all | solution.py:951
  677.2 4.2 all-to-all-start.17
  690.5 3.5 all-to-all-start.18
  (572 shorter events, 217.7 us)
Async XLA Ops:
  0.6 33.9 %collective-permute-start = (bf16[64,2048]{1,0:T(8,128)(2,1)}, bf16[64,2048]{1,0:T(8,128)(2,1)}, u32[]{:S(2)}, u32[]{:S(2)}) collective-permute-start(bf16[64,2048]{1,0:T(8,128)(2,1)} %param.17), channel_id=1, source_target_pairs={{0,1},{1,2},{2,3},{3,0},{4,5},{5,6},{6,7},{7,4},{8,9},{9,10},{10,1... | collective-permute-start | bytes 786440 | tf_op jit(solution)/shard_map/ppermute | solution.py:423
  3.7 30.8 %collective-permute-start.1 = (bf16[64,2048]{1,0:T(8,128)(2,1)}, bf16[64,2048]{1,0:T(8,128)(2,1)}, u32[]{:S(2)}, u32[]{:S(2)}) collective-permute-start(bf16[64,2048]{1,0:T(8,128)(2,1)} %param.17), channel_id=1, source_target_pairs={{0,2},{1,3},{2,0},{3,1},{4,6},{5,7},{6,4},{7,5},{8,10},{9,11},{10,... | collective-permute-start | bytes 786440 | tf_op jit(solution)/shard_map/ppermute | solution.py:423
  6.3 28.2 %collective-permute-start.2 = (bf16[64,2048]{1,0:T(8,128)(2,1)}, bf16[64,2048]{1,0:T(8,128)(2,1)}, u32[]{:S(2)}, u32[]{:S(2)}) collective-permute-start(bf16[64,2048]{1,0:T(8,128)(2,1)} %param.17), channel_id=1, source_target_pairs={{0,3},{1,0},{2,1},{3,2},{4,7},{5,4},{6,5},{7,6},{8,11},{9,8},{10,9... | collective-permute-start | bytes 786440 | tf_op jit(solution)/shard_map/ppermute | solution.py:423
  13.6 24.0 %all-to-all-start = ((bf16[4,64,1664]{2,1,0:T(8,128)(2,1)}), bf16[4,64,1664]{2,1,0:T(8,128)(2,1)}, u32[]{:S(2)}, u32[]{:S(2)}) async-start(bf16[4,64,1664]{2,1,0:T(8,128)(2,1)} %pack.1), calls=%async_computation | async-start | bytes 1703936 | tf_op jit(solution)/shard_map/all_to_all | solution.py:417
  37.6 95.6 %collective-permute-start.3 = (bf16[4,64,1664]{2,1,0:T(8,128)(2,1)}, bf16[4,64,1664]{2,1,0:T(8,128)(2,1)}, u32[]{:S(2)}, u32[]{:S(2)}) collective-permute-start(bf16[4,64,1664]{2,1,0:T(8,128)(2,1)} %all-to-all-done.refs_0_), channel_id=1, source_target_pairs={{0,1},{1,2},{2,3},{3,0},{4,5},{5,6},{6,7},{7,4},{8,9},{9,10},{10,1... | collective-permute-start | bytes 2555912 | tf_op jit(solution)/shard_map/ppermute | solution.py:423
  38.4 94.8 %collective-permute-start.4 = (bf16[4,64,1664]{2,1,0:T(8,128)(2,1)}, bf16[4,64,1664]{2,1,0:T(8,128)(2,1)}, u32[]{:S(2)}, u32[]{:S(2)}) collective-permute-start(bf16[4,64,1664]{2,1,0:T(8,128)(2,1)} %all-to-all-done.refs_0_), channel_id=1, source_target_pairs={{0,2},{1,3},{2,0},{3,1},{4,6},{5,7},{6,4},{7,5},{8,10},{9,11},{10,... | collective-permute-start | bytes 2555912 | tf_op jit(solution)/shard_map/ppermute | solution.py:423
  38.7 94.5 %collective-permute-start.5 = (bf16[4,64,1664]{2,1,0:T(8,128)(2,1)}, bf16[4,64,1664]{2,1,0:T(8,128)(2,1)}, u32[]{:S(2)}, u32[]{:S(2)}) collective-permute-start(bf16[4,64,1664]{2,1,0:T(8,128)(2,1)} %all-to-all-done.refs_0_), channel_id=1, source_target_pairs={{0,3},{1,0},{2,1},{3,2},{4,7},{5,4},{6,5},{7,6},{8,11},{9,8},{10,9... | collective-permute-start | bytes 2555912 | tf_op jit(solution)/shard_map/ppermute | solution.py:423
  41.5 99.0 %collective-permute-start.6 = (bf16[4,64,1664]{2,1,0:T(8,128)(2,1)}, bf16[4,64,1664]{2,1,0:T(8,128)(2,1)}, u32[]{:S(2)}, u32[]{:S(2)}) collective-permute-start(bf16[4,64,1664]{2,1,0:T(8,128)(2,1)} %all-to-all-done.refs_0_), channel_id=1, source_target_pairs={{0,16},{16,0},{1,17},{17,1},{2,18},{18,2},{3,19},{19,3},{4,20},{20... | collective-permute-start | bytes 2555912 | tf_op jit(solution)/shard_map/ppermute | solution.py:426
  44.1 53.5 %all-to-all-start.1 = ((bf16[4,4,64,2048]{3,2,1,0:T(8,128)(2,1)}), bf16[4,4,64,2048]{3,2,1,0:T(8,128)(2,1)}, u32[]{:S(2)}, u32[]{:S(2)}) async-start(bf16[4,4,64,2048]{3,2,1,0:T(8,128)(2,1)} %broadcast_in_dim.54), calls=%async_computation.1 | async-start | bytes 8388608 | tf_op jit(solution)/shard_map/all_to_all | solution.py:417
  48.9 48.6 %copy-start.46 = (bf16[136,2048]{1,0:T(8,128)(2,1)S(1)}, bf16[136,2048]{1,0:T(8,128)(2,1)}, u32[]{:S(2)}) copy-start(bf16[136,2048]{1,0:T(8,128)(2,1)} %reshape.424) | copy-start | bytes 1671172
  99.2 31.2 %all-to-all-start.2 = ((bf16[4,136,2048]{2,1,0:T(8,128)(2,1)}), bf16[4,136,2048]{2,1,0:T(8,128)(2,1)}, u32[]{:S(2)}, u32[]{:S(2)}) async-start(bf16[4,136,2048]{2,1,0:T(8,128)(2,1)} %broadcast_in_dim.55), calls=%async_computation.2 | async-start | bytes 4456448 | tf_op jit(solution)/shard_map/all_to_all | solution.py:417
  133.2 7.3 %collective-permute-start.7 = (bf16[4,64,1664]{2,1,0:T(8,128)(2,1)}, bf16[4,64,1664]{2,1,0:T(8,128)(2,1)S(1)}, u32[]{:S(2)}, u32[]{:S(2)}) collective-permute-start(bf16[4,64,1664]{2,1,0:T(8,128)(2,1)} %collective-permute-done.3.refs_1_), channel_id=1, source_target_pairs={{0,16},{16,0},{1,17},{17,1},{2,18},{18,2},{3,19},{19,3},{4,20},{20... | collective-permute-start | bytes 2555912 | tf_op jit(solution)/shard_map/ppermute | solution.py:426
  133.3 7.3 %collective-permute-start.8 = (bf16[4,64,1664]{2,1,0:T(8,128)(2,1)}, bf16[4,64,1664]{2,1,0:T(8,128)(2,1)}, u32[]{:S(2)}, u32[]{:S(2)}) collective-permute-start(bf16[4,64,1664]{2,1,0:T(8,128)(2,1)} %collective-permute-done.4.refs_2_), channel_id=1, source_target_pairs={{0,16},{16,0},{1,17},{17,1},{2,18},{18,2},{3,19},{19,3},{4,20},{20... | collective-permute-start | bytes 2555912 | tf_op jit(solution)/shard_map/ppermute | solution.py:426
  133.8 6.8 collective-permute-start.9
  136.1 52.6 %copy-start = (f32[544,544]{1,0:T(8,128)}, f32[544,544]{1,0:T(8,128)S(1)}, u32[]{:S(2)}) copy-start(f32[544,544]{1,0:T(8,128)S(1)} %fusion.22.pair_ref) | copy-start | bytes 3551236
  136.1 64.5 %all-to-all-start.3 = ((bf16[4,1,72,2048]{3,2,1,0:T(8,128)(2,1)}), bf16[4,1,72,2048]{3,2,1,0:T(8,128)(2,1)}, u32[]{:S(2)}, u32[]{:S(2)}) async-start(bf16[4,1,72,2048]{3,2,1,0:T(8,128)(2,1)} %bitcast.36), calls=%async_computation.3 | async-start | bytes 2359296 | tf_op jit(solution)/shard_map/all_to_all | solution.py:417
  165.2 55.2 %collective-permute-start.12 = (bf16[136,2048]{1,0:T(8,128)(2,1)}, bf16[136,2048]{1,0:T(8,128)(2,1)}, u32[]{:S(2)}, u32[]{:S(2)}) collective-permute-start(bf16[136,2048]{1,0:T(8,128)(2,1)} %pad_maximum_fusion.3), channel_id=1, source_target_pairs={{0,1},{1,2},{2,3},{3,0},{4,5},{5,6},{6,7},{7,4},{8,9},{9,10},{10,1... | collective-permute-start | bytes 1671176 | tf_op jit(solution)/shard_map/ppermute | solution.py:423
  165.9 54.6 %collective-permute-start.13 = (bf16[136,2048]{1,0:T(8,128)(2,1)}, bf16[136,2048]{1,0:T(8,128)(2,1)}, u32[]{:S(2)}, u32[]{:S(2)}) collective-permute-start(bf16[136,2048]{1,0:T(8,128)(2,1)} %pad_maximum_fusion.3), channel_id=1, source_target_pairs={{0,2},{1,3},{2,0},{3,1},{4,6},{5,7},{6,4},{7,5},{8,10},{9,11},{10,... | collective-permute-start | bytes 1671176 | tf_op jit(solution)/shard_map/ppermute | solution.py:423
  167.4 53.1 %collective-permute-start.14 = (bf16[136,2048]{1,0:T(8,128)(2,1)}, bf16[136,2048]{1,0:T(8,128)(2,1)}, u32[]{:S(2)}, u32[]{:S(2)}) collective-permute-start(bf16[136,2048]{1,0:T(8,128)(2,1)} %pad_maximum_fusion.3), channel_id=1, source_target_pairs={{0,3},{1,0},{2,1},{3,2},{4,7},{5,4},{6,5},{7,6},{8,11},{9,8},{10,9... | collective-permute-start | bytes 1671176 | tf_op jit(solution)/shard_map/ppermute | solution.py:423
  170.2 9.2 %collective-permute-start.10 = (f32[2,544]{0,1:T(8,128)S(1)}, f32[2,544]{0,1:T(8,128)S(1)}, u32[]{:S(2)}, u32[]{:S(2)}) collective-permute-start(f32[2,544]{0,1:T(8,128)S(1)} %copy.101), channel_id=1, source_target_pairs={{0,4},{4,0},{8,12},{12,8},{1,5},{5,1},{9,13},{13,9},{2,6},{6,2},{1... | collective-permute-start | bytes 13064 | tf_op jit(solution)/shard_map/ppermute | solution.py:414
  179.5 7.7 %collective-permute-start.11 = (f32[2,544]{0,1:T(8,128)S(1)}, f32[2,544]{0,1:T(8,128)S(1)}, u32[]{:S(2)}, u32[]{:S(2)}) collective-permute-start(f32[2,544]{0,1:T(8,128)S(1)} %add.353), channel_id=1, source_target_pairs={{0,8},{4,12},{8,0},{12,4},{1,9},{5,13},{9,1},{13,5},{2,10},{6,14},... | collective-permute-start | bytes 13064 | tf_op jit(solution)/shard_map/ppermute | solution.py:414
  187.3 48.6 %collective-permute-start.15 = (bf16[4,4,64,2048]{3,2,1,0:T(8,128)(2,1)}, bf16[4,4,64,2048]{3,2,1,0:T(8,128)(2,1)}, u32[]{:S(2)}, u32[]{:S(2)}) collective-permute-start(bf16[4,4,64,2048]{3,2,1,0:T(8,128)(2,1)} %all-to-all-done.1), channel_id=1, source_target_pairs={{0,16},{16,0},{1,17},{17,1},{2,18},{18,2},{3,19},{19,3},{4,20},{20... | collective-permute-start | bytes 12582920 | tf_op jit(solution)/shard_map/ppermute | solution.py:426
  200.6 13.5 %all-to-all-start.4 = ((bf16[4,136,512]{2,1,0:T(8,128)(2,1)}), bf16[4,136,512]{2,1,0:T(8,128)(2,1)}, u32[]{:S(2)}, u32[]{:S(2)}) async-start(bf16[4,136,512]{2,1,0:T(8,128)(2,1)} %bitcast.37), calls=%async_computation.4 | async-start | bytes 1114112 | tf_op jit(solution)/shard_map/all_to_all | solution.py:417
  225.7 45.3 %all-to-all-start.5 = ((bf16[4,3,72,2048]{3,2,1,0:T(8,128)(2,1)}), bf16[4,3,72,2048]{3,2,1,0:T(8,128)(2,1)}, u32[]{:S(2)}, u32[]{:S(2)}) async-start(bf16[4,3,72,2048]{3,2,1,0:T(8,128)(2,1)} %bitcast.310), calls=%async_computation.5 | async-start | bytes 7077888 | tf_op jit(solution)/shard_map/all_to_all | solution.py:417
  241.1 32.1 %collective-permute-start.16 = (bf16[136,2048]{1,0:T(8,128)(2,1)}, bf16[136,2048]{1,0:T(8,128)(2,1)}, u32[]{:S(2)}, u32[]{:S(2)}) collective-permute-start(bf16[136,2048]{1,0:T(8,128)(2,1)} %multiply_convert_fusion), channel_id=1, source_target_pairs={{0,1},{1,2},{2,3},{3,0},{4,5},{5,6},{6,7},{7,4},{8,9},{9,10},{10,1... | collective-permute-start | bytes 1671176 | tf_op jit(solution)/shard_map/ppermute | solution.py:423
  241.4 34.0 %copy-start.59 = (bf16[4,2,72,272]{3,2,1,0:T(8,128)(2,1)S(1)}, bf16[4,2,72,272]{3,2,1,0:T(8,128)(2,1)}, u32[]{:S(2)}) copy-start(bf16[4,2,72,272]{3,2,1,0:T(8,128)(2,1)} %fusion.47) | copy-start | bytes 940036
  273.2 26.1 %collective-permute-start.17 = (bf16[136,2048]{1,0:T(8,128)(2,1)}, bf16[136,2048]{1,0:T(8,128)(2,1)}, u32[]{:S(2)}, u32[]{:S(2)}) collective-permute-start(bf16[136,2048]{1,0:T(8,128)(2,1)} %multiply_convert_fusion), channel_id=1, source_target_pairs={{0,2},{1,3},{2,0},{3,1},{4,6},{5,7},{6,4},{7,5},{8,10},{9,11},{10,... | collective-permute-start | bytes 1671176 | tf_op jit(solution)/shard_map/ppermute | solution.py:423
  274.2 25.5 %collective-permute-start.18 = (bf16[136,2048]{1,0:T(8,128)(2,1)}, bf16[136,2048]{1,0:T(8,128)(2,1)}, u32[]{:S(2)}, u32[]{:S(2)}) collective-permute-start(bf16[136,2048]{1,0:T(8,128)(2,1)} %multiply_convert_fusion), channel_id=1, source_target_pairs={{0,3},{1,0},{2,1},{3,2},{4,7},{5,4},{6,5},{7,6},{8,11},{9,8},{10,9... | collective-permute-start | bytes 1671176 | tf_op jit(solution)/shard_map/ppermute | solution.py:423
  279.3 31.2 %all-to-all-start.6 = ((bf16[4,2,72,2048]{3,2,1,0:T(8,128)(2,1)}), bf16[4,2,72,2048]{3,2,1,0:T(8,128)(2,1)}, u32[]{:S(2)}, u32[]{:S(2)}) async-start(bf16[4,2,72,2048]{3,2,1,0:T(8,128)(2,1)} %bitcast.312), calls=%async_computation.6 | async-start | bytes 4718592 | tf_op jit(solution)/shard_map/all_to_all | solution.py:417
  314.5 31.7 %all-to-all-start.7 = ((bf16[4,2,72,2048]{3,2,1,0:T(8,128)(2,1)}), bf16[4,2,72,2048]{3,2,1,0:T(8,128)(2,1)}, u32[]{:S(2)}, u32[]{:S(2)}) async-start(bf16[4,2,72,2048]{3,2,1,0:T(8,128)(2,1)} %bitcast.313), calls=%async_computation.7 | async-start | bytes 4718592 | tf_op jit(solution)/shard_map/all_to_all | solution.py:417
  346.2 29.2 %all-to-all-start.8 = ((bf16[4,72,2176]{2,1,0:T(8,128)(2,1)}), bf16[4,72,2176]{2,1,0:T(8,128)(2,1)}, u32[]{:S(2)}, u32[]{:S(2)}) async-start(bf16[4,72,2176]{2,1,0:T(8,128)(2,1)} %get-tuple-element.220), calls=%async_computation.8 | async-start | bytes 2506752 | tf_op jit(solution)/shard_map/all_to_all | solution.py:417
  378.2 19.6 %all-to-all-start.9 = ((bf16[4,72,2176]{2,1,0:T(8,128)(2,1)}), bf16[4,72,2176]{2,1,0:T(8,128)(2,1)}, u32[]{:S(2)}, u32[]{:S(2)}) async-start(bf16[4,72,2176]{2,1,0:T(8,128)(2,1)} %get-tuple-element.228), calls=%async_computation.9 | async-start | bytes 2506752 | tf_op jit(solution)/shard_map/all_to_all | solution.py:417
  382.5 66.8 %collective-permute-start.19 = (bf16[136,2176]{1,0:T(8,128)(2,1)}, bf16[136,2176]{1,0:T(8,128)(2,1)}, u32[]{:S(2)}, u32[]{:S(2)}) collective-permute-start(bf16[136,2176]{1,0:T(8,128)(2,1)} %fusion.2), channel_id=1, source_target_pairs={{0,3},{1,0},{2,1},{3,2},{4,7},{5,4},{6,5},{7,6},{8,11},{9,8},{10,9... | collective-permute-start | bytes 1775624 | tf_op jit(solution)/shard_map/ppermute | solution.py:423
  400.6 48.8 %collective-permute-start.20 = (bf16[136,2176]{1,0:T(8,128)(2,1)}, bf16[136,2176]{1,0:T(8,128)(2,1)}, u32[]{:S(2)}, u32[]{:S(2)}) collective-permute-start(bf16[136,2176]{1,0:T(8,128)(2,1)} %fusion.3), channel_id=1, source_target_pairs={{0,2},{1,3},{2,0},{3,1},{4,6},{5,7},{6,4},{7,5},{8,10},{9,11},{10,... | collective-permute-start | bytes 1775624 | tf_op jit(solution)/shard_map/ppermute | solution.py:423
  401.8 19.4 %all-to-all-start.10 = ((bf16[4,72,2176]{2,1,0:T(8,128)(2,1)}), bf16[4,72,2176]{2,1,0:T(8,128)(2,1)}, u32[]{:S(2)}, u32[]{:S(2)}) async-start(bf16[4,72,2176]{2,1,0:T(8,128)(2,1)} %get-tuple-element.238), calls=%async_computation.10 | async-start | bytes 2506752 | tf_op jit(solution)/shard_map/all_to_all | solution.py:417
  423.9 25.5 %collective-permute-start.21 = (bf16[136,2176]{1,0:T(8,128)(2,1)}, bf16[136,2176]{1,0:T(8,128)(2,1)}, u32[]{:S(2)}, u32[]{:S(2)}) collective-permute-start(bf16[136,2176]{1,0:T(8,128)(2,1)} %fusion.4), channel_id=1, source_target_pairs={{0,1},{1,2},{2,3},{3,0},{4,5},{5,6},{6,7},{7,4},{8,9},{9,10},{10,1... | collective-permute-start | bytes 1775624 | tf_op jit(solution)/shard_map/ppermute | solution.py:423
  425.5 19.5 %all-to-all-start.11 = ((bf16[4,72,2176]{2,1,0:T(8,128)(2,1)}), bf16[4,72,2176]{2,1,0:T(8,128)(2,1)}, u32[]{:S(2)}, u32[]{:S(2)}) async-start(bf16[4,72,2176]{2,1,0:T(8,128)(2,1)} %get-tuple-element.246), calls=%async_computation.11 | async-start | bytes 2506752 | tf_op jit(solution)/shard_map/all_to_all | solution.py:417
  462.6 6.0 collective-permute-start.22
  465.4 6.8 collective-permute-start.23
  465.9 6.3 collective-permute-start.24
  472.2 42.3 %all-to-all-start.12 = ((bf16[4,2,72,2048]{3,2,1,0:T(8,128)(2,1)}), bf16[4,2,72,2048]{3,2,1,0:T(8,128)(2,1)}, u32[]{:S(2)}, u32[]{:S(2)}) async-start(bf16[4,2,72,2048]{3,2,1,0:T(8,128)(2,1)} %bitcast.311), calls=%async_computation.12 | async-start | bytes 4718592 | tf_op jit(solution)/shard_map/all_to_all | solution.py:417
  493.8 14.0 %collective-permute-start.25 = (f32[2,544]{0,1:T(8,128)S(1)}, f32[2,544]{0,1:T(8,128)S(1)}, u32[]{:S(2)}, u32[]{:S(2)}) collective-permute-start(f32[2,544]{0,1:T(8,128)S(1)} %copy.106), channel_id=1, source_target_pairs={{0,4},{4,0},{8,12},{12,8},{1,5},{5,1},{9,13},{13,9},{2,6},{6,2},{1... | collective-permute-start | bytes 13064 | tf_op jit(solution)/shard_map/ppermute | solution.py:414
  507.9 6.6 collective-permute-start.26
  529.7 18.2 %collective-permute-start.29 = (bf16[1024,1536]{1,0:T(8,128)(2,1)}, bf16[1024,1536]{1,0:T(8,128)(2,1)}, u32[]{:S(2)}, u32[]{:S(2)}) collective-permute-start(bf16[1024,1536]{1,0:T(8,128)(2,1)} %weight_grad.8), channel_id=1, source_target_pairs={{0,16},{16,0},{1,17},{17,1},{2,18},{18,2},{3,19},{19,3},{4,20},{20... | collective-permute-start | bytes 9437192 | tf_op jit(solution)/shard_map/ppermute | solution.py:426
  529.7 42.4 %collective-permute-start.27 = (bf16[136,2048]{1,0:T(8,128)(2,1)}, bf16[136,2048]{1,0:T(8,128)(2,1)}, u32[]{:S(2)}, u32[]{:S(2)}) collective-permute-start(bf16[136,2048]{1,0:T(8,128)(2,1)} %get-tuple-element.346), channel_id=1, source_target_pairs={{0,2},{1,3},{2,0},{3,1},{4,6},{5,7},{6,4},{7,5},{8,10},{9,11},{10,... | collective-permute-start | bytes 1671176 | tf_op jit(solution)/shard_map/ppermute | solution.py:423
  532.2 40.0 %collective-permute-start.28 = (bf16[136,2048]{1,0:T(8,128)(2,1)}, bf16[136,2048]{1,0:T(8,128)(2,1)}, u32[]{:S(2)}, u32[]{:S(2)}) collective-permute-start(bf16[136,2048]{1,0:T(8,128)(2,1)} %get-tuple-element.345), channel_id=1, source_target_pairs={{0,1},{1,2},{2,3},{3,0},{4,5},{5,6},{6,7},{7,4},{8,9},{9,10},{10,1... | collective-permute-start | bytes 1671176 | tf_op jit(solution)/shard_map/ppermute | solution.py:423
  534.1 31.4 %all-to-all-start.13 = ((bf16[4,136,2048]{2,1,0:T(8,128)(2,1)}), bf16[4,136,2048]{2,1,0:T(8,128)(2,1)}, u32[]{:S(2)}, u32[]{:S(2)}) async-start(bf16[4,136,2048]{2,1,0:T(8,128)(2,1)} %broadcast_in_dim.62), calls=%async_computation.13 | async-start | bytes 4456448 | tf_op jit(solution)/shard_map/all_to_all | solution.py:417
  565.6 33.2 %all-to-all-start.14 = ((bf16[4,2,72,2048]{3,2,1,0:T(8,128)(2,1)}), bf16[4,2,72,2048]{3,2,1,0:T(8,128)(2,1)}, u32[]{:S(2)}, u32[]{:S(2)}) async-start(bf16[4,2,72,2048]{3,2,1,0:T(8,128)(2,1)} %bitcast.62), calls=%async_computation.14 | async-start | bytes 4718592 | tf_op jit(solution)/shard_map/all_to_all | solution.py:417
  571.4 20.4 %collective-permute-start.30 = (bf16[256,1536]{1,0:T(8,128)(2,1)S(1)}, bf16[256,1536]{1,0:T(8,128)(2,1)S(1)}, u32[]{:S(2)}, u32[]{:S(2)}) collective-permute-start(bf16[256,1536]{1,0:T(8,128)(2,1)S(1)} %copy-done.57), channel_id=1, source_target_pairs={{0,1},{1,2},{2,3},{3,0},{4,5},{5,6},{6,7},{7,4},{8,9},{9,10},{10,1... | collective-permute-start | bytes 2359304 | tf_op jit(solution)/shard_map/ppermute | solution.py:423
  575.9 17.6 %collective-permute-start.32 = (bf16[256,2048]{1,0:T(8,128)(2,1)}, bf16[256,2048]{1,0:T(8,128)(2,1)S(1)}, u32[]{:S(2)}, u32[]{:S(2)}) collective-permute-start(bf16[256,2048]{1,0:T(8,128)(2,1)} %weight_grad.10), channel_id=1, source_target_pairs={{0,16},{16,0},{1,17},{17,1},{2,18},{18,2},{3,19},{19,3},{4,20},{20... | collective-permute-start | bytes 3145736 | tf_op jit(solution)/shard_map/ppermute | solution.py:426
  583.2 34.6 %collective-permute-start.33 = (bf16[512,2048]{1,0:T(8,128)(2,1)}, bf16[512,2048]{1,0:T(8,128)(2,1)}, u32[]{:S(2)}, u32[]{:S(2)}) collective-permute-start(bf16[512,2048]{1,0:T(8,128)(2,1)} %weight_grad.11), channel_id=1, source_target_pairs={{0,16},{16,0},{1,17},{17,1},{2,18},{18,2},{3,19},{19,3},{4,20},{20... | collective-permute-start | bytes 6291464 | tf_op jit(solution)/shard_map/ppermute | solution.py:426
  593.4 21.4 %collective-permute-start.31 = (bf16[256,1536]{1,0:T(8,128)(2,1)S(1)}, bf16[256,1536]{1,0:T(8,128)(2,1)}, u32[]{:S(2)}, u32[]{:S(2)}) collective-permute-start(bf16[256,1536]{1,0:T(8,128)(2,1)S(1)} %fusion.20), channel_id=1, source_target_pairs={{0,1},{1,2},{2,3},{3,0},{4,5},{5,6},{6,7},{7,4},{8,9},{9,10},{10,1... | collective-permute-start | bytes 2359304 | tf_op jit(solution)/shard_map/ppermute | solution.py:423
  598.7 34.9 %all-to-all-start.15 = ((bf16[4,136,2048]{2,1,0:T(8,128)(2,1)}), bf16[4,136,2048]{2,1,0:T(8,128)(2,1)S(1)}, u32[]{:S(2)}, u32[]{:S(2)}) async-start(bf16[4,136,2048]{2,1,0:T(8,128)(2,1)} %bitcast.314), calls=%async_computation.15 | async-start | bytes 4456448 | tf_op jit(solution)/shard_map/all_to_all | solution.py:417
  614.8 35.6 %collective-permute-start.35 = (bf16[1024,2048]{1,0:T(8,128)(2,1)}, bf16[1024,2048]{1,0:T(8,128)(2,1)}, u32[]{:S(2)}, u32[]{:S(2)}) collective-permute-start(bf16[1024,2048]{1,0:T(8,128)(2,1)} %weight_grad.13), channel_id=1, source_target_pairs={{0,16},{16,0},{1,17},{17,1},{2,18},{18,2},{3,19},{19,3},{4,20},{20... | collective-permute-start | bytes 12582920 | tf_op jit(solution)/shard_map/ppermute | solution.py:426
  617.4 70.4 %collective-permute-start.36 = (bf16[256,1536]{1,0:T(8,128)(2,1)}, bf16[256,1536]{1,0:T(8,128)(2,1)}, u32[]{:S(2)}, u32[]{:S(2)}) collective-permute-start(bf16[256,1536]{1,0:T(8,128)(2,1)} %fusion.19), channel_id=1, source_target_pairs={{0,1},{1,2},{2,3},{3,0},{4,5},{5,6},{6,7},{7,4},{8,9},{9,10},{10,1... | collective-permute-start | bytes 2359304 | tf_op jit(solution)/shard_map/ppermute | solution.py:423
  630.2 46.2 %collective-permute-start.34 = (bf16[136,2048]{1,0:T(8,128)(2,1)}, bf16[136,2048]{1,0:T(8,128)(2,1)}, u32[]{:S(2)}, u32[]{:S(2)}) collective-permute-start(bf16[136,2048]{1,0:T(8,128)(2,1)} %slice.555), channel_id=1, source_target_pairs={{0,3},{1,0},{2,1},{3,2},{4,7},{5,4},{6,5},{7,6},{8,11},{9,8},{10,9... | collective-permute-start | bytes 1671176 | tf_op jit(solution)/shard_map/ppermute | solution.py:423
  633.6 40.5 %all-to-all-start.16 = ((bf16[4,64,2048]{2,1,0:T(8,128)(2,1)}), bf16[4,64,2048]{2,1,0:T(8,128)(2,1)}, u32[]{:S(2)}, u32[]{:S(2)}) async-start(bf16[4,64,2048]{2,1,0:T(8,128)(2,1)} %convert_element_type.339), calls=%async_computation.16 | async-start | bytes 2097152 | tf_op jit(solution)/shard_map/all_to_all | solution.py:951
  647.4 2.9 collective-permute-start.37
  650.4 31.0 %slice-start = ((f32[272,2048]{1,0:T(8,128)}), f32[136,2048]{1,0:T(8,128)S(1)}, s32[]{:S(2)}) async-start(f32[272,2048]{1,0:T(8,128)} %copy-done.27), calls=%async_computation.19 | async-start | bytes 2228224 | tf_op jit(solution)/shard_map/slice | solution.py:917
  677.2 9.1 %all-to-all-start.17 = ((f32[4,1,5120]{2,1,0:T(1,128)}), f32[4,1,5120]{2,1,0:T(1,128)S(1)}, u32[]{:S(2)}, u32[]{:S(2)}) async-start(f32[4,1,5120]{2,1,0:T(1,128)} %reshape.482), calls=%async_computation.17 | async-start | bytes 163840 | tf_op jit(solution)/shard_map/all_to_all | solution.py:417
  690.5 13.4 %all-to-all-start.18 = ((bf16[4,64,1536]{2,1,0:T(8,128)(2,1)}), bf16[4,64,1536]{2,1,0:T(8,128)(2,1)S(1)}, u32[]{:S(2)}, u32[]{:S(2)}) async-start(bf16[4,64,1536]{2,1,0:T(8,128)(2,1)} %bitcast.113), calls=%async_computation.18 | async-start | bytes 1572864 | tf_op jit(solution)/shard_map/all_to_all | solution.py:417
  694.1 3.9 collective-permute-start.40
  695.2 4.6 collective-permute-start.39
  695.2 5.5 collective-permute-start.38
  (117 other events, 882.7 us)

commit v6 on v5

--- a/solution.py
+++ b/solution.py
@@ -950,7 +950,10 @@
         out_sent = gate(out_dp.astype(BF16), hidden_trade)
         out_trade = lax.all_to_all(out_sent, "exp", 0, 0, tiled=True)
         out_trade = gate(out_trade, grad_gate_up)
-        part = jnp.sum(ctx_trade(gate(part, out_trade)), axis=0)
+        whole_part = part
+        part = part_of(whole_part, 0, c)
+        for k in range(1, n_ctx):
+            part = part + ctx_swap(part_of(whole_part, 0, c ^ k), k)
         grad_out = jnp.sum(out_trade.astype(F32), axis=0)
     else:
         part = jnp.sum(ctx_trade(part), axis=0)

time: 716 us -> 717 us (level)
  the two profiles are of different devices: /device:TPU:0 before, /device:TPU:16 now
where the time goes in v6:
time: 717 us; the launch traced here: 707 us
  waiting for transfers between devices  207 us (29%)
  Pallas kernels  177 us (25%)
  starting transfers between devices  132 us (18%)
  local copies, waits for them, and re-layouts  76.7 us (11%)
  matrix products  64.6 us (9%)
  other arithmetic  44.9 us (6%)
    all_to_all x17, waiting for transfers between devices, ctx_trade(): return lax.all_to_all(x, 'ctx', 0, 0, tiled=True)  148 us
    all_to_all x17, starting transfers between devices, ctx_trade(): return lax.all_to_all(x, 'ctx', 0, 0, tiled=True)  74.7 us
    pallas_call x8, Pallas kernels, weight_grad(): pl.pallas_call(kernel, grid_spec=pltpu.PrefetchScalarGridSpec(num_scalar_...  59.9 us
    pallas_call x2, Pallas kernels, expert_rows(): pl.pallas_call(kernel, grid_spec=pltpu.PrefetchScalarGridSpec(num_scalar_...  46.5 us
    ppermute x24, starting transfers between devices, exp_shift(): return lax.ppermute(x, 'exp', [(i, (i + s) % n_exp) for i in range(n_exp)])  36.9 us
    ppermute x24, waiting for transfers between devices, exp_shift(): return lax.ppermute(x, 'exp', [(i, (i + s) % n_exp) for i in range(n_exp)])  31.9 us
    dot_general x12, matrix products, dot(): return jnp.dot(a, b, preferred_element_type=F32)  29.5 us
    ppermute x10, waiting for transfers between devices, ctx_swap(): return lax.ppermute(x, 'ctx', [(i, i ^ k) for i in range(n_ctx)])  27.5 us
  transfers between devices with their start and end apart: 62, of which 25 were waited for; matrix products, arithmetic and copies ran while one was open for 20% of the time, Pallas kernels for 24%

profile of v6, /device:TPU:16, one launch (start us, length us, event | category | flops | bytes accessed | tf_op | source)
XLA Modules:
  0.0 706.8 jit_solution(720868016565444161)
XLA Ops:
  9.8 4.2 all-to-all-start
  42.1 4.8 all-to-all-start.1
  52.6 42.9 %all-to-all-done.1 = bf16[4,4,64,2048]{3,2,1,0:T(8,128)(2,1)} async-done(((bf16[4,4,64,2048]{3,2,1,0:T(8,128)(2,1)}), bf16[4,4,64,2048]{3,2,1,0:T(8,128)(2,1)}, u32[]{:S(2)}, u32[]{:S(2)}) %all-to-all-start.1) | async-done | bytes 4194336 | tf_op jit(solution)/shard_map/all_to_all | solution.py:417
  97.2 4.5 all-to-all-start.2
  103.1 25.3 %all-to-all-done.2 = bf16[4,136,2048]{2,1,0:T(8,128)(2,1)} async-done(((bf16[4,136,2048]{2,1,0:T(8,128)(2,1)}), bf16[4,136,2048]{2,1,0:T(8,128)(2,1)}, u32[]{:S(2)}, u32[]{:S(2)}) %all-to-all-start.2) | async-done | bytes 2228256 | tf_op jit(solution)/shard_map/all_to_all | solution.py:417
  134.1 4.4 all-to-all-start.3
  139.5 6.3 assemble.1
  154.5 6.5 fusion.91.pq.pk.pv.projected_ref
  178.0 6.1 collective-permute-done.11
  185.5 8.4 %attend.1 = (bf16[544,512]{1,0:T(8,128)(2,1)}, bf16[544,512]{1,0:T(8,128)(2,1)S(1)}, bf16[544,512]{1,0:T(8,128)(2,1)S(1)}, bf16[544,512]{1,0:T(8,128)(2,1)S(1)}, f32[544,512]{1,0:T(8,128)S(1)}) custom-call(f32[544,1536]{1,0:T(8,128)} %copy-done.16, f32[544,1536]{1,0:T(8,128)} %copy-done.16, f32[544,1536]{1,0:T(8,128)} %copy-done.16, f32[544,2]{1,0:T(8,128)S(1)} %bitcast.282, ...), custom_call_target="tpu_custom_call" | custom-call | tf_op jit(solution)/shard_map/attend/pallas_call | solution.py:84
  197.6 4.2 all-to-all-start.4
  203.0 8.1 %all-to-all-done.4 = bf16[4,136,512]{2,1,0:T(8,128)(2,1)} async-done(((bf16[4,136,512]{2,1,0:T(8,128)(2,1)}), bf16[4,136,512]{2,1,0:T(8,128)(2,1)}, u32[]{:S(2)}, u32[]{:S(2)}) %all-to-all-start.4) | async-done | bytes 557088 | tf_op jit(solution)/shard_map/all_to_all | solution.py:417
  217.4 5.2 convolution_convert_fusion
  222.6 4.7 all-to-all-start.5
  229.8 3.0 convolution_add_fusion.1
  232.9 3.2 multiply_reduce_fusion.3
  239.7 28.2 %all-to-all-done.5 = bf16[4,3,72,2048]{3,2,1,0:T(8,128)(2,1)} async-done(((bf16[4,3,72,2048]{3,2,1,0:T(8,128)(2,1)}), bf16[4,3,72,2048]{3,2,1,0:T(8,128)(2,1)}, u32[]{:S(2)}, u32[]{:S(2)}) %all-to-all-start.5) | async-done | bytes 3538976 | tf_op jit(solution)/shard_map/all_to_all | solution.py:417
  272.2 4.0 convolution_convert_fusion.2
  276.2 4.5 all-to-all-start.6
  283.3 3.4 stack.81
  289.7 5.2 collective-permute-done.17
  294.8 11.8 %collective-permute-done.18 = bf16[136,2048]{1,0:T(8,128)(2,1)} collective-permute-done((bf16[136,2048]{1,0:T(8,128)(2,1)}, bf16[136,2048]{1,0:T(8,128)(2,1)}, u32[]{:S(2)}, u32[]{:S(2)}) %collective-permute-start.18) | collective-permute-done | bytes 557088 | tf_op jit(solution)/shard_map/ppermute | solution.py:423
  307.6 4.0 convolution_convert_fusion.1
  311.6 4.5 all-to-all-start.7
  317.4 23.2 %expert.2 = (bf16[4,72,2176]{2,1,0:T(8,128)(2,1)}, bf16[4,72,2176]{2,1,0:T(8,128)(2,1)}, bf16[576,1024]{1,0:T(8,128)(2,1)}, bf16[576,1024]{1,0:T(8,128)(2,1)}, b...) custom-call(s32[1]{0:T(128)} %bitcast.52.expert_ref, bf16[576,2048]{1,0:T(8,128)(2,1)} %bitcast.55.rows_ref.refs_0_, ...), custom_call_target="tpu_custom_call" | custom-call | tf_op jit(solution)/shard_map/expert/pallas_call | solution.py:281
  343.4 4.7 all-to-all-start.8
  349.3 23.3 %expert.3 = (bf16[4,72,2176]{2,1,0:T(8,128)(2,1)}, bf16[4,72,2176]{2,1,0:T(8,128)(2,1)}, bf16[576,1024]{1,0:T(8,128)(2,1)}, bf16[576,1024]{1,0:T(8,128)(2,1)}, b...) custom-call(s32[1]{0:T(128)} %bitcast.52.expert_ref, bf16[576,2048]{1,0:T(8,128)(2,1)} %bitcast.59.rows_ref.refs_1_, ...), custom_call_target="tpu_custom_call" | custom-call | tf_op jit(solution)/shard_map/expert/pallas_call | solution.py:281
  375.3 4.3 all-to-all-start.9
  383.4 7.0 expert_outs.2
  390.4 4.5 all-to-all-done.9
  399.5 4.3 all-to-all-start.10
  405.0 7.0 expert_outs.3
  412.0 6.8 all-to-all-done.10
  423.9 4.5 all-to-all-start.11
  429.7 13.7 %all-to-all-done.11 = bf16[4,72,2176]{2,1,0:T(8,128)(2,1)} async-done(((bf16[4,72,2176]{2,1,0:T(8,128)(2,1)}), bf16[4,72,2176]{2,1,0:T(8,128)(2,1)}, u32[]{:S(2)}, u32[]{:S(2)}) %all-to-all-start.11) | async-done | bytes 1253408 | tf_op jit(solution)/shard_map/all_to_all | solution.py:417
  443.4 2.9 convolution_bitcast_fusion
  453.0 3.9 fusion.25
  456.9 3.7 fusion.27
  467.0 3.6 collective-permute-done.23
  470.6 4.5 all-to-all-start.12
  478.6 12.6 %attend_back.1 = (f32[544,512]{1,0:T(8,128)S(1)}, f32[544,512]{1,0:T(8,128)}, bf16[544,512]{1,0:T(8,128)(2,1)S(1)}, f32[2,512]{1,0:T(2,128)S(1)}, f32[544,256]{1,0:T(8,128)S(1)}) custom-call(bf16[544,512]{1,0:T(8,128)(2,1)S(1)} %bitcast.285, bf16[544,512]{1,0:T(8,128)(2,1)S(1)} %copy-done.6, bf16[544,512]{1,0:T(8,128)(2,1)S(1)} %copy-done.8, ...), custom_call_target="tpu_custom_call" | custom-call | tf_op jit(solution)/shard_map/attend_back/pallas_call | solution.py:159
  496.1 10.1 %collective-permute-done.25 = f32[2,544]{0,1:T(8,128)S(1)} collective-permute-done((f32[2,544]{0,1:T(8,128)S(1)}, f32[2,544]{0,1:T(8,128)S(1)}, u32[]{:S(2)}, u32[]{:S(2)}) %collective-permute-start.25) | collective-permute-done | bytes 4384 | tf_op jit(solution)/shard_map/ppermute | solution.py:414
  509.2 3.6 collective-permute-done.26
  521.9 6.1 weight_grad.8
  530.9 4.7 all-to-all-start.13
  537.1 7.6 %convolution_convert_fusion.3 = bf16[544,2048]{1,0:T(8,128)(2,1)} fusion(bf16[544,1536]{1,0:T(8,128)(2,1)S(1)} %copy-done.2, bf16[2048,1536]{1,0:T(8,128)(2,1)} %bitcast.344), kind=kOutput, calls=%fused_computation.15 | convolution fusion | flops 3423666176 | bytes 10190848 | tf_op jit(solution)/shard_map/dot_general | solution.py:49
  544.7 7.4 %weight_grad.9 = f32[1024,1536]{1,0:T(8,128)} custom-call(s32[1]{0:T(128)} %bitcast.18.part_ref, bf16[544,2048]{1,0:T(8,128)(2,1)} %copy-done.23, bf16[544,1536]{1,0:T(8,128)(2,1)} %copy-done.1, bf16[1024,1536]{1,0:T(8,128)(2,1)} %collective-permute-done.29.refs_2_), custom_call_target="tpu_custom_call" | custom-call | flops 3422552064 | bytes 9076736 | tf_op jit(solution)/shard_map/weight_grad/pallas_call | solution.py:358
  554.4 7.9 %all-to-all-done.13 = bf16[4,136,2048]{2,1,0:T(8,128)(2,1)} async-done(((bf16[4,136,2048]{2,1,0:T(8,128)(2,1)}), bf16[4,136,2048]{2,1,0:T(8,128)(2,1)}, u32[]{:S(2)}, u32[]{:S(2)}) %all-to-all-start.13) | async-done | bytes 2228256 | tf_op jit(solution)/shard_map/all_to_all | solution.py:417
  562.3 4.5 all-to-all-start.14
  568.2 3.2 collective-permute-start.30
  571.5 3.7 weight_grad.10
  575.2 7.2 %weight_grad.11 = bf16[512,2048]{1,0:T(8,128)(2,1)} custom-call(s32[1]{0:T(128)} %bitcast.84.part_ref, bf16[576,1024]{1,0:T(8,128)(2,1)} %get-tuple-element.308.act_ref.refs_0_, bf16[576,1024]{1,0:T(8,128)(2,1)} %get-tuple-element.309.act_ref.refs_1_, bf16[576,2048]{1,0:T(8,128)(2,1)} %get-tuple-element.288.refs_2_, bf16[576,2048]{1,0:T(8,128)(2,1)} %get-tuple-element.289.refs_3_), custom_call_target="tpu_custom_call" | custom-call | flops 4831838208 | bytes 10092544 | tf_op jit(solution)/shard_map/weight_grad/pallas_call | solution.py:358
  592.6 4.3 weight_grad.12
  597.0 3.9 all-to-all-start.15
  600.8 11.0 %weight_grad.13 = bf16[1024,2048]{1,0:T(8,128)(2,1)} custom-call(s32[1]{0:T(128)} %bitcast.84.part_ref, bf16[576,2048]{1,0:T(8,128)(2,1)} %bitcast.55.rows_ref.refs_0_, bf16[576,2048]{1,0:T(8,128)(2,1)} %bitcast.59.rows_ref.refs_1_, bf16[576,1024]{1,0:T(8,128)(2,1)} %get-tuple-element.301.refs_2_, bf16[576,1024]{1,0:T(8,128)(2,1)} %get-tuple-element.304.refs_3_, ...), custom_call_target="tpu_custom_call" | custom-call | flops 9663676416 | bytes 15466496 | tf_op jit(solution)/shard_map/weight_grad/pallas_call | solution.py:358
  617.8 8.0 %weight_grad.14 = f32[512,2048]{1,0:T(8,128)} custom-call(s32[1]{0:T(128)} %bitcast.89.part_ref, bf16[576,1024]{1,0:T(8,128)(2,1)} %get-tuple-element.308.act_ref.refs_0_, bf16[576,1024]{1,0:T(8,128)(2,1)} %get-tuple-element.309.act_ref.refs_1_, bf16[576,2048]{1,0:T(8,128)(2,1)} %get-tuple-element.288.refs_2_, bf16[576,2048]{1,0:T(8,128)(2,1)} %get-tuple-element.289.refs_3_, ...), custom_call_target="tpu_custom_call" | custom-call | flops 4831838208 | bytes 10092544 | tf_op jit(solution)/shard_map/weight_grad/pallas_call | solution.py:358
  630.9 4.5 all-to-all-start.16
  638.7 3.2 copy.105
  646.1 3.0 collective-permute-start.40
  654.4 3.3 collective-permute-start.42
  661.9 11.2 %collective-permute-done.41 = f32[20,64]{1,0:T(8,128)S(1)} collective-permute-done((f32[20,64]{1,0:T(8,128)S(1)}, f32[20,64]{1,0:T(8,128)S(1)}, u32[]{:S(2)}, u32[]{:S(2)}) %collective-permute-start.41) | collective-permute-done | bytes 5152 | tf_op jit(solution)/shard_map/ppermute | solution.py:423
  674.3 12.1 %weight_grad.15 = f32[1024,2048]{1,0:T(8,128)} custom-call(s32[1]{0:T(128)} %bitcast.89.part_ref, bf16[576,2048]{1,0:T(8,128)(2,1)} %bitcast.55.rows_ref.refs_0_, bf16[576,2048]{1,0:T(8,128)(2,1)} %bitcast.59.rows_ref.refs_1_, bf16[576,1024]{1,0:T(8,128)(2,1)} %get-tuple-element.301.refs_2_, bf16[576,1024]{1,0:T(8,128)(2,1)} %get-tuple-element.304.refs_3_, ...), custom_call_target="tpu_custom_call" | custom-call | flops 9663676416 | bytes 15466496 | tf_op jit(solution)/shard_map/weight_grad/pallas_call | solution.py:358
  693.0 3.5 all-to-all-start.17
  698.0 6.5 all-to-all-done.17
  (575 shorter events, 220.1 us)
Async XLA Ops:
  0.6 30.1 %collective-permute-start = (bf16[64,2048]{1,0:T(8,128)(2,1)}, bf16[64,2048]{1,0:T(8,128)(2,1)}, u32[]{:S(2)}, u32[]{:S(2)}) collective-permute-start(bf16[64,2048]{1,0:T(8,128)(2,1)} %param.17), channel_id=1, source_target_pairs={{0,1},{1,2},{2,3},{3,0},{4,5},{5,6},{6,7},{7,4},{8,9},{9,10},{10,1... | collective-permute-start | bytes 786440 | tf_op jit(solution)/shard_map/ppermute | solution.py:423
  2.3 28.5 %collective-permute-start.1 = (bf16[64,2048]{1,0:T(8,128)(2,1)}, bf16[64,2048]{1,0:T(8,128)(2,1)}, u32[]{:S(2)}, u32[]{:S(2)}) collective-permute-start(bf16[64,2048]{1,0:T(8,128)(2,1)} %param.17), channel_id=1, source_target_pairs={{0,2},{1,3},{2,0},{3,1},{4,6},{5,7},{6,4},{7,5},{8,10},{9,11},{10,... | collective-permute-start | bytes 786440 | tf_op jit(solution)/shard_map/ppermute | solution.py:423
  2.6 28.1 %collective-permute-start.2 = (bf16[64,2048]{1,0:T(8,128)(2,1)}, bf16[64,2048]{1,0:T(8,128)(2,1)}, u32[]{:S(2)}, u32[]{:S(2)}) collective-permute-start(bf16[64,2048]{1,0:T(8,128)(2,1)} %param.17), channel_id=1, source_target_pairs={{0,3},{1,0},{2,1},{3,2},{4,7},{5,4},{6,5},{7,6},{8,11},{9,8},{10,9... | collective-permute-start | bytes 786440 | tf_op jit(solution)/shard_map/ppermute | solution.py:423
  9.8 24.0 %all-to-all-start = ((bf16[4,64,1664]{2,1,0:T(8,128)(2,1)}), bf16[4,64,1664]{2,1,0:T(8,128)(2,1)}, u32[]{:S(2)}, u32[]{:S(2)}) async-start(bf16[4,64,1664]{2,1,0:T(8,128)(2,1)} %pack.1), calls=%async_computation | async-start | bytes 1703936 | tf_op jit(solution)/shard_map/all_to_all | solution.py:417
  33.8 97.4 %collective-permute-start.3 = (bf16[4,64,1664]{2,1,0:T(8,128)(2,1)}, bf16[4,64,1664]{2,1,0:T(8,128)(2,1)}, u32[]{:S(2)}, u32[]{:S(2)}) collective-permute-start(bf16[4,64,1664]{2,1,0:T(8,128)(2,1)} %all-to-all-done.refs_0_), channel_id=1, source_target_pairs={{0,1},{1,2},{2,3},{3,0},{4,5},{5,6},{6,7},{7,4},{8,9},{9,10},{10,1... | collective-permute-start | bytes 2555912 | tf_op jit(solution)/shard_map/ppermute | solution.py:423
  34.7 96.5 %collective-permute-start.4 = (bf16[4,64,1664]{2,1,0:T(8,128)(2,1)}, bf16[4,64,1664]{2,1,0:T(8,128)(2,1)}, u32[]{:S(2)}, u32[]{:S(2)}) collective-permute-start(bf16[4,64,1664]{2,1,0:T(8,128)(2,1)} %all-to-all-done.refs_0_), channel_id=1, source_target_pairs={{0,2},{1,3},{2,0},{3,1},{4,6},{5,7},{6,4},{7,5},{8,10},{9,11},{10,... | collective-permute-start | bytes 2555912 | tf_op jit(solution)/shard_map/ppermute | solution.py:423
  37.3 93.9 %collective-permute-start.5 = (bf16[4,64,1664]{2,1,0:T(8,128)(2,1)}, bf16[4,64,1664]{2,1,0:T(8,128)(2,1)}, u32[]{:S(2)}, u32[]{:S(2)}) collective-permute-start(bf16[4,64,1664]{2,1,0:T(8,128)(2,1)} %all-to-all-done.refs_0_), channel_id=1, source_target_pairs={{0,3},{1,0},{2,1},{3,2},{4,7},{5,4},{6,5},{7,6},{8,11},{9,8},{10,9... | collective-permute-start | bytes 2555912 | tf_op jit(solution)/shard_map/ppermute | solution.py:423
  39.5 99.0 %collective-permute-start.6 = (bf16[4,64,1664]{2,1,0:T(8,128)(2,1)}, bf16[4,64,1664]{2,1,0:T(8,128)(2,1)}, u32[]{:S(2)}, u32[]{:S(2)}) collective-permute-start(bf16[4,64,1664]{2,1,0:T(8,128)(2,1)} %all-to-all-done.refs_0_), channel_id=1, source_target_pairs={{0,16},{16,0},{1,17},{17,1},{2,18},{18,2},{3,19},{19,3},{4,20},{20... | collective-permute-start | bytes 2555912 | tf_op jit(solution)/shard_map/ppermute | solution.py:426
  42.1 53.4 %all-to-all-start.1 = ((bf16[4,4,64,2048]{3,2,1,0:T(8,128)(2,1)}), bf16[4,4,64,2048]{3,2,1,0:T(8,128)(2,1)}, u32[]{:S(2)}, u32[]{:S(2)}) async-start(bf16[4,4,64,2048]{3,2,1,0:T(8,128)(2,1)} %broadcast_in_dim.54), calls=%async_computation.1 | async-start | bytes 8388608 | tf_op jit(solution)/shard_map/all_to_all | solution.py:417
  46.9 48.6 %copy-start.46 = (bf16[136,2048]{1,0:T(8,128)(2,1)S(1)}, bf16[136,2048]{1,0:T(8,128)(2,1)}, u32[]{:S(2)}) copy-start(bf16[136,2048]{1,0:T(8,128)(2,1)} %reshape.424) | copy-start | bytes 1671172
  97.2 31.2 %all-to-all-start.2 = ((bf16[4,136,2048]{2,1,0:T(8,128)(2,1)}), bf16[4,136,2048]{2,1,0:T(8,128)(2,1)}, u32[]{:S(2)}, u32[]{:S(2)}) async-start(bf16[4,136,2048]{2,1,0:T(8,128)(2,1)} %broadcast_in_dim.55), calls=%async_computation.2 | async-start | bytes 4456448 | tf_op jit(solution)/shard_map/all_to_all | solution.py:417
  131.2 7.3 %collective-permute-start.7 = (bf16[4,64,1664]{2,1,0:T(8,128)(2,1)}, bf16[4,64,1664]{2,1,0:T(8,128)(2,1)S(1)}, u32[]{:S(2)}, u32[]{:S(2)}) collective-permute-start(bf16[4,64,1664]{2,1,0:T(8,128)(2,1)} %collective-permute-done.3.refs_1_), channel_id=1, source_target_pairs={{0,16},{16,0},{1,17},{17,1},{2,18},{18,2},{3,19},{19,3},{4,20},{20... | collective-permute-start | bytes 2555912 | tf_op jit(solution)/shard_map/ppermute | solution.py:426
  131.3 7.3 %collective-permute-start.8 = (bf16[4,64,1664]{2,1,0:T(8,128)(2,1)}, bf16[4,64,1664]{2,1,0:T(8,128)(2,1)}, u32[]{:S(2)}, u32[]{:S(2)}) collective-permute-start(bf16[4,64,1664]{2,1,0:T(8,128)(2,1)} %collective-permute-done.4.refs_2_), channel_id=1, source_target_pairs={{0,16},{16,0},{1,17},{17,1},{2,18},{18,2},{3,19},{19,3},{4,20},{20... | collective-permute-start | bytes 2555912 | tf_op jit(solution)/shard_map/ppermute | solution.py:426
  131.8 6.8 collective-permute-start.9
  134.1 51.5 %copy-start = (f32[544,544]{1,0:T(8,128)}, f32[544,544]{1,0:T(8,128)S(1)}, u32[]{:S(2)}) copy-start(f32[544,544]{1,0:T(8,128)S(1)} %fusion.22.pair_ref) | copy-start | bytes 3551236
  134.1 63.5 %all-to-all-start.3 = ((bf16[4,1,72,2048]{3,2,1,0:T(8,128)(2,1)}), bf16[4,1,72,2048]{3,2,1,0:T(8,128)(2,1)}, u32[]{:S(2)}, u32[]{:S(2)}) async-start(bf16[4,1,72,2048]{3,2,1,0:T(8,128)(2,1)} %bitcast.36), calls=%async_computation.3 | async-start | bytes 2359296 | tf_op jit(solution)/shard_map/all_to_all | solution.py:417
  163.3 54.1 %collective-permute-start.12 = (bf16[136,2048]{1,0:T(8,128)(2,1)}, bf16[136,2048]{1,0:T(8,128)(2,1)}, u32[]{:S(2)}, u32[]{:S(2)}) collective-permute-start(bf16[136,2048]{1,0:T(8,128)(2,1)} %pad_maximum_fusion.3), channel_id=1, source_target_pairs={{0,1},{1,2},{2,3},{3,0},{4,5},{5,6},{6,7},{7,4},{8,9},{9,10},{10,1... | collective-permute-start | bytes 1671176 | tf_op jit(solution)/shard_map/ppermute | solution.py:423
  163.4 54.0 %collective-permute-start.13 = (bf16[136,2048]{1,0:T(8,128)(2,1)}, bf16[136,2048]{1,0:T(8,128)(2,1)}, u32[]{:S(2)}, u32[]{:S(2)}) collective-permute-start(bf16[136,2048]{1,0:T(8,128)(2,1)} %pad_maximum_fusion.3), channel_id=1, source_target_pairs={{0,2},{1,3},{2,0},{3,1},{4,6},{5,7},{6,4},{7,5},{8,10},{9,11},{10,... | collective-permute-start | bytes 1671176 | tf_op jit(solution)/shard_map/ppermute | solution.py:423
  164.8 52.6 %collective-permute-start.14 = (bf16[136,2048]{1,0:T(8,128)(2,1)}, bf16[136,2048]{1,0:T(8,128)(2,1)}, u32[]{:S(2)}, u32[]{:S(2)}) collective-permute-start(bf16[136,2048]{1,0:T(8,128)(2,1)} %pad_maximum_fusion.3), channel_id=1, source_target_pairs={{0,3},{1,0},{2,1},{3,2},{4,7},{5,4},{6,5},{7,6},{8,11},{9,8},{10,9... | collective-permute-start | bytes 1671176 | tf_op jit(solution)/shard_map/ppermute | solution.py:423
  167.2 9.2 %collective-permute-start.10 = (f32[2,544]{0,1:T(8,128)S(1)}, f32[2,544]{0,1:T(8,128)S(1)}, u32[]{:S(2)}, u32[]{:S(2)}) collective-permute-start(f32[2,544]{0,1:T(8,128)S(1)} %copy.99), channel_id=1, source_target_pairs={{0,4},{4,0},{8,12},{12,8},{1,5},{5,1},{9,13},{13,9},{2,6},{6,2},{1... | collective-permute-start | bytes 13064 | tf_op jit(solution)/shard_map/ppermute | solution.py:414
  176.5 7.7 %collective-permute-start.11 = (f32[2,544]{0,1:T(8,128)S(1)}, f32[2,544]{0,1:T(8,128)S(1)}, u32[]{:S(2)}, u32[]{:S(2)}) collective-permute-start(f32[2,544]{0,1:T(8,128)S(1)} %add.367), channel_id=1, source_target_pairs={{0,8},{4,12},{8,0},{12,4},{1,9},{5,13},{9,1},{13,5},{2,10},{6,14},... | collective-permute-start | bytes 13064 | tf_op jit(solution)/shard_map/ppermute | solution.py:414
  184.2 48.7 %collective-permute-start.15 = (bf16[4,4,64,2048]{3,2,1,0:T(8,128)(2,1)}, bf16[4,4,64,2048]{3,2,1,0:T(8,128)(2,1)}, u32[]{:S(2)}, u32[]{:S(2)}) collective-permute-start(bf16[4,4,64,2048]{3,2,1,0:T(8,128)(2,1)} %all-to-all-done.1), channel_id=1, source_target_pairs={{0,16},{16,0},{1,17},{17,1},{2,18},{18,2},{3,19},{19,3},{4,20},{20... | collective-permute-start | bytes 12582920 | tf_op jit(solution)/shard_map/ppermute | solution.py:426
  197.6 13.5 %all-to-all-start.4 = ((bf16[4,136,512]{2,1,0:T(8,128)(2,1)}), bf16[4,136,512]{2,1,0:T(8,128)(2,1)}, u32[]{:S(2)}, u32[]{:S(2)}) async-start(bf16[4,136,512]{2,1,0:T(8,128)(2,1)} %bitcast.37), calls=%async_computation.4 | async-start | bytes 1114112 | tf_op jit(solution)/shard_map/all_to_all | solution.py:417
  222.6 45.3 %all-to-all-start.5 = ((bf16[4,3,72,2048]{3,2,1,0:T(8,128)(2,1)}), bf16[4,3,72,2048]{3,2,1,0:T(8,128)(2,1)}, u32[]{:S(2)}, u32[]{:S(2)}) async-start(bf16[4,3,72,2048]{3,2,1,0:T(8,128)(2,1)} %bitcast.319), calls=%async_computation.5 | async-start | bytes 7077888 | tf_op jit(solution)/shard_map/all_to_all | solution.py:417
  238.1 32.1 %collective-permute-start.16 = (bf16[136,2048]{1,0:T(8,128)(2,1)}, bf16[136,2048]{1,0:T(8,128)(2,1)}, u32[]{:S(2)}, u32[]{:S(2)}) collective-permute-start(bf16[136,2048]{1,0:T(8,128)(2,1)} %multiply_convert_fusion), channel_id=1, source_target_pairs={{0,1},{1,2},{2,3},{3,0},{4,5},{5,6},{6,7},{7,4},{8,9},{9,10},{10,1... | collective-permute-start | bytes 1671176 | tf_op jit(solution)/shard_map/ppermute | solution.py:423
  270.1 24.7 %collective-permute-start.17 = (bf16[136,2048]{1,0:T(8,128)(2,1)}, bf16[136,2048]{1,0:T(8,128)(2,1)}, u32[]{:S(2)}, u32[]{:S(2)}) collective-permute-start(bf16[136,2048]{1,0:T(8,128)(2,1)} %multiply_convert_fusion), channel_id=1, source_target_pairs={{0,2},{1,3},{2,0},{3,1},{4,6},{5,7},{6,4},{7,5},{8,10},{9,11},{10,... | collective-permute-start | bytes 1671176 | tf_op jit(solution)/shard_map/ppermute | solution.py:423
  272.1 34.5 %collective-permute-start.18 = (bf16[136,2048]{1,0:T(8,128)(2,1)}, bf16[136,2048]{1,0:T(8,128)(2,1)}, u32[]{:S(2)}, u32[]{:S(2)}) collective-permute-start(bf16[136,2048]{1,0:T(8,128)(2,1)} %multiply_convert_fusion), channel_id=1, source_target_pairs={{0,3},{1,0},{2,1},{3,2},{4,7},{5,4},{6,5},{7,6},{8,11},{9,8},{10,9... | collective-permute-start | bytes 1671176 | tf_op jit(solution)/shard_map/ppermute | solution.py:423
  276.2 31.4 %all-to-all-start.6 = ((bf16[4,2,72,2048]{3,2,1,0:T(8,128)(2,1)}), bf16[4,2,72,2048]{3,2,1,0:T(8,128)(2,1)}, u32[]{:S(2)}, u32[]{:S(2)}) async-start(bf16[4,2,72,2048]{3,2,1,0:T(8,128)(2,1)} %bitcast.321), calls=%async_computation.6 | async-start | bytes 4718592 | tf_op jit(solution)/shard_map/all_to_all | solution.py:417
  311.6 31.7 %all-to-all-start.7 = ((bf16[4,2,72,2048]{3,2,1,0:T(8,128)(2,1)}), bf16[4,2,72,2048]{3,2,1,0:T(8,128)(2,1)}, u32[]{:S(2)}, u32[]{:S(2)}) async-start(bf16[4,2,72,2048]{3,2,1,0:T(8,128)(2,1)} %bitcast.322), calls=%async_computation.7 | async-start | bytes 4718592 | tf_op jit(solution)/shard_map/all_to_all | solution.py:417
  343.4 29.2 %all-to-all-start.8 = ((bf16[4,72,2176]{2,1,0:T(8,128)(2,1)}), bf16[4,72,2176]{2,1,0:T(8,128)(2,1)}, u32[]{:S(2)}, u32[]{:S(2)}) async-start(bf16[4,72,2176]{2,1,0:T(8,128)(2,1)} %get-tuple-element.219), calls=%async_computation.8 | async-start | bytes 2506752 | tf_op jit(solution)/shard_map/all_to_all | solution.py:417
  375.3 19.6 %all-to-all-start.9 = ((bf16[4,72,2176]{2,1,0:T(8,128)(2,1)}), bf16[4,72,2176]{2,1,0:T(8,128)(2,1)}, u32[]{:S(2)}, u32[]{:S(2)}) async-start(bf16[4,72,2176]{2,1,0:T(8,128)(2,1)} %get-tuple-element.227), calls=%async_computation.9 | async-start | bytes 2506752 | tf_op jit(solution)/shard_map/all_to_all | solution.py:417
  379.6 68.1 %collective-permute-start.19 = (bf16[136,2176]{1,0:T(8,128)(2,1)}, bf16[136,2176]{1,0:T(8,128)(2,1)}, u32[]{:S(2)}, u32[]{:S(2)}) collective-permute-start(bf16[136,2176]{1,0:T(8,128)(2,1)} %fusion.2), channel_id=1, source_target_pairs={{0,3},{1,0},{2,1},{3,2},{4,7},{5,4},{6,5},{7,6},{8,11},{9,8},{10,9... | collective-permute-start | bytes 1775624 | tf_op jit(solution)/shard_map/ppermute | solution.py:423
  397.7 50.1 %collective-permute-start.20 = (bf16[136,2176]{1,0:T(8,128)(2,1)}, bf16[136,2176]{1,0:T(8,128)(2,1)}, u32[]{:S(2)}, u32[]{:S(2)}) collective-permute-start(bf16[136,2176]{1,0:T(8,128)(2,1)} %fusion.3), channel_id=1, source_target_pairs={{0,2},{1,3},{2,0},{3,1},{4,6},{5,7},{6,4},{7,5},{8,10},{9,11},{10,... | collective-permute-start | bytes 1775624 | tf_op jit(solution)/shard_map/ppermute | solution.py:423
  399.5 19.4 %all-to-all-start.10 = ((bf16[4,72,2176]{2,1,0:T(8,128)(2,1)}), bf16[4,72,2176]{2,1,0:T(8,128)(2,1)}, u32[]{:S(2)}, u32[]{:S(2)}) async-start(bf16[4,72,2176]{2,1,0:T(8,128)(2,1)} %get-tuple-element.237), calls=%async_computation.10 | async-start | bytes 2506752 | tf_op jit(solution)/shard_map/all_to_all | solution.py:417
  421.6 26.2 %collective-permute-start.21 = (bf16[136,2176]{1,0:T(8,128)(2,1)}, bf16[136,2176]{1,0:T(8,128)(2,1)}, u32[]{:S(2)}, u32[]{:S(2)}) collective-permute-start(bf16[136,2176]{1,0:T(8,128)(2,1)} %fusion.4), channel_id=1, source_target_pairs={{0,1},{1,2},{2,3},{3,0},{4,5},{5,6},{6,7},{7,4},{8,9},{9,10},{10,1... | collective-permute-start | bytes 1775624 | tf_op jit(solution)/shard_map/ppermute | solution.py:423
  423.9 19.5 %all-to-all-start.11 = ((bf16[4,72,2176]{2,1,0:T(8,128)(2,1)}), bf16[4,72,2176]{2,1,0:T(8,128)(2,1)}, u32[]{:S(2)}, u32[]{:S(2)}) async-start(bf16[4,72,2176]{2,1,0:T(8,128)(2,1)} %get-tuple-element.245), calls=%async_computation.11 | async-start | bytes 2506752 | tf_op jit(solution)/shard_map/all_to_all | solution.py:417
  461.0 6.0 collective-permute-start.22
  463.8 6.8 collective-permute-start.23
  464.3 6.2 collective-permute-start.24
  470.6 42.3 %all-to-all-start.12 = ((bf16[4,2,72,2048]{3,2,1,0:T(8,128)(2,1)}), bf16[4,2,72,2048]{3,2,1,0:T(8,128)(2,1)}, u32[]{:S(2)}, u32[]{:S(2)}) async-start(bf16[4,2,72,2048]{3,2,1,0:T(8,128)(2,1)} %bitcast.320), calls=%async_computation.12 | async-start | bytes 4718592 | tf_op jit(solution)/shard_map/all_to_all | solution.py:417
  492.2 14.0 %collective-permute-start.25 = (f32[2,544]{0,1:T(8,128)S(1)}, f32[2,544]{0,1:T(8,128)S(1)}, u32[]{:S(2)}, u32[]{:S(2)}) collective-permute-start(f32[2,544]{0,1:T(8,128)S(1)} %copy.104), channel_id=1, source_target_pairs={{0,4},{4,0},{8,12},{12,8},{1,5},{5,1},{9,13},{13,9},{2,6},{6,2},{1... | collective-permute-start | bytes 13064 | tf_op jit(solution)/shard_map/ppermute | solution.py:414
  506.2 6.6 collective-permute-start.26
  528.1 16.6 %collective-permute-start.29 = (bf16[1024,1536]{1,0:T(8,128)(2,1)}, bf16[1024,1536]{1,0:T(8,128)(2,1)}, u32[]{:S(2)}, u32[]{:S(2)}) collective-permute-start(bf16[1024,1536]{1,0:T(8,128)(2,1)} %weight_grad.8), channel_id=1, source_target_pairs={{0,16},{16,0},{1,17},{17,1},{2,18},{18,2},{3,19},{19,3},{4,20},{20... | collective-permute-start | bytes 9437192 | tf_op jit(solution)/shard_map/ppermute | solution.py:426
  528.1 43.4 %collective-permute-start.27 = (bf16[136,2048]{1,0:T(8,128)(2,1)}, bf16[136,2048]{1,0:T(8,128)(2,1)}, u32[]{:S(2)}, u32[]{:S(2)}) collective-permute-start(bf16[136,2048]{1,0:T(8,128)(2,1)} %get-tuple-element.344), channel_id=1, source_target_pairs={{0,2},{1,3},{2,0},{3,1},{4,6},{5,7},{6,4},{7,5},{8,10},{9,11},{10,... | collective-permute-start | bytes 1671176 | tf_op jit(solution)/shard_map/ppermute | solution.py:423
  528.6 42.9 %collective-permute-start.28 = (bf16[136,2048]{1,0:T(8,128)(2,1)}, bf16[136,2048]{1,0:T(8,128)(2,1)}, u32[]{:S(2)}, u32[]{:S(2)}) collective-permute-start(bf16[136,2048]{1,0:T(8,128)(2,1)} %get-tuple-element.343), channel_id=1, source_target_pairs={{0,1},{1,2},{2,3},{3,0},{4,5},{5,6},{6,7},{7,4},{8,9},{9,10},{10,1... | collective-permute-start | bytes 1671176 | tf_op jit(solution)/shard_map/ppermute | solution.py:423
  530.9 31.4 %all-to-all-start.13 = ((bf16[4,136,2048]{2,1,0:T(8,128)(2,1)}), bf16[4,136,2048]{2,1,0:T(8,128)(2,1)}, u32[]{:S(2)}, u32[]{:S(2)}) async-start(bf16[4,136,2048]{2,1,0:T(8,128)(2,1)} %broadcast_in_dim.62), calls=%async_computation.13 | async-start | bytes 4456448 | tf_op jit(solution)/shard_map/all_to_all | solution.py:417
  562.3 34.6 %all-to-all-start.14 = ((bf16[4,2,72,2048]{3,2,1,0:T(8,128)(2,1)}), bf16[4,2,72,2048]{3,2,1,0:T(8,128)(2,1)}, u32[]{:S(2)}, u32[]{:S(2)}) async-start(bf16[4,2,72,2048]{3,2,1,0:T(8,128)(2,1)} %bitcast.62), calls=%async_computation.14 | async-start | bytes 4718592 | tf_op jit(solution)/shard_map/all_to_all | solution.py:417
  568.2 19.3 %collective-permute-start.30 = (bf16[256,1536]{1,0:T(8,128)(2,1)S(1)}, bf16[256,1536]{1,0:T(8,128)(2,1)S(1)}, u32[]{:S(2)}, u32[]{:S(2)}) collective-permute-start(bf16[256,1536]{1,0:T(8,128)(2,1)S(1)} %copy-done.57), channel_id=1, source_target_pairs={{0,1},{1,2},{2,3},{3,0},{4,5},{5,6},{6,7},{7,4},{8,9},{9,10},{10,1... | collective-permute-start | bytes 2359304 | tf_op jit(solution)/shard_map/ppermute | solution.py:423
  575.2 16.5 %collective-permute-start.32 = (bf16[256,2048]{1,0:T(8,128)(2,1)}, bf16[256,2048]{1,0:T(8,128)(2,1)S(1)}, u32[]{:S(2)}, u32[]{:S(2)}) collective-permute-start(bf16[256,2048]{1,0:T(8,128)(2,1)} %weight_grad.10), channel_id=1, source_target_pairs={{0,16},{16,0},{1,17},{17,1},{2,18},{18,2},{3,19},{19,3},{4,20},{20... | collective-permute-start | bytes 3145736 | tf_op jit(solution)/shard_map/ppermute | solution.py:426
  582.4 35.4 %collective-permute-start.33 = (bf16[512,2048]{1,0:T(8,128)(2,1)}, bf16[512,2048]{1,0:T(8,128)(2,1)}, u32[]{:S(2)}, u32[]{:S(2)}) collective-permute-start(bf16[512,2048]{1,0:T(8,128)(2,1)} %weight_grad.11), channel_id=1, source_target_pairs={{0,16},{16,0},{1,17},{17,1},{2,18},{18,2},{3,19},{19,3},{4,20},{20... | collective-permute-start | bytes 6291464 | tf_op jit(solution)/shard_map/ppermute | solution.py:426
  589.1 23.9 %collective-permute-start.31 = (bf16[256,1536]{1,0:T(8,128)(2,1)S(1)}, bf16[256,1536]{1,0:T(8,128)(2,1)}, u32[]{:S(2)}, u32[]{:S(2)}) collective-permute-start(bf16[256,1536]{1,0:T(8,128)(2,1)S(1)} %fusion.20), channel_id=1, source_target_pairs={{0,1},{1,2},{2,3},{3,0},{4,5},{5,6},{6,7},{7,4},{8,9},{9,10},{10,1... | collective-permute-start | bytes 2359304 | tf_op jit(solution)/shard_map/ppermute | solution.py:423
  597.0 33.9 %all-to-all-start.15 = ((bf16[4,136,2048]{2,1,0:T(8,128)(2,1)}), bf16[4,136,2048]{2,1,0:T(8,128)(2,1)S(1)}, u32[]{:S(2)}, u32[]{:S(2)}) async-start(bf16[4,136,2048]{2,1,0:T(8,128)(2,1)} %bitcast.323), calls=%async_computation.15 | async-start | bytes 4456448 | tf_op jit(solution)/shard_map/all_to_all | solution.py:417
  613.0 61.3 %collective-permute-start.35 = (bf16[1024,2048]{1,0:T(8,128)(2,1)}, bf16[1024,2048]{1,0:T(8,128)(2,1)}, u32[]{:S(2)}, u32[]{:S(2)}) collective-permute-start(bf16[1024,2048]{1,0:T(8,128)(2,1)} %weight_grad.13), channel_id=1, source_target_pairs={{0,16},{16,0},{1,17},{17,1},{2,18},{18,2},{3,19},{19,3},{4,20},{20... | collective-permute-start | bytes 12582920 | tf_op jit(solution)/shard_map/ppermute | solution.py:426
  615.7 74.7 %collective-permute-start.36 = (bf16[256,1536]{1,0:T(8,128)(2,1)}, bf16[256,1536]{1,0:T(8,128)(2,1)}, u32[]{:S(2)}, u32[]{:S(2)}) collective-permute-start(bf16[256,1536]{1,0:T(8,128)(2,1)} %fusion.19), channel_id=1, source_target_pairs={{0,1},{1,2},{2,3},{3,0},{4,5},{5,6},{6,7},{7,4},{8,9},{9,10},{10,1... | collective-permute-start | bytes 2359304 | tf_op jit(solution)/shard_map/ppermute | solution.py:423
  630.9 55.6 %all-to-all-start.16 = ((bf16[4,64,2048]{2,1,0:T(8,128)(2,1)}), bf16[4,64,2048]{2,1,0:T(8,128)(2,1)}, u32[]{:S(2)}, u32[]{:S(2)}) async-start(bf16[4,64,2048]{2,1,0:T(8,128)(2,1)} %convert_element_type.339), calls=%async_computation.16 | async-start | bytes 2097152 | tf_op jit(solution)/shard_map/all_to_all | solution.py:951
  644.6 1.5 collective-permute-start.37
  646.1 5.0 collective-permute-start.40
  649.1 4.0 collective-permute-start.39
  649.7 4.0 collective-permute-start.38
  653.8 5.7 collective-permute-start.43
  654.4 7.5 %collective-permute-start.42 = (f32[20,64]{1,0:T(8,128)S(1)}, f32[20,64]{1,0:T(8,128)S(1)}, u32[]{:S(2)}, u32[]{:S(2)}) collective-permute-start(f32[20,64]{1,0:T(8,128)S(1)} %bitcast.334), channel_id=1, source_target_pairs={{0,2},{1,3},{2,0},{3,1},{4,6},{5,7},{6,4},{7,5},{8,10},{9,11},{10,... | collective-permute-start | bytes 15368 | tf_op jit(solution)/shard_map/ppermute | solution.py:423
  657.6 15.5 %collective-permute-start.41 = (f32[20,64]{1,0:T(8,128)S(1)}, f32[20,64]{1,0:T(8,128)S(1)}, u32[]{:S(2)}, u32[]{:S(2)}) collective-permute-start(f32[20,64]{1,0:T(8,128)S(1)} %bitcast.336), channel_id=1, source_target_pairs={{0,1},{1,2},{2,3},{3,0},{4,5},{5,6},{6,7},{7,4},{8,9},{9,10},{10,1... | collective-permute-start | bytes 15368 | tf_op jit(solution)/shard_map/ppermute | solution.py:423
  659.4 29.3 %collective-permute-start.34 = (bf16[136,2048]{1,0:T(8,128)(2,1)S(1)}, bf16[136,2048]{1,0:T(8,128)(2,1)S(1)}, u32[]{:S(2)}, u32[]{:S(2)}) collective-permute-start(bf16[136,2048]{1,0:T(8,128)(2,1)S(1)} %copy-done.59), channel_id=1, source_target_pairs={{0,3},{1,0},{2,1},{3,2},{4,7},{5,4},{6,5},{7,6},{8,11},{9,8},{10,9... | collective-permute-start | bytes 1671176 | tf_op jit(solution)/shard_map/ppermute | solution.py:423
  693.0 11.5 %all-to-all-start.17 = ((bf16[4,64,1536]{2,1,0:T(8,128)(2,1)}), bf16[4,64,1536]{2,1,0:T(8,128)(2,1)S(1)}, u32[]{:S(2)}, u32[]{:S(2)}) async-start(bf16[4,64,1536]{2,1,0:T(8,128)(2,1)} %bitcast.117), calls=%async_computation.17 | async-start | bytes 1572864 | tf_op jit(solution)/shard_map/all_to_all | solution.py:417
  (120 other events, 922.2 us)
